TPU v7x, 32 devices: a whole 2x2x4 slice. The times are simulated.
32 devices in a mesh: fsdp: 8 (over y, x, core), ctx: 4 (over z).
Axes of the slice: x: 2, y: 2, z: 4, core: 2. Of those that a mesh axis runs over, the one named last changes fastest.
Arguments:
- features: bfloat16 [3, 4096, 8192], P(None, 'ctx', 'fsdp'), may hold values from -6 to 6
- short_taps: float32 [3, 3, 8192], P(None, None, 'fsdp'), may hold values from -3.5 to 3.5
- decay_rates: float32 [512, 16], P('fsdp'), may hold values from 6.1035156e-05 to 0.1
- mode_gains: float32 [512, 16], P('fsdp'), may hold values from -2.5 to 2.5
- cotangent: bfloat16 [4096, 8192], P('ctx', 'fsdp'), may hold values from -6 to 6
Outputs:
- mixer_output: bfloat16 [4096, 8192], P('ctx', 'fsdp')
- feature_grads: bfloat16 [3, 4096, 8192], P(None, 'ctx', 'fsdp')
- gain_grads: float32 [512, 16], P('fsdp')
- rate_grads: float32 [512, 16], P('fsdp')
All inputs are finite; a program needn't handle non-finite values.
Results may differ from a plain program's by a relative error of at most 0.0048.
Values may be sent and summed in bfloat16 or wider, within the bound.
No kernel may reach another device: no remote copies, remote signals or barrier semaphores. Data moves between devices by JAX's collectives and lax.ppermute only.
A program may use at most 128 MiB of HBM per device.

v0:
```python
import jax
import jax.numpy as jnp
from jax import lax
from jax.sharding import PartitionSpec as P

precise = lax.Precision.HIGHEST
threepass = lax.Precision.HIGH


def passed_along(value, axis, steps):
    count = lax.axis_size(axis)
    leading, last = (max(0, -steps), min(count, count - steps))
    return lax.ppermute(value, axis, [(source, source + steps) for source in range(leading, last)])


def diagonal_sums(gram_acc):
    group_count, block_len, width_same = gram_acc.shape
    flipped = jnp.flip(gram_acc, axis=2)
    padded = jnp.concatenate([flipped, jnp.zeros_like(flipped)], axis=2)
    flattened = padded.reshape(group_count, 2 * block_len * block_len)[
        :, : block_len * (2 * block_len - 1)
    ]
    sheared = flattened.reshape(group_count, block_len, 2 * block_len - 1)
    return jnp.sum(sheared, axis=1)[:, block_len - 1 :]


def short_conv(taps_table, row_data, tokens, rim_rows, forward):
    summed = jnp.zeros((3, tokens, row_data.shape[2]), jnp.float32)
    for offset in range(taps_table.shape[1]):
        start_row = rim_rows - offset if forward else offset
        summed = (
            summed + taps_table[:, offset, None, :] * row_data[:, start_row : start_row + tokens, :]
        )
    return summed


def per_device(features, short_taps, decay_rates, mode_gains, cotangent):
    tokens = features.shape[1]
    channels = features.shape[2]
    group_count = decay_rates.shape[0]
    order_count = decay_rates.shape[1]
    members = channels // group_count
    rim_rows = short_taps.shape[1] - 1
    block_len = 128
    block_count = tokens // block_len
    ctx_count = lax.axis_size("ctx")
    ctx_index = lax.axis_index("ctx")
    earlier_rows = passed_along(features[:, tokens - rim_rows :, :], "ctx", 1)
    extended = jnp.concatenate([earlier_rows, features], axis=1)
    shaped = short_conv(short_taps, extended, tokens, rim_rows, True)
    query_part, key_part, value_part = (shaped[0], shaped[1], shaped[2])
    product = (key_part * value_part).astype(jnp.bfloat16)
    adjoint = cotangent * query_part
    grouped_z = product.reshape(tokens, group_count, members)
    grouped_e = adjoint.reshape(tokens, group_count, members)
    mode_coefs = mode_gains * jnp.sqrt(2.0 * decay_rates)
    rate_axis = decay_rates[:, :, None]
    positions = jnp.arange(tokens, dtype=jnp.float32)[None, None, :]
    decay_from = jnp.exp(-rate_axis * positions)
    end_tables = jnp.stack([jnp.flip(decay_from, 2), -jnp.flip(positions * decay_from, 2)])
    end_states = jnp.einsum(
        "kgns,sgm->kngm", end_tables, grouped_z.astype(jnp.float32), precision=threepass
    )
    start_state = jnp.einsum("gnt,tgm->ngm", decay_from, grouped_e, precision=precise)
    local_states = jnp.stack([end_states[0], end_states[1], start_state]).reshape(
        3, order_count, channels
    )
    rate_cols = jnp.repeat(decay_rates.T, members, axis=1)
    everyone = lax.all_gather(local_states[None], "ctx", axis=0, tiled=True)
    device_ids = jnp.arange(ctx_count, dtype=jnp.int32)
    ahead_steps = (ctx_index - 1 - device_ids).astype(jnp.float32)[:, None, None]
    behind_steps = (device_ids - ctx_index - 1).astype(jnp.float32)[:, None, None]
    ahead_weight = jnp.where(
        ahead_steps >= 0, jnp.exp(-rate_cols[None] * (tokens * jnp.maximum(ahead_steps, 0.0))), 0.0
    )
    behind_weight = jnp.where(
        behind_steps >= 0,
        jnp.exp(-rate_cols[None] * (tokens * jnp.maximum(behind_steps, 0.0))),
        0.0,
    )
    prev_state = jnp.sum(ahead_weight * everyone[:, 0], axis=0)
    prev_lagged = jnp.sum(
        ahead_weight * (everyone[:, 1] - tokens * ahead_steps * everyone[:, 0]), axis=0
    )
    next_state = jnp.sum(behind_weight * everyone[:, 2], axis=0)
    lag_axis = jnp.arange(block_len, dtype=jnp.float32)[None, None, :]
    block_pow = jnp.exp(-rate_axis * lag_axis)
    block_after = block_pow * jnp.exp(-rate_axis)
    block_moments = jnp.stack([block_after, (lag_axis + 1.0) * block_after])
    coef_after = mode_coefs[:, :, None] * block_after
    block_ends = jnp.stack([jnp.flip(block_pow, 2), -jnp.flip(lag_axis * block_pow, 2)])
    coef_tail = mode_coefs[:, :, None] * jnp.flip(block_after, 2)
    block_span = jnp.exp(-decay_rates * block_len).T[:, :, None]
    filter_taps = jnp.sum(mode_coefs[:, :, None] * block_pow, axis=1)
    lag_index = (
        jnp.arange(block_len, dtype=jnp.int32)[:, None]
        - jnp.arange(block_len, dtype=jnp.int32)[None, :]
    )
    toeplitz = jnp.where(lag_index[None] >= 0, filter_taps[:, jnp.maximum(lag_index, 0)], 0.0)
    z_blocks = grouped_z.reshape(block_count, block_len, group_count, members)
    e_blocks = grouped_e.reshape(block_count, block_len, group_count, members)

    def forward_block(carried_in, inputs):
        mode_state, lagged, first_acc, lag_acc, gram_acc = carried_in
        z_block, e_block = inputs
        z_wide = z_block.astype(jnp.float32)
        inside_part = jnp.einsum("gts,sgm->tgm", toeplitz, z_wide, precision=threepass)
        carried = jnp.einsum("gnt,ngm->tgm", coef_after, mode_state, precision=precise)
        moments = jnp.einsum("kgnt,tgm->kngm", block_moments, e_block, precision=precise)
        first_acc = first_acc + jnp.sum(moments[0] * mode_state, axis=2)
        lag_acc = lag_acc + jnp.sum(moments[0] * lagged - moments[1] * mode_state, axis=2)
        gram_acc = gram_acc + jnp.einsum("tgm,sgm->gts", e_block, z_wide, precision=precise)
        fresh_part = jnp.einsum("kgns,sgm->kngm", block_ends, z_wide, precision=threepass)
        new_lagged = block_span * lagged - block_len * block_span * mode_state + fresh_part[1]
        new_state = block_span * mode_state + fresh_part[0]
        return ((new_state, new_lagged, first_acc, lag_acc, gram_acc), inside_part + carried)

    zero_state = jnp.zeros((order_count, group_count, members), jnp.float32)
    zero_pairs = jnp.zeros((order_count, group_count), jnp.float32)
    zero_gram = jnp.zeros((group_count, block_len, block_len), jnp.float32)
    final_carry, inner_blocks = lax.scan(
        forward_block,
        (zero_state, zero_state, zero_pairs, zero_pairs, zero_gram),
        (z_blocks, e_blocks),
    )
    first_acc, lag_acc, gram_acc = (final_carry[2], final_carry[3], final_carry[4])

    def backward_block(later_state, e_block):
        inside_part = jnp.einsum("gts,tgm->sgm", toeplitz, e_block, precision=precise)
        carried = jnp.einsum("gns,ngm->sgm", coef_tail, later_state, precision=precise)
        fresh_part = jnp.einsum("gnt,tgm->ngm", block_pow, e_block, precision=precise)
        return (block_span * later_state + fresh_part, inside_part + carried)

    top_state, grad_blocks = lax.scan(backward_block, zero_state, e_blocks, reverse=True)
    prev_grouped = prev_state.reshape(order_count, group_count, members)
    lagged_grouped = prev_lagged.reshape(order_count, group_count, members)
    next_grouped = next_state.reshape(order_count, group_count, members)
    device_after = decay_from * jnp.exp(-rate_axis)
    inner_sum = inner_blocks.reshape(tokens, group_count, members) + jnp.einsum(
        "gnt,ngm->tgm", mode_coefs[:, :, None] * device_after, prev_grouped, precision=precise
    )
    first_moment = jnp.exp(-decay_rates).T[:, :, None] * start_state
    second_moment = jnp.einsum(
        "gnt,tgm->ngm", (positions + 1.0) * device_after, grouped_e, precision=precise
    )
    first_acc = first_acc + jnp.sum(first_moment * prev_grouped, axis=2)
    lag_acc = lag_acc + jnp.sum(
        first_moment * lagged_grouped - second_moment * prev_grouped, axis=2
    )
    device_tail = mode_coefs[:, :, None] * jnp.flip(device_after, 2)
    product_grad = grad_blocks.reshape(tokens, group_count, members) + jnp.einsum(
        "gns,ngm->sgm", device_tail, next_grouped, precision=precise
    )
    lag_totals = diagonal_sums(gram_acc)
    first_total = first_acc.T + jnp.sum(lag_totals[:, None, :] * block_pow, axis=2)
    lag_total = lag_acc.T - jnp.sum(lag_totals[:, None, :] * lag_axis * block_pow, axis=2)
    gain_part = jnp.sqrt(2.0 * decay_rates) * first_total
    rate_part = mode_coefs * (0.5 * first_total + decay_rates * lag_total)
    inner_flat = inner_sum.reshape(tokens, channels)
    mixer_output = (query_part * inner_flat).astype(jnp.bfloat16)
    grad_flat = product_grad.reshape(tokens, channels)
    feature_adj = jnp.stack([cotangent * inner_flat, grad_flat * value_part, grad_flat * key_part])
    later_rows = passed_along(feature_adj[:, :rim_rows, :], "ctx", -1)
    appended = jnp.concatenate([feature_adj, later_rows], axis=1)
    feature_grads = short_conv(short_taps, appended, tokens, rim_rows, False).astype(jnp.bfloat16)
    filter_local = jnp.stack([gain_part, rate_part])
    entry_count = 2 * group_count * order_count * lax.axis_size("fsdp")
    summed = lax.psum(filter_local, "ctx")
    squares = lax.psum(jnp.sum(summed * summed), "fsdp")
    factor = jnp.minimum(1.0, lax.rsqrt(squares / entry_count + 1e-06))
    clipped = summed * factor
    return (mixer_output, feature_grads, clipped[0], clipped[1])


def solution(mesh):
    return jax.shard_map(
        per_device,
        mesh=mesh,
        in_specs=(
            P(None, "ctx", "fsdp"),
            P(None, None, "fsdp"),
            P("fsdp", None),
            P("fsdp", None),
            P("ctx", "fsdp"),
        ),
        out_specs=(P("ctx", "fsdp"), P(None, "ctx", "fsdp"), P("fsdp", None), P("fsdp", None)),
        check_vma=False,
    )
```

profile of v0, /device:TPU:0, one launch (start us, length us, event | category | flops | bytes accessed | tf_op | source)
XLA Modules:
  0.0 923.6 jit_solution(9972772861217722462)
XLA Ops:
  31.0 54.8 %gather_fusion = f32[16384,64]{1,0:T(8,128)} fusion(f32[64,128]{0,1:T(8,128)S(1)} %copy.132, s32[16384]{0:T(1024)S(1)} %bitcast_clamp_fusion), kind=kCustom, calls=%fused_computation | custom fusion | bytes 8454144 | tf_op jit(solution)/shard_map/gather | solution.py:99
  98.3 8.6 copy.125
  123.6 16.1 %multiply_add_fusion = f32[3,1024,1024]{1,2,0:T(8,128)S(1)} fusion(bf16[3,1024,1024]{1,2,0:T(8,128)(2,1)} %copy.125, bf16[3,2,1024]{1,2,0:T(8,128)(2,1)S(1)} %copy.126, f32[3,1024]{1,0:T(4,128)S(1)} %get-tuple-element.555, f32[3,1024]{1,0:T(4,128)S(1)} %get-tuple-element.556, f32[3,1024]{1,0:T(4,128)S(1)} %bitcast.285), kind=kLoop, calls=%fused_computation.73 | loop fusion | flops 44040192 | bytes 18923520 | tf_op jit(solution)/shard_map/add | solution.py:32
  148.5 10.8 %fusion.85 = f32[2,16,64,16]{1,3,0,2:T(8,128)} fusion(bf16[1024,64,16,1]{0,2,3,1:T(8,128)(2,1)S(1)} %bitcast.277, f32[1,64,16,1024]{3,2,0,1:T(8,128)S(1)} %copy-done.10, f32[1,64,16,1024]{3,2,0,1:T(8,128)S(1)} %bitcast.274), kind=kOutput, calls=%fused_computation.113 | convolution fusion | flops 203423744 | bytes 10616832 | tf_op jit(solution)/shard_map/kgns,sgm->kngm/dot_general | solution.py:61
  167.5 19.1 %fusion.70 = f32[64,16,16]{2,1,0:T(8,128)S(1)} fusion(f32[1024,64,16]{0,2,1:T(8,128)S(1)} %bitcast.267, f32[64,16]{1,0:T(8,128)S(1)} %get-tuple-element.780), kind=kOutput, calls=%fused_computation.103 | convolution fusion | flops 202375168 | bytes 4263936 | tf_op jit(solution)/shard_map/gnt,tgm->ngm/dot_general | solution.py:64
  186.8 17.7 %all_gather.3 = f32[4,3,16,1024]{3,2,1,0:T(8,128)S(1)} all-gather(f32[1,3,16,1024]{3,2,1,0:T(8,128)S(1)} %pad_maximum_fusion.5), channel_id=1, replica_groups=mesh['fsdp'=8,'ctx'=4] {'ctx'}, dimensions={0}, use_global_device_ids=true | all-gather | bytes 983040 | tf_op jit(solution)/shard_map/all_gather | solution.py:69
  217.6 332.2 %while.38 = (s32[]{:T(128)}, f32[16,64,16]{0,2,1:T(8,128)S(1)}, f32[16,64,16]{0,2,1:T(8,128)}, f32[16,64]{0,1:T(8,128)S(1)}, f32[16,64]{0,1:T(8,128)S(1)}, /*ind...) while((s32[]{:T(128)}, f32[16,64,16]{0,2,1:T(8,128)S(1)}, ...), condition=%wide.region_4.5_spmd.clone, body=%wide.region_1.0_spmd.clone.sunk | while | flops 405523456 | bytes 20577004 | solution.py:121
  237.3 14.3 %dynamic_update_slice.17 = f32[8,128,64,16]{1,0,3,2:T(8,128)} dynamic-update-slice(f32[8,128,64,16]{1,0,3,2:T(8,128)} %get-tuple-element.743, f32[1,128,64,16]{1,0,3,2:T(1,128)S(1)} %bitcast.266, s32[]{:T(128)} %get-tuple-element.737, s32[]{:T(128)} %constant.78.clone.1..sunk, s32[]{:T(128)} %constant.78.clone.1..sunk, s32[]{:T(128)} %constant.78.clone.1..sunk) | dynamic-update-slice | bytes 1048580 | tf_op jit(solution)/shard_map/while/body/jit(dynamic_update_index_in_dim)/dynamic_update_slice | solution.py:121
  277.6 14.3 %dynamic_update_slice.17 = f32[8,128,64,16]{1,0,3,2:T(8,128)} dynamic-update-slice(f32[8,128,64,16]{1,0,3,2:T(8,128)} %get-tuple-element.743, f32[1,128,64,16]{1,0,3,2:T(1,128)S(1)} %bitcast.266, s32[]{:T(128)} %get-tuple-element.737, s32[]{:T(128)} %constant.78.clone.1..sunk, s32[]{:T(128)} %constant.78.clone.1..sunk, s32[]{:T(128)} %constant.78.clone.1..sunk) | dynamic-update-slice | bytes 1048580 | tf_op jit(solution)/shard_map/while/body/jit(dynamic_update_index_in_dim)/dynamic_update_slice | solution.py:121
  319.3 14.3 %dynamic_update_slice.17 = f32[8,128,64,16]{1,0,3,2:T(8,128)} dynamic-update-slice(f32[8,128,64,16]{1,0,3,2:T(8,128)} %get-tuple-element.743, f32[1,128,64,16]{1,0,3,2:T(1,128)S(1)} %bitcast.266, s32[]{:T(128)} %get-tuple-element.737, s32[]{:T(128)} %constant.78.clone.1..sunk, s32[]{:T(128)} %constant.78.clone.1..sunk, s32[]{:T(128)} %constant.78.clone.1..sunk) | dynamic-update-slice | bytes 1048580 | tf_op jit(solution)/shard_map/while/body/jit(dynamic_update_index_in_dim)/dynamic_update_slice | solution.py:121
  361.0 14.3 %dynamic_update_slice.17 = f32[8,128,64,16]{1,0,3,2:T(8,128)} dynamic-update-slice(f32[8,128,64,16]{1,0,3,2:T(8,128)} %get-tuple-element.743, f32[1,128,64,16]{1,0,3,2:T(1,128)S(1)} %bitcast.266, s32[]{:T(128)} %get-tuple-element.737, s32[]{:T(128)} %constant.78.clone.1..sunk, s32[]{:T(128)} %constant.78.clone.1..sunk, s32[]{:T(128)} %constant.78.clone.1..sunk) | dynamic-update-slice | bytes 1048580 | tf_op jit(solution)/shard_map/while/body/jit(dynamic_update_index_in_dim)/dynamic_update_slice | solution.py:121
  402.7 14.3 %dynamic_update_slice.17 = f32[8,128,64,16]{1,0,3,2:T(8,128)} dynamic-update-slice(f32[8,128,64,16]{1,0,3,2:T(8,128)} %get-tuple-element.743, f32[1,128,64,16]{1,0,3,2:T(1,128)S(1)} %bitcast.266, s32[]{:T(128)} %get-tuple-element.737, s32[]{:T(128)} %constant.78.clone.1..sunk, s32[]{:T(128)} %constant.78.clone.1..sunk, s32[]{:T(128)} %constant.78.clone.1..sunk) | dynamic-update-slice | bytes 1048580 | tf_op jit(solution)/shard_map/while/body/jit(dynamic_update_index_in_dim)/dynamic_update_slice | solution.py:121
  434.4 8.5 convolution_bitcast_fusion.5
  444.4 14.3 %dynamic_update_slice.17 = f32[8,128,64,16]{1,0,3,2:T(8,128)} dynamic-update-slice(f32[8,128,64,16]{1,0,3,2:T(8,128)} %get-tuple-element.743, f32[1,128,64,16]{1,0,3,2:T(1,128)S(1)} %bitcast.266, s32[]{:T(128)} %get-tuple-element.737, s32[]{:T(128)} %constant.78.clone.1..sunk, s32[]{:T(128)} %constant.78.clone.1..sunk, s32[]{:T(128)} %constant.78.clone.1..sunk) | dynamic-update-slice | bytes 1048580 | tf_op jit(solution)/shard_map/while/body/jit(dynamic_update_index_in_dim)/dynamic_update_slice | solution.py:121
  486.1 14.3 %dynamic_update_slice.17 = f32[8,128,64,16]{1,0,3,2:T(8,128)} dynamic-update-slice(f32[8,128,64,16]{1,0,3,2:T(8,128)} %get-tuple-element.743, f32[1,128,64,16]{1,0,3,2:T(1,128)S(1)} %bitcast.266, s32[]{:T(128)} %get-tuple-element.737, s32[]{:T(128)} %constant.78.clone.1..sunk, s32[]{:T(128)} %constant.78.clone.1..sunk, s32[]{:T(128)} %constant.78.clone.1..sunk) | dynamic-update-slice | bytes 1048580 | tf_op jit(solution)/shard_map/while/body/jit(dynamic_update_index_in_dim)/dynamic_update_slice | solution.py:121
  527.8 14.3 %dynamic_update_slice.17 = f32[8,128,64,16]{1,0,3,2:T(8,128)} dynamic-update-slice(f32[8,128,64,16]{1,0,3,2:T(8,128)} %get-tuple-element.743, f32[1,128,64,16]{1,0,3,2:T(1,128)S(1)} %bitcast.266, s32[]{:T(128)} %get-tuple-element.737, s32[]{:T(128)} %constant.78.clone.1..sunk, s32[]{:T(128)} %constant.78.clone.1..sunk, s32[]{:T(128)} %constant.78.clone.1..sunk) | dynamic-update-slice | bytes 1048580 | tf_op jit(solution)/shard_map/while/body/jit(dynamic_update_index_in_dim)/dynamic_update_slice | solution.py:121
  549.8 34.3 %rev.30 = f32[64,128,128]{2,1,0:T(8,128)} reverse(f32[64,128,128]{2,1,0:T(8,128)} %get-tuple-element.242), dimensions={2} | reverse | bytes 8388608 | tf_op jit(solution)/shard_map/jit(_flip)/rev | solution.py:18
  595.9 16.3 %reshape.172 = f32[64,128,255]{2,1,0:T(8,128)} reshape(f32[64,32640]{1,0:T(8,128)} %slice.116) | data formatting | bytes 16711680 | tf_op jit(solution)/shard_map/reshape | solution.py:23
  625.7 17.6 %psum.14 = f32[2,64,16]{1,2,0:T(8,128)S(1)} all-reduce(f32[2,64,16]{1,2,0:T(8,128)S(1)} %pad_maximum_fusion.6), channel_id=1, replica_groups=mesh['fsdp'=8,'ctx'=4] {'ctx'}, use_global_device_ids=true, to_apply=%region_15.16 | all-reduce | flops 2048 | bytes 16384 | tf_op jit(solution)/shard_map/psum | solution.py:168
  651.2 12.6 %psum.15 = f32[]{:T(128)} all-reduce(f32[]{:T(128)} %multiply_reduce_fusion.6), channel_id=1, replica_groups=mesh['fsdp'=8,'ctx'=4] {'fsdp'}, use_global_device_ids=true, to_apply=%region_17.18 | all-reduce | flops 1 | bytes 8 | tf_op jit(solution)/shard_map/psum | solution.py:169
  667.6 179.6 %while.39 = (s32[]{:T(128)}, f32[16,64,16]{0,2,1:T(8,128)S(1)}, f32[8,128,64,16]{1,0,3,2:T(8,128)}, f32[16,64,1]{0,1,2:T(8,128)S(1)}, f32[8,128,64,16]{1,3,2,0:T...) while((s32[]{:T(128)}, f32[16,64,16]{0,2,1:T(8,128)S(1)}, ...), condition=%wide.region_7.8_spmd.clone, body=%wide.region_6.7_spmd.clone.sunk | while | flops 251985920 | bytes 8593552 | solution.py:134
  673.6 14.3 %dynamic_update_slice.18 = f32[8,128,64,16]{1,0,3,2:T(8,128)} dynamic-update-slice(f32[8,128,64,16]{1,0,3,2:T(8,128)} %get-tuple-element.786, f32[1,128,64,16]{1,0,3,2:T(1,128)S(1)} %bitcast.265, s32[]{:T(128)S(6)} %sub.157, s32[]{:T(128)} %constant.78.clone.1..sunk.1, s32[]{:T(128)} %constant.78.clone.1..sunk.1, s32[]{:T(128)} %constant.78.clone.1..sunk.1) | dynamic-update-slice | bytes 1048580 | tf_op jit(solution)/shard_map/while/body/jit(dynamic_update_index_in_dim)/dynamic_update_slice | solution.py:121
  696.1 14.3 %dynamic_update_slice.18 = f32[8,128,64,16]{1,0,3,2:T(8,128)} dynamic-update-slice(f32[8,128,64,16]{1,0,3,2:T(8,128)} %get-tuple-element.786, f32[1,128,64,16]{1,0,3,2:T(1,128)S(1)} %bitcast.265, s32[]{:T(128)S(6)} %sub.157, s32[]{:T(128)} %constant.78.clone.1..sunk.1, s32[]{:T(128)} %constant.78.clone.1..sunk.1, s32[]{:T(128)} %constant.78.clone.1..sunk.1) | dynamic-update-slice | bytes 1048580 | tf_op jit(solution)/shard_map/while/body/jit(dynamic_update_index_in_dim)/dynamic_update_slice | solution.py:121
  718.5 14.3 %dynamic_update_slice.18 = f32[8,128,64,16]{1,0,3,2:T(8,128)} dynamic-update-slice(f32[8,128,64,16]{1,0,3,2:T(8,128)} %get-tuple-element.786, f32[1,128,64,16]{1,0,3,2:T(1,128)S(1)} %bitcast.265, s32[]{:T(128)S(6)} %sub.157, s32[]{:T(128)} %constant.78.clone.1..sunk.1, s32[]{:T(128)} %constant.78.clone.1..sunk.1, s32[]{:T(128)} %constant.78.clone.1..sunk.1) | dynamic-update-slice | bytes 1048580 | tf_op jit(solution)/shard_map/while/body/jit(dynamic_update_index_in_dim)/dynamic_update_slice | solution.py:121
  741.0 14.3 %dynamic_update_slice.18 = f32[8,128,64,16]{1,0,3,2:T(8,128)} dynamic-update-slice(f32[8,128,64,16]{1,0,3,2:T(8,128)} %get-tuple-element.786, f32[1,128,64,16]{1,0,3,2:T(1,128)S(1)} %bitcast.265, s32[]{:T(128)S(6)} %sub.157, s32[]{:T(128)} %constant.78.clone.1..sunk.1, s32[]{:T(128)} %constant.78.clone.1..sunk.1, s32[]{:T(128)} %constant.78.clone.1..sunk.1) | dynamic-update-slice | bytes 1048580 | tf_op jit(solution)/shard_map/while/body/jit(dynamic_update_index_in_dim)/dynamic_update_slice | solution.py:121
  763.4 14.3 %dynamic_update_slice.18 = f32[8,128,64,16]{1,0,3,2:T(8,128)} dynamic-update-slice(f32[8,128,64,16]{1,0,3,2:T(8,128)} %get-tuple-element.786, f32[1,128,64,16]{1,0,3,2:T(1,128)S(1)} %bitcast.265, s32[]{:T(128)S(6)} %sub.157, s32[]{:T(128)} %constant.78.clone.1..sunk.1, s32[]{:T(128)} %constant.78.clone.1..sunk.1, s32[]{:T(128)} %constant.78.clone.1..sunk.1) | dynamic-update-slice | bytes 1048580 | tf_op jit(solution)/shard_map/while/body/jit(dynamic_update_index_in_dim)/dynamic_update_slice | solution.py:121
  785.9 14.3 %dynamic_update_slice.18 = f32[8,128,64,16]{1,0,3,2:T(8,128)} dynamic-update-slice(f32[8,128,64,16]{1,0,3,2:T(8,128)} %get-tuple-element.786, f32[1,128,64,16]{1,0,3,2:T(1,128)S(1)} %bitcast.265, s32[]{:T(128)S(6)} %sub.157, s32[]{:T(128)} %constant.78.clone.1..sunk.1, s32[]{:T(128)} %constant.78.clone.1..sunk.1, s32[]{:T(128)} %constant.78.clone.1..sunk.1) | dynamic-update-slice | bytes 1048580 | tf_op jit(solution)/shard_map/while/body/jit(dynamic_update_index_in_dim)/dynamic_update_slice | solution.py:121
  808.3 14.3 %dynamic_update_slice.18 = f32[8,128,64,16]{1,0,3,2:T(8,128)} dynamic-update-slice(f32[8,128,64,16]{1,0,3,2:T(8,128)} %get-tuple-element.786, f32[1,128,64,16]{1,0,3,2:T(1,128)S(1)} %bitcast.265, s32[]{:T(128)S(6)} %sub.157, s32[]{:T(128)} %constant.78.clone.1..sunk.1, s32[]{:T(128)} %constant.78.clone.1..sunk.1, s32[]{:T(128)} %constant.78.clone.1..sunk.1) | dynamic-update-slice | bytes 1048580 | tf_op jit(solution)/shard_map/while/body/jit(dynamic_update_index_in_dim)/dynamic_update_slice | solution.py:121
  830.8 14.3 %dynamic_update_slice.18 = f32[8,128,64,16]{1,0,3,2:T(8,128)} dynamic-update-slice(f32[8,128,64,16]{1,0,3,2:T(8,128)} %get-tuple-element.786, f32[1,128,64,16]{1,0,3,2:T(1,128)S(1)} %bitcast.265, s32[]{:T(128)S(6)} %sub.157, s32[]{:T(128)} %constant.78.clone.1..sunk.1, s32[]{:T(128)} %constant.78.clone.1..sunk.1, s32[]{:T(128)} %constant.78.clone.1..sunk.1) | dynamic-update-slice | bytes 1048580 | tf_op jit(solution)/shard_map/while/body/jit(dynamic_update_index_in_dim)/dynamic_update_slice | solution.py:121
  859.4 9.1 bitcast_multiply_fusion.1
  904.0 10.8 %fusion.54 = bf16[3,1024,1024]{1,2,0:T(8,128)(2,1)} fusion(f32[3,1026,1024]{1,2,0:T(8,128)S(1)} %pad_maximum_fusion, f32[3,1024]{1,0:T(4,128)S(1)} %get-tuple-element.555, f32[3,1024]{1,0:T(4,128)S(1)} %copy-done.22, f32[3,1024]{1,0:T(4,128)S(1)} %bitcast.286, f32[1,1024,1024]{1,2,0:T(8,128)S(1)} %copy-done.4, f32[1,1024,1024]{1,2,0:T(8,128)S(1)} %copy-done.2, ...), kind=kLoop, calls=%fused_computation.69 | loop fusion | flops 25165824 | bytes 44077056 | tf_op jit(solution)/shard_map/convert_element_type | solution.py:165
  914.7 8.6 copy.155
  (271 shorter events, 447.6 us)
Async XLA Ops:
  1.4 121.0 %collective-permute-start = (bf16[3,2,1024]{2,1,0:T(2,128)(2,1)S(1)}, bf16[3,2,1024]{2,1,0:T(2,128)(2,1)}, u32[]{:S(2)}, u32[]{:S(2)}) collective-permute-start(bf16[3,2,1024]{2,1,0:T(2,128)(2,1)S(1)} %slice.79), channel_id=1, source_target_pairs={{0,1},{1,2},{2,3},{4,5},{5,6},{6,7},{8,9},{9,10},{10,11},{12,13},{... | collective-permute-start | bytes 36872 | tf_op jit(solution)/shard_map/ppermute | solution.py:13
  23.8 5.0 copy-start.26
  85.8 7.5 copy-start.18
  93.2 30.5 %copy-start.21 = (f32[3,1024]{1,0:T(4,128)}, f32[3,1024]{1,0:T(4,128)S(1)}, u32[]{:S(2)}) copy-start(f32[3,1024]{1,0:T(4,128)S(1)} %get-tuple-element.556) | copy-start | bytes 36868
  114.3 25.5 %copy-start.23 = (f32[3,1,1024]{2,0,1:T(4,128)}, f32[3,1,1024]{2,0,1:T(4,128)S(1)}, u32[]{:S(2)}) copy-start(f32[3,1,1024]{2,0,1:T(4,128)S(1)} %copy.190) | copy-start | bytes 36868
  165.6 39.0 %copy-start.20 = (f32[16,1024]{1,0:T(8,128)S(1)}, f32[16,1024]{1,0:T(8,128)}, u32[]{:S(2)}) copy-start(f32[16,1024]{1,0:T(8,128)} %neg.32) | copy-start | bytes 196612
  165.6 39.0 %copy-start.28 = (pred[4]{0:T(512)(128)(4,1)S(1)}, pred[4]{0:T(512)(128)(4,1)}, u32[]{:S(2)}) copy-start(pred[4]{0:T(512)(128)(4,1)} %get-tuple-element.559) | copy-start | bytes 16
  165.6 39.0 %copy-start.29 = (pred[4]{0:T(512)(128)(4,1)S(1)}, pred[4]{0:T(512)(128)(4,1)}, u32[]{:S(2)}) copy-start(pred[4]{0:T(512)(128)(4,1)} %get-tuple-element.560) | copy-start | bytes 16
  165.6 38.9 %copy-start.30 = (f32[4]{0:T(128)S(1)}, f32[4]{0:T(128)}, u32[]{:S(2)}) copy-start(f32[4]{0:T(128)} %get-tuple-element.557) | copy-start | bytes 52
  165.6 38.9 %copy-start.31 = (f32[4]{0:T(128)S(1)}, f32[4]{0:T(128)}, u32[]{:S(2)}) copy-start(f32[4]{0:T(128)} %get-tuple-element.558) | copy-start | bytes 52
  165.6 38.9 %copy-start.32 = (f32[4]{0:T(128)S(1)}, f32[4]{0:T(128)}, u32[]{:S(2)}) copy-start(f32[4]{0:T(128)} %maximum_multiply_fusion) | copy-start | bytes 52
  186.6 23.4 %copy-start.16 = (f32[64,16,16]{2,1,0:T(8,128)}, f32[64,16,16]{2,1,0:T(8,128)S(1)}, u32[]{:S(2)}) copy-start(f32[64,16,16]{2,1,0:T(8,128)S(1)} %fusion.70) | copy-start | bytes 196612
  222.2 13.6 %copy-start.12 = (f32[16,64,16]{0,2,1:T(8,128)S(1)}, f32[16,64,16]{0,2,1:T(8,128)}, u32[]{:S(2)}) copy-start(f32[16,64,16]{0,2,1:T(8,128)} %get-tuple-element.739) | copy-start | bytes 196612 | tf_op jit(solution)/shard_map/while
  262.5 13.6 %copy-start.12 = (f32[16,64,16]{0,2,1:T(8,128)S(1)}, f32[16,64,16]{0,2,1:T(8,128)}, u32[]{:S(2)}) copy-start(f32[16,64,16]{0,2,1:T(8,128)} %get-tuple-element.739) | copy-start | bytes 196612 | tf_op jit(solution)/shard_map/while
  304.2 13.6 %copy-start.12 = (f32[16,64,16]{0,2,1:T(8,128)S(1)}, f32[16,64,16]{0,2,1:T(8,128)}, u32[]{:S(2)}) copy-start(f32[16,64,16]{0,2,1:T(8,128)} %get-tuple-element.739) | copy-start | bytes 196612 | tf_op jit(solution)/shard_map/while
  345.9 13.6 %copy-start.12 = (f32[16,64,16]{0,2,1:T(8,128)S(1)}, f32[16,64,16]{0,2,1:T(8,128)}, u32[]{:S(2)}) copy-start(f32[16,64,16]{0,2,1:T(8,128)} %get-tuple-element.739) | copy-start | bytes 196612 | tf_op jit(solution)/shard_map/while
  387.6 13.6 %copy-start.12 = (f32[16,64,16]{0,2,1:T(8,128)S(1)}, f32[16,64,16]{0,2,1:T(8,128)}, u32[]{:S(2)}) copy-start(f32[16,64,16]{0,2,1:T(8,128)} %get-tuple-element.739) | copy-start | bytes 196612 | tf_op jit(solution)/shard_map/while
  429.3 13.6 %copy-start.12 = (f32[16,64,16]{0,2,1:T(8,128)S(1)}, f32[16,64,16]{0,2,1:T(8,128)}, u32[]{:S(2)}) copy-start(f32[16,64,16]{0,2,1:T(8,128)} %get-tuple-element.739) | copy-start | bytes 196612 | tf_op jit(solution)/shard_map/while
  471.0 13.6 %copy-start.12 = (f32[16,64,16]{0,2,1:T(8,128)S(1)}, f32[16,64,16]{0,2,1:T(8,128)}, u32[]{:S(2)}) copy-start(f32[16,64,16]{0,2,1:T(8,128)} %get-tuple-element.739) | copy-start | bytes 196612 | tf_op jit(solution)/shard_map/while
  512.7 13.6 %copy-start.12 = (f32[16,64,16]{0,2,1:T(8,128)S(1)}, f32[16,64,16]{0,2,1:T(8,128)}, u32[]{:S(2)}) copy-start(f32[16,64,16]{0,2,1:T(8,128)} %get-tuple-element.739) | copy-start | bytes 196612 | tf_op jit(solution)/shard_map/while
  612.2 5.3 copy-start.15
  612.2 5.3 copy-start.17
  612.2 5.3 copy-start.25
  612.2 5.5 copy-start.19
  612.3 5.5 copy-start.27
  873.4 6.4 copy-start.8
  889.4 5.7 collective-permute-start.1
  895.6 6.6 copy-start.2
  895.6 7.2 copy-start.4
  895.6 8.3 copy-start.6
  895.6 8.3 copy-start.22
  895.6 8.3 copy-start.24
  (17 other events, 36.0 us)
where the time goes:
time: 933 us; the launch traced here: 924 us
  local copies, waits for them, and re-layouts  457 us (49%)
  matrix products  322 us (35%)
  other arithmetic  85.6 us (9%)
  blocking collectives  47.9 us (5%)
    dynamic_update_slice x16, local copies, waits for them, and re-layouts, per_device(): lax.scan(forward_block, (zero_state, zero_state, zero_pairs, zero_pairs,...  228 us
    dot_general x8, matrix products, forward_block(): jnp.einsum('kgnt,tgm->kngm', block_moments, e_block, precision=precise)  67.6 us
    gather x2, local copies, waits for them, and re-layouts, per_device(): filter_taps[:, jnp.maximum(lag_index, 0)]  62.1 us
    dot_general x8, matrix products, forward_block(): jnp.einsum('tgm,sgm->gts', e_block, z_wide, precision=precise)  61 us
    unnamed x76, local copies, waits for them, and re-layouts  50.4 us
    dot_general x8, matrix products, backward_block(): jnp.einsum('gts,tgm->sgm', toeplitz, e_block, precision=precise)  43.3 us
    dot_general x8, matrix products, forward_block(): jnp.einsum('gts,sgm->tgm', toeplitz, z_wide, precision=threepass)  36.4 us
    rev x1, local copies, waits for them, and re-layouts, diagonal_sums(): flipped = jnp.flip(gram_acc, axis=2)  34.3 us
  transfers between devices with their start and end apart: 2, of which 1 were waited for; matrix products, arithmetic and copies ran while one was open for 13% of the time, Pallas kernels for 0%

commit v1 on v0

v1 whole, which is shorter than its diff:
```python
import jax
import jax.numpy as jnp
from jax import lax
from jax.experimental import pallas as pl
from jax.experimental.pallas import tpu as pltpu
from jax.sharding import PartitionSpec as P

LANES = 128
MODES = 16
MEMBERS = 16
TILE_GROUPS = LANES // MEMBERS
ROWS = LANES
f32 = jnp.float32
bf16 = jnp.bfloat16


def split(value):
    high = value.astype(bf16)
    return high, (value - high.astype(f32)).astype(bf16)


def dot_nt(left, right):
    return lax.dot_general(left, right, (((1,), (1,)), ((), ())), preferred_element_type=f32)


def dot_tn(left, right):
    return lax.dot_general(left, right, (((0,), (0,)), ((), ())), preferred_element_type=f32)


def dot_nn(left, right):
    return lax.dot_general(left, right, (((1,), (0,)), ((), ())), preferred_element_type=f32)


def iota(axis, shape):
    return lax.broadcasted_iota(jnp.int32, shape, axis)


def widen(feat_ref, halo_ref, wide, tokens):
    for i in range(3):
        wide[i, 0:8, :] = halo_ref[i]
        wide[i, 8 : 8 + tokens, :] = feat_ref[i].astype(f32)


def short_block(wide, taps_ref, i, start, count):
    return (
        taps_ref[i, 0:1, :] * wide[i, start + 8 : start + 8 + count, :]
        + taps_ref[i, 1:2, :] * wide[i, start + 7 : start + 7 + count, :]
        + taps_ref[i, 2:3, :] * wide[i, start + 6 : start + 6 + count, :]
    )


def sheared(row8):
    which = iota(0, row8.shape)
    for bit in (1, 2, 4):
        row8 = jnp.where((which & bit) != 0, pltpu.roll(row8, LANES - bit, 1), row8)
    return row8


def spread_rows(row):
    rows = jnp.broadcast_to(row, (8, LANES))
    which = iota(0, rows.shape)
    for bit in (1, 2, 4):
        rows = jnp.where((which & bit) != 0, pltpu.roll(rows, bit, 1), rows)
    return rows


def circulant(row):
    base = spread_rows(row)
    return jnp.concatenate(
        [base if r == 0 else pltpu.roll(base, 8 * r, 1) for r in range(LANES // 8)], axis=0
    )


def local_kernel(
    feat_ref, halo_ref, taps_ref, cot_ref, par_ref, rate_ref,
    inner_ref, grad_ref, carry_ref, state_ref, diag_ref, cross_ref,
    wide, z_all, eh_all, el_all,
):
    tokens = feat_ref.shape[1]
    blocks = tokens // LANES
    widen(feat_ref, halo_ref, wide, tokens)
    for b in range(blocks):
        query = short_block(wide, taps_ref, 0, b * LANES, LANES)
        key = short_block(wide, taps_ref, 1, b * LANES, LANES)
        value = short_block(wide, taps_ref, 2, b * LANES, LANES)
        z_t = jnp.transpose((key * value).astype(bf16))
        e_t = jnp.transpose(cot_ref[b * LANES : (b + 1) * LANES, :].astype(f32) * query)
        e_high, e_low = split(e_t)
        at = slice(b * MEMBERS, (b + 1) * MEMBERS)
        for g in range(TILE_GROUPS):
            of = slice(g * MEMBERS, (g + 1) * MEMBERS)
            z_all[g, at, :] = z_t[of]
            eh_all[g, at, :] = e_high[of]
            el_all[g, at, :] = e_low[of]

    lag = iota(1, (MODES, LANES)).astype(f32)
    row_at = iota(0, (LANES, LANES))
    lane_at = iota(1, (LANES, LANES))
    lane_row = iota(1, (1, LANES))
    slot_x = jnp.where((lane_row >= 48) & (lane_row < 64), float(LANES), 0.0)
    slot_y = jnp.where((lane_row >= 96) & (lane_row < 112), float(LANES), 0.0)
    nothing = jnp.zeros((4 * MODES, LANES), bf16)
    first_acc = jnp.zeros((MODES, LANES), f32)
    lag_acc = jnp.zeros((MODES, LANES), f32)
    ends, starts = [], []
    for g in range(TILE_GROUPS):
        rates = par_ref[0, g]
        coefs = par_ref[1, g]
        power = jnp.exp(-rates * lag)
        power_back = jnp.exp(-rates * (LANES - 1.0 - lag))
        power_after = power * jnp.exp(-rates)
        taps = jnp.sum(coefs * power, axis=0, keepdims=True)
        taps_back = jnp.sum(coefs * power_back, axis=0, keepdims=True)
        toep_f = jnp.where(row_at >= lane_at, circulant(pltpu.roll(taps_back, 1, 1)), 0.0)
        toep_b = jnp.where(lane_at >= row_at, circulant(taps), 0.0)
        tf_high, tf_low = split(toep_f)
        tb_high, tb_low = split(toep_b)
        s_high, s_low = split(power_back)
        l_high, l_low = split((LANES - 1.0 - lag) * power_back)
        m_high, m_low = split(power_after)
        n_high, n_low = split((lag + 1.0) * power_after)
        wf_high = jnp.concatenate([tf_high, s_high, s_high, s_high, l_high, nothing], axis=0)
        wf_low = jnp.concatenate([tf_low, s_low, s_low, s_low, l_low, nothing], axis=0)
        wb_high = jnp.concatenate([tb_high, nothing, m_high, m_high, n_high, m_high], axis=0)
        wb_low = jnp.concatenate([tb_low, nothing, m_low, m_low, n_low, m_low], axis=0)
        z = z_all[g]
        eh = eh_all[g]
        el = el_all[g]
        from_z = dot_nt(jnp.concatenate([z, z], axis=1), jnp.concatenate([wf_high, wf_low], axis=1))
        from_e = dot_nt(
            jnp.concatenate([eh, el], axis=1), jnp.concatenate([wb_high, wb_high], axis=1)
        ) + dot_nt(eh, wb_low)
        inner_ref[g] = from_z[:, :LANES]
        grad_ref[g] = from_e[:, :LANES]
        x_own = from_z[:, LANES:]
        y_own = from_e[:, LANES:]
        span = jnp.exp(rate_ref[g : g + 1, :] * (-float(LANES)))
        x_now = jnp.zeros((MEMBERS, LANES), f32)
        y_now = jnp.zeros((MEMBERS, LANES), f32)
        x_prev = []
        y_next = [None] * blocks
        for b in range(blocks):
            x_prev.append(x_now)
            x_now = (
                span * (x_now + slot_x * pltpu.roll(x_now, MODES, 1))
                + x_own[b * MEMBERS : (b + 1) * MEMBERS]
            )
        for b in reversed(range(blocks)):
            y_next[b] = y_now
            y_now = (
                span * (y_now + slot_y * pltpu.roll(y_now, MODES, 1))
                + y_own[b * MEMBERS : (b + 1) * MEMBERS]
            )
        ends.append(x_now)
        starts.append(y_now)
        x_prev = jnp.concatenate(x_prev, axis=0)
        carry_ref[g] = x_prev + jnp.concatenate(y_next, axis=0)
        cross_ref[g : g + 1, :] = jnp.sum(
            x_prev * pltpu.roll(y_own, 4 * MODES, 1), axis=0, keepdims=True
        )
        gram = dot_tn(jnp.concatenate([z, z], axis=0), jnp.concatenate([eh, el], axis=0))
        gram = jnp.where(lane_at >= row_at, gram, 0.0)
        folded = gram[0:8]
        for r in range(1, LANES // 8):
            folded = folded + pltpu.roll(gram[8 * r : 8 * r + 8], LANES - 8 * r, 1)
        corr = jnp.sum(sheared(folded), axis=0, keepdims=True)
        weighted = power * corr
        first_col = jnp.sum(weighted, axis=1, keepdims=True)
        lag_col = jnp.sum(lag * weighted, axis=1, keepdims=True)
        mine = iota(1, (MODES, LANES)) == g
        first_acc = first_acc + jnp.where(mine, first_col, 0.0)
        lag_acc = lag_acc + jnp.where(mine, lag_col, 0.0)
    diag_ref[0, 0] = first_acc
    diag_ref[0, 1] = lag_acc
    both = jnp.concatenate(ends, axis=0) + jnp.concatenate(starts, axis=0)
    turned = jnp.transpose(both)
    state_ref[0:16] = turned[0:16]
    state_ref[16:32] = turned[48:64]
    state_ref[32:48] = turned[64:80]
    state_ref[48:64] = turned[96:112]


def output_kernel(
    feat_ref, halo_ref, next_ref, taps_ref, cot_ref, par_ref, rate_ref,
    inner_ref, grad_ref, carry_ref, bound_ref, wide_rate_ref, wide_coef_ref,
    mixer_ref, fgrad_ref,
    wide, adj, inner_t, grad_t,
):
    tokens = feat_ref.shape[1]
    blocks = tokens // LANES
    widen(feat_ref, halo_ref, wide, tokens)
    for i in range(3):
        wide[i, 8 + tokens : 16 + tokens, :] = next_ref[i]
    lag = iota(1, (MODES, LANES)).astype(f32)
    lane_row = iota(1, (1, LANES))
    lane_16 = iota(1, (MEMBERS, LANES))
    is_low = ((lane_16 >= 16) & (lane_16 < 32)) | ((lane_16 >= 80) & (lane_16 < 96))
    before = bound_ref[0:16]
    after = bound_ref[16:32]
    gap = jnp.zeros((MODES, LANES), f32)
    stacked = jnp.concatenate([before, before, before, gap, after, after, gap, after], axis=0)
    turned = jnp.transpose(stacked)
    none_16 = jnp.zeros((MODES, LANES), bf16)
    none_64 = jnp.zeros((4 * MODES, LANES), bf16)
    for g in range(TILE_GROUPS):
        rates = par_ref[0, g]
        coefs = par_ref[1, g]
        cz_high, cz_low = split(coefs * jnp.exp(-rates * (lag + 1.0)))
        ce_high, ce_low = split(coefs * jnp.exp(-rates * (LANES - 1.0 - lag)))
        right = jnp.concatenate(
            [
                jnp.concatenate([cz_high, cz_high, cz_low, none_16, none_64], axis=0),
                jnp.concatenate([none_64, ce_high, ce_high, none_16, ce_low], axis=0),
            ],
            axis=1,
        )
        rate_row = rate_ref[g : g + 1, :]
        mine = turned[g * MEMBERS : (g + 1) * MEMBERS]
        rows = []
        for b in range(blocks):
            steps = jnp.where(lane_row < 64, float(b * LANES), float((blocks - 1 - b) * LANES))
            value = carry_ref[g, b * MEMBERS : (b + 1) * MEMBERS, :] + mine * jnp.exp(
                -rate_row * steps
            )
            high, low = split(value)
            rows.append(jnp.where(is_low, low.astype(f32), high.astype(f32)).astype(bf16))
        carried = dot_nn(jnp.concatenate(rows, axis=0), right)
        whole_inner = inner_ref[g] + carried[:, :LANES]
        whole_grad = grad_ref[g] + carried[:, LANES:]
        of = slice(g * MEMBERS, (g + 1) * MEMBERS)
        for b in range(blocks):
            at = slice(b * MEMBERS, (b + 1) * MEMBERS)
            inner_t[b, of, :] = whole_inner[at]
            grad_t[b, of, :] = whole_grad[at]
    for b in range(blocks):
        at = slice(b * LANES, (b + 1) * LANES)
        query = short_block(wide, taps_ref, 0, b * LANES, LANES)
        key = short_block(wide, taps_ref, 1, b * LANES, LANES)
        value = short_block(wide, taps_ref, 2, b * LANES, LANES)
        inner = jnp.transpose(inner_t[b])
        grad = jnp.transpose(grad_t[b])
        mixer_ref[at, :] = (query * inner).astype(bf16)
        adj[0, at, :] = cot_ref[at, :].astype(f32) * inner
        adj[1, at, :] = grad * value
        adj[2, at, :] = grad * key
    key = short_block(wide, taps_ref, 1, tokens, 8)
    value = short_block(wide, taps_ref, 2, tokens, 8)
    query = short_block(wide, taps_ref, 0, tokens, 8)
    z = (key * value).astype(bf16).astype(f32)
    e = next_ref[3] * query
    rates = wide_rate_ref[...]
    coefs = wide_coef_ref[...]
    decay = jnp.exp(-rates)
    grow = jnp.exp(rates)
    state = bound_ref[32:48]
    sum_0 = jnp.sum(coefs, axis=0, keepdims=True)
    sum_1 = jnp.sum(coefs * decay, axis=0, keepdims=True)
    inner_0 = jnp.sum(coefs * decay * state, axis=0, keepdims=True) + sum_0 * z[0:1]
    inner_1 = (
        jnp.sum(coefs * decay * decay * state, axis=0, keepdims=True)
        + sum_1 * z[0:1]
        + sum_0 * z[1:2]
    )
    grad_0 = jnp.sum(coefs * grow * after, axis=0, keepdims=True)
    grad_1 = jnp.sum(coefs * grow * (grow * after - e[0:1]), axis=0, keepdims=True)
    which = iota(0, (8, LANES))
    inner_8 = jnp.where(which == 0, inner_0, jnp.where(which == 1, inner_1, 0.0))
    grad_8 = jnp.where(which == 0, grad_0, jnp.where(which == 1, grad_1, 0.0))
    adj[0, tokens : tokens + 8, :] = next_ref[3] * inner_8
    adj[1, tokens : tokens + 8, :] = grad_8 * value
    adj[2, tokens : tokens + 8, :] = grad_8 * key
    for b in range(blocks):
        start = b * LANES
        for i in range(3):
            fgrad_ref[i, start : start + LANES, :] = (
                taps_ref[i, 0:1, :] * adj[i, start : start + LANES, :]
                + taps_ref[i, 1:2, :] * adj[i, start + 1 : start + 1 + LANES, :]
                + taps_ref[i, 2:3, :] * adj[i, start + 2 : start + 2 + LANES, :]
            ).astype(bf16)


def shifted(value, axis, steps):
    count = lax.axis_size(axis)
    return lax.ppermute(value, axis, [(i, (i + steps) % count) for i in range(count)])


def swapped(value, axis, key):
    count = lax.axis_size(axis)
    return lax.ppermute(value, axis, [(i, i ^ key) for i in range(count)])


def per_device(features, short_taps, decay_rates, mode_gains, cotangent):
    tokens = features.shape[1]
    channels = features.shape[2]
    groups = decay_rates.shape[0]
    tiles = channels // LANES
    blocks = tokens // LANES
    ctx_count = lax.axis_size("ctx")
    ctx_index = lax.axis_index("ctx")

    tail = shifted(features[:, tokens - 2 :, :], "ctx", 1).astype(f32)
    tail = jnp.where(ctx_index == 0, 0.0, tail)
    halo = jnp.pad(tail, ((0, 0), (6, 0), (0, 0)))
    head = jnp.concatenate([features[:, :2, :], cotangent[None, :2, :]], axis=0)
    ahead = shifted(head, "ctx", -1).astype(f32)
    ahead = jnp.where(ctx_index == ctx_count - 1, 0.0, ahead)
    ahead = jnp.pad(ahead, ((0, 0), (0, 6), (0, 0)))

    mode_coefs = mode_gains * jnp.sqrt(2.0 * decay_rates)
    params = jnp.broadcast_to(
        jnp.stack([decay_rates, mode_coefs])[:, :, :, None], (2, groups, MODES, LANES)
    )
    rate_rows = jnp.tile(decay_rates, (1, LANES // MODES))
    rate_cols = jnp.repeat(decay_rates.T, MEMBERS, axis=1)
    coef_cols = jnp.repeat(mode_coefs.T, MEMBERS, axis=1)

    per_group = pl.BlockSpec((TILE_GROUPS, ROWS, LANES), lambda j: (j, 0, 0))
    feat_spec = pl.BlockSpec((3, tokens, LANES), lambda j: (0, 0, j))
    halo_spec = pl.BlockSpec((3, 8, LANES), lambda j: (0, 0, j))
    taps_spec = pl.BlockSpec((3, 3, LANES), lambda j: (0, 0, j))
    cot_spec = pl.BlockSpec((tokens, LANES), lambda j: (0, j))
    par_spec = pl.BlockSpec((2, TILE_GROUPS, MODES, LANES), lambda j: (0, j, 0, 0))
    rate_spec = pl.BlockSpec((TILE_GROUPS, LANES), lambda j: (j, 0))
    rows = blocks * MEMBERS
    big = jax.ShapeDtypeStruct((groups, rows, LANES), f32)
    inner, grad, carry, states, diag, cross = pl.pallas_call(
        local_kernel,
        grid=(tiles,),
        in_specs=[feat_spec, halo_spec, taps_spec, cot_spec, par_spec, rate_spec],
        out_specs=[
            per_group,
            per_group,
            per_group,
            pl.BlockSpec((4 * MODES, LANES), lambda j: (0, j)),
            pl.BlockSpec((1, 2, MODES, LANES), lambda j: (j, 0, 0, 0)),
            rate_spec,
        ],
        out_shape=[
            big,
            big,
            big,
            jax.ShapeDtypeStruct((4 * MODES, channels), f32),
            jax.ShapeDtypeStruct((tiles, 2, MODES, LANES), f32),
            jax.ShapeDtypeStruct((groups, LANES), f32),
        ],
        scratch_shapes=[
            pltpu.VMEM((3, tokens + 8, LANES), f32),
            pltpu.VMEM((TILE_GROUPS, rows, LANES), bf16),
            pltpu.VMEM((TILE_GROUPS, rows, LANES), bf16),
            pltpu.VMEM((TILE_GROUPS, rows, LANES), bf16),
        ],
        compiler_params=pltpu.CompilerParams(vmem_limit_bytes=40 * 2**20),
        name="local_part",
    )(features, halo, short_taps, cotangent, params, rate_rows)

    ends, lagged, moment_0, moment_1 = (
        states[0:16],
        states[16:32],
        states[32:48],
        states[48:64],
    )
    s_prev = jnp.zeros_like(ends)
    l_prev = jnp.zeros_like(ends)
    e_next = jnp.zeros_like(ends)
    for key in range(1, ctx_count):
        other = ctx_index ^ key
        earlier = other < ctx_index
        sent = jnp.where(earlier, states[32:64], states[0:32])
        got = swapped(sent, "ctx", key)
        away = (jnp.abs(ctx_index - other) - 1).astype(f32) * tokens
        weight = jnp.exp(-rate_cols * away)
        s_part = weight * got[:16]
        s_prev = s_prev + jnp.where(earlier, s_part, 0.0)
        l_prev = l_prev + jnp.where(earlier, weight * got[16:] + away * s_part, 0.0)
        e_next = e_next + jnp.where(earlier, 0.0, s_part)
    own_end = ends + jnp.exp(-rate_cols * tokens) * s_prev
    bound = jnp.concatenate([s_prev, e_next, own_end], axis=0)

    summed_first = (moment_0 * s_prev).reshape(MODES, groups, MEMBERS).sum(axis=2).T
    summed_lag = (
        (moment_1 * s_prev + moment_0 * l_prev).reshape(MODES, groups, MEMBERS).sum(axis=2).T
    )
    diag = diag[:, :, :, :TILE_GROUPS].transpose(1, 0, 3, 2).reshape(2, groups, MODES)
    first_total = diag[0] + cross[:, 0:16] + summed_first
    lag_total = -(diag[1] + cross[:, 32:48] + cross[:, 48:64] + summed_lag)
    gain_part = jnp.sqrt(2.0 * decay_rates) * first_total
    rate_part = mode_coefs * (0.5 * first_total + decay_rates * lag_total)
    local = jnp.stack([gain_part, rate_part])
    terms = [local] + [swapped(local, "ctx", key) for key in range(1, ctx_count)]
    while len(terms) > 1:
        terms = [terms[i] + terms[i + 1] for i in range(0, len(terms), 2)]
    summed = terms[0]
    squares = jnp.broadcast_to(jnp.sum(summed * summed), (8, LANES))
    fsdp_count = lax.axis_size("fsdp")
    step = 1
    while step < fsdp_count:
        squares = squares + swapped(squares, "fsdp", step)
        step *= 2
    entry_count = 2 * groups * MODES * fsdp_count
    factor = jnp.minimum(1.0, lax.rsqrt(squares[0, 0] / entry_count + 1e-06))
    clipped = summed * factor

    wide_spec = pl.BlockSpec((MODES, LANES), lambda j: (0, j))
    mixer, feature_grads = pl.pallas_call(
        output_kernel,
        grid=(tiles,),
        in_specs=[
            feat_spec,
            halo_spec,
            pl.BlockSpec((4, 8, LANES), lambda j: (0, 0, j)),
            taps_spec,
            cot_spec,
            par_spec,
            rate_spec,
            per_group,
            per_group,
            per_group,
            pl.BlockSpec((3 * MODES, LANES), lambda j: (0, j)),
            wide_spec,
            wide_spec,
        ],
        out_specs=[cot_spec, feat_spec],
        out_shape=[
            jax.ShapeDtypeStruct((tokens, channels), bf16),
            jax.ShapeDtypeStruct((3, tokens, channels), bf16),
        ],
        scratch_shapes=[
            pltpu.VMEM((3, tokens + 16, LANES), f32),
            pltpu.VMEM((3, tokens + 8, LANES), f32),
            pltpu.VMEM((blocks, LANES, LANES), f32),
            pltpu.VMEM((blocks, LANES, LANES), f32),
        ],
        compiler_params=pltpu.CompilerParams(vmem_limit_bytes=40 * 2**20),
        name="output_part",
    )(
        features, halo, ahead, short_taps, cotangent, params, rate_rows,
        inner, grad, carry, bound, rate_cols, coef_cols,
    )
    return (mixer, feature_grads, clipped[0], clipped[1])


def solution(mesh):
    return jax.shard_map(
        per_device,
        mesh=mesh,
        in_specs=(
            P(None, "ctx", "fsdp"),
            P(None, None, "fsdp"),
            P("fsdp", None),
            P("fsdp", None),
            P("ctx", "fsdp"),
        ),
        out_specs=(P("ctx", "fsdp"), P(None, "ctx", "fsdp"), P("fsdp", None), P("fsdp", None)),
        check_vma=False,
    )
```

time: 933 us -> 138 us (0.15)
  local copies, waits for them, and re-layouts: 457 us -> 36 us
  matrix products: 322 us -> 0 us
  other arithmetic: 85.6 us -> 15.1 us
  Pallas kernels: 0 us -> 58 us
  blocking collectives: 47.9 us -> 0 us
  starting transfers between devices: 6.82 us -> 16.3 us
    dot_general x69 -> x0, matrix products: 322 us -> none  [the longest x8 67.6 us: forward_block(): jnp.einsum('kgnt,tgm->kngm', block_moments, e_block, precision=precise)]
    dynamic_update_slice x16 -> x0, local copies, waits for them, and re-layouts: 228 us -> none  [per_device(): lax.scan(forward_block, (zero_state, zero_state, zero_pairs, zero_pairs,...]
    gather x2 -> x0, local copies, waits for them, and re-layouts: 62.1 us -> none  [per_device(): filter_taps[:, jnp.maximum(lag_index, 0)]]
    pallas_call x0 -> x2, Pallas kernels: none -> 58 us  [the longest x1 43.9 us: per_device(): pl.pallas_call(local_kernel, grid=(tiles,), in_specs=[feat_spec, halo_spe...]
    rev x7 -> x0, local copies, waits for them, and re-layouts: 56.8 us -> none  [the longest x1 34.3 us: diagonal_sums(): flipped = jnp.flip(gram_acc, axis=2)]
    unnamed x76 -> x30, local copies, waits for them, and re-layouts: 50.4 us -> 14.6 us
    psum x2 -> x0, blocking collectives: 30.2 us -> none  [the longest x1 17.6 us: per_device(): summed = lax.psum(filter_local, 'ctx')]
    reshape x4, local copies, waits for them, and re-layouts: 26.3 us -> 5.26 us  [the longest x1 1.84 us: per_device(): (moment_1 * s_prev + moment_0 * l_prev).reshape(MODES, groups, MEMBERS)]
  transfers between devices with their start and end apart: 2 -> 11, of which waited for: 1 -> 4; matrix products, arithmetic and copies ran while one was open for 13% -> 12% of each run, Pallas kernels for 0% -> 10%
where the time goes in v1:
time: 138 us; the launch traced here: 136 us
  Pallas kernels  58 us (42%)
  local copies, waits for them, and re-layouts  36 us (26%)
  starting transfers between devices  16.3 us (12%)
  other arithmetic  15.1 us (11%)
  waiting for transfers between devices  8.9 us (6%)
  between operations  1.55 us (1%)
    pallas_call x1, Pallas kernels, per_device(): pl.pallas_call(local_kernel, grid=(tiles,), in_specs=[feat_spec, halo_spe...  43.9 us
    unnamed x30, local copies, waits for them, and re-layouts  14.6 us
    pallas_call x1, Pallas kernels, per_device(): pl.pallas_call(output_kernel, grid=(tiles,), in_specs=[feat_spec, halo_sp...  14.1 us
    ppermute x9, starting transfers between devices, swapped(): return lax.ppermute(value, axis, [(i, i ^ key) for i in range(count)])  11.2 us
    ppermute x9, waiting for transfers between devices, swapped(): return lax.ppermute(value, axis, [(i, i ^ key) for i in range(count)])  8.89 us
    ppermute x2, starting transfers between devices, shifted(): lax.ppermute(value, axis, [(i, (i + steps) % count) for i in range(count)])  5.11 us
  transfers between devices with their start and end apart: 11, of which 4 were waited for; matrix products, arithmetic and copies ran while one was open for 12% of the time, Pallas kernels for 10%

profile of v1, /device:TPU:0, one launch (start us, length us, event | category | flops | bytes accessed | tf_op | source)
XLA Modules:
  0.0 135.8 jit_solution(16017210486761964692)
XLA Ops:
  0.6 1.0 fusion.19
  1.6 3.1 %collective-permute-start = (bf16[3,2,1024]{2,1,0:T(2,128)(2,1)S(1)}, bf16[3,2,1024]{2,1,0:T(2,128)(2,1)S(1)}, u32[]{:S(2)}, u32[]{:S(2)}) collective-permute-start(bf16[3,2,1024]{2,1,0:T(2,128)(2,1)S(1)} %get-tuple-element.33), channel_id=1, source_target_pairs={{0,1},{1,2},{2,3},{3,0},{4,5},{5,6},{6,7},{7,4},{8,9},{9,10},{10,1... | collective-permute-start | bytes 36872 | tf_op jit(solution)/shard_map/ppermute | solution.py:284
  10.2 43.9 %local_part.1 = (f32[64,128,128]{2,1,0:T(8,128)S(1)}, f32[64,128,128]{2,1,0:T(8,128)S(1)}, f32[64,128,128]{2,1,0:T(8,128)}, f32[64,1024]{1,0:T(8,128)S(1)}, f32[...) custom-call(bf16[3,1024,1024]{2,1,0:T(8,128)(2,1)} %feat_ref.3, f32[3,8,1024]{2,1,0:T(8,128)S(1)} %pad.8.halo_ref, ...), custom_call_target="tpu_custom_call" | custom-call | tf_op jit(solution)/shard_map/local_part/pallas_call | solution.py:326
  54.1 2.0 %copy-done.1 = f32[64,128,128]{2,1,0:T(8,128)} copy-done((f32[64,128,128]{2,1,0:T(8,128)}, f32[64,128,128]{2,1,0:T(8,128)S(1)}, u32[]{:S(2)}) %copy-start.1) | copy-done | bytes 4194328
  56.1 2.0 %copy-done.3 = f32[64,128,128]{2,1,0:T(8,128)} copy-done((f32[64,128,128]{2,1,0:T(8,128)}, f32[64,128,128]{2,1,0:T(8,128)S(1)}, u32[]{:S(2)}) %copy-start.3) | copy-done | bytes 4194328
  59.0 1.6 %collective-permute-start.2 = (f32[32,1024]{1,0:T(8,128)}, f32[32,1024]{1,0:T(8,128)}, u32[]{:S(2)}, u32[]{:S(2)}) collective-permute-start(f32[32,1024]{1,0:T(8,128)} %get-tuple-element.36), channel_id=1, source_target_pairs={{0,1},{1,0},{2,3},{3,2},{4,5},{5,4},{6,7},{7,6},{8,9},{9,8},{10,11... | collective-permute-start | bytes 393224 | tf_op jit(solution)/shard_map/ppermute | solution.py:289
  60.5 2.5 %collective-permute-start.4 = (f32[32,1024]{1,0:T(8,128)}, f32[32,1024]{1,0:T(8,128)}, u32[]{:S(2)}, u32[]{:S(2)}) collective-permute-start(f32[32,1024]{1,0:T(8,128)} %get-tuple-element.37), channel_id=1, source_target_pairs={{0,3},{1,2},{2,1},{3,0},{4,7},{5,6},{6,5},{7,4},{8,11},{9,10},{10,... | collective-permute-start | bytes 393224 | tf_op jit(solution)/shard_map/ppermute | solution.py:289
  63.7 1.5 %copy.50 = f32[1,8,8,16]{3,2,1,0:T(8,128)} copy(f32[1,8,8,16]{2,3,0,1:T(8,128)} %get-tuple-element.41) | data formatting | bytes 8192 | tf_op jit(solution)/shard_map/slice | solution.py:384
  65.2 1.5 %copy.52 = f32[1,8,8,16]{3,2,1,0:T(8,128)} copy(f32[1,8,8,16]{2,3,0,1:T(8,128)} %get-tuple-element.42) | data formatting | bytes 8192 | tf_op jit(solution)/shard_map/slice | solution.py:385
  66.7 3.7 %collective-permute-done.4 = f32[32,1024]{1,0:T(8,128)} collective-permute-done((f32[32,1024]{1,0:T(8,128)}, f32[32,1024]{1,0:T(8,128)}, u32[]{:S(2)}, u32[]{:S(2)}) %collective-permute-start.4) | collective-permute-done | bytes 131104 | tf_op jit(solution)/shard_map/ppermute | solution.py:289
  70.5 3.7 %collective-permute-done.3 = f32[32,1024]{1,0:T(8,128)} collective-permute-done((f32[32,1024]{1,0:T(8,128)}, f32[32,1024]{1,0:T(8,128)}, u32[]{:S(2)}, u32[]{:S(2)}) %collective-permute-start.3) | collective-permute-done | bytes 131104 | tf_op jit(solution)/shard_map/ppermute | solution.py:289
  74.1 1.6 %slice_multiply_fusion.6 = (f32[16,1024]{1,0:T(8,128)}, f32[16,1024]{1,0:T(8,128)S(1)}) fusion(f32[64,1024]{1,0:T(8,128)S(1)} %get-tuple-element.15, f32[32,1024]{1,0:T(8,128)} %collective-permute-done.4, f32[]{:T(128)S(6)} %mul.116, pred[]{:T(512)S(6)} %lt.11, f32[32,1024]{1,0:T(8,128)} %collective-permute-done.3, f32[]{:T(128)S(6)} %mul.112, pred[]{:T(512)S(6)} %lt.10, ...), kind=kLoop, calls=%fused_computation.28 | loop fusion | flops 212992 | bytes 458767 | tf_op jit(solution)/shard_map/mul | solution.py:379
  76.3 1.7 %fusion.4 = (f32[16,1024]{1,0:T(8,128)}, f32[16,1024]{1,0:T(8,128)}) fusion(f32[32,1024]{1,0:T(8,128)} %collective-permute-done.4, f32[32,1024]{1,0:T(8,128)} %collective-permute-done.3, f32[32,1024]{1,0:T(8,128)} %collective-permute-done.2, f32[16,1024]{1,0:T(8,128)S(1)} %get-tuple-element.31, f32[64,1024]{1,0:T(8,128)S(1)} %get-tuple-element.15, ...), kind=kLoop, calls=%fused_computation.10 | loop fusion | flops 475136 | bytes 786447 | tf_op jit(solution)/shard_map/add | solution.py:381
  78.1 1.8 %reshape.40 = f32[16,64,16]{2,1,0:T(8,128)} reshape(f32[16,1024]{1,0:T(8,128)} %get-tuple-element.34) | data formatting | bytes 131072 | tf_op jit(solution)/shard_map/reshape | solution.py:381
  79.9 1.9 %reduce_sum.28 = f32[16,64]{1,0:T(8,128)} reduce(f32[16,64,16]{2,1,0:T(8,128)} %reshape.40, f32[]{:T(128)} %constant.10.clone.1), dimensions={2}, to_apply=%region_1.2 | reduce | flops 15360 | bytes 69636 | tf_op jit(solution)/shard_map/reduce_sum | solution.py:381
  81.8 1.4 %copy.53 = f32[16,64]{0,1:T(8,128)} copy(f32[16,64]{1,0:T(8,128)} %reduce_sum.28) | data formatting | bytes 8192 | tf_op jit(solution)/shard_map/reduce_sum | solution.py:381
  83.2 1.8 %reshape.39 = f32[16,64,16]{2,1,0:T(8,128)} reshape(f32[16,1024]{1,0:T(8,128)} %get-tuple-element.30) | data formatting | bytes 131072 | tf_op jit(solution)/shard_map/reshape | solution.py:379
  85.0 1.9 %reduce_sum.27 = f32[16,64]{1,0:T(8,128)} reduce(f32[16,64,16]{2,1,0:T(8,128)} %reshape.39, f32[]{:T(128)} %constant.10.clone.1), dimensions={2}, to_apply=%region_0.1 | reduce | flops 15360 | bytes 69636 | tf_op jit(solution)/shard_map/reduce_sum | solution.py:379
  86.9 1.4 %copy.51 = f32[16,64]{0,1:T(8,128)} copy(f32[16,64]{1,0:T(8,128)} %reduce_sum.27) | data formatting | bytes 8192 | tf_op jit(solution)/shard_map/reduce_sum | solution.py:379
  88.2 1.6 %multiply_bitcast_fusion = (f32[1,64,16]{2,1,0:T(8,128)}, f32[1,64,16]{2,1,0:T(8,128)}, f32[16,64]{0,1:T(8,128)}) fusion(f32[64,16]{1,0:T(8,128)} %copy-done.11, f32[16,64]{0,1:T(8,128)} %copy.51, f32[64,128]{1,0:T(8,128)S(1)} %get-tuple-element.19, f32[1,8,8,16]{3,2,1,0:T(8,128)} %copy.50, f32[16,64]{0,1:T(8,128)} %copy.53, f32[1,8,8,16]{3,2,1,0:T(8,128)} %copy.52, ...), kind=kLoop, calls=%fused_computation.39 | loop fusion | flops 13312 | bytes 49152 | tf_op jit(solution)/shard_map/stack | solution.py:388
  92.1 2.0 %collective-permute-start.7 = (f32[2,64,16]{1,2,0:T(8,128)}, f32[2,64,16]{1,2,0:T(8,128)}, u32[]{:S(2)}, u32[]{:S(2)}) collective-permute-start(f32[2,64,16]{1,2,0:T(8,128)} %pad_maximum_fusion.3), channel_id=1, source_target_pairs={{0,3},{1,2},{2,1},{3,0},{4,7},{5,6},{6,5},{7,4},{8,11},{9,10},{10,... | collective-permute-start | bytes 24584 | tf_op jit(solution)/shard_map/ppermute | solution.py:289
  94.1 1.5 %collective-permute-start.5 = (f32[2,64,16]{1,2,0:T(8,128)}, f32[2,64,16]{1,2,0:T(8,128)}, u32[]{:S(2)}, u32[]{:S(2)}) collective-permute-start(f32[2,64,16]{1,2,0:T(8,128)} %pad_maximum_fusion.3), channel_id=1, source_target_pairs={{0,1},{1,0},{2,3},{3,2},{4,5},{5,4},{6,7},{7,6},{8,9},{9,8},{10,11... | collective-permute-start | bytes 24584 | tf_op jit(solution)/shard_map/ppermute | solution.py:289
  96.2 2.0 %collective-permute-start.1 = (bf16[4,2,1024]{2,1,0:T(2,128)(2,1)}, bf16[4,2,1024]{2,1,0:T(2,128)(2,1)S(1)}, u32[]{:S(2)}, u32[]{:S(2)}) collective-permute-start(bf16[4,2,1024]{2,1,0:T(2,128)(2,1)} %pad_maximum_fusion.2), channel_id=1, source_target_pairs={{0,3},{1,0},{2,1},{3,2},{4,7},{5,4},{6,5},{7,6},{8,11},{9,8},{10,9... | collective-permute-start | bytes 49160 | tf_op jit(solution)/shard_map/ppermute | solution.py:284
  98.8 1.4 %multiply_reduce_fusion = (f32[]{:T(128)}, f32[2,64,16]{1,2,0:T(8,128)S(1)}) fusion(f32[2,64,16]{1,2,0:T(8,128)} %copy-done.13, f32[2,64,16]{1,2,0:T(8,128)} %collective-permute-done.7, f32[2,64,16]{1,2,0:T(8,128)} %collective-permute-done.5, f32[1,64,16]{1,2,0:T(8,128)S(1)} %copy.56, f32[1,64,16]{1,2,0:T(8,128)S(1)} %copy.55), kind=kLoop, calls=%fused_computation.46 | loop fusion | flops 12287 | bytes 40964 | tf_op jit(solution)/shard_map/reduce_sum | solution.py:393
  102.7 1.8 %collective-permute-start.9 = (f32[8,128]{1,0:T(8,128)S(1)}, f32[8,128]{1,0:T(8,128)S(1)}, u32[]{:S(2)}, u32[]{:S(2)}) collective-permute-start(f32[8,128]{1,0:T(8,128)S(1)} %broadcast_add_fusion), channel_id=1, source_target_pairs={{0,8},{4,12},{8,0},{12,4},{16,24},{20,28},{24,16},{28,20},{1,9},{5... | collective-permute-start | bytes 12296 | tf_op jit(solution)/shard_map/ppermute | solution.py:289
  105.4 1.0 collective-permute-done.9
  107.1 1.8 %collective-permute-start.10 = (f32[8,128]{1,0:T(8,128)S(1)}, f32[8,128]{1,0:T(8,128)S(1)}, u32[]{:S(2)}, u32[]{:S(2)}) collective-permute-start(f32[8,128]{1,0:T(8,128)S(1)} %fusion.21), channel_id=1, source_target_pairs={{0,16},{4,20},{8,24},{12,28},{16,0},{20,4},{24,8},{28,12},{1,17},{... | collective-permute-start | bytes 12296 | tf_op jit(solution)/shard_map/ppermute | solution.py:289
  110.6 1.0 broadcast_in_dim.45
  111.6 1.3 reshape.38.wide_coef_ref
  112.9 2.2 %copy-done.2 = f32[64,128,128]{2,1,0:T(8,128)S(1)} copy-done((f32[64,128,128]{2,1,0:T(8,128)S(1)}, f32[64,128,128]{2,1,0:T(8,128)}, u32[]{:S(2)}) %copy-start.2) | copy-done | bytes 4194328
  115.1 2.2 %copy-done.4 = f32[64,128,128]{2,1,0:T(8,128)S(1)} copy-done((f32[64,128,128]{2,1,0:T(8,128)S(1)}, f32[64,128,128]{2,1,0:T(8,128)}, u32[]{:S(2)}) %copy-start.4) | copy-done | bytes 4194328
  119.8 14.1 %output_part.1 = (bf16[1024,1024]{1,0:T(8,128)(2,1)}, bf16[3,1024,1024]{2,1,0:T(8,128)(2,1)}) custom-call(bf16[3,1024,1024]{2,1,0:T(8,128)(2,1)} %feat_ref.3, f32[3,8,1024]{2,1,0:T(8,128)S(1)} %copy-done.6, f32[4,8,1024]{2,1,0:T(8,128)S(1)} %copy-done.7, f32[3,3,1024]{2,1,0:T(4,128)S(1)} %copy-done.9, bf16[1024,1024]{1,0:T(8,128)(2,1)S(1)} %copy-done, ...), custom_call_target="tpu_custom_call" | custom-call | tf_op jit(solution)/shard_map/output_part/pallas_call | solution.py:404
  (66 shorter events, 20.4 us)
Async XLA Ops:
  0.6 8.8 %copy-start = (bf16[1024,1024]{1,0:T(8,128)(2,1)S(1)}, bf16[1024,1024]{1,0:T(8,128)(2,1)}, u32[]{:S(2)}) copy-start(bf16[1024,1024]{1,0:T(8,128)(2,1)} %cot_ref.3) | copy-start | bytes 6291460
  1.6 7.4 %collective-permute-start = (bf16[3,2,1024]{2,1,0:T(2,128)(2,1)S(1)}, bf16[3,2,1024]{2,1,0:T(2,128)(2,1)S(1)}, u32[]{:S(2)}, u32[]{:S(2)}) collective-permute-start(bf16[3,2,1024]{2,1,0:T(2,128)(2,1)S(1)} %get-tuple-element.33), channel_id=1, source_target_pairs={{0,1},{1,2},{2,3},{3,0},{4,5},{5,6},{6,7},{7,4},{8,9},{9,10},{10,1... | collective-permute-start | bytes 36872 | tf_op jit(solution)/shard_map/ppermute | solution.py:284
  6.2 1.6 %copy-start.11 = (f32[64,16]{1,0:T(8,128)}, f32[64,16]{1,0:T(8,128)S(1)}, u32[]{:S(2)}) copy-start(f32[64,16]{1,0:T(8,128)S(1)} %copy.44) | copy-start | bytes 12292
  7.0 0.9 copy-start.12
  9.1 45.0 %copy-start.5 = (f32[3,8,1024]{2,1,0:T(8,128)}, f32[3,8,1024]{2,1,0:T(8,128)S(1)}, u32[]{:S(2)}) copy-start(f32[3,8,1024]{2,1,0:T(8,128)S(1)} %pad.8.halo_ref) | copy-start | bytes 294916
  9.4 0.8 copy-start.8
  54.1 2.0 %copy-start.1 = (f32[64,128,128]{2,1,0:T(8,128)}, f32[64,128,128]{2,1,0:T(8,128)S(1)}, u32[]{:S(2)}) copy-start(f32[64,128,128]{2,1,0:T(8,128)S(1)} %get-tuple-element.12.inner_ref) | copy-start | bytes 12582916
  56.1 2.0 %copy-start.3 = (f32[64,128,128]{2,1,0:T(8,128)}, f32[64,128,128]{2,1,0:T(8,128)S(1)}, u32[]{:S(2)}) copy-start(f32[64,128,128]{2,1,0:T(8,128)S(1)} %get-tuple-element.13.grad_ref) | copy-start | bytes 12582916
  59.0 7.8 %collective-permute-start.2 = (f32[32,1024]{1,0:T(8,128)}, f32[32,1024]{1,0:T(8,128)}, u32[]{:S(2)}, u32[]{:S(2)}) collective-permute-start(f32[32,1024]{1,0:T(8,128)} %get-tuple-element.36), channel_id=1, source_target_pairs={{0,1},{1,0},{2,3},{3,2},{4,5},{5,4},{6,7},{7,6},{8,9},{9,8},{10,11... | collective-permute-start | bytes 393224 | tf_op jit(solution)/shard_map/ppermute | solution.py:289
  60.5 9.9 %collective-permute-start.4 = (f32[32,1024]{1,0:T(8,128)}, f32[32,1024]{1,0:T(8,128)}, u32[]{:S(2)}, u32[]{:S(2)}) collective-permute-start(f32[32,1024]{1,0:T(8,128)} %get-tuple-element.37), channel_id=1, source_target_pairs={{0,3},{1,2},{2,1},{3,0},{4,7},{5,6},{6,5},{7,4},{8,11},{9,10},{10,... | collective-permute-start | bytes 393224 | tf_op jit(solution)/shard_map/ppermute | solution.py:289
  63.0 11.1 %collective-permute-start.3 = (f32[32,1024]{1,0:T(8,128)}, f32[32,1024]{1,0:T(8,128)}, u32[]{:S(2)}, u32[]{:S(2)}) collective-permute-start(f32[32,1024]{1,0:T(8,128)} %get-tuple-element.38), channel_id=1, source_target_pairs={{0,2},{1,3},{2,0},{3,1},{4,6},{5,7},{6,4},{7,5},{8,10},{9,11},{10,... | collective-permute-start | bytes 393224 | tf_op jit(solution)/shard_map/ppermute | solution.py:289
  75.7 0.6 copy-start.10
  92.1 6.2 %collective-permute-start.6 = (f32[2,64,16]{1,2,0:T(8,128)}, f32[2,64,16]{1,2,0:T(8,128)S(1)}, u32[]{:S(2)}, u32[]{:S(2)}) collective-permute-start(f32[2,64,16]{1,2,0:T(8,128)} %pad_maximum_fusion.3), channel_id=1, source_target_pairs={{0,2},{1,3},{2,0},{3,1},{4,6},{5,7},{6,4},{7,5},{8,10},{9,11},{10,... | collective-permute-start | bytes 24584 | tf_op jit(solution)/shard_map/ppermute | solution.py:289
  92.1 6.2 %collective-permute-start.7 = (f32[2,64,16]{1,2,0:T(8,128)}, f32[2,64,16]{1,2,0:T(8,128)}, u32[]{:S(2)}, u32[]{:S(2)}) collective-permute-start(f32[2,64,16]{1,2,0:T(8,128)} %pad_maximum_fusion.3), channel_id=1, source_target_pairs={{0,3},{1,2},{2,1},{3,0},{4,7},{5,6},{6,5},{7,4},{8,11},{9,10},{10,... | collective-permute-start | bytes 24584 | tf_op jit(solution)/shard_map/ppermute | solution.py:289
  94.1 4.7 %collective-permute-start.5 = (f32[2,64,16]{1,2,0:T(8,128)}, f32[2,64,16]{1,2,0:T(8,128)}, u32[]{:S(2)}, u32[]{:S(2)}) collective-permute-start(f32[2,64,16]{1,2,0:T(8,128)} %pad_maximum_fusion.3), channel_id=1, source_target_pairs={{0,1},{1,0},{2,3},{3,2},{4,5},{5,4},{6,7},{7,6},{8,9},{9,8},{10,11... | collective-permute-start | bytes 24584 | tf_op jit(solution)/shard_map/ppermute | solution.py:289
  96.2 4.7 %collective-permute-start.1 = (bf16[4,2,1024]{2,1,0:T(2,128)(2,1)}, bf16[4,2,1024]{2,1,0:T(2,128)(2,1)S(1)}, u32[]{:S(2)}, u32[]{:S(2)}) collective-permute-start(bf16[4,2,1024]{2,1,0:T(2,128)(2,1)} %pad_maximum_fusion.2), channel_id=1, source_target_pairs={{0,3},{1,0},{2,1},{3,2},{4,7},{5,4},{6,5},{7,6},{8,11},{9,8},{10,9... | collective-permute-start | bytes 49160 | tf_op jit(solution)/shard_map/ppermute | solution.py:284
  98.2 0.6 copy-start.13
  100.8 1.2 collective-permute-start.8
  102.7 3.7 %collective-permute-start.9 = (f32[8,128]{1,0:T(8,128)S(1)}, f32[8,128]{1,0:T(8,128)S(1)}, u32[]{:S(2)}, u32[]{:S(2)}) collective-permute-start(f32[8,128]{1,0:T(8,128)S(1)} %broadcast_add_fusion), channel_id=1, source_target_pairs={{0,8},{4,12},{8,0},{12,4},{16,24},{20,28},{24,16},{28,20},{1,9},{5... | collective-permute-start | bytes 12296 | tf_op jit(solution)/shard_map/ppermute | solution.py:289
  107.1 26.9 %collective-permute-start.10 = (f32[8,128]{1,0:T(8,128)S(1)}, f32[8,128]{1,0:T(8,128)S(1)}, u32[]{:S(2)}, u32[]{:S(2)}) collective-permute-start(f32[8,128]{1,0:T(8,128)S(1)} %fusion.21), channel_id=1, source_target_pairs={{0,16},{4,20},{8,24},{12,28},{16,0},{20,4},{24,8},{28,12},{1,17},{... | collective-permute-start | bytes 12296 | tf_op jit(solution)/shard_map/ppermute | solution.py:289
  112.9 2.2 %copy-start.2 = (f32[64,128,128]{2,1,0:T(8,128)S(1)}, f32[64,128,128]{2,1,0:T(8,128)}, u32[]{:S(2)}) copy-start(f32[64,128,128]{2,1,0:T(8,128)} %copy-done.1) | copy-start | bytes 12582916
  115.1 2.2 %copy-start.4 = (f32[64,128,128]{2,1,0:T(8,128)S(1)}, f32[64,128,128]{2,1,0:T(8,128)}, u32[]{:S(2)}) copy-start(f32[64,128,128]{2,1,0:T(8,128)} %copy-done.3) | copy-start | bytes 12582916
  117.2 0.9 copy-start.6
  118.1 0.9 copy-start.7
  119.0 0.8 copy-start.9

commit v2 on v1

v2 whole, which is shorter than its diff:
```python
import jax
import jax.numpy as jnp
from jax import lax
from jax.experimental import pallas as pl
from jax.experimental.pallas import tpu as pltpu
from jax.sharding import PartitionSpec as P

LANES = 128
MODES = 16
MEMBERS = 16
TILE_GROUPS = LANES // MEMBERS
ROWS = LANES
f32 = jnp.float32
bf16 = jnp.bfloat16


def split(value):
    high = value.astype(bf16)
    return high, (value - high.astype(f32)).astype(bf16)


def dot_nt(left, right):
    return lax.dot_general(left, right, (((1,), (1,)), ((), ())), preferred_element_type=f32)


def dot_tn(left, right):
    return lax.dot_general(left, right, (((0,), (0,)), ((), ())), preferred_element_type=f32)


def dot_nn(left, right):
    return lax.dot_general(left, right, (((1,), (0,)), ((), ())), preferred_element_type=f32)


def iota(axis, shape):
    return lax.broadcasted_iota(jnp.int32, shape, axis)


def widen(feat_ref, halo_ref, wide, tokens):
    for i in range(3):
        wide[i, 0:8, :] = halo_ref[i]
        wide[i, 8 : 8 + tokens, :] = feat_ref[i].astype(f32)


def short_block(wide, taps_ref, i, start, count):
    return (
        taps_ref[i, 0:1, :] * wide[i, start + 8 : start + 8 + count, :]
        + taps_ref[i, 1:2, :] * wide[i, start + 7 : start + 7 + count, :]
        + taps_ref[i, 2:3, :] * wide[i, start + 6 : start + 6 + count, :]
    )


def sheared(row8, period):
    which = iota(0, row8.shape) % period
    for bit in (1, 2, 4):
        row8 = jnp.where((which & bit) != 0, pltpu.roll(row8, LANES - bit, 1), row8)
    return row8


def circulant(row):
    return pltpu.roll(jnp.broadcast_to(row, (LANES, LANES)), 0, 1, stride=1, stride_axis=0)


def parameters(rate_ref, gain_ref):
    rates = jnp.concatenate([rate_ref[...]] * (LANES // MODES), axis=1)
    gains = jnp.concatenate([gain_ref[...]] * (LANES // MODES), axis=1)
    coefs = gains * jnp.sqrt(2.0 * rates)
    own = iota(0, (TILE_GROUPS, LANES)) == iota(1, (TILE_GROUPS, LANES)) // MODES

    def columns(rows):
        flat = jnp.sum(jnp.where(own, rows, 0.0), axis=0, keepdims=True)
        return jnp.transpose(jnp.broadcast_to(flat, (LANES, LANES)))

    return rates, coefs, columns(rates), columns(coefs)


def per_member(rows):
    return jnp.concatenate(
        [jnp.broadcast_to(rows[g : g + 1], (MEMBERS, LANES)) for g in range(TILE_GROUPS)], axis=0
    )


def local_kernel(
    feat_ref, halo_ref, taps_ref, cot_ref, rate_ref, gain_ref,
    inner_ref, grad_ref, carry_ref, state_ref, diag_ref, cross_ref,
    wide, z_all, eh_all, el_all, wf_all, wb_all, x_all, y_all, power_all, fold_all,
):
    tokens = feat_ref.shape[1]
    blocks = tokens // LANES
    rate_rows, _, rates, coefs = parameters(rate_ref, gain_ref)
    lag = iota(1, (LANES, LANES)).astype(f32)
    row_at = iota(0, (LANES, LANES))
    lane_at = iota(1, (LANES, LANES))
    lane_row = iota(1, (1, LANES))

    power = jnp.exp(-rates * lag)
    power_back = jnp.exp(-rates * (LANES - 1.0 - lag))
    power_after = power * jnp.exp(-rates)
    power_all[...] = power
    by_group = (TILE_GROUPS, MODES, LANES)
    taps = jnp.sum((coefs * power).reshape(by_group), axis=1)
    taps_back = pltpu.roll(jnp.sum((coefs * power_back).reshape(by_group), axis=1), 1, 1)
    s_parts = split(power_back)
    l_parts = split((LANES - 1.0 - lag) * power_back)
    m_parts = split(power_after)
    n_parts = split((lag + 1.0) * power_after)
    nothing = jnp.zeros((4 * MODES, LANES), bf16)
    for g in range(TILE_GROUPS):
        of = slice(g * MODES, (g + 1) * MODES)
        toep_f = split(jnp.where(row_at >= lane_at, circulant(taps_back[g : g + 1]), 0.0))
        toep_b = split(jnp.where(lane_at >= row_at, circulant(taps[g : g + 1]), 0.0))
        for part in range(2):
            at = slice(part * LANES, (part + 1) * LANES)
            wf_all[g, 0:LANES, at] = toep_f[part]
            wb_all[g, 0:LANES, at] = toep_b[part]
            s_of, l_of = s_parts[part][of], l_parts[part][of]
            m_of, n_of = m_parts[part][of], n_parts[part][of]
            wf_all[g, LANES:, at] = jnp.concatenate([s_of, s_of, s_of, l_of, nothing], axis=0)
            wb_all[g, LANES:, at] = jnp.concatenate([nothing, m_of, m_of, n_of, m_of], axis=0)

    widen(feat_ref, halo_ref, wide, tokens)
    for b in range(blocks):
        query = short_block(wide, taps_ref, 0, b * LANES, LANES)
        key = short_block(wide, taps_ref, 1, b * LANES, LANES)
        value = short_block(wide, taps_ref, 2, b * LANES, LANES)
        z_t = jnp.transpose((key * value).astype(bf16))
        e_t = jnp.transpose(cot_ref[b * LANES : (b + 1) * LANES, :].astype(f32) * query)
        e_high, e_low = split(e_t)
        at = slice(b * MEMBERS, (b + 1) * MEMBERS)
        for g in range(TILE_GROUPS):
            of = slice(g * MEMBERS, (g + 1) * MEMBERS)
            z_all[g, at, :] = z_t[of]
            eh_all[g, at, :] = e_high[of]
            el_all[g, at, :] = e_low[of]

    for g in range(TILE_GROUPS):
        of = slice(g * MEMBERS, (g + 1) * MEMBERS)
        z = z_all[g]
        eh = eh_all[g]
        el = el_all[g]
        from_z = dot_nt(jnp.concatenate([z, z], axis=1), wf_all[g])
        wb = wb_all[g]
        wb_high = wb[:, :LANES]
        from_e = dot_nt(
            jnp.concatenate([eh, el, eh], axis=1),
            jnp.concatenate([wb_high, wb_high, wb[:, LANES:]], axis=1),
        )
        inner_ref[g] = from_z[:, :LANES]
        grad_ref[g] = from_e[:, :LANES]
        for b in range(blocks):
            at = slice(b * MEMBERS, (b + 1) * MEMBERS)
            x_all[b, of, :] = from_z[at, LANES:]
            y_all[b, of, :] = from_e[at, LANES:]
        z_back = jnp.transpose(z)
        gram = dot_nn(jnp.concatenate([z_back, z_back], axis=1), jnp.concatenate([eh, el], axis=0))
        gram = jnp.where(lane_at >= row_at, gram, 0.0)
        folded = [gram[0:8]] + [
            pltpu.roll(gram[8 * r : 8 * r + 8], LANES - 8 * r, 1) for r in range(1, LANES // 8)
        ]
        while len(folded) > 1:
            folded = [folded[i] + folded[i + 1] for i in range(0, len(folded), 2)]
        fold_all[8 * g : 8 * g + 8, :] = folded[0]

    span = per_member(jnp.exp(rate_rows * (-float(LANES))))
    in_x = jnp.where((lane_row >= 48) & (lane_row < 64), float(LANES), 0.0)
    in_y = jnp.where((lane_row >= 96) & (lane_row < 112), float(LANES), 0.0)
    x_now = jnp.zeros((LANES, LANES), f32)
    y_now = jnp.zeros((LANES, LANES), f32)
    x_lag = jnp.zeros((LANES, LANES), f32)
    y_lag = jnp.zeros((LANES, LANES), f32)
    cross = jnp.zeros((LANES, LANES), f32)
    for b in range(blocks):
        own = x_all[b]
        cross = cross + x_now * pltpu.roll(y_all[b], 4 * MODES, 1)
        carry_ref[0, b] = x_now
        x_now = span * (x_now + x_lag) + own
        x_lag = span * x_lag + in_x * pltpu.roll(own, MODES, 1)
    for b in reversed(range(blocks)):
        own = y_all[b]
        carry_ref[0, b] = carry_ref[0, b] + y_now
        y_now = span * (y_now + y_lag) + own
        y_lag = span * y_lag + in_y * pltpu.roll(own, MODES, 1)
    cross_ref[...] = jnp.sum(cross.reshape(TILE_GROUPS, MEMBERS, LANES), axis=1)
    turned = jnp.transpose(x_now + y_now)
    state_ref[0:16] = turned[0:16]
    state_ref[16:32] = turned[48:64]
    state_ref[32:48] = turned[64:80]
    state_ref[48:64] = turned[96:112]

    corr = jnp.sum(
        sheared(fold_all[...], 8).reshape(TILE_GROUPS, 8, LANES), axis=1
    )
    weighted = power_all[...] * per_member(corr)
    first_col = jnp.sum(weighted, axis=1, keepdims=True)
    lag_col = jnp.sum(lag * weighted, axis=1, keepdims=True)
    packed = jnp.where(lane_at == 0, first_col, jnp.where(lane_at == 1, lag_col, 0.0))
    diag_ref[0] = jnp.transpose(packed)[0:8]


def output_kernel(
    feat_ref, halo_ref, next_ref, taps_ref, cot_ref, rate_ref, gain_ref,
    inner_ref, grad_ref, carry_ref, bound_ref,
    mixer_ref, fgrad_ref,
    wide, adj, inner_t, grad_t, left_all,
):
    tokens = feat_ref.shape[1]
    blocks = tokens // LANES
    widen(feat_ref, halo_ref, wide, tokens)
    for i in range(3):
        wide[i, 8 + tokens : 16 + tokens, :] = next_ref[i]
    rate_rows, coef_rows, rates, coefs = parameters(rate_ref, gain_ref)
    lag = iota(1, (LANES, LANES)).astype(f32)
    lane_row = iota(1, (1, LANES))
    lane_at = iota(1, (LANES, LANES))
    is_low = ((lane_at >= 16) & (lane_at < 32)) | ((lane_at >= 80) & (lane_at < 96))
    before = bound_ref[0:16]
    after = bound_ref[16:32]
    gap = jnp.zeros((MODES, LANES), f32)
    stacked = jnp.concatenate([before, before, before, gap, after, after, gap, after], axis=0)
    turned = jnp.transpose(stacked)
    none_16 = jnp.zeros((MODES, LANES), bf16)
    none_64 = jnp.zeros((4 * MODES, LANES), bf16)
    member_rates = per_member(rate_rows)
    for b in range(blocks):
        steps = jnp.where(lane_row < 64, float(b * LANES), float((blocks - 1 - b) * LANES))
        value = carry_ref[0, b] + turned * jnp.exp(-member_rates * steps)
        high = value.astype(bf16).astype(f32)
        mixed = jnp.where(is_low, value - high, value).astype(bf16)
        for g in range(TILE_GROUPS):
            left_all[g, b * MEMBERS : (b + 1) * MEMBERS, :] = mixed[
                g * MEMBERS : (g + 1) * MEMBERS
            ]
    cz_parts = split(coefs * jnp.exp(-rates * (lag + 1.0)))
    ce_parts = split(coefs * jnp.exp(-rates * (LANES - 1.0 - lag)))
    for g in range(TILE_GROUPS):
        of = slice(g * MODES, (g + 1) * MODES)
        cz_high, cz_low = cz_parts[0][of], cz_parts[1][of]
        ce_high, ce_low = ce_parts[0][of], ce_parts[1][of]
        right = jnp.concatenate(
            [
                jnp.concatenate([cz_high, cz_high, cz_low, none_16, none_64], axis=0),
                jnp.concatenate([none_64, ce_high, ce_high, none_16, ce_low], axis=0),
            ],
            axis=1,
        )
        carried = dot_nn(left_all[g], right)
        whole_inner = inner_ref[g] + carried[:, :LANES]
        whole_grad = grad_ref[g] + carried[:, LANES:]
        for b in range(blocks):
            at = slice(b * MEMBERS, (b + 1) * MEMBERS)
            inner_t[b, of, :] = whole_inner[at]
            grad_t[b, of, :] = whole_grad[at]
    for b in range(blocks):
        at = slice(b * LANES, (b + 1) * LANES)
        query = short_block(wide, taps_ref, 0, b * LANES, LANES)
        key = short_block(wide, taps_ref, 1, b * LANES, LANES)
        value = short_block(wide, taps_ref, 2, b * LANES, LANES)
        inner = jnp.transpose(inner_t[b])
        grad = jnp.transpose(grad_t[b])
        mixer_ref[at, :] = (query * inner).astype(bf16)
        adj[0, at, :] = cot_ref[at, :].astype(f32) * inner
        adj[1, at, :] = grad * value
        adj[2, at, :] = grad * key
    key = short_block(wide, taps_ref, 1, tokens, 8)
    value = short_block(wide, taps_ref, 2, tokens, 8)
    query = short_block(wide, taps_ref, 0, tokens, 8)
    z = (key * value).astype(bf16).astype(f32)
    e = next_ref[3] * query
    rates = jnp.transpose(member_rates)[0:MODES]
    coefs = jnp.transpose(per_member(coef_rows))[0:MODES]
    decay = jnp.exp(-rates)
    grow = jnp.exp(rates)
    state = bound_ref[32:48]
    sum_0 = jnp.sum(coefs, axis=0, keepdims=True)
    sum_1 = jnp.sum(coefs * decay, axis=0, keepdims=True)
    inner_0 = jnp.sum(coefs * decay * state, axis=0, keepdims=True) + sum_0 * z[0:1]
    inner_1 = (
        jnp.sum(coefs * decay * decay * state, axis=0, keepdims=True)
        + sum_1 * z[0:1]
        + sum_0 * z[1:2]
    )
    grad_0 = jnp.sum(coefs * grow * after, axis=0, keepdims=True)
    grad_1 = jnp.sum(coefs * grow * (grow * after - e[0:1]), axis=0, keepdims=True)
    which = iota(0, (8, LANES))
    inner_8 = jnp.where(which == 0, inner_0, jnp.where(which == 1, inner_1, 0.0))
    grad_8 = jnp.where(which == 0, grad_0, jnp.where(which == 1, grad_1, 0.0))
    adj[0, tokens : tokens + 8, :] = next_ref[3] * inner_8
    adj[1, tokens : tokens + 8, :] = grad_8 * value
    adj[2, tokens : tokens + 8, :] = grad_8 * key
    for b in range(blocks):
        start = b * LANES
        for i in range(3):
            fgrad_ref[i, start : start + LANES, :] = (
                taps_ref[i, 0:1, :] * adj[i, start : start + LANES, :]
                + taps_ref[i, 1:2, :] * adj[i, start + 1 : start + 1 + LANES, :]
                + taps_ref[i, 2:3, :] * adj[i, start + 2 : start + 2 + LANES, :]
            ).astype(bf16)


def shifted(value, axis, steps):
    count = lax.axis_size(axis)
    return lax.ppermute(value, axis, [(i, (i + steps) % count) for i in range(count)])


def swapped(value, axis, key):
    count = lax.axis_size(axis)
    return lax.ppermute(value, axis, [(i, i ^ key) for i in range(count)])


def per_device(features, short_taps, decay_rates, mode_gains, cotangent):
    tokens = features.shape[1]
    channels = features.shape[2]
    groups = decay_rates.shape[0]
    tiles = channels // LANES
    blocks = tokens // LANES
    ctx_count = lax.axis_size("ctx")
    ctx_index = lax.axis_index("ctx")

    tail = shifted(features[:, tokens - 2 :, :], "ctx", 1).astype(f32)
    tail = jnp.where(ctx_index == 0, 0.0, tail)
    halo = jnp.pad(tail, ((0, 0), (6, 0), (0, 0)))
    head = jnp.concatenate([features[:, :2, :], cotangent[None, :2, :]], axis=0)
    ahead = shifted(head, "ctx", -1).astype(f32)
    ahead = jnp.where(ctx_index == ctx_count - 1, 0.0, ahead)
    ahead = jnp.pad(ahead, ((0, 0), (0, 6), (0, 0)))

    mode_coefs = mode_gains * jnp.sqrt(2.0 * decay_rates)
    rate_cols = jnp.repeat(decay_rates.T, MEMBERS, axis=1)

    per_group = pl.BlockSpec((TILE_GROUPS, ROWS, LANES), lambda j: (j, 0, 0))
    feat_spec = pl.BlockSpec((3, tokens, LANES), lambda j: (0, 0, j))
    halo_spec = pl.BlockSpec((3, 8, LANES), lambda j: (0, 0, j))
    taps_spec = pl.BlockSpec((3, 3, LANES), lambda j: (0, 0, j))
    cot_spec = pl.BlockSpec((tokens, LANES), lambda j: (0, j))
    rate_spec = pl.BlockSpec((TILE_GROUPS, MODES), lambda j: (j, 0))
    carry_spec = pl.BlockSpec((1, blocks, LANES, LANES), lambda j: (j, 0, 0, 0))
    rows = blocks * MEMBERS
    big = jax.ShapeDtypeStruct((groups, rows, LANES), f32)
    inner, grad, carry, states, diag, cross = pl.pallas_call(
        local_kernel,
        grid=(tiles,),
        in_specs=[feat_spec, halo_spec, taps_spec, cot_spec, rate_spec, rate_spec],
        out_specs=[
            per_group,
            per_group,
            carry_spec,
            pl.BlockSpec((4 * MODES, LANES), lambda j: (0, j)),
            pl.BlockSpec((1, 8, LANES), lambda j: (j, 0, 0)),
            pl.BlockSpec((TILE_GROUPS, LANES), lambda j: (j, 0)),
        ],
        out_shape=[
            big,
            big,
            jax.ShapeDtypeStruct((tiles, blocks, LANES, LANES), f32),
            jax.ShapeDtypeStruct((4 * MODES, channels), f32),
            jax.ShapeDtypeStruct((tiles, 8, LANES), f32),
            jax.ShapeDtypeStruct((groups, LANES), f32),
        ],
        scratch_shapes=[
            pltpu.VMEM((3, tokens + 8, LANES), f32),
            pltpu.VMEM((TILE_GROUPS, rows, LANES), bf16),
            pltpu.VMEM((TILE_GROUPS, rows, LANES), bf16),
            pltpu.VMEM((TILE_GROUPS, rows, LANES), bf16),
            pltpu.VMEM((TILE_GROUPS, 2 * LANES, 2 * LANES), bf16),
            pltpu.VMEM((TILE_GROUPS, 2 * LANES, 2 * LANES), bf16),
            pltpu.VMEM((blocks, LANES, LANES), f32),
            pltpu.VMEM((blocks, LANES, LANES), f32),
            pltpu.VMEM((LANES, LANES), f32),
            pltpu.VMEM((8 * TILE_GROUPS, LANES), f32),
        ],
        compiler_params=pltpu.CompilerParams(vmem_limit_bytes=40 * 2**20),
        name="local_part",
    )(features, halo, short_taps, cotangent, decay_rates, mode_gains)

    ends, lagged, moment_0, moment_1 = (
        states[0:16],
        states[16:32],
        states[32:48],
        states[48:64],
    )
    s_prev = jnp.zeros_like(ends)
    l_prev = jnp.zeros_like(ends)
    e_next = jnp.zeros_like(ends)
    for key in range(1, ctx_count):
        other = ctx_index ^ key
        earlier = other < ctx_index
        sent = jnp.where(earlier, states[32:64], states[0:32])
        got = swapped(sent, "ctx", key)
        away = (jnp.abs(ctx_index - other) - 1).astype(f32) * tokens
        weight = jnp.exp(-rate_cols * away)
        s_part = weight * got[:16]
        s_prev = s_prev + jnp.where(earlier, s_part, 0.0)
        l_prev = l_prev + jnp.where(earlier, weight * got[16:] + away * s_part, 0.0)
        e_next = e_next + jnp.where(earlier, 0.0, s_part)
    own_end = ends + jnp.exp(-rate_cols * tokens) * s_prev
    bound = jnp.concatenate([s_prev, e_next, own_end], axis=0)

    summed_first = (moment_0 * s_prev).reshape(MODES, groups, MEMBERS).sum(axis=2).T
    summed_lag = (
        (moment_1 * s_prev + moment_0 * l_prev).reshape(MODES, groups, MEMBERS).sum(axis=2).T
    )
    diag = [diag[:, i, :].reshape(groups, MODES) for i in range(2)]
    first_total = diag[0] + cross[:, 0:16] + summed_first
    lag_total = -(diag[1] + cross[:, 32:48] + cross[:, 48:64] + summed_lag)
    gain_part = jnp.sqrt(2.0 * decay_rates) * first_total
    rate_part = mode_coefs * (0.5 * first_total + decay_rates * lag_total)
    local = jnp.stack([gain_part, rate_part])
    terms = [local] + [swapped(local, "ctx", key) for key in range(1, ctx_count)]
    while len(terms) > 1:
        terms = [terms[i] + terms[i + 1] for i in range(0, len(terms), 2)]
    summed = terms[0]
    squares = jnp.broadcast_to(jnp.sum(summed * summed), (8, LANES))
    fsdp_count = lax.axis_size("fsdp")
    step = 1
    while step < fsdp_count:
        squares = squares + swapped(squares, "fsdp", step)
        step *= 2
    entry_count = 2 * groups * MODES * fsdp_count
    factor = jnp.minimum(1.0, lax.rsqrt(squares[0, 0] / entry_count + 1e-06))
    clipped = summed * factor

    mixer, feature_grads = pl.pallas_call(
        output_kernel,
        grid=(tiles,),
        in_specs=[
            feat_spec,
            halo_spec,
            pl.BlockSpec((4, 8, LANES), lambda j: (0, 0, j)),
            taps_spec,
            cot_spec,
            rate_spec,
            rate_spec,
            per_group,
            per_group,
            carry_spec,
            pl.BlockSpec((3 * MODES, LANES), lambda j: (0, j)),
        ],
        out_specs=[cot_spec, feat_spec],
        out_shape=[
            jax.ShapeDtypeStruct((tokens, channels), bf16),
            jax.ShapeDtypeStruct((3, tokens, channels), bf16),
        ],
        scratch_shapes=[
            pltpu.VMEM((3, tokens + 16, LANES), f32),
            pltpu.VMEM((3, tokens + 8, LANES), f32),
            pltpu.VMEM((blocks, LANES, LANES), f32),
            pltpu.VMEM((blocks, LANES, LANES), f32),
            pltpu.VMEM((TILE_GROUPS, rows, LANES), bf16),
        ],
        compiler_params=pltpu.CompilerParams(vmem_limit_bytes=40 * 2**20),
        name="output_part",
    )(
        features, halo, ahead, short_taps, cotangent, decay_rates, mode_gains,
        inner, grad, carry, bound,
    )
    return (mixer, feature_grads, clipped[0], clipped[1])


def solution(mesh):
    return jax.shard_map(
        per_device,
        mesh=mesh,
        in_specs=(
            P(None, "ctx", "fsdp"),
            P(None, None, "fsdp"),
            P("fsdp", None),
            P("fsdp", None),
            P("ctx", "fsdp"),
        ),
        out_specs=(P("ctx", "fsdp"), P(None, "ctx", "fsdp"), P("fsdp", None), P("fsdp", None)),
        check_vma=False,
    )
```

time: 138 us -> 93.5 us (0.68); the launches traced: 136 us -> 92.7 us
  Pallas kernels: 58 us -> 37.1 us
  local copies, waits for them, and re-layouts: 36 us -> 17.7 us
  other arithmetic: 15.1 us -> 5.89 us
  waiting for transfers between devices: 8.9 us -> 12.8 us
  starting transfers between devices: 16.3 us -> 17.7 us
    pallas_call x1, Pallas kernels: 43.9 us -> 22.6 us  [per_device(): pl.pallas_call(local_kernel, grid=(tiles,), in_specs=[feat_spec, halo_spe...]
    slice x3 -> x1, local copies, waits for them, and re-layouts: 3.73 us -> 0.02 us  [per_device(): diag = [diag[:, i, :].reshape(groups, MODES) for i in range(2)]]
    ppermute x9, waiting for transfers between devices: 8.89 us -> 11.4 us  [swapped(): return lax.ppermute(value, axis, [(i, i ^ key) for i in range(count)])]
    unnamed x30 -> x18, local copies, waits for them, and re-layouts: 14.6 us -> 12.3 us
    another operation x2, other arithmetic: 2.17 us -> 0.1 us  [per_device(): local = jnp.stack([gain_part, rate_part])]
    reduce_sum x1, other arithmetic: 1.85 us -> 0.21 us  [per_device(): (moment_0 * s_prev).reshape(MODES, groups, MEMBERS).sum(axis=2)]
    reduce_sum x1, other arithmetic: 1.85 us -> 0.21 us  [per_device(): (moment_1 * s_prev + moment_0 * l_prev).reshape(MODES, groups, MEMBERS)]
    reshape x1, local copies, waits for them, and re-layouts: 1.84 us -> 0.2 us  [per_device(): (moment_1 * s_prev + moment_0 * l_prev).reshape(MODES, groups, MEMBERS)]
  transfers between devices with their start and end apart: 11 -> 11, of which waited for: 4 -> 6; matrix products, arithmetic and copies ran while one was open for 12% -> 6% of each run, Pallas kernels for 10% -> 16%
where the time goes in v2:
time: 93.5 us; the launch traced here: 92.7 us
  Pallas kernels  37.1 us (40%)
  local copies, waits for them, and re-layouts  17.7 us (19%)
  starting transfers between devices  17.7 us (19%)
  waiting for transfers between devices  12.8 us (14%)
  other arithmetic  5.89 us (6%)
  between operations  1.57 us (2%)
    pallas_call x1, Pallas kernels, per_device(): pl.pallas_call(local_kernel, grid=(tiles,), in_specs=[feat_spec, halo_spe...  22.6 us
    pallas_call x1, Pallas kernels, per_device(): pl.pallas_call(output_kernel, grid=(tiles,), in_specs=[feat_spec, halo_sp...  14.5 us
    unnamed x18, local copies, waits for them, and re-layouts  12.3 us
    ppermute x9, starting transfers between devices, swapped(): return lax.ppermute(value, axis, [(i, i ^ key) for i in range(count)])  12.1 us
    ppermute x9, waiting for transfers between devices, swapped(): return lax.ppermute(value, axis, [(i, i ^ key) for i in range(count)])  11.4 us
    ppermute x2, starting transfers between devices, shifted(): lax.ppermute(value, axis, [(i, (i + steps) % count) for i in range(count)])  5.57 us
  transfers between devices with their start and end apart: 11, of which 6 were waited for; matrix products, arithmetic and copies ran while one was open for 6% of the time, Pallas kernels for 16%

profile of v2, /device:TPU:0, one launch (start us, length us, event | category | flops | bytes accessed | tf_op | source)
XLA Modules:
  0.0 92.7 jit_solution(17310128428623443558)
XLA Ops:
  0.6 0.8 fusion.15
  1.5 3.1 %collective-permute-start = (bf16[3,2,1024]{2,1,0:T(2,128)(2,1)S(1)}, bf16[3,2,1024]{2,1,0:T(2,128)(2,1)S(1)}, u32[]{:S(2)}, u32[]{:S(2)}) collective-permute-start(bf16[3,2,1024]{2,1,0:T(2,128)(2,1)S(1)} %get-tuple-element.35), channel_id=1, source_target_pairs={{0,1},{1,2},{2,3},{3,0},{4,5},{5,6},{6,7},{7,4},{8,9},{9,10},{10,1... | collective-permute-start | bytes 36872 | tf_op jit(solution)/shard_map/ppermute | solution.py:301
  4.6 0.7 exponential_bitcast_fusion.3
  5.3 0.8 copy.29.rate_ref
  6.1 0.8 copy.30.gain_ref
  6.8 1.4 %collective-permute-done = bf16[3,2,1024]{2,1,0:T(2,128)(2,1)S(1)} collective-permute-done((bf16[3,2,1024]{2,1,0:T(2,128)(2,1)S(1)}, bf16[3,2,1024]{2,1,0:T(2,128)(2,1)S(1)}, u32[]{:S(2)}, u32[]{:S(2)}) %collective-permute-start) | collective-permute-done | bytes 12320 | tf_op jit(solution)/shard_map/ppermute | solution.py:301
  8.3 1.6 %copy-done = bf16[1024,1024]{1,0:T(8,128)(2,1)S(1)} copy-done((bf16[1024,1024]{1,0:T(8,128)(2,1)S(1)}, bf16[1024,1024]{1,0:T(8,128)(2,1)}, u32[]{:S(2)}) %copy-start) | copy-done | bytes 2097176
  9.9 0.8 copy-done.6
  10.7 22.6 %local_part.1 = (f32[64,128,128]{2,1,0:T(8,128)S(1)}, f32[64,128,128]{2,1,0:T(8,128)S(1)}, f32[8,8,128,128]{3,2,1,0:T(8,128)}, f32[64,1024]{1,0:T(8,128)S(1)}, f...) custom-call(bf16[3,1024,1024]{2,1,0:T(8,128)(2,1)} %feat_ref.3, f32[3,8,1024]{2,1,0:T(8,128)S(1)} %pad.8.halo_ref, ...), custom_call_target="tpu_custom_call" | custom-call | tf_op jit(solution)/shard_map/local_part/pallas_call | solution.py:338
  33.3 2.0 %copy-done.2 = f32[64,128,128]{2,1,0:T(8,128)} copy-done((f32[64,128,128]{2,1,0:T(8,128)}, f32[64,128,128]{2,1,0:T(8,128)S(1)}, u32[]{:S(2)}) %copy-start.2) | copy-done | bytes 4194328
  35.3 2.0 %copy-done.4 = f32[64,128,128]{2,1,0:T(8,128)} copy-done((f32[64,128,128]{2,1,0:T(8,128)}, f32[64,128,128]{2,1,0:T(8,128)S(1)}, u32[]{:S(2)}) %copy-start.4) | copy-done | bytes 4194328
  37.3 0.8 slice_select_fusion.2
  38.2 2.4 %collective-permute-start.3 = (f32[32,1024]{1,0:T(8,128)}, f32[32,1024]{1,0:T(8,128)}, u32[]{:S(2)}, u32[]{:S(2)}) collective-permute-start(f32[32,1024]{1,0:T(8,128)} %get-tuple-element.39), channel_id=1, source_target_pairs={{0,2},{1,3},{2,0},{3,1},{4,6},{5,7},{6,4},{7,5},{8,10},{9,11},{10,... | collective-permute-start | bytes 393224 | tf_op jit(solution)/shard_map/ppermute | solution.py:306
  40.6 1.8 %collective-permute-start.4 = (f32[32,1024]{1,0:T(8,128)}, f32[32,1024]{1,0:T(8,128)}, u32[]{:S(2)}, u32[]{:S(2)}) collective-permute-start(f32[32,1024]{1,0:T(8,128)} %get-tuple-element.38), channel_id=1, source_target_pairs={{0,3},{1,2},{2,1},{3,0},{4,7},{5,6},{6,5},{7,4},{8,11},{9,10},{10,... | collective-permute-start | bytes 393224 | tf_op jit(solution)/shard_map/ppermute | solution.py:306
  44.3 6.8 %collective-permute-done.3 = f32[32,1024]{1,0:T(8,128)} collective-permute-done((f32[32,1024]{1,0:T(8,128)}, f32[32,1024]{1,0:T(8,128)}, u32[]{:S(2)}, u32[]{:S(2)}) %collective-permute-start.3) | collective-permute-done | bytes 131104 | tf_op jit(solution)/shard_map/ppermute | solution.py:306
  51.1 0.9 slice_multiply_fusion.6
  52.0 1.0 %fusion.4 = f32[16,1024]{1,0:T(8,128)S(1)} fusion(f32[16,1024]{1,0:T(8,128)S(1)} %exp.48, f32[32,1024]{1,0:T(8,128)} %collective-permute-done.4, f32[16,1024]{1,0:T(8,128)S(1)} %exp.45, f32[32,1024]{1,0:T(8,128)} %collective-permute-done.3, f32[16,1024]{1,0:T(8,128)S(1)} %exp.42, f32[32,1024]{1,0:T(8,128)S(1)} %collective-permute-done.2, ...), kind=kLoop, calls=%fused_computation.9 | loop fusion | flops 327680 | bytes 851983 | tf_op jit(solution)/shard_map/add | solution.py:399
  54.3 2.0 %collective-permute-start.5 = (f32[2,64,16]{1,2,0:T(8,128)S(1)}, f32[2,64,16]{1,2,0:T(8,128)S(1)}, u32[]{:S(2)}, u32[]{:S(2)}) collective-permute-start(f32[2,64,16]{1,2,0:T(8,128)S(1)} %pad_maximum_fusion.2), channel_id=1, source_target_pairs={{0,1},{1,0},{2,3},{3,2},{4,5},{5,4},{6,7},{7,6},{8,9},{9,8},{10,11... | collective-permute-start | bytes 24584 | tf_op jit(solution)/shard_map/ppermute | solution.py:306
  56.3 1.1 %collective-permute-start.6 = (f32[2,64,16]{1,2,0:T(8,128)S(1)}, f32[2,64,16]{1,2,0:T(8,128)S(1)}, u32[]{:S(2)}, u32[]{:S(2)}) collective-permute-start(f32[2,64,16]{1,2,0:T(8,128)S(1)} %pad_maximum_fusion.2), channel_id=1, source_target_pairs={{0,2},{1,3},{2,0},{3,1},{4,6},{5,7},{6,4},{7,5},{8,10},{9,11},{10,... | collective-permute-start | bytes 24584 | tf_op jit(solution)/shard_map/ppermute | solution.py:306
  57.4 1.4 %collective-permute-start.7 = (f32[2,64,16]{1,2,0:T(8,128)S(1)}, f32[2,64,16]{1,2,0:T(8,128)S(1)}, u32[]{:S(2)}, u32[]{:S(2)}) collective-permute-start(f32[2,64,16]{1,2,0:T(8,128)S(1)} %pad_maximum_fusion.2), channel_id=1, source_target_pairs={{0,3},{1,2},{2,1},{3,0},{4,7},{5,6},{6,5},{7,4},{8,11},{9,10},{10,... | collective-permute-start | bytes 24584 | tf_op jit(solution)/shard_map/ppermute | solution.py:306
  58.8 2.5 %collective-permute-start.1 = (bf16[4,2,1024]{2,1,0:T(2,128)(2,1)S(1)}, bf16[4,2,1024]{2,1,0:T(2,128)(2,1)S(1)}, u32[]{:S(2)}, u32[]{:S(2)}) collective-permute-start(bf16[4,2,1024]{2,1,0:T(2,128)(2,1)S(1)} %pad_maximum_fusion.1), channel_id=1, source_target_pairs={{0,3},{1,0},{2,1},{3,2},{4,7},{5,4},{6,5},{7,6},{8,11},{9,8},{10,9... | collective-permute-start | bytes 49160 | tf_op jit(solution)/shard_map/ppermute | solution.py:301
  61.8 1.1 %collective-permute-done.7 = f32[2,64,16]{1,2,0:T(8,128)S(1)} collective-permute-done((f32[2,64,16]{1,2,0:T(8,128)S(1)}, f32[2,64,16]{1,2,0:T(8,128)S(1)}, u32[]{:S(2)}, u32[]{:S(2)}) %collective-permute-start.7) | collective-permute-done | bytes 8224 | tf_op jit(solution)/shard_map/ppermute | solution.py:306
  63.5 0.6 broadcast_in_dim.44
  64.3 1.1 %collective-permute-done.8 = f32[8,128]{1,0:T(8,128)S(1)} collective-permute-done((f32[8,128]{1,0:T(8,128)S(1)}, f32[8,128]{1,0:T(8,128)S(1)}, u32[]{:S(2)}, u32[]{:S(2)}) %collective-permute-start.8) | collective-permute-done | bytes 4128 | tf_op jit(solution)/shard_map/ppermute | solution.py:306
  65.4 0.6 broadcast_add_fusion
  66.0 1.6 %collective-permute-start.9 = (f32[8,128]{1,0:T(8,128)S(1)}, f32[8,128]{1,0:T(8,128)S(1)}, u32[]{:S(2)}, u32[]{:S(2)}) collective-permute-start(f32[8,128]{1,0:T(8,128)S(1)} %broadcast_add_fusion), channel_id=1, source_target_pairs={{0,8},{4,12},{8,0},{12,4},{16,24},{20,28},{24,16},{28,20},{1,9},{5... | collective-permute-start | bytes 12296 | tf_op jit(solution)/shard_map/ppermute | solution.py:306
  67.6 2.1 %collective-permute-done.9 = f32[8,128]{1,0:T(8,128)S(1)} collective-permute-done((f32[8,128]{1,0:T(8,128)S(1)}, f32[8,128]{1,0:T(8,128)S(1)}, u32[]{:S(2)}, u32[]{:S(2)}) %collective-permute-start.9) | collective-permute-done | bytes 4128 | tf_op jit(solution)/shard_map/ppermute | solution.py:306
  69.7 0.6 fusion.16
  70.4 1.6 %collective-permute-start.10 = (f32[8,128]{1,0:T(8,128)S(1)}, f32[8,128]{1,0:T(8,128)S(1)}, u32[]{:S(2)}, u32[]{:S(2)}) collective-permute-start(f32[8,128]{1,0:T(8,128)S(1)} %fusion.16), channel_id=1, source_target_pairs={{0,16},{4,20},{8,24},{12,28},{16,0},{20,4},{24,8},{28,12},{1,17},{... | collective-permute-start | bytes 12296 | tf_op jit(solution)/shard_map/ppermute | solution.py:306
  72.0 2.2 %copy-done.3 = f32[64,128,128]{2,1,0:T(8,128)S(1)} copy-done((f32[64,128,128]{2,1,0:T(8,128)S(1)}, f32[64,128,128]{2,1,0:T(8,128)}, u32[]{:S(2)}) %copy-start.3) | copy-done | bytes 4194328
  74.2 2.2 %copy-done.5 = f32[64,128,128]{2,1,0:T(8,128)S(1)} copy-done((f32[64,128,128]{2,1,0:T(8,128)S(1)}, f32[64,128,128]{2,1,0:T(8,128)}, u32[]{:S(2)}) %copy-start.5) | copy-done | bytes 4194328
  76.4 14.5 %output_part.1 = (bf16[1024,1024]{1,0:T(8,128)(2,1)}, bf16[3,1024,1024]{2,1,0:T(8,128)(2,1)}) custom-call(bf16[3,1024,1024]{2,1,0:T(8,128)(2,1)} %feat_ref.3, f32[3,8,1024]{2,1,0:T(8,128)S(1)} %pad.8.halo_ref, f32[4,8,1024]{2,1,0:T(8,128)S(1)} %pad.9.next_ref, f32[3,3,1024]{2,1,0:T(4,128)S(1)} %copy-done.7, bf16[1024,1024]{1,0:T(8,128)(2,1)S(1)} %copy-done.1, ...), custom_call_target="tpu_custom_call" | custom-call | tf_op jit(solution)/shard_map/output_part/pallas_call | solution.py:421
  (52 shorter events, 5.6 us)
Async XLA Ops:
  1.5 6.8 %collective-permute-start = (bf16[3,2,1024]{2,1,0:T(2,128)(2,1)S(1)}, bf16[3,2,1024]{2,1,0:T(2,128)(2,1)S(1)}, u32[]{:S(2)}, u32[]{:S(2)}) collective-permute-start(bf16[3,2,1024]{2,1,0:T(2,128)(2,1)S(1)} %get-tuple-element.35), channel_id=1, source_target_pairs={{0,1},{1,2},{2,3},{3,0},{4,5},{5,6},{6,7},{7,4},{8,9},{9,10},{10,1... | collective-permute-start | bytes 36872 | tf_op jit(solution)/shard_map/ppermute | solution.py:301
  8.3 1.6 %copy-start = (bf16[1024,1024]{1,0:T(8,128)(2,1)S(1)}, bf16[1024,1024]{1,0:T(8,128)(2,1)}, u32[]{:S(2)}) copy-start(bf16[1024,1024]{1,0:T(8,128)(2,1)} %cot_ref.3) | copy-start | bytes 6291460
  9.9 0.8 copy-start.6
  33.3 2.0 %copy-start.2 = (f32[64,128,128]{2,1,0:T(8,128)}, f32[64,128,128]{2,1,0:T(8,128)S(1)}, u32[]{:S(2)}) copy-start(f32[64,128,128]{2,1,0:T(8,128)S(1)} %get-tuple-element.12.inner_ref) | copy-start | bytes 12582916
  35.3 2.0 %copy-start.4 = (f32[64,128,128]{2,1,0:T(8,128)}, f32[64,128,128]{2,1,0:T(8,128)S(1)}, u32[]{:S(2)}) copy-start(f32[64,128,128]{2,1,0:T(8,128)S(1)} %get-tuple-element.13.grad_ref) | copy-start | bytes 12582916
  38.1 6.3 %collective-permute-start.2 = (f32[32,1024]{1,0:T(8,128)}, f32[32,1024]{1,0:T(8,128)S(1)}, u32[]{:S(2)}, u32[]{:S(2)}) collective-permute-start(f32[32,1024]{1,0:T(8,128)} %get-tuple-element.37), channel_id=1, source_target_pairs={{0,1},{1,0},{2,3},{3,2},{4,5},{5,4},{6,7},{7,6},{8,9},{9,8},{10,11... | collective-permute-start | bytes 393224 | tf_op jit(solution)/shard_map/ppermute | solution.py:306
  38.2 12.9 %collective-permute-start.3 = (f32[32,1024]{1,0:T(8,128)}, f32[32,1024]{1,0:T(8,128)}, u32[]{:S(2)}, u32[]{:S(2)}) collective-permute-start(f32[32,1024]{1,0:T(8,128)} %get-tuple-element.39), channel_id=1, source_target_pairs={{0,2},{1,3},{2,0},{3,1},{4,6},{5,7},{6,4},{7,5},{8,10},{9,11},{10,... | collective-permute-start | bytes 393224 | tf_op jit(solution)/shard_map/ppermute | solution.py:306
  40.6 10.5 %collective-permute-start.4 = (f32[32,1024]{1,0:T(8,128)}, f32[32,1024]{1,0:T(8,128)}, u32[]{:S(2)}, u32[]{:S(2)}) collective-permute-start(f32[32,1024]{1,0:T(8,128)} %get-tuple-element.38), channel_id=1, source_target_pairs={{0,3},{1,2},{2,1},{3,0},{4,7},{5,6},{6,5},{7,4},{8,11},{9,10},{10,... | collective-permute-start | bytes 393224 | tf_op jit(solution)/shard_map/ppermute | solution.py:306
  43.1 28.9 %copy-start.1 = (bf16[1024,1024]{1,0:T(8,128)(2,1)S(1)}, bf16[1024,1024]{1,0:T(8,128)(2,1)}, u32[]{:S(2)}) copy-start(bf16[1024,1024]{1,0:T(8,128)(2,1)} %cot_ref.3) | copy-start | bytes 6291460
  43.1 28.9 %copy-start.7 = (f32[3,3,1024]{2,1,0:T(4,128)S(1)}, f32[3,3,1024]{2,1,0:T(4,128)}, u32[]{:S(2)}) copy-start(f32[3,3,1024]{2,1,0:T(4,128)} %taps_ref.3) | copy-start | bytes 110596
  54.3 7.4 %collective-permute-start.5 = (f32[2,64,16]{1,2,0:T(8,128)S(1)}, f32[2,64,16]{1,2,0:T(8,128)S(1)}, u32[]{:S(2)}, u32[]{:S(2)}) collective-permute-start(f32[2,64,16]{1,2,0:T(8,128)S(1)} %pad_maximum_fusion.2), channel_id=1, source_target_pairs={{0,1},{1,0},{2,3},{3,2},{4,5},{5,4},{6,7},{7,6},{8,9},{9,8},{10,11... | collective-permute-start | bytes 24584 | tf_op jit(solution)/shard_map/ppermute | solution.py:306
  56.3 5.5 %collective-permute-start.6 = (f32[2,64,16]{1,2,0:T(8,128)S(1)}, f32[2,64,16]{1,2,0:T(8,128)S(1)}, u32[]{:S(2)}, u32[]{:S(2)}) collective-permute-start(f32[2,64,16]{1,2,0:T(8,128)S(1)} %pad_maximum_fusion.2), channel_id=1, source_target_pairs={{0,2},{1,3},{2,0},{3,1},{4,6},{5,7},{6,4},{7,5},{8,10},{9,11},{10,... | collective-permute-start | bytes 24584 | tf_op jit(solution)/shard_map/ppermute | solution.py:306
  57.4 5.5 %collective-permute-start.7 = (f32[2,64,16]{1,2,0:T(8,128)S(1)}, f32[2,64,16]{1,2,0:T(8,128)S(1)}, u32[]{:S(2)}, u32[]{:S(2)}) collective-permute-start(f32[2,64,16]{1,2,0:T(8,128)S(1)} %pad_maximum_fusion.2), channel_id=1, source_target_pairs={{0,3},{1,2},{2,1},{3,0},{4,7},{5,6},{6,5},{7,4},{8,11},{9,10},{10,... | collective-permute-start | bytes 24584 | tf_op jit(solution)/shard_map/ppermute | solution.py:306
  58.8 5.5 %collective-permute-start.1 = (bf16[4,2,1024]{2,1,0:T(2,128)(2,1)S(1)}, bf16[4,2,1024]{2,1,0:T(2,128)(2,1)S(1)}, u32[]{:S(2)}, u32[]{:S(2)}) collective-permute-start(bf16[4,2,1024]{2,1,0:T(2,128)(2,1)S(1)} %pad_maximum_fusion.1), channel_id=1, source_target_pairs={{0,3},{1,0},{2,1},{3,2},{4,7},{5,4},{6,5},{7,6},{8,11},{9,8},{10,9... | collective-permute-start | bytes 49160 | tf_op jit(solution)/shard_map/ppermute | solution.py:301
  64.2 1.2 %collective-permute-start.8 = (f32[8,128]{1,0:T(8,128)S(1)}, f32[8,128]{1,0:T(8,128)S(1)}, u32[]{:S(2)}, u32[]{:S(2)}) collective-permute-start(f32[8,128]{1,0:T(8,128)S(1)} %broadcast_in_dim.44), channel_id=1, source_target_pairs={{0,4},{4,0},{8,12},{12,8},{16,20},{20,16},{24,28},{28,24},{1,5},{5... | collective-permute-start | bytes 12296 | tf_op jit(solution)/shard_map/ppermute | solution.py:306
  66.0 3.7 %collective-permute-start.9 = (f32[8,128]{1,0:T(8,128)S(1)}, f32[8,128]{1,0:T(8,128)S(1)}, u32[]{:S(2)}, u32[]{:S(2)}) collective-permute-start(f32[8,128]{1,0:T(8,128)S(1)} %broadcast_add_fusion), channel_id=1, source_target_pairs={{0,8},{4,12},{8,0},{12,4},{16,24},{20,28},{24,16},{28,20},{1,9},{5... | collective-permute-start | bytes 12296 | tf_op jit(solution)/shard_map/ppermute | solution.py:306
  70.4 20.5 %collective-permute-start.10 = (f32[8,128]{1,0:T(8,128)S(1)}, f32[8,128]{1,0:T(8,128)S(1)}, u32[]{:S(2)}, u32[]{:S(2)}) collective-permute-start(f32[8,128]{1,0:T(8,128)S(1)} %fusion.16), channel_id=1, source_target_pairs={{0,16},{4,20},{8,24},{12,28},{16,0},{20,4},{24,8},{28,12},{1,17},{... | collective-permute-start | bytes 12296 | tf_op jit(solution)/shard_map/ppermute | solution.py:306
  72.0 2.2 %copy-start.3 = (f32[64,128,128]{2,1,0:T(8,128)S(1)}, f32[64,128,128]{2,1,0:T(8,128)}, u32[]{:S(2)}) copy-start(f32[64,128,128]{2,1,0:T(8,128)} %copy-done.2) | copy-start | bytes 12582916
  74.2 2.2 %copy-start.5 = (f32[64,128,128]{2,1,0:T(8,128)S(1)}, f32[64,128,128]{2,1,0:T(8,128)}, u32[]{:S(2)}) copy-start(f32[64,128,128]{2,1,0:T(8,128)} %copy-done.4) | copy-start | bytes 12582916

commit v3 on v2

v3 whole, which is shorter than its diff:
```python
import functools

import jax
import jax.numpy as jnp
from jax import lax
from jax.experimental import pallas as pl
from jax.experimental.pallas import tpu as pltpu
from jax.sharding import PartitionSpec as P

LANES = 128
MODES = 16
MEMBERS = 16
TILE_GROUPS = LANES // MEMBERS
ROWS = LANES
f32 = jnp.float32
bf16 = jnp.bfloat16
VMEM_LIMIT = 58 * 2**20


def split(value):
    high = value.astype(bf16)
    return high, (value - high.astype(f32)).astype(bf16)


def dot_nt(left, right):
    return lax.dot_general(left, right, (((1,), (1,)), ((), ())), preferred_element_type=f32)


def dot_tn(left, right):
    return lax.dot_general(left, right, (((0,), (0,)), ((), ())), preferred_element_type=f32)


def dot_nn(left, right):
    return lax.dot_general(left, right, (((1,), (0,)), ((), ())), preferred_element_type=f32)


def iota(axis, shape):
    return lax.broadcasted_iota(jnp.int32, shape, axis)


def widen(feat_ref, tail_ref, me_ref, wide, tokens):
    for i in range(3):
        wide[i, 6:8, :] = jnp.where(me_ref[0] == 0, 0.0, tail_ref[i].astype(f32))
        wide[i, 8 : 8 + tokens, :] = feat_ref[i].astype(f32)


def short_block(wide, taps_ref, i, start, count):
    return (
        taps_ref[i, 0:1, :] * wide[i, start + 8 : start + 8 + count, :]
        + taps_ref[i, 1:2, :] * wide[i, start + 7 : start + 7 + count, :]
        + taps_ref[i, 2:3, :] * wide[i, start + 6 : start + 6 + count, :]
    )


def sheared(row8, period):
    which = iota(0, row8.shape) % period
    for bit in (1, 2, 4):
        row8 = jnp.where((which & bit) != 0, pltpu.roll(row8, LANES - bit, 1), row8)
    return row8


def circulant(row):
    return pltpu.roll(jnp.broadcast_to(row, (LANES, LANES)), 0, 1, stride=1, stride_axis=0)


def table_rows(source_ref, rows_ref):
    tall = jnp.concatenate([source_ref[...]] * (LANES // MODES), axis=0)
    missing = LANES - tall.shape[1]
    if missing:
        tall = jnp.concatenate([tall, jnp.zeros((LANES, missing), f32)], axis=1)
    rows_ref[...] = jnp.transpose(tall)


def parameters(rate_ref, gain_ref, rate_rows, gain_rows):
    tile = pl.program_id(0)

    @pl.when(tile == 0)
    def _():
        table_rows(rate_ref, rate_rows)
        table_rows(gain_ref, gain_rows)

    at = pl.ds(pl.multiple_of(tile * TILE_GROUPS, TILE_GROUPS), TILE_GROUPS)
    rates = rate_rows[at, :]
    return rates, gain_rows[at, :] * jnp.sqrt(2.0 * rates)


def per_mode(rows):
    own = iota(0, (TILE_GROUPS, LANES)) == iota(1, (TILE_GROUPS, LANES)) // MODES
    flat = jnp.sum(jnp.where(own, rows, 0.0), axis=0, keepdims=True)
    return jnp.transpose(jnp.broadcast_to(flat, (LANES, LANES)))


def per_member(rows):
    return jnp.concatenate(
        [jnp.broadcast_to(rows[g : g + 1], (MEMBERS, LANES)) for g in range(TILE_GROUPS)], axis=0
    )


def state_kernel(
    me_ref, feat_ref, tail_ref, taps_ref, cot_ref, rate_ref, gain_ref,
    z_ref, eh_ref, el_ref, carry_ref, state_ref, cross_ref,
    wide, own_all, table_all, rate_rows, gain_rows,
):
    tokens = feat_ref.shape[1]
    blocks = tokens // LANES
    rate_tile, _ = parameters(rate_ref, gain_ref, rate_rows, gain_rows)
    rates = per_mode(rate_tile)
    lag = iota(1, (LANES, LANES)).astype(f32)
    lane_at = iota(1, (LANES, LANES))
    lane_row = iota(1, (1, LANES))

    back = jnp.exp(-rates * (LANES - 1.0 - lag))
    after = jnp.exp(-rates * (lag + 1.0))
    s_parts = split(back)
    l_parts = split((LANES - 1.0 - lag) * back)
    m_parts = split(after)
    n_parts = split((lag + 1.0) * after)
    for g in range(TILE_GROUPS):
        of = slice(g * MODES, (g + 1) * MODES)
        for part in range(2):
            s_of, l_of = s_parts[part][of], l_parts[part][of]
            m_of, n_of = m_parts[part][of], n_parts[part][of]
            table_all[g, :, part * LANES : (part + 1) * LANES] = jnp.concatenate(
                [s_of, s_of, s_of, l_of, m_of, m_of, n_of, m_of], axis=0
            )

    widen(feat_ref, tail_ref, me_ref, wide, tokens)
    for b in range(blocks):
        query = short_block(wide, taps_ref, 0, b * LANES, LANES)
        key = short_block(wide, taps_ref, 1, b * LANES, LANES)
        value = short_block(wide, taps_ref, 2, b * LANES, LANES)
        z_t = jnp.transpose((key * value).astype(bf16))
        e_t = jnp.transpose(cot_ref[b * LANES : (b + 1) * LANES, :].astype(f32) * query)
        e_high, e_low = split(e_t)
        at = slice(b * MEMBERS, (b + 1) * MEMBERS)
        for g in range(TILE_GROUPS):
            of = slice(g * MEMBERS, (g + 1) * MEMBERS)
            z_ref[g, at, :] = z_t[of]
            eh_ref[g, at, :] = e_high[of]
            el_ref[g, at, :] = e_low[of]

    for g in range(TILE_GROUPS):
        of = slice(g * MEMBERS, (g + 1) * MEMBERS)
        z, eh, el = z_ref[g], eh_ref[g], el_ref[g]
        left = jnp.concatenate(
            [
                jnp.concatenate([z, z], axis=1),
                jnp.concatenate([eh, eh], axis=1),
                jnp.concatenate([el, jnp.zeros_like(el)], axis=1),
            ],
            axis=0,
        )
        got = dot_nt(left, table_all[g])
        rows = z.shape[0]
        own = jnp.where(
            iota(1, (rows, LANES)) < 64, got[:rows], got[rows : 2 * rows] + got[2 * rows :]
        )
        for b in range(blocks):
            own_all[b, of, :] = own[b * MEMBERS : (b + 1) * MEMBERS]

    span = per_member(jnp.exp(rate_tile * (-float(LANES))))
    in_x = jnp.where((lane_row >= 48) & (lane_row < 64), float(LANES), 0.0)
    in_y = jnp.where((lane_row >= 96) & (lane_row < 112), float(LANES), 0.0)
    x_now = jnp.zeros((LANES, LANES), f32)
    y_now = jnp.zeros((LANES, LANES), f32)
    x_lag = jnp.zeros((LANES, LANES), f32)
    y_lag = jnp.zeros((LANES, LANES), f32)
    cross = jnp.zeros((LANES, LANES), f32)
    for b in range(blocks):
        own = own_all[b]
        cross = cross + x_now * pltpu.roll(own, 4 * MODES, 1)
        carry_ref[0, b] = x_now
        x_now = span * (x_now + x_lag) + own
        x_lag = span * x_lag + in_x * pltpu.roll(own, MODES, 1)
    for b in reversed(range(blocks)):
        own = own_all[b]
        carry_ref[0, b] = jnp.where(lane_at < 64, carry_ref[0, b], y_now)
        y_now = span * (y_now + y_lag) + own
        y_lag = span * y_lag + in_y * pltpu.roll(own, MODES, 1)
    cross_ref[...] = jnp.sum(cross.reshape(TILE_GROUPS, MEMBERS, LANES), axis=1)
    turned = jnp.transpose(jnp.where(lane_at < 64, x_now, y_now))
    state_ref[0:16] = turned[0:16]
    state_ref[16:32] = turned[48:64]
    state_ref[32:48] = turned[64:80]
    state_ref[48:64] = turned[96:112]


def inside_kernel(
    z_ref, eh_ref, el_ref, rate_ref, gain_ref,
    inner_ref, grad_ref, diag_ref,
    toep_all, power_all, fold_all, rate_rows, gain_rows,
):
    rate_tile, coef_tile = parameters(rate_ref, gain_ref, rate_rows, gain_rows)
    rates, coefs = per_mode(rate_tile), per_mode(coef_tile)
    lag = iota(1, (LANES, LANES)).astype(f32)
    row_at = iota(0, (LANES, LANES))
    lane_at = iota(1, (LANES, LANES))
    power = jnp.exp(-rates * lag)
    power_all[...] = power
    taps = jnp.sum((coefs * power).reshape(TILE_GROUPS, MODES, LANES), axis=1)
    for g in range(TILE_GROUPS):
        high, low = split(jnp.where(lane_at >= row_at, circulant(taps[g : g + 1]), 0.0))
        toep_all[g, 0:LANES, :] = high
        toep_all[g, LANES:, :] = low
    for g in range(TILE_GROUPS):
        z, eh, el = z_ref[g], eh_ref[g], el_ref[g]
        high = toep_all[g, 0:LANES, :]
        inner_ref[g] = dot_nn(jnp.concatenate([z, z], axis=1), toep_all[g])
        grad_ref[g] = dot_nt(
            jnp.concatenate([eh, el, eh], axis=1),
            jnp.concatenate([high, high, toep_all[g, LANES:, :]], axis=1),
        )
        z_back = jnp.transpose(z)
        gram = dot_nn(jnp.concatenate([z_back, z_back], axis=1), jnp.concatenate([eh, el], axis=0))
        gram = jnp.where(lane_at >= row_at, gram, 0.0)
        folded = [gram[0:8]] + [
            pltpu.roll(gram[8 * r : 8 * r + 8], LANES - 8 * r, 1) for r in range(1, LANES // 8)
        ]
        while len(folded) > 1:
            folded = [folded[i] + folded[i + 1] for i in range(0, len(folded), 2)]
        fold_all[8 * g : 8 * g + 8, :] = folded[0]

    corr = jnp.sum(sheared(fold_all[...], 8).reshape(TILE_GROUPS, 8, LANES), axis=1)
    weighted = power_all[...] * per_member(corr)
    first_col = jnp.sum(weighted, axis=1, keepdims=True)
    lag_col = jnp.sum(lag * weighted, axis=1, keepdims=True)
    mode_at = row_at % MODES
    placed = jnp.where(lane_at == mode_at, first_col, 0.0) + jnp.where(
        lane_at == mode_at + 32, lag_col, 0.0
    )
    diag_ref[...] = jnp.sum(placed.reshape(TILE_GROUPS, MODES, LANES), axis=1)


def exact_dot(left, right, dims):
    return lax.dot_general(
        left, right, (dims, ((), ())), precision=lax.Precision.HIGHEST, preferred_element_type=f32
    )


def join_kernel(tokens, me_ref, state_ref, diag_ref, cross_ref, rate_ref, gain_ref, *refs):
    gots, (bound_ref, local_ref) = refs[:-2], refs[-2:]
    me = me_ref[0]
    channels = state_ref.shape[1]
    groups = rate_ref.shape[1]
    chosen = (iota(0, (groups, channels)) == iota(1, (groups, channels)) // MEMBERS).astype(f32)
    rates = rate_ref[...]
    rate_cols = exact_dot(rates, chosen, ((1,), (0,)))
    zero = jnp.zeros((MODES, channels), f32)
    s_prev, l_prev, e_next = zero, zero, zero
    ahead = jnp.zeros((8, channels), f32)
    for key, got in enumerate(gots, 1):
        other = me ^ key
        earlier = other < me
        away = ((jnp.abs(me - other) - 1) * tokens).astype(f32)
        weight = jnp.exp(-rate_cols * away)
        part = weight * got[0:16]
        s_prev = s_prev + jnp.where(earlier, part, 0.0)
        l_prev = l_prev + jnp.where(earlier, weight * got[16:32] + away * part, 0.0)
        e_next = e_next + jnp.where(earlier, 0.0, part)
        ahead = ahead + jnp.where(other == me + 1, got[32:40], 0.0)
    bound_ref[0:16] = s_prev
    bound_ref[16:32] = e_next
    bound_ref[32:48] = state_ref[0:16] + jnp.exp(-rate_cols * float(tokens)) * s_prev
    bound_ref[48:56] = ahead
    moment_0, moment_1 = state_ref[32:48], state_ref[48:64]
    terms = jnp.concatenate([moment_0 * s_prev, moment_1 * s_prev + moment_0 * l_prev], axis=0)
    sums = exact_dot(terms, chosen, ((1,), (1,)))
    own = jnp.transpose(cross_ref[...] + diag_ref[...])
    first = sums[0:16] + own[0:16]
    lagged = -(sums[16:32] + own[32:48] + own[48:64])
    root = jnp.sqrt(2.0 * rates)
    local_ref[0:16] = root * first
    local_ref[16:32] = gain_ref[...] * root * (0.5 * first + rates * lagged)


def output_kernel(
    me_ref, feat_ref, tail_ref, taps_ref, cot_ref, rate_ref, gain_ref,
    inner_ref, grad_ref, carry_ref, bound_ref,
    mixer_ref, fgrad_ref,
    wide, adj, inner_t, grad_t, left_all, rate_rows, gain_rows,
):
    tokens = feat_ref.shape[1]
    blocks = tokens // LANES
    widen(feat_ref, tail_ref, me_ref, wide, tokens)
    for i in range(3):
        wide[i, 8 + tokens : 16 + tokens, :] = jnp.zeros((8, LANES), f32)
        wide[i, 8 + tokens : 10 + tokens, :] = bound_ref[48 + 2 * i : 50 + 2 * i]
    rate_tile, coef_tile = parameters(rate_ref, gain_ref, rate_rows, gain_rows)
    rates, coefs = per_mode(rate_tile), per_mode(coef_tile)
    lag = iota(1, (LANES, LANES)).astype(f32)
    lane_row = iota(1, (1, LANES))
    lane_at = iota(1, (LANES, LANES))
    is_low = ((lane_at >= 16) & (lane_at < 32)) | ((lane_at >= 80) & (lane_at < 96))
    before = bound_ref[0:16]
    after = bound_ref[16:32]
    gap = jnp.zeros((MODES, LANES), f32)
    stacked = jnp.concatenate([before, before, before, gap, after, after, gap, after], axis=0)
    turned = jnp.transpose(stacked)
    none_16 = jnp.zeros((MODES, LANES), bf16)
    none_64 = jnp.zeros((4 * MODES, LANES), bf16)
    member_rates = per_member(rate_tile)
    for b in range(blocks):
        steps = jnp.where(lane_row < 64, float(b * LANES), float((blocks - 1 - b) * LANES))
        value = carry_ref[0, b] + turned * jnp.exp(-member_rates * steps)
        high = value.astype(bf16).astype(f32)
        mixed = jnp.where(is_low, value - high, value).astype(bf16)
        for g in range(TILE_GROUPS):
            left_all[g, b * MEMBERS : (b + 1) * MEMBERS, :] = mixed[
                g * MEMBERS : (g + 1) * MEMBERS
            ]
    cz_parts = split(coefs * jnp.exp(-rates * (lag + 1.0)))
    ce_parts = split(coefs * jnp.exp(-rates * (LANES - 1.0 - lag)))
    for g in range(TILE_GROUPS):
        of = slice(g * MODES, (g + 1) * MODES)
        cz_high, cz_low = cz_parts[0][of], cz_parts[1][of]
        ce_high, ce_low = ce_parts[0][of], ce_parts[1][of]
        right = jnp.concatenate(
            [
                jnp.concatenate([cz_high, cz_high, cz_low, none_16, none_64], axis=0),
                jnp.concatenate([none_64, ce_high, ce_high, none_16, ce_low], axis=0),
            ],
            axis=1,
        )
        carried = dot_nn(left_all[g], right)
        whole_inner = inner_ref[g] + carried[:, :LANES]
        whole_grad = grad_ref[g] + carried[:, LANES:]
        for b in range(blocks):
            at = slice(b * MEMBERS, (b + 1) * MEMBERS)
            inner_t[b, of, :] = whole_inner[at]
            grad_t[b, of, :] = whole_grad[at]
    for b in range(blocks):
        at = slice(b * LANES, (b + 1) * LANES)
        query = short_block(wide, taps_ref, 0, b * LANES, LANES)
        key = short_block(wide, taps_ref, 1, b * LANES, LANES)
        value = short_block(wide, taps_ref, 2, b * LANES, LANES)
        inner = jnp.transpose(inner_t[b])
        grad = jnp.transpose(grad_t[b])
        mixer_ref[at, :] = (query * inner).astype(bf16)
        adj[0, at, :] = cot_ref[at, :].astype(f32) * inner
        adj[1, at, :] = grad * value
        adj[2, at, :] = grad * key
    key = short_block(wide, taps_ref, 1, tokens, 8)
    value = short_block(wide, taps_ref, 2, tokens, 8)
    query = short_block(wide, taps_ref, 0, tokens, 8)
    z = (key * value).astype(bf16).astype(f32)
    upstream = jnp.concatenate([bound_ref[54:56], jnp.zeros((6, LANES), f32)], axis=0)
    e = upstream * query
    rates = jnp.transpose(member_rates)[0:MODES]
    coefs = jnp.transpose(per_member(coef_tile))[0:MODES]
    decay = jnp.exp(-rates)
    grow = jnp.exp(rates)
    state = bound_ref[32:48]
    sum_0 = jnp.sum(coefs, axis=0, keepdims=True)
    sum_1 = jnp.sum(coefs * decay, axis=0, keepdims=True)
    inner_0 = jnp.sum(coefs * decay * state, axis=0, keepdims=True) + sum_0 * z[0:1]
    inner_1 = (
        jnp.sum(coefs * decay * decay * state, axis=0, keepdims=True)
        + sum_1 * z[0:1]
        + sum_0 * z[1:2]
    )
    grad_0 = jnp.sum(coefs * grow * after, axis=0, keepdims=True)
    grad_1 = jnp.sum(coefs * grow * (grow * after - e[0:1]), axis=0, keepdims=True)
    which = iota(0, (8, LANES))
    inner_8 = jnp.where(which == 0, inner_0, jnp.where(which == 1, inner_1, 0.0))
    grad_8 = jnp.where(which == 0, grad_0, jnp.where(which == 1, grad_1, 0.0))
    adj[0, tokens : tokens + 8, :] = upstream * inner_8
    adj[1, tokens : tokens + 8, :] = grad_8 * value
    adj[2, tokens : tokens + 8, :] = grad_8 * key
    for b in range(blocks):
        start = b * LANES
        for i in range(3):
            fgrad_ref[i, start : start + LANES, :] = (
                taps_ref[i, 0:1, :] * adj[i, start : start + LANES, :]
                + taps_ref[i, 1:2, :] * adj[i, start + 1 : start + 1 + LANES, :]
                + taps_ref[i, 2:3, :] * adj[i, start + 2 : start + 2 + LANES, :]
            ).astype(bf16)


def shifted(value, axis, steps):
    count = lax.axis_size(axis)
    return lax.ppermute(value, axis, [(i, (i + steps) % count) for i in range(count)])


def swapped(value, axis, key):
    count = lax.axis_size(axis)
    return lax.ppermute(value, axis, [(i, i ^ key) for i in range(count)])


def per_device(features, short_taps, decay_rates, mode_gains, cotangent):
    tokens = features.shape[1]
    channels = features.shape[2]
    groups = decay_rates.shape[0]
    tiles = channels // LANES
    blocks = tokens // LANES
    ctx_count = lax.axis_size("ctx")
    ctx_index = lax.axis_index("ctx")

    tail = shifted(features[:, tokens - 2 :, :], "ctx", 1)
    head = jnp.concatenate([features[:, :2, :], cotangent[None, :2, :]], axis=0)
    head = head.astype(f32).reshape(8, channels)
    me = ctx_index.astype(jnp.int32).reshape(1)
    rates, gains = decay_rates.T, mode_gains.T

    per_group = pl.BlockSpec((TILE_GROUPS, ROWS, LANES), lambda j: (j, 0, 0))
    feat_spec = pl.BlockSpec((3, tokens, LANES), lambda j: (0, 0, j))
    tail_spec = pl.BlockSpec((3, 2, LANES), lambda j: (0, 0, j))
    taps_spec = pl.BlockSpec((3, 3, LANES), lambda j: (0, 0, j))
    cot_spec = pl.BlockSpec((tokens, LANES), lambda j: (0, j))
    table_spec = pl.BlockSpec((MODES, groups), lambda j: (0, 0))
    carry_spec = pl.BlockSpec((1, blocks, LANES, LANES), lambda j: (j, 0, 0, 0))
    slot_spec = pl.BlockSpec((TILE_GROUPS, LANES), lambda j: (j, 0))
    me_spec = pl.BlockSpec(memory_space=pltpu.SMEM)
    rows = blocks * MEMBERS
    turned = jax.ShapeDtypeStruct((groups, rows, LANES), bf16)
    wide_turned = jax.ShapeDtypeStruct((groups, rows, LANES), f32)
    slots = jax.ShapeDtypeStruct((groups, LANES), f32)
    table_scratch = [pltpu.VMEM((LANES, LANES), f32), pltpu.VMEM((LANES, LANES), f32)]
    compiler_params = pltpu.CompilerParams(vmem_limit_bytes=VMEM_LIMIT)
    z, eh, el, carry, states, cross = pl.pallas_call(
        state_kernel,
        grid=(tiles,),
        in_specs=[me_spec, feat_spec, tail_spec, taps_spec, cot_spec, table_spec, table_spec],
        out_specs=[
            per_group,
            per_group,
            per_group,
            carry_spec,
            pl.BlockSpec((4 * MODES, LANES), lambda j: (0, j)),
            slot_spec,
        ],
        out_shape=[
            turned,
            turned,
            turned,
            jax.ShapeDtypeStruct((tiles, blocks, LANES, LANES), f32),
            jax.ShapeDtypeStruct((4 * MODES, channels), f32),
            slots,
        ],
        scratch_shapes=[
            pltpu.VMEM((3, tokens + 8, LANES), f32),
            pltpu.VMEM((blocks, LANES, LANES), f32),
            pltpu.VMEM((TILE_GROUPS, LANES, 2 * LANES), bf16),
        ]
        + table_scratch,
        compiler_params=compiler_params,
        name="state_part",
    )(me, features, tail, short_taps, cotangent, rates, gains)

    gots = []
    for key in range(1, ctx_count):
        earlier = (ctx_index ^ key) < ctx_index
        sent = jnp.where(earlier, states[32:64], states[0:32])
        gots.append(swapped(jnp.concatenate([sent, head], axis=0), "ctx", key))

    inner, grad, diag = pl.pallas_call(
        inside_kernel,
        grid=(tiles,),
        in_specs=[per_group, per_group, per_group, table_spec, table_spec],
        out_specs=[per_group, per_group, slot_spec],
        out_shape=[wide_turned, wide_turned, slots],
        scratch_shapes=[
            pltpu.VMEM((TILE_GROUPS, 2 * LANES, LANES), bf16),
            pltpu.VMEM((LANES, LANES), f32),
            pltpu.VMEM((8 * TILE_GROUPS, LANES), f32),
        ]
        + table_scratch,
        compiler_params=compiler_params,
        cost_estimate=pl.CostEstimate(
            flops=2 * groups * rows * LANES * LANES * 7, bytes_accessed=14 * 2**20, transcendentals=0
        ),
        name="inside_part",
    )(z, eh, el, rates, gains)

    whole = pl.BlockSpec(memory_space=pltpu.VMEM)
    bound, local = pl.pallas_call(
        functools.partial(join_kernel, tokens),
        in_specs=[me_spec] + [whole] * (5 + len(gots)),
        out_specs=[whole, whole],
        out_shape=[
            jax.ShapeDtypeStruct((56, channels), f32),
            jax.ShapeDtypeStruct((2 * MODES, groups), f32),
        ],
        compiler_params=compiler_params,
        name="join_part",
    )(me, states, diag, cross, rates, gains, *gots)

    terms = [local] + [swapped(local, "ctx", key) for key in range(1, ctx_count)]
    while len(terms) > 1:
        terms = [terms[i] + terms[i + 1] for i in range(0, len(terms), 2)]
    summed = terms[0]
    squares = jnp.broadcast_to(jnp.sum(summed * summed), (8, LANES))
    fsdp_count = lax.axis_size("fsdp")
    step = 1
    while step < fsdp_count:
        squares = squares + swapped(squares, "fsdp", step)
        step *= 2
    entry_count = 2 * groups * MODES * fsdp_count
    factor = jnp.minimum(1.0, lax.rsqrt(squares[0, 0] / entry_count + 1e-06))
    clipped = summed * factor

    mixer, feature_grads = pl.pallas_call(
        output_kernel,
        grid=(tiles,),
        in_specs=[
            me_spec,
            feat_spec,
            tail_spec,
            taps_spec,
            cot_spec,
            table_spec,
            table_spec,
            per_group,
            per_group,
            carry_spec,
            pl.BlockSpec((56, LANES), lambda j: (0, j)),
        ],
        out_specs=[cot_spec, feat_spec],
        out_shape=[
            jax.ShapeDtypeStruct((tokens, channels), bf16),
            jax.ShapeDtypeStruct((3, tokens, channels), bf16),
        ],
        scratch_shapes=[
            pltpu.VMEM((3, tokens + 16, LANES), f32),
            pltpu.VMEM((3, tokens + 8, LANES), f32),
            pltpu.VMEM((blocks, LANES, LANES), f32),
            pltpu.VMEM((blocks, LANES, LANES), f32),
            pltpu.VMEM((TILE_GROUPS, rows, LANES), bf16),
        ]
        + table_scratch,
        compiler_params=compiler_params,
        cost_estimate=pl.CostEstimate(
            flops=2 * groups * rows * LANES * LANES * 4, bytes_accessed=28 * 2**20, transcendentals=0
        ),
        name="output_part",
    )(me, features, tail, short_taps, cotangent, rates, gains, inner, grad, carry, bound)
    return (mixer, feature_grads, clipped[:MODES].T, clipped[MODES:].T)


def solution(mesh):
    return jax.shard_map(
        per_device,
        mesh=mesh,
        in_specs=(
            P(None, "ctx", "fsdp"),
            P(None, None, "fsdp"),
            P("fsdp", None),
            P("fsdp", None),
            P("ctx", "fsdp"),
        ),
        out_specs=(P("ctx", "fsdp"), P(None, "ctx", "fsdp"), P("fsdp", None), P("fsdp", None)),
        check_vma=False,
    )
```

time: 93.5 us -> 78.2 us (0.84)
  local copies, waits for them, and re-layouts: 17.7 us -> 4.68 us
  Pallas kernels: 37.1 us -> 43.7 us
  waiting for transfers between devices: 12.8 us -> 8.66 us
  starting transfers between devices: 17.7 us -> 15.1 us
  other arithmetic: 5.89 us -> 3.7 us
    unnamed x18 -> x8, local copies, waits for them, and re-layouts: 12.3 us -> 1.32 us
    pallas_call x2 -> x4, Pallas kernels: 37.1 us -> 43.7 us  [the longest x1 16.3 us: per_device(): pl.pallas_call(output_kernel, grid=(tiles,), in_specs=[me_spec, feat_spec...]
    ppermute x9, waiting for transfers between devices: 11.4 us -> 5.75 us  [swapped(): return lax.ppermute(value, axis, [(i, i ^ key) for i in range(count)])]
    ppermute x2 -> x1, starting transfers between devices: 5.57 us -> 3.08 us  [shifted(): lax.ppermute(value, axis, [(i, (i + steps) % count) for i in range(count)])]
    ppermute x2 -> x1, waiting for transfers between devices: 1.43 us -> 2.91 us  [shifted(): lax.ppermute(value, axis, [(i, (i + steps) % count) for i in range(count)])]
    exp x4 -> x0, local copies, waits for them, and re-layouts: 1.08 us -> none  [the longest x3 0.81 us: per_device(): weight = jnp.exp(-rate_cols * away)]
    add x2 -> x0, other arithmetic: 1.01 us -> none  [the longest x1 1 us: per_device(): moment_1 * s_prev + moment_0 * l_prev]
  transfers between devices with their start and end apart: 11 -> 10, of which waited for: 6 -> 5; matrix products, arithmetic and copies ran while one was open for 6% -> 1% of each run, Pallas kernels for 16% -> 36%
where the time goes in v3:
time: 78.2 us; the launch traced here: 77.3 us
  Pallas kernels  43.7 us (56%)
  starting transfers between devices  15.1 us (19%)
  waiting for transfers between devices  8.66 us (11%)
  local copies, waits for them, and re-layouts  4.68 us (6%)
  other arithmetic  3.7 us (5%)
  between operations  1.47 us (2%)
    pallas_call x1, Pallas kernels, per_device(): pl.pallas_call(output_kernel, grid=(tiles,), in_specs=[me_spec, feat_spec...  16.3 us
    pallas_call x1, Pallas kernels, per_device(): pl.pallas_call(state_kernel, grid=(tiles,), in_specs=[me_spec, feat_spec,...  13.4 us
    ppermute x9, starting transfers between devices, swapped(): return lax.ppermute(value, axis, [(i, i ^ key) for i in range(count)])  12.1 us
    pallas_call x1, Pallas kernels, per_device(): pl.pallas_call(inside_kernel, grid=(tiles,), in_specs=[per_group, per_gro...  11.6 us
    ppermute x9, waiting for transfers between devices, swapped(): return lax.ppermute(value, axis, [(i, i ^ key) for i in range(count)])  5.75 us
    ppermute x1, starting transfers between devices, shifted(): lax.ppermute(value, axis, [(i, (i + steps) % count) for i in range(count)])  3.08 us
    ppermute x1, waiting for transfers between devices, shifted(): lax.ppermute(value, axis, [(i, (i + steps) % count) for i in range(count)])  2.91 us
    pallas_call x1, Pallas kernels, per_device(): pl.pallas_call(functools.partial(join_kernel, tokens), in_specs=[me_spec]...  2.32 us
  transfers between devices with their start and end apart: 10, of which 5 were waited for; matrix products, arithmetic and copies ran while one was open for 1% of the time, Pallas kernels for 36%

profile of v3, /device:TPU:0, one launch (start us, length us, event | category | flops | bytes accessed | tf_op | source)
XLA Modules:
  0.0 77.3 jit_solution(17215690515052098951)
XLA Ops:
  0.6 0.8 %fusion = (bf16[3,2,1024]{2,1,0:T(2,128)(2,1)S(1)}, bf16[3,2,1024]{2,1,0:T(2,128)(2,1)S(1)}) fusion(bf16[3,1024,1024]{2,1,0:T(8,128)(2,1)} %feat_ref.3), kind=kLoop, calls=%fused_computation.14 | loop fusion | bytes 49152 | tf_op jit(solution)/shard_map/slice | solution.py:399
  1.5 3.1 %collective-permute-start = (bf16[3,2,1024]{2,1,0:T(2,128)(2,1)S(1)}, bf16[3,2,1024]{2,1,0:T(2,128)(2,1)S(1)}, u32[]{:S(2)}, u32[]{:S(2)}) collective-permute-start(bf16[3,2,1024]{2,1,0:T(2,128)(2,1)S(1)} %get-tuple-element.33), channel_id=1, source_target_pairs={{0,1},{1,2},{2,3},{3,0},{4,5},{5,6},{6,7},{7,4},{8,9},{9,10},{10,1... | collective-permute-start | bytes 36872 | tf_op jit(solution)/shard_map/ppermute | solution.py:381
  4.6 0.7 slice_bitcast_fusion.2
  5.3 2.9 %collective-permute-done.tail_ref = bf16[3,2,1024]{2,1,0:T(2,128)(2,1)S(1)} collective-permute-done((bf16[3,2,1024]{2,1,0:T(2,128)(2,1)S(1)}, bf16[3,2,1024]{2,1,0:T(2,128)(2,1)S(1)}, u32[]{:S(2)}, u32[]{:S(2)}) %collective-permute-start) | collective-permute-done | bytes 12320 | tf_op jit(solution)/shard_map/ppermute | solution.py:381
  8.3 0.6 copy-done.3
  8.9 13.4 %state_part.1 = (bf16[64,128,128]{2,1,0:T(8,128)(2,1)}, bf16[64,128,128]{2,1,0:T(8,128)(2,1)}, bf16[64,128,128]{2,1,0:T(8,128)(2,1)}, f32[8,8,128,128]{3,2,1,0:T...) custom-call(s32[1]{0:T(128)} %bitcast.me_ref, bf16[3,1024,1024]{2,1,0:T(8,128)(2,1)} %feat_ref.3, ...), custom_call_target="tpu_custom_call" | custom-call | tf_op jit(solution)/shard_map/state_part/pallas_call | solution.py:419
  22.3 1.0 %slice_select_fusion = (f32[32,1024]{1,0:T(8,128)S(1)}, f32[32,1024]{1,0:T(8,128)S(1)}, f32[32,1024]{1,0:T(8,128)S(1)}) fusion(f32[64,1024]{1,0:T(8,128)} %get-tuple-element.23.state_ref, pred[]{:T(512)S(6)} %lt.11, pred[]{:T(512)S(6)} %lt.9, pred[]{:T(512)S(6)} %lt.10), kind=kLoop, calls=%fused_computation.3 | loop fusion | flops 98304 | bytes 655363 | tf_op jit(solution)/shard_map/jit(_where)/select_n | solution.py:452
  23.3 2.1 %collective-permute-start.3 = (f32[40,1024]{1,0:T(8,128)S(1)}, f32[40,1024]{1,0:T(8,128)S(1)}, u32[]{:S(2)}, u32[]{:S(2)}) collective-permute-start(f32[40,1024]{1,0:T(8,128)S(1)} %get-tuple-element.37), channel_id=1, source_target_pairs={{0,3},{1,2},{2,1},{3,0},{4,7},{5,6},{6,5},{7,4},{8,11},{9,10},{10,... | collective-permute-start | bytes 491528 | tf_op jit(solution)/shard_map/ppermute | solution.py:386
  25.4 2.4 %collective-permute-start.1 = (f32[40,1024]{1,0:T(8,128)S(1)}, f32[40,1024]{1,0:T(8,128)S(1)}, u32[]{:S(2)}, u32[]{:S(2)}) collective-permute-start(f32[40,1024]{1,0:T(8,128)S(1)} %get-tuple-element.39), channel_id=1, source_target_pairs={{0,1},{1,0},{2,3},{3,2},{4,5},{5,4},{6,7},{7,6},{8,9},{9,8},{10,11... | collective-permute-start | bytes 491528 | tf_op jit(solution)/shard_map/ppermute | solution.py:386
  27.8 11.6 %inside_part.1 = (f32[64,128,128]{2,1,0:T(8,128)}, f32[64,128,128]{2,1,0:T(8,128)}, f32[64,128]{1,0:T(8,128)}) custom-call(bf16[64,128,128]{2,1,0:T(8,128)(2,1)} %get-tuple-element.17.z_ref, bf16[64,128,128]{2,1,0:T(8,128)(2,1)} %get-tuple-element.18.eh_ref, bf16[64,128,128]{2,1,0:T(8,128)(2,1)} %get-tuple-element.19.el_ref, f32[16,64]{1,0:T(8,128)} %bitcast.11, ...), custom_call_target="tpu_custom_call" | custom-call | flops 1879048192 | bytes 14680064 | tf_op jit(solution)/shard_map/inside_part/pallas_call | solution.py:455
  39.4 0.0 copy-start.1
  39.4 0.0 copy-start.2
  39.5 0.6 copy-done
  40.1 0.1 copy-done.1
  40.1 0.1 copy-done.2
  40.2 2.3 %join_part.1 = (f32[56,1024]{1,0:T(8,128)}, f32[32,64]{1,0:T(8,128)}) custom-call(s32[1]{0:T(128)} %bitcast.me_ref, f32[64,1024]{1,0:T(8,128)} %get-tuple-element.23.state_ref, f32[64,128]{1,0:T(8,128)} %get-tuple-element.24.diag_ref, f32[64,128]{1,0:T(8,128)} %get-tuple-element.25.cross_ref, f32[16,64]{1,0:T(8,128)} %bitcast.12, f32[16,64]{1,0:T(8,128)} %bitcast.16, ...), custom_call_target="tpu_custom_call" | custom-call | tf_op jit(solution)/shard_map/join_part/pallas_call | solution.py:475
  42.5 2.0 %collective-permute-start.6 = (f32[32,64]{1,0:T(8,128)}, f32[32,64]{1,0:T(8,128)S(1)}, u32[]{:S(2)}, u32[]{:S(2)}) collective-permute-start(f32[32,64]{1,0:T(8,128)} %get-tuple-element.29), channel_id=1, source_target_pairs={{0,3},{1,2},{2,1},{3,0},{4,7},{5,6},{6,5},{7,4},{8,11},{9,10},{10,... | collective-permute-start | bytes 24584 | tf_op jit(solution)/shard_map/ppermute | solution.py:386
  44.5 2.4 %collective-permute-start.4 = (f32[32,64]{1,0:T(8,128)}, f32[32,64]{1,0:T(8,128)S(1)}, u32[]{:S(2)}, u32[]{:S(2)}) collective-permute-start(f32[32,64]{1,0:T(8,128)} %get-tuple-element.29), channel_id=1, source_target_pairs={{0,1},{1,0},{2,3},{3,2},{4,5},{5,4},{6,7},{7,6},{8,9},{9,8},{10,11... | collective-permute-start | bytes 24584 | tf_op jit(solution)/shard_map/ppermute | solution.py:386
  46.9 1.4 %collective-permute-done.6 = f32[32,64]{1,0:T(8,128)S(1)} collective-permute-done((f32[32,64]{1,0:T(8,128)}, f32[32,64]{1,0:T(8,128)S(1)}, u32[]{:S(2)}, u32[]{:S(2)}) %collective-permute-start.6) | collective-permute-done | bytes 8224 | tf_op jit(solution)/shard_map/ppermute | solution.py:386
  48.2 1.1 %collective-permute-done.5 = f32[32,64]{1,0:T(8,128)S(1)} collective-permute-done((f32[32,64]{1,0:T(8,128)}, f32[32,64]{1,0:T(8,128)S(1)}, u32[]{:S(2)}, u32[]{:S(2)}) %collective-permute-start.5) | collective-permute-done | bytes 8224 | tf_op jit(solution)/shard_map/ppermute | solution.py:386
  49.4 1.3 %multiply_reduce_fusion = (f32[]{:T(128)}, f32[32,64]{1,0:T(8,128)S(1)}) fusion(f32[32,64]{1,0:T(8,128)S(1)} %collective-permute-done.5, f32[32,64]{1,0:T(8,128)S(1)} %collective-permute-done.6, f32[32,64]{1,0:T(8,128)} %get-tuple-element.29, f32[32,64]{1,0:T(8,128)S(1)} %collective-permute-done.4), kind=kLoop, calls=%fused_computation.7 | loop fusion | flops 10239 | bytes 40964 | tf_op jit(solution)/shard_map/reduce_sum | solution.py:491
  50.7 0.6 broadcast_in_dim.7
  51.4 0.1 collective-permute-start.7
  51.4 1.2 %collective-permute-done.7 = f32[8,128]{1,0:T(8,128)S(1)} collective-permute-done((f32[8,128]{1,0:T(8,128)S(1)}, f32[8,128]{1,0:T(8,128)S(1)}, u32[]{:S(2)}, u32[]{:S(2)}) %collective-permute-start.7) | collective-permute-done | bytes 4128 | tf_op jit(solution)/shard_map/ppermute | solution.py:386
  52.6 0.6 broadcast_add_fusion
  53.2 1.6 %collective-permute-start.8 = (f32[8,128]{1,0:T(8,128)S(1)}, f32[8,128]{1,0:T(8,128)S(1)}, u32[]{:S(2)}, u32[]{:S(2)}) collective-permute-start(f32[8,128]{1,0:T(8,128)S(1)} %broadcast_add_fusion), channel_id=1, source_target_pairs={{0,8},{4,12},{8,0},{12,4},{16,24},{20,28},{24,16},{28,20},{1,9},{5... | collective-permute-start | bytes 12296 | tf_op jit(solution)/shard_map/ppermute | solution.py:386
  54.8 2.1 %collective-permute-done.8 = f32[8,128]{1,0:T(8,128)S(1)} collective-permute-done((f32[8,128]{1,0:T(8,128)S(1)}, f32[8,128]{1,0:T(8,128)S(1)}, u32[]{:S(2)}, u32[]{:S(2)}) %collective-permute-start.8) | collective-permute-done | bytes 4128 | tf_op jit(solution)/shard_map/ppermute | solution.py:386
  56.9 0.6 fusion.1
  57.6 1.6 %collective-permute-start.9 = (f32[8,128]{1,0:T(8,128)S(1)}, f32[8,128]{1,0:T(8,128)S(1)}, u32[]{:S(2)}, u32[]{:S(2)}) collective-permute-start(f32[8,128]{1,0:T(8,128)S(1)} %fusion.1), channel_id=1, source_target_pairs={{0,16},{4,20},{8,24},{12,28},{16,0},{20,4},{24,8},{28,12},{1,17},{... | collective-permute-start | bytes 12296 | tf_op jit(solution)/shard_map/ppermute | solution.py:386
  59.2 16.3 %output_part.1 = (bf16[1024,1024]{1,0:T(8,128)(2,1)}, bf16[3,1024,1024]{2,1,0:T(8,128)(2,1)}) custom-call(s32[1]{0:T(128)} %bitcast.me_ref, bf16[3,1024,1024]{2,1,0:T(8,128)(2,1)} %feat_ref.3, bf16[3,2,1024]{2,1,0:T(2,128)(2,1)} %copy-done.3, f32[3,3,1024]{2,1,0:T(4,128)} %taps_ref.3, bf16[1024,1024]{1,0:T(8,128)(2,1)} %cot_ref.3, f32[16,64]{1,0:T(8,128)} %bitcast.13, ...), custom_call_target="tpu_custom_call" | custom-call | flops 1073741824 | bytes 29360128 | tf_op jit(solution)/shard_map/output_part/pallas_call | solution.py:501
  75.5 0.5 slice.33
  76.7 0.6 slice_bitcast_fusion
  (14 shorter events, 0.1 us)
Async XLA Ops:
  1.5 6.8 %collective-permute-start = (bf16[3,2,1024]{2,1,0:T(2,128)(2,1)S(1)}, bf16[3,2,1024]{2,1,0:T(2,128)(2,1)S(1)}, u32[]{:S(2)}, u32[]{:S(2)}) collective-permute-start(bf16[3,2,1024]{2,1,0:T(2,128)(2,1)S(1)} %get-tuple-element.33), channel_id=1, source_target_pairs={{0,1},{1,2},{2,3},{3,0},{4,5},{5,6},{6,7},{7,4},{8,9},{9,10},{10,1... | collective-permute-start | bytes 36872 | tf_op jit(solution)/shard_map/ppermute | solution.py:381
  8.3 0.6 copy-start.3
  23.3 16.1 %collective-permute-start.3 = (f32[40,1024]{1,0:T(8,128)S(1)}, f32[40,1024]{1,0:T(8,128)S(1)}, u32[]{:S(2)}, u32[]{:S(2)}) collective-permute-start(f32[40,1024]{1,0:T(8,128)S(1)} %get-tuple-element.37), channel_id=1, source_target_pairs={{0,3},{1,2},{2,1},{3,0},{4,7},{5,6},{6,5},{7,4},{8,11},{9,10},{10,... | collective-permute-start | bytes 491528 | tf_op jit(solution)/shard_map/ppermute | solution.py:386
  25.4 14.0 %collective-permute-start.2 = (f32[40,1024]{1,0:T(8,128)S(1)}, f32[40,1024]{1,0:T(8,128)S(1)}, u32[]{:S(2)}, u32[]{:S(2)}) collective-permute-start(f32[40,1024]{1,0:T(8,128)S(1)} %get-tuple-element.38), channel_id=1, source_target_pairs={{0,2},{1,3},{2,0},{3,1},{4,6},{5,7},{6,4},{7,5},{8,10},{9,11},{10,... | collective-permute-start | bytes 491528 | tf_op jit(solution)/shard_map/ppermute | solution.py:386
  25.4 14.0 %collective-permute-start.1 = (f32[40,1024]{1,0:T(8,128)S(1)}, f32[40,1024]{1,0:T(8,128)S(1)}, u32[]{:S(2)}, u32[]{:S(2)}) collective-permute-start(f32[40,1024]{1,0:T(8,128)S(1)} %get-tuple-element.39), channel_id=1, source_target_pairs={{0,1},{1,0},{2,3},{3,2},{4,5},{5,4},{6,7},{7,6},{8,9},{9,8},{10,11... | collective-permute-start | bytes 491528 | tf_op jit(solution)/shard_map/ppermute | solution.py:386
  39.4 0.7 copy-start
  39.4 0.7 copy-start.1
  39.4 0.7 copy-start.2
  42.5 5.7 %collective-permute-start.6 = (f32[32,64]{1,0:T(8,128)}, f32[32,64]{1,0:T(8,128)S(1)}, u32[]{:S(2)}, u32[]{:S(2)}) collective-permute-start(f32[32,64]{1,0:T(8,128)} %get-tuple-element.29), channel_id=1, source_target_pairs={{0,3},{1,2},{2,1},{3,0},{4,7},{5,6},{6,5},{7,4},{8,11},{9,10},{10,... | collective-permute-start | bytes 24584 | tf_op jit(solution)/shard_map/ppermute | solution.py:386
  44.5 4.8 %collective-permute-start.5 = (f32[32,64]{1,0:T(8,128)}, f32[32,64]{1,0:T(8,128)S(1)}, u32[]{:S(2)}, u32[]{:S(2)}) collective-permute-start(f32[32,64]{1,0:T(8,128)} %get-tuple-element.29), channel_id=1, source_target_pairs={{0,2},{1,3},{2,0},{3,1},{4,6},{5,7},{6,4},{7,5},{8,10},{9,11},{10,... | collective-permute-start | bytes 24584 | tf_op jit(solution)/shard_map/ppermute | solution.py:386
  44.5 4.8 %collective-permute-start.4 = (f32[32,64]{1,0:T(8,128)}, f32[32,64]{1,0:T(8,128)S(1)}, u32[]{:S(2)}, u32[]{:S(2)}) collective-permute-start(f32[32,64]{1,0:T(8,128)} %get-tuple-element.29), channel_id=1, source_target_pairs={{0,1},{1,0},{2,3},{3,2},{4,5},{5,4},{6,7},{7,6},{8,9},{9,8},{10,11... | collective-permute-start | bytes 24584 | tf_op jit(solution)/shard_map/ppermute | solution.py:386
  51.4 1.2 %collective-permute-start.7 = (f32[8,128]{1,0:T(8,128)S(1)}, f32[8,128]{1,0:T(8,128)S(1)}, u32[]{:S(2)}, u32[]{:S(2)}) collective-permute-start(f32[8,128]{1,0:T(8,128)S(1)} %broadcast_in_dim.7), channel_id=1, source_target_pairs={{0,4},{4,0},{8,12},{12,8},{16,20},{20,16},{24,28},{28,24},{1,5},{5... | collective-permute-start | bytes 12296 | tf_op jit(solution)/shard_map/ppermute | solution.py:386
  53.2 3.7 %collective-permute-start.8 = (f32[8,128]{1,0:T(8,128)S(1)}, f32[8,128]{1,0:T(8,128)S(1)}, u32[]{:S(2)}, u32[]{:S(2)}) collective-permute-start(f32[8,128]{1,0:T(8,128)S(1)} %broadcast_add_fusion), channel_id=1, source_target_pairs={{0,8},{4,12},{8,0},{12,4},{16,24},{20,28},{24,16},{28,20},{1,9},{5... | collective-permute-start | bytes 12296 | tf_op jit(solution)/shard_map/ppermute | solution.py:386
  57.6 17.9 %collective-permute-start.9 = (f32[8,128]{1,0:T(8,128)S(1)}, f32[8,128]{1,0:T(8,128)S(1)}, u32[]{:S(2)}, u32[]{:S(2)}) collective-permute-start(f32[8,128]{1,0:T(8,128)S(1)} %fusion.1), channel_id=1, source_target_pairs={{0,16},{4,20},{8,24},{12,28},{16,0},{20,4},{24,8},{28,12},{1,17},{... | collective-permute-start | bytes 12296 | tf_op jit(solution)/shard_map/ppermute | solution.py:386

commit v4 on v3

--- a/solution.py
+++ b/solution.py
@@ -14,7 +14,6 @@
 ROWS = LANES
 f32 = jnp.float32
 bf16 = jnp.bfloat16
-VMEM_LIMIT = 58 * 2**20
 
 
 def split(value):
@@ -376,6 +375,14 @@
             ).astype(bf16)
 
 
+def far(*arrays):
+    return [pltpu.with_memory_space_constraint(array, pltpu.HBM) for array in arrays]
+
+
+def near(*arrays):
+    return [pltpu.with_memory_space_constraint(array, pltpu.VMEM) for array in arrays]
+
+
 def shifted(value, axis, steps):
     count = lax.axis_size(axis)
     return lax.ppermute(value, axis, [(i, (i + steps) % count) for i in range(count)])
@@ -411,11 +418,14 @@
     slot_spec = pl.BlockSpec((TILE_GROUPS, LANES), lambda j: (j, 0))
     me_spec = pl.BlockSpec(memory_space=pltpu.SMEM)
     rows = blocks * MEMBERS
-    turned = jax.ShapeDtypeStruct((groups, rows, LANES), bf16)
-    wide_turned = jax.ShapeDtypeStruct((groups, rows, LANES), f32)
+    turned = pltpu.VMEM((groups, rows, LANES), bf16)
+    wide_turned = pltpu.VMEM((groups, rows, LANES), f32)
     slots = jax.ShapeDtypeStruct((groups, LANES), f32)
     table_scratch = [pltpu.VMEM((LANES, LANES), f32), pltpu.VMEM((LANES, LANES), f32)]
-    compiler_params = pltpu.CompilerParams(vmem_limit_bytes=VMEM_LIMIT)
+
+    def room(mebibytes):
+        return pltpu.CompilerParams(vmem_limit_bytes=mebibytes * 2**20)
+
     z, eh, el, carry, states, cross = pl.pallas_call(
         state_kernel,
         grid=(tiles,),
@@ -432,7 +442,7 @@
             turned,
             turned,
             turned,
-            jax.ShapeDtypeStruct((tiles, blocks, LANES, LANES), f32),
+            pltpu.VMEM((tiles, blocks, LANES, LANES), f32),
             jax.ShapeDtypeStruct((4 * MODES, channels), f32),
             slots,
         ],
@@ -442,9 +452,9 @@
             pltpu.VMEM((TILE_GROUPS, LANES, 2 * LANES), bf16),
         ]
         + table_scratch,
-        compiler_params=compiler_params,
+        compiler_params=room(24),
         name="state_part",
-    )(me, features, tail, short_taps, cotangent, rates, gains)
+    )(me, *far(features, tail, short_taps, cotangent, rates, gains))
 
     gots = []
     for key in range(1, ctx_count):
@@ -464,12 +474,12 @@
             pltpu.VMEM((8 * TILE_GROUPS, LANES), f32),
         ]
         + table_scratch,
-        compiler_params=compiler_params,
+        compiler_params=room(24),
         cost_estimate=pl.CostEstimate(
             flops=2 * groups * rows * LANES * LANES * 7, bytes_accessed=14 * 2**20, transcendentals=0
         ),
         name="inside_part",
-    )(z, eh, el, rates, gains)
+    )(*near(z, eh, el), *far(rates, gains))
 
     whole = pl.BlockSpec(memory_space=pltpu.VMEM)
     bound, local = pl.pallas_call(
@@ -480,7 +490,7 @@
             jax.ShapeDtypeStruct((56, channels), f32),
             jax.ShapeDtypeStruct((2 * MODES, groups), f32),
         ],
-        compiler_params=compiler_params,
+        compiler_params=room(24),
         name="join_part",
     )(me, states, diag, cross, rates, gains, *gots)
 
@@ -527,12 +537,12 @@
             pltpu.VMEM((TILE_GROUPS, rows, LANES), bf16),
         ]
         + table_scratch,
-        compiler_params=compiler_params,
+        compiler_params=room(24),
         cost_estimate=pl.CostEstimate(
             flops=2 * groups * rows * LANES * LANES * 4, bytes_accessed=28 * 2**20, transcendentals=0
         ),
         name="output_part",
-    )(me, features, tail, short_taps, cotangent, rates, gains, inner, grad, carry, bound)
+    )(me, *far(features, tail, short_taps, cotangent, rates, gains), *near(inner, grad, carry), bound)
     return (mixer, feature_grads, clipped[:MODES].T, clipped[MODES:].T)
 
 

time: 78.2 us -> 69.6 us (0.89)
  Pallas kernels: 43.7 us -> 37.4 us
  other arithmetic: 3.7 us -> 2.01 us
    pallas_call x1, Pallas kernels: 16.3 us -> 13.9 us  [per_device(): pl.pallas_call(output_kernel, grid=(tiles,), in_specs=[me_spec, feat_spec...]
    pallas_call x1, Pallas kernels: 2.32 us -> 0.5 us  [per_device(): pl.pallas_call(functools.partial(join_kernel, tokens), in_specs=[me_spec]...]
    pallas_call x1, Pallas kernels: 11.6 us -> 10.4 us  [per_device(): pl.pallas_call(inside_kernel, grid=(tiles,), in_specs=[per_group, per_gro...]
    select_n x1, other arithmetic: 1 us -> 0.04 us  [per_device(): sent = jnp.where(earlier, states[32:64], states[0:32])]
    pallas_call x1, Pallas kernels: 13.4 us -> 12.6 us  [per_device(): pl.pallas_call(state_kernel, grid=(tiles,), in_specs=[me_spec, feat_spec,...]
  transfers between devices with their start and end apart: 10 -> 10, of which waited for: 5 -> 6; matrix products, arithmetic and copies ran while one was open for 1% -> 1% of each run, Pallas kernels for 36% -> 35%
where the time goes in v4:
time: 69.6 us; the launch traced here: 69 us
  Pallas kernels  37.4 us (54%)
  starting transfers between devices  15.2 us (22%)
  waiting for transfers between devices  8.98 us (13%)
  local copies, waits for them, and re-layouts  3.97 us (6%)
  other arithmetic  2.01 us (3%)
  between operations  1.46 us (2%)
    pallas_call x1, Pallas kernels, per_device(): pl.pallas_call(output_kernel, grid=(tiles,), in_specs=[me_spec, feat_spec...  13.9 us
    pallas_call x1, Pallas kernels, per_device(): pl.pallas_call(state_kernel, grid=(tiles,), in_specs=[me_spec, feat_spec,...  12.6 us
    ppermute x9, starting transfers between devices, swapped(): return lax.ppermute(value, axis, [(i, i ^ key) for i in range(count)])  12.1 us
    pallas_call x1, Pallas kernels, per_device(): pl.pallas_call(inside_kernel, grid=(tiles,), in_specs=[per_group, per_gro...  10.4 us
    ppermute x9, waiting for transfers between devices, swapped(): return lax.ppermute(value, axis, [(i, i ^ key) for i in range(count)])  6.07 us
    ppermute x1, starting transfers between devices, shifted(): lax.ppermute(value, axis, [(i, (i + steps) % count) for i in range(count)])  3.08 us
    ppermute x1, waiting for transfers between devices, shifted(): lax.ppermute(value, axis, [(i, (i + steps) % count) for i in range(count)])  2.91 us
  transfers between devices with their start and end apart: 10, of which 6 were waited for; matrix products, arithmetic and copies ran while one was open for 1% of the time, Pallas kernels for 35%

profile of v4, /device:TPU:0, one launch (start us, length us, event | category | flops | bytes accessed | tf_op | source)
XLA Modules:
  0.0 69.0 jit_solution(3367109635235620415)
XLA Ops:
  0.6 0.8 %fusion = (bf16[3,2,1024]{2,1,0:T(2,128)(2,1)S(1)}, bf16[3,2,1024]{2,1,0:T(2,128)(2,1)S(1)}) fusion(bf16[3,1024,1024]{2,1,0:T(8,128)(2,1)} %feat_ref.3), kind=kLoop, calls=%fused_computation.14 | loop fusion | bytes 49152 | tf_op jit(solution)/shard_map/slice | solution.py:406
  1.5 3.1 %collective-permute-start = (bf16[3,2,1024]{2,1,0:T(2,128)(2,1)S(1)}, bf16[3,2,1024]{2,1,0:T(2,128)(2,1)S(1)}, u32[]{:S(2)}, u32[]{:S(2)}) collective-permute-start(bf16[3,2,1024]{2,1,0:T(2,128)(2,1)S(1)} %get-tuple-element.33), channel_id=1, source_target_pairs={{0,1},{1,2},{2,3},{3,0},{4,5},{5,6},{6,7},{7,4},{8,9},{9,10},{10,1... | collective-permute-start | bytes 36872 | tf_op jit(solution)/shard_map/ppermute | solution.py:388
  4.6 0.7 %slice_bitcast_fusion.2 = bf16[1,2,1024]{2,1,0:T(2,128)(2,1)S(1)} fusion(bf16[1024,1024]{1,0:T(8,128)(2,1)} %cot_ref.3), kind=kLoop, calls=%fused_computation.12 | loop fusion | bytes 8192 | tf_op jit(solution)/shard_map/broadcast_in_dim | solution.py:406
  5.3 2.9 %collective-permute-done.tail_ref = bf16[3,2,1024]{2,1,0:T(2,128)(2,1)S(1)} collective-permute-done((bf16[3,2,1024]{2,1,0:T(2,128)(2,1)S(1)}, bf16[3,2,1024]{2,1,0:T(2,128)(2,1)S(1)}, u32[]{:S(2)}, u32[]{:S(2)}) %collective-permute-start) | collective-permute-done | bytes 12320 | tf_op jit(solution)/shard_map/ppermute | solution.py:388
  8.3 0.6 copy-done.2
  8.9 12.6 %state_part.1 = (bf16[64,128,128]{2,1,0:T(8,128)(2,1)S(1)}, bf16[64,128,128]{2,1,0:T(8,128)(2,1)S(1)}, bf16[64,128,128]{2,1,0:T(8,128)(2,1)S(1)}, f32[8,8,128,12...) custom-call(s32[1]{0:T(128)} %bitcast.me_ref, bf16[3,1024,1024]{2,1,0:T(8,128)(2,1)} %feat_ref.3, ...), custom_call_target="tpu_custom_call" | custom-call | tf_op jit(solution)/shard_map/state_part/pallas_call | solution.py:429
  21.4 0.0 copy-start
  21.4 0.0 copy-start.1
  21.6 2.1 %collective-permute-start.3 = (f32[40,1024]{1,0:T(8,128)S(1)}, f32[40,1024]{1,0:T(8,128)S(1)}, u32[]{:S(2)}, u32[]{:S(2)}) collective-permute-start(f32[40,1024]{1,0:T(8,128)S(1)} %get-tuple-element.37), channel_id=1, source_target_pairs={{0,3},{1,2},{2,1},{3,0},{4,7},{5,6},{6,5},{7,4},{8,11},{9,10},{10,... | collective-permute-start | bytes 491528 | tf_op jit(solution)/shard_map/ppermute | solution.py:393
  23.6 0.0 collective-permute-start.2
  23.6 2.4 %collective-permute-start.1 = (f32[40,1024]{1,0:T(8,128)S(1)}, f32[40,1024]{1,0:T(8,128)S(1)}, u32[]{:S(2)}, u32[]{:S(2)}) collective-permute-start(f32[40,1024]{1,0:T(8,128)S(1)} %get-tuple-element.39), channel_id=1, source_target_pairs={{0,1},{1,0},{2,3},{3,2},{4,5},{5,4},{6,7},{7,6},{8,9},{9,8},{10,11... | collective-permute-start | bytes 491528 | tf_op jit(solution)/shard_map/ppermute | solution.py:393
  26.0 10.4 %inside_part.1 = (f32[64,128,128]{2,1,0:T(8,128)S(1)}, f32[64,128,128]{2,1,0:T(8,128)S(1)}, f32[64,128]{1,0:T(8,128)S(1)}) custom-call(bf16[64,128,128]{2,1,0:T(8,128)(2,1)S(1)} %get-tuple-element.17.z_ref, bf16[64,128,128]{2,1,0:T(8,128)(2,1)S(1)} %get-tuple-element.18.eh_ref, bf16[64,128,128]{2,1,0:T(8,128)(2,1)S(1)} %get-tuple-element.19.el_ref, ...), custom_call_target="tpu_custom_call" | custom-call | flops 1879048192 | bytes 14680064 | tf_op jit(solution)/shard_map/inside_part/pallas_call | solution.py:465
  36.5 0.5 collective-permute-done.2.refs_1_
  36.9 0.5 join_part.1
  37.4 2.2 %collective-permute-start.6 = (f32[32,64]{1,0:T(8,128)S(1)}, f32[32,64]{1,0:T(8,128)S(1)}, u32[]{:S(2)}, u32[]{:S(2)}) collective-permute-start(f32[32,64]{1,0:T(8,128)S(1)} %get-tuple-element.29), channel_id=1, source_target_pairs={{0,3},{1,2},{2,1},{3,0},{4,7},{5,6},{6,5},{7,4},{8,11},{9,10},{10,... | collective-permute-start | bytes 24584 | tf_op jit(solution)/shard_map/ppermute | solution.py:393
  39.6 0.0 collective-permute-start.5
  39.6 2.3 %collective-permute-start.4 = (f32[32,64]{1,0:T(8,128)S(1)}, f32[32,64]{1,0:T(8,128)S(1)}, u32[]{:S(2)}, u32[]{:S(2)}) collective-permute-start(f32[32,64]{1,0:T(8,128)S(1)} %get-tuple-element.29), channel_id=1, source_target_pairs={{0,1},{1,0},{2,3},{3,2},{4,5},{5,4},{6,7},{7,6},{8,9},{9,8},{10,11... | collective-permute-start | bytes 24584 | tf_op jit(solution)/shard_map/ppermute | solution.py:393
  41.9 1.1 %collective-permute-done.6 = f32[32,64]{1,0:T(8,128)S(1)} collective-permute-done((f32[32,64]{1,0:T(8,128)S(1)}, f32[32,64]{1,0:T(8,128)S(1)}, u32[]{:S(2)}, u32[]{:S(2)}) %collective-permute-start.6) | collective-permute-done | bytes 8224 | tf_op jit(solution)/shard_map/ppermute | solution.py:393
  43.0 1.2 %collective-permute-done.5 = f32[32,64]{1,0:T(8,128)S(1)} collective-permute-done((f32[32,64]{1,0:T(8,128)S(1)}, f32[32,64]{1,0:T(8,128)S(1)}, u32[]{:S(2)}, u32[]{:S(2)}) %collective-permute-start.5) | collective-permute-done | bytes 8224 | tf_op jit(solution)/shard_map/ppermute | solution.py:393
  44.2 0.0 collective-permute-done.4
  44.2 0.6 multiply_reduce_fusion
  44.8 0.6 broadcast_in_dim.7
  45.5 0.1 collective-permute-start.7
  45.6 1.2 %collective-permute-done.7 = f32[8,128]{1,0:T(8,128)S(1)} collective-permute-done((f32[8,128]{1,0:T(8,128)S(1)}, f32[8,128]{1,0:T(8,128)S(1)}, u32[]{:S(2)}, u32[]{:S(2)}) %collective-permute-start.7) | collective-permute-done | bytes 4128 | tf_op jit(solution)/shard_map/ppermute | solution.py:393
  46.7 0.6 broadcast_add_fusion
  47.4 1.6 %collective-permute-start.8 = (f32[8,128]{1,0:T(8,128)S(1)}, f32[8,128]{1,0:T(8,128)S(1)}, u32[]{:S(2)}, u32[]{:S(2)}) collective-permute-start(f32[8,128]{1,0:T(8,128)S(1)} %broadcast_add_fusion), channel_id=1, source_target_pairs={{0,8},{4,12},{8,0},{12,4},{16,24},{20,28},{24,16},{28,20},{1,9},{5... | collective-permute-start | bytes 12296 | tf_op jit(solution)/shard_map/ppermute | solution.py:393
  48.9 2.1 %collective-permute-done.8 = f32[8,128]{1,0:T(8,128)S(1)} collective-permute-done((f32[8,128]{1,0:T(8,128)S(1)}, f32[8,128]{1,0:T(8,128)S(1)}, u32[]{:S(2)}, u32[]{:S(2)}) %collective-permute-start.8) | collective-permute-done | bytes 4128 | tf_op jit(solution)/shard_map/ppermute | solution.py:393
  51.0 0.6 fusion.1
  51.7 1.6 %collective-permute-start.9 = (f32[8,128]{1,0:T(8,128)S(1)}, f32[8,128]{1,0:T(8,128)S(1)}, u32[]{:S(2)}, u32[]{:S(2)}) collective-permute-start(f32[8,128]{1,0:T(8,128)S(1)} %fusion.1), channel_id=1, source_target_pairs={{0,16},{4,20},{8,24},{12,28},{16,0},{20,4},{24,8},{28,12},{1,17},{... | collective-permute-start | bytes 12296 | tf_op jit(solution)/shard_map/ppermute | solution.py:393
  53.3 13.9 %output_part.1 = (bf16[1024,1024]{1,0:T(8,128)(2,1)}, bf16[3,1024,1024]{2,1,0:T(8,128)(2,1)}) custom-call(s32[1]{0:T(128)} %bitcast.me_ref, bf16[3,1024,1024]{2,1,0:T(8,128)(2,1)} %feat_ref.3, bf16[3,2,1024]{2,1,0:T(2,128)(2,1)} %copy-done.2, f32[3,3,1024]{2,1,0:T(4,128)} %taps_ref.3, bf16[1024,1024]{1,0:T(8,128)(2,1)} %cot_ref.3, f32[16,64]{1,0:T(8,128)} %bitcast.12, ...), custom_call_target="tpu_custom_call" | custom-call | flops 1073741824 | bytes 29360128 | tf_op jit(solution)/shard_map/output_part/pallas_call | solution.py:511
  67.2 0.5 slice.33
  68.4 0.6 slice_bitcast_fusion
  (12 shorter events, 0.1 us)
Async XLA Ops:
  1.5 6.8 %collective-permute-start = (bf16[3,2,1024]{2,1,0:T(2,128)(2,1)S(1)}, bf16[3,2,1024]{2,1,0:T(2,128)(2,1)S(1)}, u32[]{:S(2)}, u32[]{:S(2)}) collective-permute-start(bf16[3,2,1024]{2,1,0:T(2,128)(2,1)S(1)} %get-tuple-element.33), channel_id=1, source_target_pairs={{0,1},{1,2},{2,3},{3,0},{4,5},{5,6},{6,7},{7,4},{8,9},{9,10},{10,1... | collective-permute-start | bytes 36872 | tf_op jit(solution)/shard_map/ppermute | solution.py:388
  8.3 0.6 copy-start.2
  21.4 15.5 %copy-start = (f32[64,16]{0,1:T(8,128)S(1)}, f32[64,16]{0,1:T(8,128)}, u32[]{:S(2)}) copy-start(f32[64,16]{0,1:T(8,128)} %param.7) | copy-start | bytes 12292
  21.4 15.5 %copy-start.1 = (f32[64,16]{0,1:T(8,128)S(1)}, f32[64,16]{0,1:T(8,128)}, u32[]{:S(2)}) copy-start(f32[64,16]{0,1:T(8,128)} %param.8) | copy-start | bytes 12292
  21.6 14.9 %collective-permute-start.3 = (f32[40,1024]{1,0:T(8,128)S(1)}, f32[40,1024]{1,0:T(8,128)S(1)}, u32[]{:S(2)}, u32[]{:S(2)}) collective-permute-start(f32[40,1024]{1,0:T(8,128)S(1)} %get-tuple-element.37), channel_id=1, source_target_pairs={{0,3},{1,2},{2,1},{3,0},{4,7},{5,6},{6,5},{7,4},{8,11},{9,10},{10,... | collective-permute-start | bytes 491528 | tf_op jit(solution)/shard_map/ppermute | solution.py:393
  23.6 13.3 %collective-permute-start.2 = (f32[40,1024]{1,0:T(8,128)S(1)}, f32[40,1024]{1,0:T(8,128)S(1)}, u32[]{:S(2)}, u32[]{:S(2)}) collective-permute-start(f32[40,1024]{1,0:T(8,128)S(1)} %get-tuple-element.38), channel_id=1, source_target_pairs={{0,2},{1,3},{2,0},{3,1},{4,6},{5,7},{6,4},{7,5},{8,10},{9,11},{10,... | collective-permute-start | bytes 491528 | tf_op jit(solution)/shard_map/ppermute | solution.py:393
  23.6 13.3 %collective-permute-start.1 = (f32[40,1024]{1,0:T(8,128)S(1)}, f32[40,1024]{1,0:T(8,128)S(1)}, u32[]{:S(2)}, u32[]{:S(2)}) collective-permute-start(f32[40,1024]{1,0:T(8,128)S(1)} %get-tuple-element.39), channel_id=1, source_target_pairs={{0,1},{1,0},{2,3},{3,2},{4,5},{5,4},{6,7},{7,6},{8,9},{9,8},{10,11... | collective-permute-start | bytes 491528 | tf_op jit(solution)/shard_map/ppermute | solution.py:393
  37.4 5.6 %collective-permute-start.6 = (f32[32,64]{1,0:T(8,128)S(1)}, f32[32,64]{1,0:T(8,128)S(1)}, u32[]{:S(2)}, u32[]{:S(2)}) collective-permute-start(f32[32,64]{1,0:T(8,128)S(1)} %get-tuple-element.29), channel_id=1, source_target_pairs={{0,3},{1,2},{2,1},{3,0},{4,7},{5,6},{6,5},{7,4},{8,11},{9,10},{10,... | collective-permute-start | bytes 24584 | tf_op jit(solution)/shard_map/ppermute | solution.py:393
  39.6 4.6 %collective-permute-start.5 = (f32[32,64]{1,0:T(8,128)S(1)}, f32[32,64]{1,0:T(8,128)S(1)}, u32[]{:S(2)}, u32[]{:S(2)}) collective-permute-start(f32[32,64]{1,0:T(8,128)S(1)} %get-tuple-element.29), channel_id=1, source_target_pairs={{0,2},{1,3},{2,0},{3,1},{4,6},{5,7},{6,4},{7,5},{8,10},{9,11},{10,... | collective-permute-start | bytes 24584 | tf_op jit(solution)/shard_map/ppermute | solution.py:393
  39.6 4.6 %collective-permute-start.4 = (f32[32,64]{1,0:T(8,128)S(1)}, f32[32,64]{1,0:T(8,128)S(1)}, u32[]{:S(2)}, u32[]{:S(2)}) collective-permute-start(f32[32,64]{1,0:T(8,128)S(1)} %get-tuple-element.29), channel_id=1, source_target_pairs={{0,1},{1,0},{2,3},{3,2},{4,5},{5,4},{6,7},{7,6},{8,9},{9,8},{10,11... | collective-permute-start | bytes 24584 | tf_op jit(solution)/shard_map/ppermute | solution.py:393
  45.5 1.2 %collective-permute-start.7 = (f32[8,128]{1,0:T(8,128)S(1)}, f32[8,128]{1,0:T(8,128)S(1)}, u32[]{:S(2)}, u32[]{:S(2)}) collective-permute-start(f32[8,128]{1,0:T(8,128)S(1)} %broadcast_in_dim.7), channel_id=1, source_target_pairs={{0,4},{4,0},{8,12},{12,8},{16,20},{20,16},{24,28},{28,24},{1,5},{5... | collective-permute-start | bytes 12296 | tf_op jit(solution)/shard_map/ppermute | solution.py:393
  47.4 3.7 %collective-permute-start.8 = (f32[8,128]{1,0:T(8,128)S(1)}, f32[8,128]{1,0:T(8,128)S(1)}, u32[]{:S(2)}, u32[]{:S(2)}) collective-permute-start(f32[8,128]{1,0:T(8,128)S(1)} %broadcast_add_fusion), channel_id=1, source_target_pairs={{0,8},{4,12},{8,0},{12,4},{16,24},{20,28},{24,16},{28,20},{1,9},{5... | collective-permute-start | bytes 12296 | tf_op jit(solution)/shard_map/ppermute | solution.py:393
  51.7 15.5 %collective-permute-start.9 = (f32[8,128]{1,0:T(8,128)S(1)}, f32[8,128]{1,0:T(8,128)S(1)}, u32[]{:S(2)}, u32[]{:S(2)}) collective-permute-start(f32[8,128]{1,0:T(8,128)S(1)} %fusion.1), channel_id=1, source_target_pairs={{0,16},{4,20},{8,24},{12,28},{16,0},{20,4},{24,8},{28,12},{1,17},{... | collective-permute-start | bytes 12296 | tf_op jit(solution)/shard_map/ppermute | solution.py:393

commit v5 on v4

--- a/solution.py
+++ b/solution.py
@@ -62,6 +62,10 @@
     return pltpu.roll(jnp.broadcast_to(row, (LANES, LANES)), 0, 1, stride=1, stride_axis=0)
 
 
+def of_tile(whole, first=0):
+    return whole.at[pl.ds((pl.program_id(0) + first) * TILE_GROUPS, TILE_GROUPS)]
+
+
 def table_rows(source_ref, rows_ref):
     tall = jnp.concatenate([source_ref[...]] * (LANES // MODES), axis=0)
     missing = LANES - tall.shape[1]
@@ -70,10 +74,10 @@
     rows_ref[...] = jnp.transpose(tall)
 
 
-def parameters(rate_ref, gain_ref, rate_rows, gain_rows):
-    tile = pl.program_id(0)
-
-    @pl.when(tile == 0)
+def parameters(rate_ref, gain_ref, rate_rows, gain_rows, first=0):
+    tile = pl.program_id(0) + first
+
+    @pl.when(pl.program_id(0) == 0)
     def _():
         table_rows(rate_ref, rate_rows)
         table_rows(gain_ref, gain_rows)
@@ -97,9 +101,12 @@
 
 def state_kernel(
     me_ref, feat_ref, tail_ref, taps_ref, cot_ref, rate_ref, gain_ref,
-    z_ref, eh_ref, el_ref, carry_ref, state_ref, cross_ref,
+    z_whole, eh_whole, el_whole, carry_whole, short_whole, state_ref, cross_ref,
     wide, own_all, table_all, rate_rows, gain_rows,
 ):
+    z_ref, eh_ref, el_ref = of_tile(z_whole), of_tile(eh_whole), of_tile(el_whole)
+    carry_ref = carry_whole.at[pl.program_id(0)]
+    short_ref = short_whole.at[pl.program_id(0)]
     tokens = feat_ref.shape[1]
     blocks = tokens // LANES
     rate_tile, _ = parameters(rate_ref, gain_ref, rate_rows, gain_rows)
@@ -128,6 +135,9 @@
         query = short_block(wide, taps_ref, 0, b * LANES, LANES)
         key = short_block(wide, taps_ref, 1, b * LANES, LANES)
         value = short_block(wide, taps_ref, 2, b * LANES, LANES)
+        short_ref[0, b * LANES : (b + 1) * LANES, :] = query
+        short_ref[1, b * LANES : (b + 1) * LANES, :] = key
+        short_ref[2, b * LANES : (b + 1) * LANES, :] = value
         z_t = jnp.transpose((key * value).astype(bf16))
         e_t = jnp.transpose(cot_ref[b * LANES : (b + 1) * LANES, :].astype(f32) * query)
         e_high, e_low = split(e_t)
@@ -151,33 +161,32 @@
         )
         got = dot_nt(left, table_all[g])
         rows = z.shape[0]
-        own = jnp.where(
-            iota(1, (rows, LANES)) < 64, got[:rows], got[rows : 2 * rows] + got[2 * rows :]
-        )
+        from_e = got[rows : 2 * rows] + got[2 * rows :]
         for b in range(blocks):
-            own_all[b, of, :] = own[b * MEMBERS : (b + 1) * MEMBERS]
+            at = slice(b * MEMBERS, (b + 1) * MEMBERS)
+            opposite = slice((blocks - 1 - b) * MEMBERS, (blocks - b) * MEMBERS)
+            own_all[b, of, :] = jnp.where(
+                iota(1, (MEMBERS, LANES)) < 64, got[at], from_e[opposite]
+            )
 
     span = per_member(jnp.exp(rate_tile * (-float(LANES))))
-    in_x = jnp.where((lane_row >= 48) & (lane_row < 64), float(LANES), 0.0)
-    in_y = jnp.where((lane_row >= 96) & (lane_row < 112), float(LANES), 0.0)
-    x_now = jnp.zeros((LANES, LANES), f32)
-    y_now = jnp.zeros((LANES, LANES), f32)
-    x_lag = jnp.zeros((LANES, LANES), f32)
-    y_lag = jnp.zeros((LANES, LANES), f32)
+    in_lag = jnp.where(
+        ((lane_row >= 48) & (lane_row < 64)) | ((lane_row >= 96) & (lane_row < 112)),
+        float(LANES),
+        0.0,
+    )
+    now = jnp.zeros((LANES, LANES), f32)
+    lagged = jnp.zeros((LANES, LANES), f32)
     cross = jnp.zeros((LANES, LANES), f32)
     for b in range(blocks):
         own = own_all[b]
-        cross = cross + x_now * pltpu.roll(own, 4 * MODES, 1)
-        carry_ref[0, b] = x_now
-        x_now = span * (x_now + x_lag) + own
-        x_lag = span * x_lag + in_x * pltpu.roll(own, MODES, 1)
-    for b in reversed(range(blocks)):
-        own = own_all[b]
-        carry_ref[0, b] = jnp.where(lane_at < 64, carry_ref[0, b], y_now)
-        y_now = span * (y_now + y_lag) + own
-        y_lag = span * y_lag + in_y * pltpu.roll(own, MODES, 1)
+        cross = cross + now * pltpu.roll(own_all[blocks - 1 - b], 4 * MODES, 1)
+        carry_ref[b] = now
+        now = span * (now + lagged) + own
+        if b < blocks - 1:
+            lagged = span * lagged + in_lag * pltpu.roll(own, MODES, 1)
     cross_ref[...] = jnp.sum(cross.reshape(TILE_GROUPS, MEMBERS, LANES), axis=1)
-    turned = jnp.transpose(jnp.where(lane_at < 64, x_now, y_now))
+    turned = jnp.transpose(now)
     state_ref[0:16] = turned[0:16]
     state_ref[16:32] = turned[48:64]
     state_ref[32:48] = turned[64:80]
@@ -185,10 +194,12 @@
 
 
 def inside_kernel(
-    z_ref, eh_ref, el_ref, rate_ref, gain_ref,
-    inner_ref, grad_ref, diag_ref,
+    z_whole, eh_whole, el_whole, rate_ref, gain_ref,
+    inner_whole, grad_whole, diag_ref,
     toep_all, power_all, fold_all, rate_rows, gain_rows,
 ):
+    z_ref, eh_ref, el_ref = of_tile(z_whole), of_tile(eh_whole), of_tile(el_whole)
+    inner_ref, grad_ref = of_tile(inner_whole), of_tile(grad_whole)
     rate_tile, coef_tile = parameters(rate_ref, gain_ref, rate_rows, gain_rows)
     rates, coefs = per_mode(rate_tile), per_mode(coef_tile)
     lag = iota(1, (LANES, LANES)).astype(f32)
@@ -273,21 +284,19 @@
 
 
 def output_kernel(
-    me_ref, feat_ref, tail_ref, taps_ref, cot_ref, rate_ref, gain_ref,
-    inner_ref, grad_ref, carry_ref, bound_ref,
-    mixer_ref, fgrad_ref,
-    wide, adj, inner_t, grad_t, left_all, rate_rows, gain_rows,
+    first, edge_ref, taps_ref, cot_ref, rate_ref, gain_ref,
+    inner_whole, grad_whole, carry_whole, short_whole, bound_ref,
+    *refs,
 ):
-    tokens = feat_ref.shape[1]
+    mixer_ref, fgrad_ref, wide, adj, inner_t, grad_t, left_all, rate_rows, gain_rows = refs[-9:]
+    inner_ref, grad_ref = of_tile(inner_whole, first), of_tile(grad_whole, first)
+    carry_ref = carry_whole.at[pl.program_id(0) + first]
+    short_ref = short_whole.at[pl.program_id(0) + first]
+    tokens = cot_ref.shape[0]
     blocks = tokens // LANES
-    widen(feat_ref, tail_ref, me_ref, wide, tokens)
-    for i in range(3):
-        wide[i, 8 + tokens : 16 + tokens, :] = jnp.zeros((8, LANES), f32)
-        wide[i, 8 + tokens : 10 + tokens, :] = bound_ref[48 + 2 * i : 50 + 2 * i]
-    rate_tile, coef_tile = parameters(rate_ref, gain_ref, rate_rows, gain_rows)
+    rate_tile, coef_tile = parameters(rate_ref, gain_ref, rate_rows, gain_rows, first)
     rates, coefs = per_mode(rate_tile), per_mode(coef_tile)
     lag = iota(1, (LANES, LANES)).astype(f32)
-    lane_row = iota(1, (1, LANES))
     lane_at = iota(1, (LANES, LANES))
     is_low = ((lane_at >= 16) & (lane_at < 32)) | ((lane_at >= 80) & (lane_at < 96))
     before = bound_ref[0:16]
@@ -298,9 +307,11 @@
     none_16 = jnp.zeros((MODES, LANES), bf16)
     none_64 = jnp.zeros((4 * MODES, LANES), bf16)
     member_rates = per_member(rate_tile)
+    span = jnp.exp(member_rates * (-float(LANES)))
+    from_others = turned
     for b in range(blocks):
-        steps = jnp.where(lane_row < 64, float(b * LANES), float((blocks - 1 - b) * LANES))
-        value = carry_ref[0, b] + turned * jnp.exp(-member_rates * steps)
+        value = carry_ref[b] + from_others
+        from_others = from_others * span
         high = value.astype(bf16).astype(f32)
         mixed = jnp.where(is_low, value - high, value).astype(bf16)
         for g in range(TILE_GROUPS):
@@ -321,26 +332,24 @@
             axis=1,
         )
         carried = dot_nn(left_all[g], right)
-        whole_inner = inner_ref[g] + carried[:, :LANES]
-        whole_grad = grad_ref[g] + carried[:, LANES:]
         for b in range(blocks):
             at = slice(b * MEMBERS, (b + 1) * MEMBERS)
-            inner_t[b, of, :] = whole_inner[at]
-            grad_t[b, of, :] = whole_grad[at]
+            opposite = slice((blocks - 1 - b) * MEMBERS, (blocks - b) * MEMBERS)
+            inner_t[b, of, :] = inner_ref[g, at, :] + carried[at, :LANES]
+            grad_t[b, of, :] = grad_ref[g, at, :] + carried[opposite, LANES:]
     for b in range(blocks):
         at = slice(b * LANES, (b + 1) * LANES)
-        query = short_block(wide, taps_ref, 0, b * LANES, LANES)
-        key = short_block(wide, taps_ref, 1, b * LANES, LANES)
-        value = short_block(wide, taps_ref, 2, b * LANES, LANES)
         inner = jnp.transpose(inner_t[b])
         grad = jnp.transpose(grad_t[b])
-        mixer_ref[at, :] = (query * inner).astype(bf16)
+        mixer_ref[at, :] = (short_ref[0, at, :] * inner).astype(bf16)
         adj[0, at, :] = cot_ref[at, :].astype(f32) * inner
-        adj[1, at, :] = grad * value
-        adj[2, at, :] = grad * key
-    key = short_block(wide, taps_ref, 1, tokens, 8)
-    value = short_block(wide, taps_ref, 2, tokens, 8)
-    query = short_block(wide, taps_ref, 0, tokens, 8)
+        adj[1, at, :] = grad * short_ref[2, at, :]
+        adj[2, at, :] = grad * short_ref[1, at, :]
+    for i in range(3):
+        wide[i, 0:8, :] = edge_ref[i, 8:16, :].astype(f32)
+        wide[i, 8:16, :] = jnp.zeros((8, LANES), f32)
+        wide[i, 8:10, :] = bound_ref[48 + 2 * i : 50 + 2 * i]
+    query, key, value = [short_block(wide, taps_ref, i, 0, 8) for i in range(3)]
     z = (key * value).astype(bf16).astype(f32)
     upstream = jnp.concatenate([bound_ref[54:56], jnp.zeros((6, LANES), f32)], axis=0)
     e = upstream * query
@@ -375,6 +384,22 @@
             ).astype(bf16)
 
 
+def resident(shape, dtype):
+    return pltpu.VMEM(shape, dtype)
+
+
+def sum_kernel(*refs):
+    *terms, summed_ref, square_ref = refs
+    terms = [term[...] for term in terms]
+    while len(terms) > 1:
+        terms = [terms[i] + terms[i + 1] for i in range(0, len(terms), 2)]
+    summed_ref[...] = terms[0]
+    square_ref[...] = jnp.broadcast_to(
+        jnp.sum(jnp.sum(terms[0] * terms[0], axis=0, keepdims=True), axis=1, keepdims=True),
+        square_ref.shape,
+    )
+
+
 def far(*arrays):
     return [pltpu.with_memory_space_constraint(array, pltpu.HBM) for array in arrays]
 
@@ -408,33 +433,33 @@
     me = ctx_index.astype(jnp.int32).reshape(1)
     rates, gains = decay_rates.T, mode_gains.T
 
-    per_group = pl.BlockSpec((TILE_GROUPS, ROWS, LANES), lambda j: (j, 0, 0))
+    whole = pl.BlockSpec(memory_space=pltpu.VMEM)
     feat_spec = pl.BlockSpec((3, tokens, LANES), lambda j: (0, 0, j))
     tail_spec = pl.BlockSpec((3, 2, LANES), lambda j: (0, 0, j))
     taps_spec = pl.BlockSpec((3, 3, LANES), lambda j: (0, 0, j))
     cot_spec = pl.BlockSpec((tokens, LANES), lambda j: (0, j))
     table_spec = pl.BlockSpec((MODES, groups), lambda j: (0, 0))
-    carry_spec = pl.BlockSpec((1, blocks, LANES, LANES), lambda j: (j, 0, 0, 0))
     slot_spec = pl.BlockSpec((TILE_GROUPS, LANES), lambda j: (j, 0))
     me_spec = pl.BlockSpec(memory_space=pltpu.SMEM)
     rows = blocks * MEMBERS
-    turned = pltpu.VMEM((groups, rows, LANES), bf16)
-    wide_turned = pltpu.VMEM((groups, rows, LANES), f32)
+    turned = resident((groups, rows, LANES), bf16)
+    wide_turned = resident((groups, rows, LANES), f32)
     slots = jax.ShapeDtypeStruct((groups, LANES), f32)
     table_scratch = [pltpu.VMEM((LANES, LANES), f32), pltpu.VMEM((LANES, LANES), f32)]
 
     def room(mebibytes):
         return pltpu.CompilerParams(vmem_limit_bytes=mebibytes * 2**20)
 
-    z, eh, el, carry, states, cross = pl.pallas_call(
+    z, eh, el, carry, short, states, cross = pl.pallas_call(
         state_kernel,
         grid=(tiles,),
         in_specs=[me_spec, feat_spec, tail_spec, taps_spec, cot_spec, table_spec, table_spec],
         out_specs=[
-            per_group,
-            per_group,
-            per_group,
-            carry_spec,
+            whole,
+            whole,
+            whole,
+            whole,
+            whole,
             pl.BlockSpec((4 * MODES, LANES), lambda j: (0, j)),
             slot_spec,
         ],
@@ -442,7 +467,8 @@
             turned,
             turned,
             turned,
-            pltpu.VMEM((tiles, blocks, LANES, LANES), f32),
+            resident((tiles, blocks, LANES, LANES), f32),
+            resident((tiles, 3, tokens, LANES), f32),
             jax.ShapeDtypeStruct((4 * MODES, channels), f32),
             slots,
         ],
@@ -452,7 +478,7 @@
             pltpu.VMEM((TILE_GROUPS, LANES, 2 * LANES), bf16),
         ]
         + table_scratch,
-        compiler_params=room(24),
+        compiler_params=room(14),
         name="state_part",
     )(me, *far(features, tail, short_taps, cotangent, rates, gains))
 
@@ -465,8 +491,8 @@
     inner, grad, diag = pl.pallas_call(
         inside_kernel,
         grid=(tiles,),
-        in_specs=[per_group, per_group, per_group, table_spec, table_spec],
-        out_specs=[per_group, per_group, slot_spec],
+        in_specs=[whole, whole, whole, table_spec, table_spec],
+        out_specs=[whole, whole, slot_spec],
         out_shape=[wide_turned, wide_turned, slots],
         scratch_shapes=[
             pltpu.VMEM((TILE_GROUPS, 2 * LANES, LANES), bf16),
@@ -474,14 +500,13 @@
             pltpu.VMEM((8 * TILE_GROUPS, LANES), f32),
         ]
         + table_scratch,
-        compiler_params=room(24),
+        compiler_params=room(14),
         cost_estimate=pl.CostEstimate(
             flops=2 * groups * rows * LANES * LANES * 7, bytes_accessed=14 * 2**20, transcendentals=0
         ),
         name="inside_part",
     )(*near(z, eh, el), *far(rates, gains))
 
-    whole = pl.BlockSpec(memory_space=pltpu.VMEM)
     bound, local = pl.pallas_call(
         functools.partial(join_kernel, tokens),
         in_specs=[me_spec] + [whole] * (5 + len(gots)),
@@ -490,59 +515,85 @@
             jax.ShapeDtypeStruct((56, channels), f32),
             jax.ShapeDtypeStruct((2 * MODES, groups), f32),
         ],
-        compiler_params=room(24),
+        compiler_params=room(14),
         name="join_part",
     )(me, states, diag, cross, rates, gains, *gots)
 
+    def outputs(first, count, *written):
+        columns = lambda j: (0, j + first)
+        layers = lambda j: (0, 0, j + first)
+        mine = [pl.BlockSpec((tokens, LANES), columns), pl.BlockSpec((3, tokens, LANES), layers)]
+        return pl.pallas_call(
+            functools.partial(output_kernel, first),
+            grid=(count,),
+            in_specs=[
+                pl.BlockSpec((3, 16, LANES), lambda j: (0, tokens // 16 - 1, j + first)),
+                pl.BlockSpec((3, 3, LANES), layers),
+                pl.BlockSpec((tokens, LANES), columns),
+                table_spec,
+                table_spec,
+                whole,
+                whole,
+                whole,
+                whole,
+                pl.BlockSpec((56, LANES), columns),
+            ]
+            + [pl.BlockSpec(memory_space=pl.ANY)] * len(written),
+            out_specs=mine,
+            out_shape=[
+                jax.ShapeDtypeStruct((tokens, channels), bf16),
+                jax.ShapeDtypeStruct((3, tokens, channels), bf16),
+            ],
+            scratch_shapes=[
+                pltpu.VMEM((3, 16, LANES), f32),
+                pltpu.VMEM((3, tokens + 8, LANES), f32),
+                pltpu.VMEM((blocks, LANES, LANES), f32),
+                pltpu.VMEM((blocks, LANES, LANES), f32),
+                pltpu.VMEM((TILE_GROUPS, rows, LANES), bf16),
+            ]
+            + table_scratch,
+            compiler_params=room(14),
+            input_output_aliases={10: 0, 11: 1} if written else {},
+            cost_estimate=pl.CostEstimate(
+                flops=2 * count * TILE_GROUPS * rows * LANES * LANES * 8,
+                bytes_accessed=count * 4 * 2**20,
+                transcendentals=0,
+            ),
+            name="output_part",
+        )(
+            *far(features, short_taps, cotangent, rates, gains),
+            *near(inner, grad, carry, short),
+            bound,
+            *written,
+        )
+
+    half = tiles // 2
     terms = [local] + [swapped(local, "ctx", key) for key in range(1, ctx_count)]
-    while len(terms) > 1:
-        terms = [terms[i] + terms[i + 1] for i in range(0, len(terms), 2)]
-    summed = terms[0]
-    squares = jnp.broadcast_to(jnp.sum(summed * summed), (8, LANES))
+    written = outputs(0, half)
+    terms, written = lax.optimization_barrier((terms, written))
+    summed, squares = pl.pallas_call(
+        sum_kernel,
+        in_specs=[whole] * len(terms),
+        out_specs=[whole, whole],
+        out_shape=[
+            jax.ShapeDtypeStruct((2 * MODES, groups), f32),
+            jax.ShapeDtypeStruct((1, groups), f32),
+        ],
+        compiler_params=room(14),
+        name="sum_part",
+    )(*terms)
     fsdp_count = lax.axis_size("fsdp")
     step = 1
-    while step < fsdp_count:
+    while step * 4 < fsdp_count:
         squares = squares + swapped(squares, "fsdp", step)
         step *= 2
+    squares, written = lax.optimization_barrier((squares, written))
+    parts = [squares] + [swapped(squares, "fsdp", key) for key in range(step, fsdp_count, step)]
+    mixer, feature_grads = outputs(half, tiles - half, *written)
+    while len(parts) > 1:
+        parts = [parts[i] + parts[i + 1] for i in range(0, len(parts), 2)]
     entry_count = 2 * groups * MODES * fsdp_count
-    factor = jnp.minimum(1.0, lax.rsqrt(squares[0, 0] / entry_count + 1e-06))
-    clipped = summed * factor
-
-    mixer, feature_grads = pl.pallas_call(
-        output_kernel,
-        grid=(tiles,),
-        in_specs=[
-            me_spec,
-            feat_spec,
-            tail_spec,
-            taps_spec,
-            cot_spec,
-            table_spec,
-            table_spec,
-            per_group,
-            per_group,
-            carry_spec,
-            pl.BlockSpec((56, LANES), lambda j: (0, j)),
-        ],
-        out_specs=[cot_spec, feat_spec],
-        out_shape=[
-            jax.ShapeDtypeStruct((tokens, channels), bf16),
-            jax.ShapeDtypeStruct((3, tokens, channels), bf16),
-        ],
-        scratch_shapes=[
-            pltpu.VMEM((3, tokens + 16, LANES), f32),
-            pltpu.VMEM((3, tokens + 8, LANES), f32),
-            pltpu.VMEM((blocks, LANES, LANES), f32),
-            pltpu.VMEM((blocks, LANES, LANES), f32),
-            pltpu.VMEM((TILE_GROUPS, rows, LANES), bf16),
-        ]
-        + table_scratch,
-        compiler_params=room(24),
-        cost_estimate=pl.CostEstimate(
-            flops=2 * groups * rows * LANES * LANES * 4, bytes_accessed=28 * 2**20, transcendentals=0
-        ),
-        name="output_part",
-    )(me, *far(features, tail, short_taps, cotangent, rates, gains), *near(inner, grad, carry), bound)
+    clipped = summed * jnp.minimum(1.0, lax.rsqrt(parts[0] / entry_count + 1e-06))
     return (mixer, feature_grads, clipped[:MODES].T, clipped[MODES:].T)
 
 

time: 69.6 us -> 60.4 us (0.87)
  waiting for transfers between devices: 8.98 us -> 4.05 us
  other arithmetic: 2.01 us -> 0.12 us
  local copies, waits for them, and re-layouts: 3.97 us -> 2.81 us
  Pallas kernels: 37.4 us -> 36.4 us
    ppermute x9 -> x10, waiting for transfers between devices: 6.07 us -> 1.14 us  [swapped(): return lax.ppermute(value, axis, [(i, i ^ key) for i in range(count)])]
    add x3 -> x1, other arithmetic: 1.3 us -> 0.01 us  [per_device(): squares = squares + swapped(squares, 'fsdp', step)]
    pallas_call x2 -> x4, Pallas kernels: 24.4 us -> 23.5 us  [the longest x2 12.9 us: outputs(): pl.pallas_call(functools.partial(output_kernel, first), grid=(count,), in...]
    ppermute x9 -> x10, starting transfers between devices: 12.1 us -> 12.7 us  [swapped(): return lax.ppermute(value, axis, [(i, i ^ key) for i in range(count)])]
  transfers between devices with their start and end apart: 10 -> 11, of which waited for: 6 -> 2; matrix products, arithmetic and copies ran while one was open for 1% -> 1% of each run, Pallas kernels for 35% -> 39%
where the time goes in v5:
time: 60.4 us; the launch traced here: 60 us
  Pallas kernels  36.4 us (60%)
  starting transfers between devices  15.8 us (26%)
  waiting for transfers between devices  4.05 us (7%)
  local copies, waits for them, and re-layouts  2.81 us (5%)
  between operations  0.79 us (1%)
    pallas_call x2, Pallas kernels, outputs(): pl.pallas_call(functools.partial(output_kernel, first), grid=(count,), in...  12.9 us
    ppermute x10, starting transfers between devices, swapped(): return lax.ppermute(value, axis, [(i, i ^ key) for i in range(count)])  12.7 us
    pallas_call x1, Pallas kernels, per_device(): pl.pallas_call(state_kernel, grid=(tiles,), in_specs=[me_spec, feat_spec,...  12.4 us
    pallas_call x1, Pallas kernels, per_device(): pl.pallas_call(inside_kernel, grid=(tiles,), in_specs=[whole, whole, whol...  10.5 us
    ppermute x1, starting transfers between devices, shifted(): lax.ppermute(value, axis, [(i, (i + steps) % count) for i in range(count)])  3.08 us
    ppermute x1, waiting for transfers between devices, shifted(): lax.ppermute(value, axis, [(i, (i + steps) % count) for i in range(count)])  2.91 us
  transfers between devices with their start and end apart: 11, of which 2 were waited for; matrix products, arithmetic and copies ran while one was open for 1% of the time, Pallas kernels for 39%

profile of v5, /device:TPU:0, one launch (start us, length us, event | category | flops | bytes accessed | tf_op | source)
XLA Modules:
  0.0 60.0 jit_solution(16947138303798022496)
XLA Ops:
  0.6 0.8 %fusion = (bf16[3,2,1024]{2,1,0:T(2,128)(2,1)S(1)}, bf16[3,2,1024]{2,1,0:T(2,128)(2,1)S(1)}) fusion(bf16[3,1024,1024]{2,1,0:T(8,128)(2,1)} %edge_ref.3), kind=kLoop, calls=%fused_computation.12 | loop fusion | bytes 49152 | tf_op jit(solution)/shard_map/slice | solution.py:431
  1.5 3.1 %collective-permute-start = (bf16[3,2,1024]{2,1,0:T(2,128)(2,1)S(1)}, bf16[3,2,1024]{2,1,0:T(2,128)(2,1)S(1)}, u32[]{:S(2)}, u32[]{:S(2)}) collective-permute-start(bf16[3,2,1024]{2,1,0:T(2,128)(2,1)S(1)} %get-tuple-element.59), channel_id=1, source_target_pairs={{0,1},{1,2},{2,3},{3,0},{4,5},{5,6},{6,7},{7,4},{8,9},{9,10},{10,1... | collective-permute-start | bytes 36872 | tf_op jit(solution)/shard_map/ppermute | solution.py:413
  4.6 0.7 %slice_bitcast_fusion.2 = bf16[1,2,1024]{2,1,0:T(2,128)(2,1)S(1)} fusion(bf16[1024,1024]{1,0:T(8,128)(2,1)} %cot_ref.5), kind=kLoop, calls=%fused_computation.10 | loop fusion | bytes 8192 | tf_op jit(solution)/shard_map/broadcast_in_dim | solution.py:431
  5.3 2.9 %collective-permute-done.tail_ref = bf16[3,2,1024]{2,1,0:T(2,128)(2,1)S(1)} collective-permute-done((bf16[3,2,1024]{2,1,0:T(2,128)(2,1)S(1)}, bf16[3,2,1024]{2,1,0:T(2,128)(2,1)S(1)}, u32[]{:S(2)}, u32[]{:S(2)}) %collective-permute-start) | collective-permute-done | bytes 12320 | tf_op jit(solution)/shard_map/ppermute | solution.py:413
  8.3 0.6 copy-done.2
  8.9 12.4 %state_part.1 = (bf16[64,128,128]{2,1,0:T(8,128)(2,1)S(1)}, bf16[64,128,128]{2,1,0:T(8,128)(2,1)S(1)}, bf16[64,128,128]{2,1,0:T(8,128)(2,1)S(1)}, f32[8,8,128,12...) custom-call(s32[1]{0:T(128)} %bitcast.2.me_ref, ...), custom_call_target="tpu_custom_call" | custom-call | tf_op jit(solution)/shard_map/state_part/pallas_call | solution.py:453
  21.3 0.0 copy-start
  21.3 0.0 copy-start.1
  21.4 0.1 collective-permute-start.1
  21.5 2.6 %collective-permute-start.2 = (f32[40,1024]{1,0:T(8,128)S(1)}, f32[40,1024]{1,0:T(8,128)S(1)}, u32[]{:S(2)}, u32[]{:S(2)}) collective-permute-start(f32[40,1024]{1,0:T(8,128)S(1)} %get-tuple-element.64), channel_id=1, source_target_pairs={{0,2},{1,3},{2,0},{3,1},{4,6},{5,7},{6,4},{7,5},{8,10},{9,11},{10,... | collective-permute-start | bytes 491528 | tf_op jit(solution)/shard_map/ppermute | solution.py:418
  24.1 1.8 %collective-permute-start.3 = (f32[40,1024]{1,0:T(8,128)S(1)}, f32[40,1024]{1,0:T(8,128)S(1)}, u32[]{:S(2)}, u32[]{:S(2)}) collective-permute-start(f32[40,1024]{1,0:T(8,128)S(1)} %get-tuple-element.63), channel_id=1, source_target_pairs={{0,3},{1,2},{2,1},{3,0},{4,7},{5,6},{6,5},{7,4},{8,11},{9,10},{10,... | collective-permute-start | bytes 491528 | tf_op jit(solution)/shard_map/ppermute | solution.py:418
  25.9 10.5 %inside_part.1 = (f32[64,128,128]{2,1,0:T(8,128)S(1)}, f32[64,128,128]{2,1,0:T(8,128)S(1)}, f32[64,128]{1,0:T(8,128)S(1)}) custom-call(bf16[64,128,128]{2,1,0:T(8,128)(2,1)S(1)} %get-tuple-element.31.z_whole, bf16[64,128,128]{2,1,0:T(8,128)(2,1)S(1)} %get-tuple-element.32.eh_whole, bf16[64,128,128]{2,1,0:T(8,128)(2,1)S(1)} %get-tuple-element.33.el_whole, ...), custom_call_target="tpu_custom_call" | custom-call | flops 1879048192 | bytes 14680064 | tf_op jit(solution)/shard_map/inside_part/pallas_call | solution.py:491
  36.4 0.0 collective-permute-done.1.refs_0_
  36.4 0.0 collective-permute-done.2.refs_1_
  36.4 0.0 collective-permute-done.3.refs_2_
  36.4 0.5 join_part.1
  36.9 2.3 %collective-permute-start.4 = (f32[32,64]{1,0:T(8,128)S(1)}, f32[32,64]{1,0:T(8,128)S(1)}, u32[]{:S(2)}, u32[]{:S(2)}) collective-permute-start(f32[32,64]{1,0:T(8,128)S(1)} %get-tuple-element.45.refs_0_), channel_id=1, source_target_pairs={{0,1},{1,0},{2,3},{3,2},{4,5},{5,4},{6,7},{7,6},{8,9},{9,8},{10,11... | collective-permute-start | bytes 24584 | tf_op jit(solution)/shard_map/ppermute | solution.py:418
  39.3 0.4 collective-permute-start.5
  39.7 2.0 %collective-permute-start.6 = (f32[32,64]{1,0:T(8,128)S(1)}, f32[32,64]{1,0:T(8,128)S(1)}, u32[]{:S(2)}, u32[]{:S(2)}) collective-permute-start(f32[32,64]{1,0:T(8,128)S(1)} %get-tuple-element.45.refs_0_), channel_id=1, source_target_pairs={{0,3},{1,2},{2,1},{3,0},{4,7},{5,6},{6,5},{7,4},{8,11},{9,10},{10,... | collective-permute-start | bytes 24584 | tf_op jit(solution)/shard_map/ppermute | solution.py:418
  41.7 6.4 %output_part.2 = (bf16[1024,1024]{1,0:T(8,128)(2,1)}, bf16[3,1024,1024]{2,1,0:T(8,128)(2,1)}) custom-call(bf16[3,1024,1024]{2,1,0:T(8,128)(2,1)} %edge_ref.3, f32[3,3,1024]{2,1,0:T(4,128)} %taps_ref.5, bf16[1024,1024]{1,0:T(8,128)(2,1)} %cot_ref.5, f32[16,64]{1,0:T(8,128)} %bitcast.13, f32[16,64]{1,0:T(8,128)} %bitcast.18, ...), custom_call_target="tpu_custom_call" | custom-call | flops 1073741824 | bytes 16777216 | tf_op jit(solution)/shard_map/output_part/pallas_call | solution.py:526
  48.1 0.0 collective-permute-done.4.refs_1_
  48.1 0.0 collective-permute-done.5.refs_2_
  48.1 0.1 sum_part.1
  48.2 0.0 collective-permute-start.7
  48.3 1.1 %collective-permute-done.7 = f32[1,64]{1,0:T(1,128)S(1)} collective-permute-done((f32[1,64]{1,0:T(1,128)S(1)}, f32[1,64]{1,0:T(1,128)S(1)}, u32[]{:S(2)}, u32[]{:S(2)}) %collective-permute-start.7) | collective-permute-done | bytes 288 | tf_op jit(solution)/shard_map/ppermute | solution.py:418
  49.4 2.4 %collective-permute-start.10 = (f32[1,64]{1,0:T(1,128)S(1)}, f32[1,64]{1,0:T(1,128)S(1)}, u32[]{:S(2)}, u32[]{:S(2)}) collective-permute-start(f32[1,64]{1,0:T(1,128)S(1)} %add.18), channel_id=1, source_target_pairs={{0,24},{4,28},{8,16},{12,20},{16,8},{20,12},{24,0},{28,4},{1,25},{... | collective-permute-start | bytes 776 | tf_op jit(solution)/shard_map/ppermute | solution.py:418
  51.8 0.5 collective-permute-start.8
  52.4 0.5 collective-permute-start.9
  52.9 6.5 %output_part.3 = (bf16[1024,1024]{1,0:T(8,128)(2,1)}, bf16[3,1024,1024]{2,1,0:T(8,128)(2,1)}) custom-call(bf16[3,1024,1024]{2,1,0:T(8,128)(2,1)} %edge_ref.3, f32[3,3,1024]{2,1,0:T(4,128)} %taps_ref.5, bf16[1024,1024]{1,0:T(8,128)(2,1)} %cot_ref.5, f32[16,64]{1,0:T(8,128)} %bitcast.14, ...), custom_call_target="tpu_custom_call", output_to_operand_aliasing={{0}: (10, {}), {1}: (11, {})} | custom-call | flops 1073741824 | bytes 16777216 | tf_op jit(solution)/shard_map/output_part/pallas_call | solution.py:526
  59.3 0.0 collective-permute-done.10
  59.3 0.0 collective-permute-done.8
  59.4 0.6 %slice_bitcast_fusion = (f32[64,16]{0,1:T(8,128)}, f32[64,16]{0,1:T(8,128)}) fusion(f32[32,64]{1,0:T(8,128)S(1)} %broadcast_multiply_fusion), kind=kLoop, calls=%fused_computation.7 | loop fusion | bytes 16384 | tf_op jit(solution)/shard_map/transpose | solution.py:597
  (12 shorter events, 0.2 us)
Async XLA Ops:
  1.5 6.8 %collective-permute-start = (bf16[3,2,1024]{2,1,0:T(2,128)(2,1)S(1)}, bf16[3,2,1024]{2,1,0:T(2,128)(2,1)S(1)}, u32[]{:S(2)}, u32[]{:S(2)}) collective-permute-start(bf16[3,2,1024]{2,1,0:T(2,128)(2,1)S(1)} %get-tuple-element.59), channel_id=1, source_target_pairs={{0,1},{1,2},{2,3},{3,0},{4,5},{5,6},{6,7},{7,4},{8,9},{9,10},{10,1... | collective-permute-start | bytes 36872 | tf_op jit(solution)/shard_map/ppermute | solution.py:413
  8.3 0.6 copy-start.2
  21.3 15.1 %copy-start = (f32[64,16]{0,1:T(8,128)S(1)}, f32[64,16]{0,1:T(8,128)}, u32[]{:S(2)}) copy-start(f32[64,16]{0,1:T(8,128)} %param.7) | copy-start | bytes 12292
  21.3 15.1 %copy-start.1 = (f32[64,16]{0,1:T(8,128)S(1)}, f32[64,16]{0,1:T(8,128)}, u32[]{:S(2)}) copy-start(f32[64,16]{0,1:T(8,128)} %param.8) | copy-start | bytes 12292
  21.4 14.9 %collective-permute-start.1 = (f32[40,1024]{1,0:T(8,128)S(1)}, f32[40,1024]{1,0:T(8,128)S(1)}, u32[]{:S(2)}, u32[]{:S(2)}) collective-permute-start(f32[40,1024]{1,0:T(8,128)S(1)} %get-tuple-element.65), channel_id=1, source_target_pairs={{0,1},{1,0},{2,3},{3,2},{4,5},{5,4},{6,7},{7,6},{8,9},{9,8},{10,11... | collective-permute-start | bytes 491528 | tf_op jit(solution)/shard_map/ppermute | solution.py:418
  21.5 14.9 %collective-permute-start.2 = (f32[40,1024]{1,0:T(8,128)S(1)}, f32[40,1024]{1,0:T(8,128)S(1)}, u32[]{:S(2)}, u32[]{:S(2)}) collective-permute-start(f32[40,1024]{1,0:T(8,128)S(1)} %get-tuple-element.64), channel_id=1, source_target_pairs={{0,2},{1,3},{2,0},{3,1},{4,6},{5,7},{6,4},{7,5},{8,10},{9,11},{10,... | collective-permute-start | bytes 491528 | tf_op jit(solution)/shard_map/ppermute | solution.py:418
  24.1 12.3 %collective-permute-start.3 = (f32[40,1024]{1,0:T(8,128)S(1)}, f32[40,1024]{1,0:T(8,128)S(1)}, u32[]{:S(2)}, u32[]{:S(2)}) collective-permute-start(f32[40,1024]{1,0:T(8,128)S(1)} %get-tuple-element.63), channel_id=1, source_target_pairs={{0,3},{1,2},{2,1},{3,0},{4,7},{5,6},{6,5},{7,4},{8,11},{9,10},{10,... | collective-permute-start | bytes 491528 | tf_op jit(solution)/shard_map/ppermute | solution.py:418
  36.9 11.2 %collective-permute-start.4 = (f32[32,64]{1,0:T(8,128)S(1)}, f32[32,64]{1,0:T(8,128)S(1)}, u32[]{:S(2)}, u32[]{:S(2)}) collective-permute-start(f32[32,64]{1,0:T(8,128)S(1)} %get-tuple-element.45.refs_0_), channel_id=1, source_target_pairs={{0,1},{1,0},{2,3},{3,2},{4,5},{5,4},{6,7},{7,6},{8,9},{9,8},{10,11... | collective-permute-start | bytes 24584 | tf_op jit(solution)/shard_map/ppermute | solution.py:418
  39.3 8.9 %collective-permute-start.5 = (f32[32,64]{1,0:T(8,128)S(1)}, f32[32,64]{1,0:T(8,128)S(1)}, u32[]{:S(2)}, u32[]{:S(2)}) collective-permute-start(f32[32,64]{1,0:T(8,128)S(1)} %get-tuple-element.45.refs_0_), channel_id=1, source_target_pairs={{0,2},{1,3},{2,0},{3,1},{4,6},{5,7},{6,4},{7,5},{8,10},{9,11},{10,... | collective-permute-start | bytes 24584 | tf_op jit(solution)/shard_map/ppermute | solution.py:418
  39.7 8.4 %collective-permute-start.6 = (f32[32,64]{1,0:T(8,128)S(1)}, f32[32,64]{1,0:T(8,128)S(1)}, u32[]{:S(2)}, u32[]{:S(2)}) collective-permute-start(f32[32,64]{1,0:T(8,128)S(1)} %get-tuple-element.45.refs_0_), channel_id=1, source_target_pairs={{0,3},{1,2},{2,1},{3,0},{4,7},{5,6},{6,5},{7,4},{8,11},{9,10},{10,... | collective-permute-start | bytes 24584 | tf_op jit(solution)/shard_map/ppermute | solution.py:418
  48.2 1.1 %collective-permute-start.7 = (f32[1,64]{1,0:T(1,128)S(1)}, f32[1,64]{1,0:T(1,128)S(1)}, u32[]{:S(2)}, u32[]{:S(2)}) collective-permute-start(f32[1,64]{1,0:T(1,128)S(1)} %get-tuple-element.49), channel_id=1, source_target_pairs={{0,4},{4,0},{8,12},{12,8},{16,20},{20,16},{24,28},{28,24},{1,5},{5... | collective-permute-start | bytes 776 | tf_op jit(solution)/shard_map/ppermute | solution.py:418
  49.4 10.0 %collective-permute-start.10 = (f32[1,64]{1,0:T(1,128)S(1)}, f32[1,64]{1,0:T(1,128)S(1)}, u32[]{:S(2)}, u32[]{:S(2)}) collective-permute-start(f32[1,64]{1,0:T(1,128)S(1)} %add.18), channel_id=1, source_target_pairs={{0,24},{4,28},{8,16},{12,20},{16,8},{20,12},{24,0},{28,4},{1,25},{... | collective-permute-start | bytes 776 | tf_op jit(solution)/shard_map/ppermute | solution.py:418
  51.8 7.5 %collective-permute-start.8 = (f32[1,64]{1,0:T(1,128)S(1)}, f32[1,64]{1,0:T(1,128)S(1)}, u32[]{:S(2)}, u32[]{:S(2)}) collective-permute-start(f32[1,64]{1,0:T(1,128)S(1)} %add.18), channel_id=1, source_target_pairs={{0,8},{4,12},{8,0},{12,4},{16,24},{20,28},{24,16},{28,20},{1,9},{5... | collective-permute-start | bytes 776 | tf_op jit(solution)/shard_map/ppermute | solution.py:418
  52.4 7.0 %collective-permute-start.9 = (f32[1,64]{1,0:T(1,128)S(1)}, f32[1,64]{1,0:T(1,128)S(1)}, u32[]{:S(2)}, u32[]{:S(2)}) collective-permute-start(f32[1,64]{1,0:T(1,128)S(1)} %add.18), channel_id=1, source_target_pairs={{0,16},{4,20},{8,24},{12,28},{16,0},{20,4},{24,8},{28,12},{1,17},{... | collective-permute-start | bytes 776 | tf_op jit(solution)/shard_map/ppermute | solution.py:418

commit v6 on v5

--- a/solution.py
+++ b/solution.py
@@ -37,9 +37,9 @@
     return lax.broadcasted_iota(jnp.int32, shape, axis)
 
 
-def widen(feat_ref, tail_ref, me_ref, wide, tokens):
+def widen(feat_ref, wide, tokens):
     for i in range(3):
-        wide[i, 6:8, :] = jnp.where(me_ref[0] == 0, 0.0, tail_ref[i].astype(f32))
+        wide[i, 0:8, :] = jnp.zeros((8, LANES), f32)
         wide[i, 8 : 8 + tokens, :] = feat_ref[i].astype(f32)
 
 
@@ -100,8 +100,9 @@
 
 
 def state_kernel(
-    me_ref, feat_ref, tail_ref, taps_ref, cot_ref, rate_ref, gain_ref,
+    feat_ref, taps_ref, cot_ref, rate_ref, gain_ref,
     z_whole, eh_whole, el_whole, carry_whole, short_whole, state_ref, cross_ref,
+    later_ref, earlier_ref,
     wide, own_all, table_all, rate_rows, gain_rows,
 ):
     z_ref, eh_ref, el_ref = of_tile(z_whole), of_tile(eh_whole), of_tile(el_whole)
@@ -130,7 +131,7 @@
                 [s_of, s_of, s_of, l_of, m_of, m_of, n_of, m_of], axis=0
             )
 
-    widen(feat_ref, tail_ref, me_ref, wide, tokens)
+    widen(feat_ref, wide, tokens)
     for b in range(blocks):
         query = short_block(wide, taps_ref, 0, b * LANES, LANES)
         key = short_block(wide, taps_ref, 1, b * LANES, LANES)
@@ -138,8 +139,14 @@
         short_ref[0, b * LANES : (b + 1) * LANES, :] = query
         short_ref[1, b * LANES : (b + 1) * LANES, :] = key
         short_ref[2, b * LANES : (b + 1) * LANES, :] = value
-        z_t = jnp.transpose((key * value).astype(bf16))
-        e_t = jnp.transpose(cot_ref[b * LANES : (b + 1) * LANES, :].astype(f32) * query)
+        product = key * value
+        adjoint = cot_ref[b * LANES : (b + 1) * LANES, :].astype(f32) * query
+        if b == 0:
+            inside = iota(0, (LANES, LANES)) >= 2
+            product = jnp.where(inside, product, 0.0)
+            adjoint = jnp.where(inside, adjoint, 0.0)
+        z_t = jnp.transpose(product.astype(bf16))
+        e_t = jnp.transpose(adjoint)
         e_high, e_low = split(e_t)
         at = slice(b * MEMBERS, (b + 1) * MEMBERS)
         for g in range(TILE_GROUPS):
@@ -191,6 +198,33 @@
     state_ref[16:32] = turned[48:64]
     state_ref[32:48] = turned[64:80]
     state_ref[48:64] = turned[96:112]
+
+    tile = pl.program_id(0)
+    half = later_ref.shape[1] // 2
+    here = pl.ds(pl.multiple_of(tile * LANES, LANES), LANES)
+    edges = jnp.concatenate(
+        [wide[i, 8:10, :] for i in range(3)]
+        + [cot_ref[0:2, :].astype(f32)]
+        + [wide[i, 6 + tokens : 8 + tokens, :] for i in range(3)]
+        + [jnp.zeros((2, LANES), f32)],
+        axis=0,
+    )
+    for out_ref, main in ((later_ref, turned[0:16]), (earlier_ref, turned[64:80])):
+        out_ref[0:16, here] = main
+        out_ref[24:40, here] = edges
+
+    def place(out_ref, lag_rows, start):
+        for part in range(2):
+            at = pl.ds(pl.multiple_of(start + part * half, LANES), LANES)
+            out_ref[16:24, at] = lag_rows[8 * part : 8 * part + 8]
+
+    @pl.when(tile * LANES < half)
+    def _():
+        place(later_ref, turned[48:64], tile * LANES)
+
+    @pl.when(tile * LANES >= half)
+    def _():
+        place(earlier_ref, turned[96:112], tile * LANES - half)
 
 
 def inside_kernel(
@@ -247,44 +281,117 @@
     )
 
 
-def join_kernel(tokens, me_ref, state_ref, diag_ref, cross_ref, rate_ref, gain_ref, *refs):
-    gots, (bound_ref, local_ref) = refs[:-2], refs[-2:]
+def join_kernel(
+    tokens, me_ref, state_ref, own_ref, diag_ref, cross_ref, taps_ref, rate_ref, gain_ref, *refs
+):
+    gots, (bound_ref, local_ref, edges_all) = refs[:-3], refs[-3:]
     me = me_ref[0]
     channels = state_ref.shape[1]
     groups = rate_ref.shape[1]
+    half = channels // 2
     chosen = (iota(0, (groups, channels)) == iota(1, (groups, channels)) // MEMBERS).astype(f32)
     rates = rate_ref[...]
     rate_cols = exact_dot(rates, chosen, ((1,), (0,)))
+    edges_all[me] = own_ref[24:40]
+    for key, got in enumerate(gots, 1):
+        edges_all[me ^ key] = got[24:40]
+
+    def tail_of(device):
+        return jnp.where(device > 0, edges_all[jnp.maximum(device - 1, 0)][8:14], 0.0)
+
+    def first_tokens(device):
+        head, tail = edges_all[device], tail_of(device)
+        shorts = []
+        for i in range(3):
+            tap = [taps_ref[i, j : j + 1, :] for j in range(3)]
+            now, last = head[2 * i : 2 * i + 2], tail[2 * i : 2 * i + 2]
+            shorts.append(
+                (
+                    tap[0] * now[0:1] + tap[1] * last[1:2] + tap[2] * last[0:1],
+                    tap[0] * now[1:2] + tap[1] * now[0:1] + tap[2] * last[1:2],
+                )
+            )
+        z = [(shorts[1][t] * shorts[2][t]).astype(bf16).astype(f32) for t in range(2)]
+        e = [head[6 + t : 7 + t] * shorts[0][t] for t in range(2)]
+        return z, e
+
+    decay = jnp.exp(-rate_cols)
+    decay_2 = decay * decay
+    grow = jnp.exp(rate_cols)
+    to_end = [jnp.exp(-rate_cols * float(tokens - 1)), jnp.exp(-rate_cols * float(tokens - 2))]
+    from_start = [decay, decay_2]
     zero = jnp.zeros((MODES, channels), f32)
-    s_prev, l_prev, e_next = zero, zero, zero
+    zero_half = jnp.zeros((MODES, half), f32)
+    s_prev, e_next = zero, zero
+    s_lag, e_lag = zero_half, zero_half
     ahead = jnp.zeros((8, channels), f32)
     for key, got in enumerate(gots, 1):
         other = me ^ key
         earlier = other < me
+        z, e = first_tokens(other)
+        add = [
+            jnp.where(earlier, to_end[t] * z[t], from_start[t] * e[t]) for t in range(2)
+        ]
+        steps = [
+            jnp.where(earlier, tokens - 1 - t, t + 1).astype(f32) for t in range(2)
+        ]
+        added = steps[0] * add[0] + steps[1] * add[1]
         away = ((jnp.abs(me - other) - 1) * tokens).astype(f32)
         weight = jnp.exp(-rate_cols * away)
-        part = weight * got[0:16]
+        part = weight * (got[0:16] + add[0] + add[1])
+
+        def halved(value):
+            return jnp.where(earlier, value[:, :half], value[:, half:])
+
+        lagged = jnp.concatenate([got[16:24, :half], got[16:24, half:]], axis=0) + halved(added)
+        lag_part = halved(weight) * lagged + away * halved(part)
         s_prev = s_prev + jnp.where(earlier, part, 0.0)
-        l_prev = l_prev + jnp.where(earlier, weight * got[16:32] + away * part, 0.0)
+        s_lag = s_lag + jnp.where(earlier, lag_part, 0.0)
         e_next = e_next + jnp.where(earlier, 0.0, part)
-        ahead = ahead + jnp.where(other == me + 1, got[32:40], 0.0)
-    bound_ref[0:16] = s_prev
+        e_lag = e_lag + jnp.where(earlier, 0.0, lag_part)
+        ahead = ahead + jnp.where(other == me + 1, got[24:32], 0.0)
+    z, e = first_tokens(me)
+    ends, lagged, moment_0, moment_1 = [state_ref[16 * i : 16 * i + 16] for i in range(4)]
+    at_end = [to_end[t] * z[t] for t in range(2)]
+    at_start = [from_start[t] * e[t] for t in range(2)]
+    own_s = ends + at_end[0] + at_end[1]
+    own_l = lagged + float(tokens - 1) * at_end[0] + float(tokens - 2) * at_end[1]
+    own_m = moment_0 + at_start[0] + at_start[1]
+    own_n = moment_1 + at_start[0] + 2.0 * at_start[1]
+    early_0, early_1 = grow * z[0], grow * grow * z[1]
+    early = early_0 + early_1
+    bound_ref[0:16] = s_prev + early
     bound_ref[16:32] = e_next
-    bound_ref[32:48] = state_ref[0:16] + jnp.exp(-rate_cols * float(tokens)) * s_prev
+    bound_ref[32:48] = own_s + jnp.exp(-rate_cols * float(tokens)) * s_prev
     bound_ref[48:56] = ahead
-    moment_0, moment_1 = state_ref[32:48], state_ref[48:64]
-    terms = jnp.concatenate([moment_0 * s_prev, moment_1 * s_prev + moment_0 * l_prev], axis=0)
-    sums = exact_dot(terms, chosen, ((1,), (1,)))
+    bound_ref[56:62] = tail_of(me)
+    bound_ref[62:64] = jnp.zeros((2, channels), f32)
+
+    def joined(first_half, second_half):
+        return jnp.concatenate([first_half[:, :half], second_half[:, half:]], axis=1)
+
+    back = decay * e[1] * z[0]
+    first_terms = (
+        joined(own_m * s_prev, own_s * e_next) + moment_0 * early + e[0] * z[0] + e[1] * z[1] + back
+    )
+    lag_terms = (
+        joined(own_n * s_prev, own_l * e_next)
+        + jnp.concatenate([own_m[:, :half] * s_lag, own_s[:, half:] * e_lag], axis=1)
+        + moment_1 * early
+        - moment_0 * (early_0 + 2.0 * early_1)
+        + back
+    )
+    sums = exact_dot(jnp.concatenate([first_terms, lag_terms], axis=0), chosen, ((1,), (1,)))
     own = jnp.transpose(cross_ref[...] + diag_ref[...])
     first = sums[0:16] + own[0:16]
-    lagged = -(sums[16:32] + own[32:48] + own[48:64])
+    lag_sum = -(sums[16:32] + own[32:48] + own[48:64])
     root = jnp.sqrt(2.0 * rates)
     local_ref[0:16] = root * first
-    local_ref[16:32] = gain_ref[...] * root * (0.5 * first + rates * lagged)
+    local_ref[16:32] = gain_ref[...] * root * (0.5 * first + rates * lag_sum)
 
 
 def output_kernel(
-    first, edge_ref, taps_ref, cot_ref, rate_ref, gain_ref,
+    first, start_ref, edge_ref, taps_ref, cot_ref, rate_ref, gain_ref,
     inner_whole, grad_whole, carry_whole, short_whole, bound_ref,
     *refs,
 ):
@@ -337,14 +444,43 @@
             opposite = slice((blocks - 1 - b) * MEMBERS, (blocks - b) * MEMBERS)
             inner_t[b, of, :] = inner_ref[g, at, :] + carried[at, :LANES]
             grad_t[b, of, :] = grad_ref[g, at, :] + carried[opposite, LANES:]
+    rates = jnp.transpose(member_rates)[0:MODES]
+    coefs = jnp.transpose(per_member(coef_tile))[0:MODES]
+    decay = jnp.exp(-rates)
+    grow = jnp.exp(rates)
+    state = bound_ref[32:48]
+    sum_0 = jnp.sum(coefs, axis=0, keepdims=True)
+    sum_1 = jnp.sum(coefs * decay, axis=0, keepdims=True)
+    for i in range(3):
+        wide[i, 0:8, :] = jnp.zeros((8, LANES), f32)
+        wide[i, 6:8, :] = bound_ref[56 + 2 * i : 58 + 2 * i]
+        wide[i, 8:16, :] = start_ref[i, 0:8, :].astype(f32)
+    begun = [short_block(wide, taps_ref, i, 0, 8) for i in range(3)]
+    z_own = (begun[1] * begun[2]).astype(bf16).astype(f32)
+    e_own = cot_ref[0:8, :].astype(f32) * begun[0]
+    sum_up = jnp.sum(coefs * grow, axis=0, keepdims=True)
+    which = iota(0, (8, LANES))
+    inner_fix = jnp.where(which == 0, -sum_up * z_own[1:2], 0.0)
+    grad_fix = jnp.where(
+        which == 0,
+        sum_0 * e_own[0:1] + sum_1 * e_own[1:2],
+        jnp.where(which == 1, sum_0 * e_own[1:2], 0.0),
+    )
     for b in range(blocks):
         at = slice(b * LANES, (b + 1) * LANES)
         inner = jnp.transpose(inner_t[b])
         grad = jnp.transpose(grad_t[b])
-        mixer_ref[at, :] = (short_ref[0, at, :] * inner).astype(bf16)
+        query, key, value = [short_ref[i, at, :] for i in range(3)]
+        if b == 0:
+            query, key, value = [
+                jnp.concatenate([begun[i], short_ref[i, 8:LANES, :]], axis=0) for i in range(3)
+            ]
+            inner = jnp.concatenate([inner[0:8] + inner_fix, inner[8:]], axis=0)
+            grad = jnp.concatenate([grad[0:8] + grad_fix, grad[8:]], axis=0)
+        mixer_ref[at, :] = (query * inner).astype(bf16)
         adj[0, at, :] = cot_ref[at, :].astype(f32) * inner
-        adj[1, at, :] = grad * short_ref[2, at, :]
-        adj[2, at, :] = grad * short_ref[1, at, :]
+        adj[1, at, :] = grad * value
+        adj[2, at, :] = grad * key
     for i in range(3):
         wide[i, 0:8, :] = edge_ref[i, 8:16, :].astype(f32)
         wide[i, 8:16, :] = jnp.zeros((8, LANES), f32)
@@ -353,13 +489,6 @@
     z = (key * value).astype(bf16).astype(f32)
     upstream = jnp.concatenate([bound_ref[54:56], jnp.zeros((6, LANES), f32)], axis=0)
     e = upstream * query
-    rates = jnp.transpose(member_rates)[0:MODES]
-    coefs = jnp.transpose(per_member(coef_tile))[0:MODES]
-    decay = jnp.exp(-rates)
-    grow = jnp.exp(rates)
-    state = bound_ref[32:48]
-    sum_0 = jnp.sum(coefs, axis=0, keepdims=True)
-    sum_1 = jnp.sum(coefs * decay, axis=0, keepdims=True)
     inner_0 = jnp.sum(coefs * decay * state, axis=0, keepdims=True) + sum_0 * z[0:1]
     inner_1 = (
         jnp.sum(coefs * decay * decay * state, axis=0, keepdims=True)
@@ -368,7 +497,6 @@
     )
     grad_0 = jnp.sum(coefs * grow * after, axis=0, keepdims=True)
     grad_1 = jnp.sum(coefs * grow * (grow * after - e[0:1]), axis=0, keepdims=True)
-    which = iota(0, (8, LANES))
     inner_8 = jnp.where(which == 0, inner_0, jnp.where(which == 1, inner_1, 0.0))
     grad_8 = jnp.where(which == 0, grad_0, jnp.where(which == 1, grad_1, 0.0))
     adj[0, tokens : tokens + 8, :] = upstream * inner_8
@@ -408,11 +536,6 @@
     return [pltpu.with_memory_space_constraint(array, pltpu.VMEM) for array in arrays]
 
 
-def shifted(value, axis, steps):
-    count = lax.axis_size(axis)
-    return lax.ppermute(value, axis, [(i, (i + steps) % count) for i in range(count)])
-
-
 def swapped(value, axis, key):
     count = lax.axis_size(axis)
     return lax.ppermute(value, axis, [(i, i ^ key) for i in range(count)])
@@ -427,15 +550,11 @@
     ctx_count = lax.axis_size("ctx")
     ctx_index = lax.axis_index("ctx")
 
-    tail = shifted(features[:, tokens - 2 :, :], "ctx", 1)
-    head = jnp.concatenate([features[:, :2, :], cotangent[None, :2, :]], axis=0)
-    head = head.astype(f32).reshape(8, channels)
     me = ctx_index.astype(jnp.int32).reshape(1)
     rates, gains = decay_rates.T, mode_gains.T
 
     whole = pl.BlockSpec(memory_space=pltpu.VMEM)
     feat_spec = pl.BlockSpec((3, tokens, LANES), lambda j: (0, 0, j))
-    tail_spec = pl.BlockSpec((3, 2, LANES), lambda j: (0, 0, j))
     taps_spec = pl.BlockSpec((3, 3, LANES), lambda j: (0, 0, j))
     cot_spec = pl.BlockSpec((tokens, LANES), lambda j: (0, j))
     table_spec = pl.BlockSpec((MODES, groups), lambda j: (0, 0))
@@ -450,10 +569,10 @@
     def room(mebibytes):
         return pltpu.CompilerParams(vmem_limit_bytes=mebibytes * 2**20)
 
-    z, eh, el, carry, short, states, cross = pl.pallas_call(
+    z, eh, el, carry, short, states, cross, later, early = pl.pallas_call(
         state_kernel,
         grid=(tiles,),
-        in_specs=[me_spec, feat_spec, tail_spec, taps_spec, cot_spec, table_spec, table_spec],
+        in_specs=[feat_spec, taps_spec, cot_spec, table_spec, table_spec],
         out_specs=[
             whole,
             whole,
@@ -462,6 +581,8 @@
             whole,
             pl.BlockSpec((4 * MODES, LANES), lambda j: (0, j)),
             slot_spec,
+            whole,
+            whole,
         ],
         out_shape=[
             turned,
@@ -471,6 +592,8 @@
             resident((tiles, 3, tokens, LANES), f32),
             jax.ShapeDtypeStruct((4 * MODES, channels), f32),
             slots,
+            resident((40, channels), f32),
+            resident((40, channels), f32),
         ],
         scratch_shapes=[
             pltpu.VMEM((3, tokens + 8, LANES), f32),
@@ -480,13 +603,12 @@
         + table_scratch,
         compiler_params=room(14),
         name="state_part",
-    )(me, *far(features, tail, short_taps, cotangent, rates, gains))
+    )(*far(features, short_taps, cotangent, rates, gains))
 
     gots = []
     for key in range(1, ctx_count):
-        earlier = (ctx_index ^ key) < ctx_index
-        sent = jnp.where(earlier, states[32:64], states[0:32])
-        gots.append(swapped(jnp.concatenate([sent, head], axis=0), "ctx", key))
+        sent = jnp.where((ctx_index ^ key) < ctx_index, early, later)
+        gots.append(swapped(sent, "ctx", key))
 
     inner, grad, diag = pl.pallas_call(
         inside_kernel,
@@ -509,15 +631,16 @@
 
     bound, local = pl.pallas_call(
         functools.partial(join_kernel, tokens),
-        in_specs=[me_spec] + [whole] * (5 + len(gots)),
+        in_specs=[me_spec] + [whole] * (7 + len(gots)),
         out_specs=[whole, whole],
         out_shape=[
-            jax.ShapeDtypeStruct((56, channels), f32),
+            jax.ShapeDtypeStruct((64, channels), f32),
             jax.ShapeDtypeStruct((2 * MODES, groups), f32),
         ],
+        scratch_shapes=[pltpu.VMEM((ctx_count, 16, channels), f32)],
         compiler_params=room(14),
         name="join_part",
-    )(me, states, diag, cross, rates, gains, *gots)
+    )(me, states, later, diag, cross, short_taps, rates, gains, *gots)
 
     def outputs(first, count, *written):
         columns = lambda j: (0, j + first)
@@ -527,6 +650,7 @@
             functools.partial(output_kernel, first),
             grid=(count,),
             in_specs=[
+                pl.BlockSpec((3, 16, LANES), layers),
                 pl.BlockSpec((3, 16, LANES), lambda j: (0, tokens // 16 - 1, j + first)),
                 pl.BlockSpec((3, 3, LANES), layers),
                 pl.BlockSpec((tokens, LANES), columns),
@@ -536,7 +660,7 @@
                 whole,
                 whole,
                 whole,
-                pl.BlockSpec((56, LANES), columns),
+                pl.BlockSpec((64, LANES), columns),
             ]
             + [pl.BlockSpec(memory_space=pl.ANY)] * len(written),
             out_specs=mine,
@@ -553,7 +677,7 @@
             ]
             + table_scratch,
             compiler_params=room(14),
-            input_output_aliases={10: 0, 11: 1} if written else {},
+            input_output_aliases={11: 0, 12: 1} if written else {},
             cost_estimate=pl.CostEstimate(
                 flops=2 * count * TILE_GROUPS * rows * LANES * LANES * 8,
                 bytes_accessed=count * 4 * 2**20,
@@ -561,7 +685,7 @@
             ),
             name="output_part",
         )(
-            *far(features, short_taps, cotangent, rates, gains),
+            *far(features, features, short_taps, cotangent, rates, gains),
             *near(inner, grad, carry, short),
             bound,
             *written,

time: 60.4 us -> 55.9 us (0.925)
  local copies, waits for them, and re-layouts: 2.81 us -> 0.62 us
  starting transfers between devices: 15.8 us -> 14.3 us
  waiting for transfers between devices: 4.05 us -> 3.15 us
    ppermute x1 -> x0, starting transfers between devices: 3.08 us -> none  [shifted(): lax.ppermute(value, axis, [(i, (i + steps) % count) for i in range(count)])]
    ppermute x1 -> x0, waiting for transfers between devices: 2.91 us -> none  [shifted(): lax.ppermute(value, axis, [(i, (i + steps) % count) for i in range(count)])]
    ppermute x10, waiting for transfers between devices: 1.14 us -> 3.15 us  [swapped(): return lax.ppermute(value, axis, [(i, i ^ key) for i in range(count)])]
    ppermute x10, starting transfers between devices: 12.7 us -> 14.3 us  [swapped(): return lax.ppermute(value, axis, [(i, i ^ key) for i in range(count)])]
    slice x1 -> x0, local copies, waits for them, and re-layouts: 0.85 us -> none  [per_device(): head = jnp.concatenate([features[:, :2, :], cotangent[None, :2, :]], axis=0)]
    broadcast_in_dim x1 -> x0, local copies, waits for them, and re-layouts: 0.72 us -> none  [per_device(): head = jnp.concatenate([features[:, :2, :], cotangent[None, :2, :]], axis=0)]
  transfers between devices with their start and end apart: 11 -> 10, of which waited for: 2 -> 2; matrix products, arithmetic and copies ran while one was open for 1% -> 0% of each run, Pallas kernels for 39% -> 42%
where the time goes in v6:
time: 55.9 us; the launch traced here: 55.6 us
  Pallas kernels  36.6 us (65%)
  starting transfers between devices  14.3 us (26%)
  waiting for transfers between devices  3.15 us (6%)
  between operations  0.77 us (1%)
  local copies, waits for them, and re-layouts  0.62 us (1%)
    ppermute x10, starting transfers between devices, swapped(): return lax.ppermute(value, axis, [(i, i ^ key) for i in range(count)])  14.3 us
    pallas_call x2, Pallas kernels, outputs(): pl.pallas_call(functools.partial(output_kernel, first), grid=(count,), in...  13 us
    pallas_call x1, Pallas kernels, per_device(): pl.pallas_call(state_kernel, grid=(tiles,), in_specs=[feat_spec, taps_spe...  12.4 us
    pallas_call x1, Pallas kernels, per_device(): pl.pallas_call(inside_kernel, grid=(tiles,), in_specs=[whole, whole, whol...  10.4 us
    ppermute x10, waiting for transfers between devices, swapped(): return lax.ppermute(value, axis, [(i, i ^ key) for i in range(count)])  3.15 us
  transfers between devices with their start and end apart: 10, of which 2 were waited for; matrix products, arithmetic and copies ran while one was open for 0% of the time, Pallas kernels for 42%

profile of v6, /device:TPU:0, one launch (start us, length us, event | category | flops | bytes accessed | tf_op | source)
XLA Modules:
  0.0 55.6 jit_solution(3643355245975412198)
XLA Ops:
  0.6 12.4 %state_part.1 = (bf16[64,128,128]{2,1,0:T(8,128)(2,1)S(1)}, bf16[64,128,128]{2,1,0:T(8,128)(2,1)S(1)}, bf16[64,128,128]{2,1,0:T(8,128)(2,1)S(1)}, f32[8,8,128,12...) custom-call(bf16[3,1024,1024]{2,1,0:T(8,128)(2,1)} %edge_ref.3, ...), custom_call_target="tpu_custom_call" | custom-call | tf_op jit(solution)/shard_map/state_part/pallas_call | solution.py:572
  13.0 0.0 copy-start
  13.1 0.0 copy-start.1
  13.1 0.0 copy-start.2
  13.1 0.1 broadcast_select_fusion
  13.1 3.1 %collective-permute-start = (f32[40,1024]{1,0:T(8,128)S(1)}, f32[40,1024]{1,0:T(8,128)S(1)}, u32[]{:S(2)}, u32[]{:S(2)}) collective-permute-start(f32[40,1024]{1,0:T(8,128)S(1)} %get-tuple-element.64), channel_id=1, source_target_pairs={{0,1},{1,0},{2,3},{3,2},{4,5},{5,4},{6,7},{7,6},{8,9},{9,8},{10,11... | collective-permute-start | bytes 491528 | tf_op jit(solution)/shard_map/ppermute | solution.py:541
  16.2 2.6 %collective-permute-start.1 = (f32[40,1024]{1,0:T(8,128)S(1)}, f32[40,1024]{1,0:T(8,128)S(1)}, u32[]{:S(2)}, u32[]{:S(2)}) collective-permute-start(f32[40,1024]{1,0:T(8,128)S(1)} %get-tuple-element.63), channel_id=1, source_target_pairs={{0,2},{1,3},{2,0},{3,1},{4,6},{5,7},{6,4},{7,5},{8,10},{9,11},{10,... | collective-permute-start | bytes 491528 | tf_op jit(solution)/shard_map/ppermute | solution.py:541
  18.8 0.0 collective-permute-start.2
  18.8 10.4 %inside_part.1 = (f32[64,128,128]{2,1,0:T(8,128)S(1)}, f32[64,128,128]{2,1,0:T(8,128)S(1)}, f32[64,128]{1,0:T(8,128)S(1)}) custom-call(bf16[64,128,128]{2,1,0:T(8,128)(2,1)S(1)} %get-tuple-element.33.z_whole, bf16[64,128,128]{2,1,0:T(8,128)(2,1)S(1)} %get-tuple-element.34.eh_whole, bf16[64,128,128]{2,1,0:T(8,128)(2,1)S(1)} %get-tuple-element.35.el_whole, ...), custom_call_target="tpu_custom_call" | custom-call | flops 1879048192 | bytes 14680064 | tf_op jit(solution)/shard_map/inside_part/pallas_call | solution.py:613
  29.3 0.0 collective-permute-done.refs_0_
  29.3 2.0 %collective-permute-done.1.refs_1_ = f32[40,1024]{1,0:T(8,128)S(1)} collective-permute-done((f32[40,1024]{1,0:T(8,128)S(1)}, f32[40,1024]{1,0:T(8,128)S(1)}, u32[]{:S(2)}, u32[]{:S(2)}) %collective-permute-start.1) | collective-permute-done | bytes 163872 | tf_op jit(solution)/shard_map/ppermute | solution.py:541
  31.3 0.0 collective-permute-done.2.refs_2_
  31.3 0.0 copy-done.1
  31.3 0.7 %join_part.1 = (f32[64,1024]{1,0:T(8,128)S(1)}, f32[32,64]{1,0:T(8,128)S(1)}) custom-call(s32[1]{0:T(128)} %bitcast.2.me_ref, f32[64,1024]{1,0:T(8,128)S(1)} %get-tuple-element.40.state_ref, f32[40,1024]{1,0:T(8,128)S(1)} %get-tuple-element.41.own_ref, f32[64,128]{1,0:T(8,128)S(1)} %get-tuple-element.42.diag_ref, f32[64,128]{1,0:T(8,128)S(1)} %get-tuple-element.43.cross_ref, ...), custom_call_target="tpu_custom_call" | custom-call | tf_op jit(solution)/shard_map/join_part/pallas_call | solution.py:632
  32.0 2.7 %collective-permute-start.3 = (f32[32,64]{1,0:T(8,128)S(1)}, f32[32,64]{1,0:T(8,128)S(1)}, u32[]{:S(2)}, u32[]{:S(2)}) collective-permute-start(f32[32,64]{1,0:T(8,128)S(1)} %get-tuple-element.49.refs_0_), channel_id=1, source_target_pairs={{0,1},{1,0},{2,3},{3,2},{4,5},{5,4},{6,7},{7,6},{8,9},{9,8},{10,11... | collective-permute-start | bytes 24584 | tf_op jit(solution)/shard_map/ppermute | solution.py:541
  34.7 1.1 %collective-permute-start.4 = (f32[32,64]{1,0:T(8,128)S(1)}, f32[32,64]{1,0:T(8,128)S(1)}, u32[]{:S(2)}, u32[]{:S(2)}) collective-permute-start(f32[32,64]{1,0:T(8,128)S(1)} %get-tuple-element.49.refs_0_), channel_id=1, source_target_pairs={{0,2},{1,3},{2,0},{3,1},{4,6},{5,7},{6,4},{7,5},{8,10},{9,11},{10,... | collective-permute-start | bytes 24584 | tf_op jit(solution)/shard_map/ppermute | solution.py:541
  35.8 1.4 %collective-permute-start.5 = (f32[32,64]{1,0:T(8,128)S(1)}, f32[32,64]{1,0:T(8,128)S(1)}, u32[]{:S(2)}, u32[]{:S(2)}) collective-permute-start(f32[32,64]{1,0:T(8,128)S(1)} %get-tuple-element.49.refs_0_), channel_id=1, source_target_pairs={{0,3},{1,2},{2,1},{3,0},{4,7},{5,6},{6,5},{7,4},{8,11},{9,10},{10,... | collective-permute-start | bytes 24584 | tf_op jit(solution)/shard_map/ppermute | solution.py:541
  37.2 6.5 %output_part.2 = (bf16[1024,1024]{1,0:T(8,128)(2,1)}, bf16[3,1024,1024]{2,1,0:T(8,128)(2,1)}) custom-call(bf16[3,1024,1024]{2,1,0:T(8,128)(2,1)} %edge_ref.3, bf16[3,1024,1024]{2,1,0:T(8,128)(2,1)} %edge_ref.3, f32[3,3,1024]{2,1,0:T(4,128)} %taps_ref.7, bf16[1024,1024]{1,0:T(8,128)(2,1)} %cot_ref.5, f32[16,64]{1,0:T(8,128)} %bitcast.11, f32[16,64]{1,0:T(8,128)} %bitcast.16, ...), custom_call_target="tpu_custom_call" | custom-call | flops 1073741824 | bytes 16777216 | tf_op jit(solution)/shard_map/output_part/pallas_call | solution.py:649
  43.7 0.0 collective-permute-done.3.refs_1_
  43.7 0.0 collective-permute-done.4.refs_2_
  43.7 0.0 collective-permute-done.5.refs_3_
  43.7 0.1 sum_part.1
  43.8 0.0 collective-permute-start.6
  43.8 1.1 %collective-permute-done.6 = f32[1,64]{1,0:T(1,128)S(1)} collective-permute-done((f32[1,64]{1,0:T(1,128)S(1)}, f32[1,64]{1,0:T(1,128)S(1)}, u32[]{:S(2)}, u32[]{:S(2)}) %collective-permute-start.6) | collective-permute-done | bytes 288 | tf_op jit(solution)/shard_map/ppermute | solution.py:541
  44.9 1.5 %collective-permute-start.7 = (f32[1,64]{1,0:T(1,128)S(1)}, f32[1,64]{1,0:T(1,128)S(1)}, u32[]{:S(2)}, u32[]{:S(2)}) collective-permute-start(f32[1,64]{1,0:T(1,128)S(1)} %add.18), channel_id=1, source_target_pairs={{0,8},{4,12},{8,0},{12,4},{16,24},{20,28},{24,16},{28,20},{1,9},{5... | collective-permute-start | bytes 776 | tf_op jit(solution)/shard_map/ppermute | solution.py:541
  46.4 1.5 %collective-permute-start.8 = (f32[1,64]{1,0:T(1,128)S(1)}, f32[1,64]{1,0:T(1,128)S(1)}, u32[]{:S(2)}, u32[]{:S(2)}) collective-permute-start(f32[1,64]{1,0:T(1,128)S(1)} %add.18), channel_id=1, source_target_pairs={{0,16},{4,20},{8,24},{12,28},{16,0},{20,4},{24,8},{28,12},{1,17},{... | collective-permute-start | bytes 776 | tf_op jit(solution)/shard_map/ppermute | solution.py:541
  48.0 0.5 collective-permute-start.9
  48.4 6.5 %output_part.3 = (bf16[1024,1024]{1,0:T(8,128)(2,1)}, bf16[3,1024,1024]{2,1,0:T(8,128)(2,1)}) custom-call(bf16[3,1024,1024]{2,1,0:T(8,128)(2,1)} %edge_ref.3, bf16[3,1024,1024]{2,1,0:T(8,128)(2,1)} %edge_ref.3, f32[3,3,1024]{2,1,0:T(4,128)} %taps_ref.7, bf16[1024,1024]{1,0:T(8,128)(2,1)} %cot_ref.5, ...), custom_call_target="tpu_custom_call", output_to_operand_aliasing={{0}: (11, {}), {1}: (12, {})} | custom-call | flops 1073741824 | bytes 16777216 | tf_op jit(solution)/shard_map/output_part/pallas_call | solution.py:649
  54.9 0.0 collective-permute-done.7
  54.9 0.0 collective-permute-done.8
  55.0 0.0 collective-permute-done.9
  55.0 0.6 %slice_bitcast_fusion = (f32[64,16]{0,1:T(8,128)}, f32[64,16]{0,1:T(8,128)}) fusion(f32[32,64]{1,0:T(8,128)S(1)} %broadcast_multiply_fusion), kind=kLoop, calls=%fused_computation.3 | loop fusion | bytes 16384 | tf_op jit(solution)/shard_map/transpose | solution.py:721
  (5 shorter events, 0.0 us)
Async XLA Ops:
  13.0 18.2 %copy-start = (f32[3,3,1024]{2,1,0:T(4,128)S(1)}, f32[3,3,1024]{2,1,0:T(4,128)}, u32[]{:S(2)}) copy-start(f32[3,3,1024]{2,1,0:T(4,128)} %taps_ref.7) | copy-start | bytes 110596
  13.1 18.2 %copy-start.1 = (f32[64,16]{0,1:T(8,128)S(1)}, f32[64,16]{0,1:T(8,128)}, u32[]{:S(2)}) copy-start(f32[64,16]{0,1:T(8,128)} %param.7) | copy-start | bytes 12292
  13.1 18.2 %copy-start.2 = (f32[64,16]{0,1:T(8,128)S(1)}, f32[64,16]{0,1:T(8,128)}, u32[]{:S(2)}) copy-start(f32[64,16]{0,1:T(8,128)} %param.8) | copy-start | bytes 12292
  13.1 16.1 %collective-permute-start = (f32[40,1024]{1,0:T(8,128)S(1)}, f32[40,1024]{1,0:T(8,128)S(1)}, u32[]{:S(2)}, u32[]{:S(2)}) collective-permute-start(f32[40,1024]{1,0:T(8,128)S(1)} %get-tuple-element.64), channel_id=1, source_target_pairs={{0,1},{1,0},{2,3},{3,2},{4,5},{5,4},{6,7},{7,6},{8,9},{9,8},{10,11... | collective-permute-start | bytes 491528 | tf_op jit(solution)/shard_map/ppermute | solution.py:541
  16.2 15.1 %collective-permute-start.1 = (f32[40,1024]{1,0:T(8,128)S(1)}, f32[40,1024]{1,0:T(8,128)S(1)}, u32[]{:S(2)}, u32[]{:S(2)}) collective-permute-start(f32[40,1024]{1,0:T(8,128)S(1)} %get-tuple-element.63), channel_id=1, source_target_pairs={{0,2},{1,3},{2,0},{3,1},{4,6},{5,7},{6,4},{7,5},{8,10},{9,11},{10,... | collective-permute-start | bytes 491528 | tf_op jit(solution)/shard_map/ppermute | solution.py:541
  18.8 12.5 %collective-permute-start.2 = (f32[40,1024]{1,0:T(8,128)S(1)}, f32[40,1024]{1,0:T(8,128)S(1)}, u32[]{:S(2)}, u32[]{:S(2)}) collective-permute-start(f32[40,1024]{1,0:T(8,128)S(1)} %get-tuple-element.62), channel_id=1, source_target_pairs={{0,3},{1,2},{2,1},{3,0},{4,7},{5,6},{6,5},{7,4},{8,11},{9,10},{10,... | collective-permute-start | bytes 491528 | tf_op jit(solution)/shard_map/ppermute | solution.py:541
  32.0 11.7 %collective-permute-start.3 = (f32[32,64]{1,0:T(8,128)S(1)}, f32[32,64]{1,0:T(8,128)S(1)}, u32[]{:S(2)}, u32[]{:S(2)}) collective-permute-start(f32[32,64]{1,0:T(8,128)S(1)} %get-tuple-element.49.refs_0_), channel_id=1, source_target_pairs={{0,1},{1,0},{2,3},{3,2},{4,5},{5,4},{6,7},{7,6},{8,9},{9,8},{10,11... | collective-permute-start | bytes 24584 | tf_op jit(solution)/shard_map/ppermute | solution.py:541
  34.7 9.0 %collective-permute-start.4 = (f32[32,64]{1,0:T(8,128)S(1)}, f32[32,64]{1,0:T(8,128)S(1)}, u32[]{:S(2)}, u32[]{:S(2)}) collective-permute-start(f32[32,64]{1,0:T(8,128)S(1)} %get-tuple-element.49.refs_0_), channel_id=1, source_target_pairs={{0,2},{1,3},{2,0},{3,1},{4,6},{5,7},{6,4},{7,5},{8,10},{9,11},{10,... | collective-permute-start | bytes 24584 | tf_op jit(solution)/shard_map/ppermute | solution.py:541
  35.8 7.9 %collective-permute-start.5 = (f32[32,64]{1,0:T(8,128)S(1)}, f32[32,64]{1,0:T(8,128)S(1)}, u32[]{:S(2)}, u32[]{:S(2)}) collective-permute-start(f32[32,64]{1,0:T(8,128)S(1)} %get-tuple-element.49.refs_0_), channel_id=1, source_target_pairs={{0,3},{1,2},{2,1},{3,0},{4,7},{5,6},{6,5},{7,4},{8,11},{9,10},{10,... | collective-permute-start | bytes 24584 | tf_op jit(solution)/shard_map/ppermute | solution.py:541
  43.8 1.1 %collective-permute-start.6 = (f32[1,64]{1,0:T(1,128)S(1)}, f32[1,64]{1,0:T(1,128)S(1)}, u32[]{:S(2)}, u32[]{:S(2)}) collective-permute-start(f32[1,64]{1,0:T(1,128)S(1)} %get-tuple-element.53), channel_id=1, source_target_pairs={{0,4},{4,0},{8,12},{12,8},{16,20},{20,16},{24,28},{28,24},{1,5},{5... | collective-permute-start | bytes 776 | tf_op jit(solution)/shard_map/ppermute | solution.py:541
  44.9 10.0 %collective-permute-start.7 = (f32[1,64]{1,0:T(1,128)S(1)}, f32[1,64]{1,0:T(1,128)S(1)}, u32[]{:S(2)}, u32[]{:S(2)}) collective-permute-start(f32[1,64]{1,0:T(1,128)S(1)} %add.18), channel_id=1, source_target_pairs={{0,8},{4,12},{8,0},{12,4},{16,24},{20,28},{24,16},{28,20},{1,9},{5... | collective-permute-start | bytes 776 | tf_op jit(solution)/shard_map/ppermute | solution.py:541
  46.4 8.5 %collective-permute-start.8 = (f32[1,64]{1,0:T(1,128)S(1)}, f32[1,64]{1,0:T(1,128)S(1)}, u32[]{:S(2)}, u32[]{:S(2)}) collective-permute-start(f32[1,64]{1,0:T(1,128)S(1)} %add.18), channel_id=1, source_target_pairs={{0,16},{4,20},{8,24},{12,28},{16,0},{20,4},{24,8},{28,12},{1,17},{... | collective-permute-start | bytes 776 | tf_op jit(solution)/shard_map/ppermute | solution.py:541
  48.0 7.0 %collective-permute-start.9 = (f32[1,64]{1,0:T(1,128)S(1)}, f32[1,64]{1,0:T(1,128)S(1)}, u32[]{:S(2)}, u32[]{:S(2)}) collective-permute-start(f32[1,64]{1,0:T(1,128)S(1)} %add.18), channel_id=1, source_target_pairs={{0,24},{4,28},{8,16},{12,20},{16,8},{20,12},{24,0},{28,4},{1,25},{... | collective-permute-start | bytes 776 | tf_op jit(solution)/shard_map/ppermute | solution.py:541

commit v7 on v6

--- a/solution.py
+++ b/solution.py
@@ -243,6 +243,19 @@
     power_all[...] = power
     taps = jnp.sum((coefs * power).reshape(TILE_GROUPS, MODES, LANES), axis=1)
     for g in range(TILE_GROUPS):
+        z_back = jnp.transpose(z_ref[g])
+        gram = dot_nn(
+            jnp.concatenate([z_back, z_back], axis=1),
+            jnp.concatenate([eh_ref[g], el_ref[g]], axis=0),
+        )
+        gram = jnp.where(lane_at >= row_at, gram, 0.0)
+        folded = [gram[0:8]] + [
+            pltpu.roll(gram[8 * r : 8 * r + 8], LANES - 8 * r, 1) for r in range(1, LANES // 8)
+        ]
+        while len(folded) > 1:
+            folded = [folded[i] + folded[i + 1] for i in range(0, len(folded), 2)]
+        fold_all[8 * g : 8 * g + 8, :] = folded[0]
+    for g in range(TILE_GROUPS):
         high, low = split(jnp.where(lane_at >= row_at, circulant(taps[g : g + 1]), 0.0))
         toep_all[g, 0:LANES, :] = high
         toep_all[g, LANES:, :] = low
@@ -254,16 +267,6 @@
             jnp.concatenate([eh, el, eh], axis=1),
             jnp.concatenate([high, high, toep_all[g, LANES:, :]], axis=1),
         )
-        z_back = jnp.transpose(z)
-        gram = dot_nn(jnp.concatenate([z_back, z_back], axis=1), jnp.concatenate([eh, el], axis=0))
-        gram = jnp.where(lane_at >= row_at, gram, 0.0)
-        folded = [gram[0:8]] + [
-            pltpu.roll(gram[8 * r : 8 * r + 8], LANES - 8 * r, 1) for r in range(1, LANES // 8)
-        ]
-        while len(folded) > 1:
-            folded = [folded[i] + folded[i + 1] for i in range(0, len(folded), 2)]
-        fold_all[8 * g : 8 * g + 8, :] = folded[0]
-
     corr = jnp.sum(sheared(fold_all[...], 8).reshape(TILE_GROUPS, 8, LANES), axis=1)
     weighted = power_all[...] * per_member(corr)
     first_col = jnp.sum(weighted, axis=1, keepdims=True)
@@ -608,7 +611,7 @@
     gots = []
     for key in range(1, ctx_count):
         sent = jnp.where((ctx_index ^ key) < ctx_index, early, later)
-        gots.append(swapped(sent, "ctx", key))
+        gots.append(swapped(sent.astype(bf16), "ctx", key).astype(f32))
 
     inner, grad, diag = pl.pallas_call(
         inside_kernel,

time: 55.9 us -> 50.8 us (0.909)
  Pallas kernels: 36.6 us -> 34.1 us
  waiting for transfers between devices: 3.15 us -> 1.14 us
  starting transfers between devices: 14.3 us -> 13.6 us
    pallas_call x1, Pallas kernels: 10.4 us -> 7.88 us  [per_device(): pl.pallas_call(inside_kernel, grid=(tiles,), in_specs=[whole, whole, whol...]
    ppermute x10, waiting for transfers between devices: 3.15 us -> 1.14 us  [swapped(): return lax.ppermute(value, axis, [(i, i ^ key) for i in range(count)])]
    ppermute x10, starting transfers between devices: 14.3 us -> 13.6 us  [swapped(): return lax.ppermute(value, axis, [(i, i ^ key) for i in range(count)])]
  transfers between devices with their start and end apart: 10 -> 10, of which waited for: 2 -> 1; matrix products, arithmetic and copies ran while one was open for 0% -> 0% of each run, Pallas kernels for 42% -> 41%
where the time goes in v7:
time: 50.8 us; the launch traced here: 50.4 us
  Pallas kernels  34.1 us (67%)
  starting transfers between devices  13.6 us (27%)
  waiting for transfers between devices  1.14 us (2%)
  between operations  0.83 us (2%)
  local copies, waits for them, and re-layouts  0.62 us (1%)
    ppermute x10, starting transfers between devices, swapped(): return lax.ppermute(value, axis, [(i, i ^ key) for i in range(count)])  13.6 us
    pallas_call x2, Pallas kernels, outputs(): pl.pallas_call(functools.partial(output_kernel, first), grid=(count,), in...  13 us
    pallas_call x1, Pallas kernels, per_device(): pl.pallas_call(state_kernel, grid=(tiles,), in_specs=[feat_spec, taps_spe...  12.4 us
    pallas_call x1, Pallas kernels, per_device(): pl.pallas_call(inside_kernel, grid=(tiles,), in_specs=[whole, whole, whol...  7.88 us
    ppermute x10, waiting for transfers between devices, swapped(): return lax.ppermute(value, axis, [(i, i ^ key) for i in range(count)])  1.14 us
  transfers between devices with their start and end apart: 10, of which 1 were waited for; matrix products, arithmetic and copies ran while one was open for 0% of the time, Pallas kernels for 41%

profile of v7, /device:TPU:0, one launch (start us, length us, event | category | flops | bytes accessed | tf_op | source)
XLA Modules:
  0.0 50.4 jit_solution(8595868527571333477)
XLA Ops:
  0.6 12.4 %state_part.1 = (bf16[64,128,128]{2,1,0:T(8,128)(2,1)S(1)}, bf16[64,128,128]{2,1,0:T(8,128)(2,1)S(1)}, bf16[64,128,128]{2,1,0:T(8,128)(2,1)S(1)}, f32[8,8,128,12...) custom-call(bf16[3,1024,1024]{2,1,0:T(8,128)(2,1)} %edge_ref.3, ...), custom_call_target="tpu_custom_call" | custom-call | tf_op jit(solution)/shard_map/state_part/pallas_call | solution.py:575
  13.0 0.0 copy-start
  13.1 0.0 copy-start.1
  13.1 0.0 copy-start.2
  13.1 3.1 %collective-permute-start = (bf16[40,1024]{1,0:T(8,128)(2,1)S(1)}, bf16[40,1024]{1,0:T(8,128)(2,1)S(1)}, u32[]{:S(2)}, u32[]{:S(2)}) collective-permute-start(bf16[40,1024]{1,0:T(8,128)(2,1)S(1)} %get-tuple-element.64), channel_id=1, source_target_pairs={{0,1},{1,0},{2,3},{3,2},{4,5},{5,4},{6,7},{7,6},{8,9},{9,8},{10,11... | collective-permute-start | bytes 245768 | tf_op jit(solution)/shard_map/ppermute | solution.py:544
  16.2 2.6 %collective-permute-start.1 = (bf16[40,1024]{1,0:T(8,128)(2,1)S(1)}, bf16[40,1024]{1,0:T(8,128)(2,1)S(1)}, u32[]{:S(2)}, u32[]{:S(2)}) collective-permute-start(bf16[40,1024]{1,0:T(8,128)(2,1)S(1)} %get-tuple-element.63), channel_id=1, source_target_pairs={{0,2},{1,3},{2,0},{3,1},{4,6},{5,7},{6,4},{7,5},{8,10},{9,11},{10,... | collective-permute-start | bytes 245768 | tf_op jit(solution)/shard_map/ppermute | solution.py:544
  18.8 0.0 collective-permute-start.2
  18.8 7.9 %inside_part.1 = (f32[64,128,128]{2,1,0:T(8,128)S(1)}, f32[64,128,128]{2,1,0:T(8,128)S(1)}, f32[64,128]{1,0:T(8,128)S(1)}) custom-call(bf16[64,128,128]{2,1,0:T(8,128)(2,1)S(1)} %get-tuple-element.33.z_whole, bf16[64,128,128]{2,1,0:T(8,128)(2,1)S(1)} %get-tuple-element.34.eh_whole, bf16[64,128,128]{2,1,0:T(8,128)(2,1)S(1)} %get-tuple-element.35.el_whole, ...), custom_call_target="tpu_custom_call" | custom-call | flops 1879048192 | bytes 14680064 | tf_op jit(solution)/shard_map/inside_part/pallas_call | solution.py:616
  26.7 0.0 collective-permute-done
  26.7 0.0 collective-permute-done.1
  26.8 0.0 collective-permute-done.2
  26.8 0.0 copy-done
  26.8 0.0 copy-done.1
  26.8 0.7 %join_part.1 = (f32[64,1024]{1,0:T(8,128)S(1)}, f32[32,64]{1,0:T(8,128)S(1)}) custom-call(s32[1]{0:T(128)} %bitcast.2.me_ref, f32[64,1024]{1,0:T(8,128)S(1)} %get-tuple-element.40.state_ref, f32[40,1024]{1,0:T(8,128)S(1)} %get-tuple-element.41.own_ref, f32[64,128]{1,0:T(8,128)S(1)} %get-tuple-element.42.diag_ref, f32[64,128]{1,0:T(8,128)S(1)} %get-tuple-element.43.cross_ref, ...), custom_call_target="tpu_custom_call" | custom-call | tf_op jit(solution)/shard_map/join_part/pallas_call | solution.py:635
  27.5 1.0 %collective-permute-start.3 = (f32[32,64]{1,0:T(8,128)S(1)}, f32[32,64]{1,0:T(8,128)S(1)}, u32[]{:S(2)}, u32[]{:S(2)}) collective-permute-start(f32[32,64]{1,0:T(8,128)S(1)} %get-tuple-element.49.refs_0_), channel_id=1, source_target_pairs={{0,1},{1,0},{2,3},{3,2},{4,5},{5,4},{6,7},{7,6},{8,9},{9,8},{10,11... | collective-permute-start | bytes 24584 | tf_op jit(solution)/shard_map/ppermute | solution.py:544
  28.5 3.5 %collective-permute-start.4 = (f32[32,64]{1,0:T(8,128)S(1)}, f32[32,64]{1,0:T(8,128)S(1)}, u32[]{:S(2)}, u32[]{:S(2)}) collective-permute-start(f32[32,64]{1,0:T(8,128)S(1)} %get-tuple-element.49.refs_0_), channel_id=1, source_target_pairs={{0,2},{1,3},{2,0},{3,1},{4,6},{5,7},{6,4},{7,5},{8,10},{9,11},{10,... | collective-permute-start | bytes 24584 | tf_op jit(solution)/shard_map/ppermute | solution.py:544
  32.0 0.0 collective-permute-start.5
  32.0 6.5 %output_part.2 = (bf16[1024,1024]{1,0:T(8,128)(2,1)}, bf16[3,1024,1024]{2,1,0:T(8,128)(2,1)}) custom-call(bf16[3,1024,1024]{2,1,0:T(8,128)(2,1)} %edge_ref.3, bf16[3,1024,1024]{2,1,0:T(8,128)(2,1)} %edge_ref.3, f32[3,3,1024]{2,1,0:T(4,128)} %taps_ref.7, bf16[1024,1024]{1,0:T(8,128)(2,1)} %cot_ref.5, f32[16,64]{1,0:T(8,128)} %bitcast.11, f32[16,64]{1,0:T(8,128)} %bitcast.16, ...), custom_call_target="tpu_custom_call" | custom-call | flops 1073741824 | bytes 16777216 | tf_op jit(solution)/shard_map/output_part/pallas_call | solution.py:652
  38.5 0.0 collective-permute-done.3.refs_1_
  38.5 0.0 collective-permute-done.4.refs_2_
  38.5 0.0 collective-permute-done.5.refs_3_
  38.5 0.1 sum_part.1
  38.6 0.0 collective-permute-start.6
  38.6 1.1 %collective-permute-done.6 = f32[1,64]{1,0:T(1,128)S(1)} collective-permute-done((f32[1,64]{1,0:T(1,128)S(1)}, f32[1,64]{1,0:T(1,128)S(1)}, u32[]{:S(2)}, u32[]{:S(2)}) %collective-permute-start.6) | collective-permute-done | bytes 288 | tf_op jit(solution)/shard_map/ppermute | solution.py:544
  39.8 1.7 %collective-permute-start.7 = (f32[1,64]{1,0:T(1,128)S(1)}, f32[1,64]{1,0:T(1,128)S(1)}, u32[]{:S(2)}, u32[]{:S(2)}) collective-permute-start(f32[1,64]{1,0:T(1,128)S(1)} %add.18), channel_id=1, source_target_pairs={{0,8},{4,12},{8,0},{12,4},{16,24},{20,28},{24,16},{28,20},{1,9},{5... | collective-permute-start | bytes 776 | tf_op jit(solution)/shard_map/ppermute | solution.py:544
  41.5 1.5 %collective-permute-start.8 = (f32[1,64]{1,0:T(1,128)S(1)}, f32[1,64]{1,0:T(1,128)S(1)}, u32[]{:S(2)}, u32[]{:S(2)}) collective-permute-start(f32[1,64]{1,0:T(1,128)S(1)} %add.18), channel_id=1, source_target_pairs={{0,16},{4,20},{8,24},{12,28},{16,0},{20,4},{24,8},{28,12},{1,17},{... | collective-permute-start | bytes 776 | tf_op jit(solution)/shard_map/ppermute | solution.py:544
  43.0 0.3 collective-permute-start.9
  43.3 6.5 %output_part.3 = (bf16[1024,1024]{1,0:T(8,128)(2,1)}, bf16[3,1024,1024]{2,1,0:T(8,128)(2,1)}) custom-call(bf16[3,1024,1024]{2,1,0:T(8,128)(2,1)} %edge_ref.3, bf16[3,1024,1024]{2,1,0:T(8,128)(2,1)} %edge_ref.3, f32[3,3,1024]{2,1,0:T(4,128)} %taps_ref.7, bf16[1024,1024]{1,0:T(8,128)(2,1)} %cot_ref.5, ...), custom_call_target="tpu_custom_call", output_to_operand_aliasing={{0}: (11, {}), {1}: (12, {})} | custom-call | flops 1073741824 | bytes 16777216 | tf_op jit(solution)/shard_map/output_part/pallas_call | solution.py:652
  49.8 0.0 collective-permute-done.7
  49.8 0.0 collective-permute-done.8
  49.8 0.0 collective-permute-done.9
  49.8 0.6 %slice_bitcast_fusion = (f32[64,16]{0,1:T(8,128)}, f32[64,16]{0,1:T(8,128)}) fusion(f32[32,64]{1,0:T(8,128)S(1)} %broadcast_multiply_fusion), kind=kLoop, calls=%fused_computation.3 | loop fusion | bytes 16384 | tf_op jit(solution)/shard_map/transpose | solution.py:724
  (8 shorter events, 0.1 us)
Async XLA Ops:
  13.0 13.8 %copy-start = (f32[3,3,1024]{2,1,0:T(4,128)S(1)}, f32[3,3,1024]{2,1,0:T(4,128)}, u32[]{:S(2)}) copy-start(f32[3,3,1024]{2,1,0:T(4,128)} %taps_ref.7) | copy-start | bytes 110596
  13.1 13.8 %copy-start.1 = (f32[64,16]{0,1:T(8,128)S(1)}, f32[64,16]{0,1:T(8,128)}, u32[]{:S(2)}) copy-start(f32[64,16]{0,1:T(8,128)} %param.7) | copy-start | bytes 12292
  13.1 13.7 %copy-start.2 = (f32[64,16]{0,1:T(8,128)S(1)}, f32[64,16]{0,1:T(8,128)}, u32[]{:S(2)}) copy-start(f32[64,16]{0,1:T(8,128)} %param.8) | copy-start | bytes 12292
  13.1 13.6 %collective-permute-start = (bf16[40,1024]{1,0:T(8,128)(2,1)S(1)}, bf16[40,1024]{1,0:T(8,128)(2,1)S(1)}, u32[]{:S(2)}, u32[]{:S(2)}) collective-permute-start(bf16[40,1024]{1,0:T(8,128)(2,1)S(1)} %get-tuple-element.64), channel_id=1, source_target_pairs={{0,1},{1,0},{2,3},{3,2},{4,5},{5,4},{6,7},{7,6},{8,9},{9,8},{10,11... | collective-permute-start | bytes 245768 | tf_op jit(solution)/shard_map/ppermute | solution.py:544
  16.2 10.5 %collective-permute-start.1 = (bf16[40,1024]{1,0:T(8,128)(2,1)S(1)}, bf16[40,1024]{1,0:T(8,128)(2,1)S(1)}, u32[]{:S(2)}, u32[]{:S(2)}) collective-permute-start(bf16[40,1024]{1,0:T(8,128)(2,1)S(1)} %get-tuple-element.63), channel_id=1, source_target_pairs={{0,2},{1,3},{2,0},{3,1},{4,6},{5,7},{6,4},{7,5},{8,10},{9,11},{10,... | collective-permute-start | bytes 245768 | tf_op jit(solution)/shard_map/ppermute | solution.py:544
  18.8 8.0 %collective-permute-start.2 = (bf16[40,1024]{1,0:T(8,128)(2,1)S(1)}, bf16[40,1024]{1,0:T(8,128)(2,1)S(1)}, u32[]{:S(2)}, u32[]{:S(2)}) collective-permute-start(bf16[40,1024]{1,0:T(8,128)(2,1)S(1)} %get-tuple-element.62), channel_id=1, source_target_pairs={{0,3},{1,2},{2,1},{3,0},{4,7},{5,6},{6,5},{7,4},{8,11},{9,10},{10,... | collective-permute-start | bytes 245768 | tf_op jit(solution)/shard_map/ppermute | solution.py:544
  27.5 11.0 %collective-permute-start.3 = (f32[32,64]{1,0:T(8,128)S(1)}, f32[32,64]{1,0:T(8,128)S(1)}, u32[]{:S(2)}, u32[]{:S(2)}) collective-permute-start(f32[32,64]{1,0:T(8,128)S(1)} %get-tuple-element.49.refs_0_), channel_id=1, source_target_pairs={{0,1},{1,0},{2,3},{3,2},{4,5},{5,4},{6,7},{7,6},{8,9},{9,8},{10,11... | collective-permute-start | bytes 24584 | tf_op jit(solution)/shard_map/ppermute | solution.py:544
  28.5 10.0 %collective-permute-start.4 = (f32[32,64]{1,0:T(8,128)S(1)}, f32[32,64]{1,0:T(8,128)S(1)}, u32[]{:S(2)}, u32[]{:S(2)}) collective-permute-start(f32[32,64]{1,0:T(8,128)S(1)} %get-tuple-element.49.refs_0_), channel_id=1, source_target_pairs={{0,2},{1,3},{2,0},{3,1},{4,6},{5,7},{6,4},{7,5},{8,10},{9,11},{10,... | collective-permute-start | bytes 24584 | tf_op jit(solution)/shard_map/ppermute | solution.py:544
  32.0 6.5 %collective-permute-start.5 = (f32[32,64]{1,0:T(8,128)S(1)}, f32[32,64]{1,0:T(8,128)S(1)}, u32[]{:S(2)}, u32[]{:S(2)}) collective-permute-start(f32[32,64]{1,0:T(8,128)S(1)} %get-tuple-element.49.refs_0_), channel_id=1, source_target_pairs={{0,3},{1,2},{2,1},{3,0},{4,7},{5,6},{6,5},{7,4},{8,11},{9,10},{10,... | collective-permute-start | bytes 24584 | tf_op jit(solution)/shard_map/ppermute | solution.py:544
  38.6 1.1 %collective-permute-start.6 = (f32[1,64]{1,0:T(1,128)S(1)}, f32[1,64]{1,0:T(1,128)S(1)}, u32[]{:S(2)}, u32[]{:S(2)}) collective-permute-start(f32[1,64]{1,0:T(1,128)S(1)} %get-tuple-element.53), channel_id=1, source_target_pairs={{0,4},{4,0},{8,12},{12,8},{16,20},{20,16},{24,28},{28,24},{1,5},{5... | collective-permute-start | bytes 776 | tf_op jit(solution)/shard_map/ppermute | solution.py:544
  39.8 10.0 %collective-permute-start.7 = (f32[1,64]{1,0:T(1,128)S(1)}, f32[1,64]{1,0:T(1,128)S(1)}, u32[]{:S(2)}, u32[]{:S(2)}) collective-permute-start(f32[1,64]{1,0:T(1,128)S(1)} %add.18), channel_id=1, source_target_pairs={{0,8},{4,12},{8,0},{12,4},{16,24},{20,28},{24,16},{28,20},{1,9},{5... | collective-permute-start | bytes 776 | tf_op jit(solution)/shard_map/ppermute | solution.py:544
  41.5 8.3 %collective-permute-start.8 = (f32[1,64]{1,0:T(1,128)S(1)}, f32[1,64]{1,0:T(1,128)S(1)}, u32[]{:S(2)}, u32[]{:S(2)}) collective-permute-start(f32[1,64]{1,0:T(1,128)S(1)} %add.18), channel_id=1, source_target_pairs={{0,16},{4,20},{8,24},{12,28},{16,0},{20,4},{24,8},{28,12},{1,17},{... | collective-permute-start | bytes 776 | tf_op jit(solution)/shard_map/ppermute | solution.py:544
  43.0 6.8 %collective-permute-start.9 = (f32[1,64]{1,0:T(1,128)S(1)}, f32[1,64]{1,0:T(1,128)S(1)}, u32[]{:S(2)}, u32[]{:S(2)}) collective-permute-start(f32[1,64]{1,0:T(1,128)S(1)} %add.18), channel_id=1, source_target_pairs={{0,24},{4,28},{8,16},{12,20},{16,8},{20,12},{24,0},{28,4},{1,25},{... | collective-permute-start | bytes 776 | tf_op jit(solution)/shard_map/ppermute | solution.py:544

commit v8 on v7

--- a/solution.py
+++ b/solution.py
@@ -14,6 +14,10 @@
 ROWS = LANES
 f32 = jnp.float32
 bf16 = jnp.bfloat16
+STATE_PER = 2
+OUTPUT_PER = 2
+STATE_ROOM = 18
+OUTPUT_ROOM = 18
 
 
 def split(value):
@@ -62,8 +66,22 @@
     return pltpu.roll(jnp.broadcast_to(row, (LANES, LANES)), 0, 1, stride=1, stride_axis=0)
 
 
-def of_tile(whole, first=0):
-    return whole.at[pl.ds((pl.program_id(0) + first) * TILE_GROUPS, TILE_GROUPS)]
+def of_tile(whole, tile):
+    return whole.at[pl.ds(tile * TILE_GROUPS, TILE_GROUPS)]
+
+
+def staggered(parts):
+    phase = [0] * len(parts)
+    open_parts = [True] * len(parts)
+    while any(open_parts):
+        for u, part in enumerate(parts):
+            if not open_parts[u] or (u and open_parts[u - 1] and phase[u] >= phase[u - 1]):
+                continue
+            got = next(part, None)
+            if got is None:
+                open_parts[u] = False
+            else:
+                phase[u] = got
 
 
 def table_rows(source_ref, rows_ref):
@@ -74,14 +92,14 @@
     rows_ref[...] = jnp.transpose(tall)
 
 
-def parameters(rate_ref, gain_ref, rate_rows, gain_rows, first=0):
-    tile = pl.program_id(0) + first
-
+def fill_tables(rate_ref, gain_ref, rate_rows, gain_rows):
     @pl.when(pl.program_id(0) == 0)
     def _():
         table_rows(rate_ref, rate_rows)
         table_rows(gain_ref, gain_rows)
 
+
+def parameters(tile, rate_rows, gain_rows):
     at = pl.ds(pl.multiple_of(tile * TILE_GROUPS, TILE_GROUPS), TILE_GROUPS)
     rates = rate_rows[at, :]
     return rates, gain_rows[at, :] * jnp.sqrt(2.0 * rates)
@@ -105,12 +123,32 @@
     later_ref, earlier_ref,
     wide, own_all, table_all, rate_rows, gain_rows,
 ):
-    z_ref, eh_ref, el_ref = of_tile(z_whole), of_tile(eh_whole), of_tile(el_whole)
-    carry_ref = carry_whole.at[pl.program_id(0)]
-    short_ref = short_whole.at[pl.program_id(0)]
+    fill_tables(rate_ref, gain_ref, rate_rows, gain_rows)
+    count = cot_ref.shape[1] // LANES
+    parts = []
+    for u in range(count):
+        tile = pl.program_id(0) * count + u
+        lanes = slice(u * LANES, (u + 1) * LANES)
+        parts.append(
+            state_tile(
+                tile, feat_ref.at[:, :, lanes], taps_ref.at[:, :, lanes], cot_ref.at[:, lanes],
+                of_tile(z_whole, tile), of_tile(eh_whole, tile), of_tile(el_whole, tile),
+                carry_whole.at[tile], short_whole.at[tile], state_ref.at[:, lanes],
+                cross_ref.at[u * TILE_GROUPS : (u + 1) * TILE_GROUPS], later_ref, earlier_ref,
+                wide.at[u], own_all.at[u], table_all.at[u], rate_rows, gain_rows,
+            )
+        )
+    staggered(parts)
+
+
+def state_tile(
+    tile, feat_ref, taps_ref, cot_ref,
+    z_ref, eh_ref, el_ref, carry_ref, short_ref, state_ref, cross_ref, later_ref, earlier_ref,
+    wide, own_all, table_all, rate_rows, gain_rows,
+):
     tokens = feat_ref.shape[1]
     blocks = tokens // LANES
-    rate_tile, _ = parameters(rate_ref, gain_ref, rate_rows, gain_rows)
+    rate_tile, _ = parameters(tile, rate_rows, gain_rows)
     rates = per_mode(rate_tile)
     lag = iota(1, (LANES, LANES)).astype(f32)
     lane_at = iota(1, (LANES, LANES))
@@ -154,6 +192,7 @@
             z_ref[g, at, :] = z_t[of]
             eh_ref[g, at, :] = e_high[of]
             el_ref[g, at, :] = e_low[of]
+        yield 1
 
     for g in range(TILE_GROUPS):
         of = slice(g * MEMBERS, (g + 1) * MEMBERS)
@@ -175,6 +214,7 @@
             own_all[b, of, :] = jnp.where(
                 iota(1, (MEMBERS, LANES)) < 64, got[at], from_e[opposite]
             )
+        yield 2
 
     span = per_member(jnp.exp(rate_tile * (-float(LANES))))
     in_lag = jnp.where(
@@ -192,6 +232,7 @@
         now = span * (now + lagged) + own
         if b < blocks - 1:
             lagged = span * lagged + in_lag * pltpu.roll(own, MODES, 1)
+        yield 3
     cross_ref[...] = jnp.sum(cross.reshape(TILE_GROUPS, MEMBERS, LANES), axis=1)
     turned = jnp.transpose(now)
     state_ref[0:16] = turned[0:16]
@@ -199,7 +240,6 @@
     state_ref[32:48] = turned[64:80]
     state_ref[48:64] = turned[96:112]
 
-    tile = pl.program_id(0)
     half = later_ref.shape[1] // 2
     here = pl.ds(pl.multiple_of(tile * LANES, LANES), LANES)
     edges = jnp.concatenate(
@@ -232,9 +272,11 @@
     inner_whole, grad_whole, diag_ref,
     toep_all, power_all, fold_all, rate_rows, gain_rows,
 ):
-    z_ref, eh_ref, el_ref = of_tile(z_whole), of_tile(eh_whole), of_tile(el_whole)
-    inner_ref, grad_ref = of_tile(inner_whole), of_tile(grad_whole)
-    rate_tile, coef_tile = parameters(rate_ref, gain_ref, rate_rows, gain_rows)
+    tile = pl.program_id(0)
+    z_ref, eh_ref, el_ref = [of_tile(ref, tile) for ref in (z_whole, eh_whole, el_whole)]
+    inner_ref, grad_ref = of_tile(inner_whole, tile), of_tile(grad_whole, tile)
+    fill_tables(rate_ref, gain_ref, rate_rows, gain_rows)
+    rate_tile, coef_tile = parameters(tile, rate_rows, gain_rows)
     rates, coefs = per_mode(rate_tile), per_mode(coef_tile)
     lag = iota(1, (LANES, LANES)).astype(f32)
     row_at = iota(0, (LANES, LANES))
@@ -399,12 +441,35 @@
     *refs,
 ):
     mixer_ref, fgrad_ref, wide, adj, inner_t, grad_t, left_all, rate_rows, gain_rows = refs[-9:]
-    inner_ref, grad_ref = of_tile(inner_whole, first), of_tile(grad_whole, first)
-    carry_ref = carry_whole.at[pl.program_id(0) + first]
-    short_ref = short_whole.at[pl.program_id(0) + first]
+    fill_tables(rate_ref, gain_ref, rate_rows, gain_rows)
+    count = cot_ref.shape[1] // LANES
+    parts = []
+    for u in range(count):
+        tile = pl.program_id(0) * count + u + first
+        lanes = slice(u * LANES, (u + 1) * LANES)
+        parts.append(
+            output_tile(
+                tile, start_ref.at[:, :, lanes], edge_ref.at[:, :, lanes],
+                taps_ref.at[:, :, lanes], cot_ref.at[:, lanes],
+                of_tile(inner_whole, tile), of_tile(grad_whole, tile),
+                carry_whole.at[tile], short_whole.at[tile], bound_ref.at[:, lanes],
+                mixer_ref.at[:, lanes], fgrad_ref.at[:, :, lanes],
+                wide.at[u], adj.at[u], inner_t.at[u], grad_t.at[u], left_all.at[u],
+                rate_rows, gain_rows,
+            )
+        )
+    staggered(parts)
+
+
+def output_tile(
+    tile, start_ref, edge_ref, taps_ref, cot_ref,
+    inner_ref, grad_ref, carry_ref, short_ref, bound_ref,
+    mixer_ref, fgrad_ref,
+    wide, adj, inner_t, grad_t, left_all, rate_rows, gain_rows,
+):
     tokens = cot_ref.shape[0]
     blocks = tokens // LANES
-    rate_tile, coef_tile = parameters(rate_ref, gain_ref, rate_rows, gain_rows, first)
+    rate_tile, coef_tile = parameters(tile, rate_rows, gain_rows)
     rates, coefs = per_mode(rate_tile), per_mode(coef_tile)
     lag = iota(1, (LANES, LANES)).astype(f32)
     lane_at = iota(1, (LANES, LANES))
@@ -447,6 +512,7 @@
             opposite = slice((blocks - 1 - b) * MEMBERS, (blocks - b) * MEMBERS)
             inner_t[b, of, :] = inner_ref[g, at, :] + carried[at, :LANES]
             grad_t[b, of, :] = grad_ref[g, at, :] + carried[opposite, LANES:]
+        yield 1
     rates = jnp.transpose(member_rates)[0:MODES]
     coefs = jnp.transpose(per_member(coef_tile))[0:MODES]
     decay = jnp.exp(-rates)
@@ -472,18 +538,24 @@
     for b in range(blocks):
         at = slice(b * LANES, (b + 1) * LANES)
         inner = jnp.transpose(inner_t[b])
-        grad = jnp.transpose(grad_t[b])
-        query, key, value = [short_ref[i, at, :] for i in range(3)]
+        query = short_ref[0, at, :]
         if b == 0:
-            query, key, value = [
-                jnp.concatenate([begun[i], short_ref[i, 8:LANES, :]], axis=0) for i in range(3)
-            ]
+            query = jnp.concatenate([begun[0], short_ref[0, 8:LANES, :]], axis=0)
             inner = jnp.concatenate([inner[0:8] + inner_fix, inner[8:]], axis=0)
-            grad = jnp.concatenate([grad[0:8] + grad_fix, grad[8:]], axis=0)
         mixer_ref[at, :] = (query * inner).astype(bf16)
         adj[0, at, :] = cot_ref[at, :].astype(f32) * inner
+        yield 2
+    for b in range(blocks):
+        at = slice(b * LANES, (b + 1) * LANES)
+        grad = jnp.transpose(grad_t[b])
+        key, value = short_ref[1, at, :], short_ref[2, at, :]
+        if b == 0:
+            key = jnp.concatenate([begun[1], short_ref[1, 8:LANES, :]], axis=0)
+            value = jnp.concatenate([begun[2], short_ref[2, 8:LANES, :]], axis=0)
+            grad = jnp.concatenate([grad[0:8] + grad_fix, grad[8:]], axis=0)
         adj[1, at, :] = grad * value
         adj[2, at, :] = grad * key
+        yield 2
     for i in range(3):
         wide[i, 0:8, :] = edge_ref[i, 8:16, :].astype(f32)
         wide[i, 8:16, :] = jnp.zeros((8, LANES), f32)
@@ -505,14 +577,15 @@
     adj[0, tokens : tokens + 8, :] = upstream * inner_8
     adj[1, tokens : tokens + 8, :] = grad_8 * value
     adj[2, tokens : tokens + 8, :] = grad_8 * key
-    for b in range(blocks):
-        start = b * LANES
-        for i in range(3):
+    for i in range(3):
+        for b in range(blocks):
+            start = b * LANES
             fgrad_ref[i, start : start + LANES, :] = (
                 taps_ref[i, 0:1, :] * adj[i, start : start + LANES, :]
                 + taps_ref[i, 1:2, :] * adj[i, start + 1 : start + 1 + LANES, :]
                 + taps_ref[i, 2:3, :] * adj[i, start + 2 : start + 2 + LANES, :]
             ).astype(bf16)
+            yield 3
 
 
 def resident(shape, dtype):
@@ -557,9 +630,10 @@
     rates, gains = decay_rates.T, mode_gains.T
 
     whole = pl.BlockSpec(memory_space=pltpu.VMEM)
-    feat_spec = pl.BlockSpec((3, tokens, LANES), lambda j: (0, 0, j))
-    taps_spec = pl.BlockSpec((3, 3, LANES), lambda j: (0, 0, j))
-    cot_spec = pl.BlockSpec((tokens, LANES), lambda j: (0, j))
+    per = STATE_PER if tiles % STATE_PER == 0 else 1
+    feat_spec = pl.BlockSpec((3, tokens, per * LANES), lambda j: (0, 0, j))
+    taps_spec = pl.BlockSpec((3, 3, per * LANES), lambda j: (0, 0, j))
+    cot_spec = pl.BlockSpec((tokens, per * LANES), lambda j: (0, j))
     table_spec = pl.BlockSpec((MODES, groups), lambda j: (0, 0))
     slot_spec = pl.BlockSpec((TILE_GROUPS, LANES), lambda j: (j, 0))
     me_spec = pl.BlockSpec(memory_space=pltpu.SMEM)
@@ -574,7 +648,7 @@
 
     z, eh, el, carry, short, states, cross, later, early = pl.pallas_call(
         state_kernel,
-        grid=(tiles,),
+        grid=(tiles // per,),
         in_specs=[feat_spec, taps_spec, cot_spec, table_spec, table_spec],
         out_specs=[
             whole,
@@ -582,8 +656,8 @@
             whole,
             whole,
             whole,
-            pl.BlockSpec((4 * MODES, LANES), lambda j: (0, j)),
-            slot_spec,
+            pl.BlockSpec((4 * MODES, per * LANES), lambda j: (0, j)),
+            pl.BlockSpec((per * TILE_GROUPS, LANES), lambda j: (j, 0)),
             whole,
             whole,
         ],
@@ -599,12 +673,12 @@
             resident((40, channels), f32),
         ],
         scratch_shapes=[
-            pltpu.VMEM((3, tokens + 8, LANES), f32),
-            pltpu.VMEM((blocks, LANES, LANES), f32),
-            pltpu.VMEM((TILE_GROUPS, LANES, 2 * LANES), bf16),
+            pltpu.VMEM((per, 3, tokens + 8, LANES), f32),
+            pltpu.VMEM((per, blocks, LANES, LANES), f32),
+            pltpu.VMEM((per, TILE_GROUPS, LANES, 2 * LANES), bf16),
         ]
         + table_scratch,
-        compiler_params=room(14),
+        compiler_params=room(STATE_ROOM),
         name="state_part",
     )(*far(features, short_taps, cotangent, rates, gains))
 
@@ -646,24 +720,26 @@
     )(me, states, later, diag, cross, short_taps, rates, gains, *gots)
 
     def outputs(first, count, *written):
-        columns = lambda j: (0, j + first)
-        layers = lambda j: (0, 0, j + first)
-        mine = [pl.BlockSpec((tokens, LANES), columns), pl.BlockSpec((3, tokens, LANES), layers)]
+        per = OUTPUT_PER if count % OUTPUT_PER == 0 and first % OUTPUT_PER == 0 else 1
+        wide_lanes = per * LANES
+        columns = lambda j: (0, j + first // per)
+        layers = lambda j: (0, 0, j + first // per)
+        mine = [pl.BlockSpec((tokens, wide_lanes), columns), pl.BlockSpec((3, tokens, wide_lanes), layers)]
         return pl.pallas_call(
             functools.partial(output_kernel, first),
-            grid=(count,),
+            grid=(count // per,),
             in_specs=[
-                pl.BlockSpec((3, 16, LANES), layers),
-                pl.BlockSpec((3, 16, LANES), lambda j: (0, tokens // 16 - 1, j + first)),
-                pl.BlockSpec((3, 3, LANES), layers),
-                pl.BlockSpec((tokens, LANES), columns),
+                pl.BlockSpec((3, 16, wide_lanes), layers),
+                pl.BlockSpec((3, 16, wide_lanes), lambda j: (0, tokens // 16 - 1, j + first // per)),
+                pl.BlockSpec((3, 3, wide_lanes), layers),
+                pl.BlockSpec((tokens, wide_lanes), columns),
                 table_spec,
                 table_spec,
                 whole,
                 whole,
                 whole,
                 whole,
-                pl.BlockSpec((64, LANES), columns),
+                pl.BlockSpec((64, wide_lanes), columns),
             ]
             + [pl.BlockSpec(memory_space=pl.ANY)] * len(written),
             out_specs=mine,
@@ -672,14 +748,14 @@
                 jax.ShapeDtypeStruct((3, tokens, channels), bf16),
             ],
             scratch_shapes=[
-                pltpu.VMEM((3, 16, LANES), f32),
-                pltpu.VMEM((3, tokens + 8, LANES), f32),
-                pltpu.VMEM((blocks, LANES, LANES), f32),
-                pltpu.VMEM((blocks, LANES, LANES), f32),
-                pltpu.VMEM((TILE_GROUPS, rows, LANES), bf16),
+                pltpu.VMEM((per, 3, 16, LANES), f32),
+                pltpu.VMEM((per, 3, tokens + 8, LANES), f32),
+                pltpu.VMEM((per, blocks, LANES, LANES), f32),
+                pltpu.VMEM((per, blocks, LANES, LANES), f32),
+                pltpu.VMEM((per, TILE_GROUPS, rows, LANES), bf16),
             ]
             + table_scratch,
-            compiler_params=room(14),
+            compiler_params=room(OUTPUT_ROOM),
             input_output_aliases={11: 0, 12: 1} if written else {},
             cost_estimate=pl.CostEstimate(
                 flops=2 * count * TILE_GROUPS * rows * LANES * LANES * 8,

time: 50.8 us -> 48.8 us (0.961)
  Pallas kernels: 34.1 us -> 32.3 us
    pallas_call x3, Pallas kernels: 25.4 us -> 23.6 us  [the longest x2 12.2 us: outputs(): pl.pallas_call(functools.partial(output_kernel, first), grid=(count // pe...]
where the time goes in v8:
time: 48.8 us; the launch traced here: 48.6 us
  Pallas kernels  32.3 us (66%)
  starting transfers between devices  13.6 us (28%)
  waiting for transfers between devices  1.14 us (2%)
  between operations  0.83 us (2%)
  local copies, waits for them, and re-layouts  0.62 us (1%)
    ppermute x10, starting transfers between devices, swapped(): return lax.ppermute(value, axis, [(i, i ^ key) for i in range(count)])  13.6 us
    pallas_call x2, Pallas kernels, outputs(): pl.pallas_call(functools.partial(output_kernel, first), grid=(count // pe...  12.2 us
    pallas_call x1, Pallas kernels, per_device(): pl.pallas_call(state_kernel, grid=(tiles // per,), in_specs=[feat_spec, t...  11.4 us
    pallas_call x1, Pallas kernels, per_device(): pl.pallas_call(inside_kernel, grid=(tiles,), in_specs=[whole, whole, whol...  7.87 us
    ppermute x10, waiting for transfers between devices, swapped(): return lax.ppermute(value, axis, [(i, i ^ key) for i in range(count)])  1.14 us
  transfers between devices with their start and end apart: 10, of which 1 were waited for; matrix products, arithmetic and copies ran while one was open for 0% of the time, Pallas kernels for 41%

profile of v8, /device:TPU:0, one launch (start us, length us, event | category | flops | bytes accessed | tf_op | source)
XLA Modules:
  0.0 48.6 jit_solution(450189849253226919)
XLA Ops:
  0.6 11.4 %state_part.1 = (bf16[64,128,128]{2,1,0:T(8,128)(2,1)S(1)}, bf16[64,128,128]{2,1,0:T(8,128)(2,1)S(1)}, bf16[64,128,128]{2,1,0:T(8,128)(2,1)S(1)}, f32[8,8,128,12...) custom-call(bf16[3,1024,1024]{2,1,0:T(8,128)(2,1)} %edge_ref.3, ...), custom_call_target="tpu_custom_call" | custom-call | tf_op jit(solution)/shard_map/state_part/pallas_call | solution.py:649
  12.1 0.0 copy-start
  12.1 0.0 copy-start.1
  12.1 0.0 copy-start.2
  12.1 3.1 %collective-permute-start = (bf16[40,1024]{1,0:T(8,128)(2,1)S(1)}, bf16[40,1024]{1,0:T(8,128)(2,1)S(1)}, u32[]{:S(2)}, u32[]{:S(2)}) collective-permute-start(bf16[40,1024]{1,0:T(8,128)(2,1)S(1)} %get-tuple-element.64), channel_id=1, source_target_pairs={{0,1},{1,0},{2,3},{3,2},{4,5},{5,4},{6,7},{7,6},{8,9},{9,8},{10,11... | collective-permute-start | bytes 245768 | tf_op jit(solution)/shard_map/ppermute | solution.py:617
  15.2 2.6 %collective-permute-start.1 = (bf16[40,1024]{1,0:T(8,128)(2,1)S(1)}, bf16[40,1024]{1,0:T(8,128)(2,1)S(1)}, u32[]{:S(2)}, u32[]{:S(2)}) collective-permute-start(bf16[40,1024]{1,0:T(8,128)(2,1)S(1)} %get-tuple-element.63), channel_id=1, source_target_pairs={{0,2},{1,3},{2,0},{3,1},{4,6},{5,7},{6,4},{7,5},{8,10},{9,11},{10,... | collective-permute-start | bytes 245768 | tf_op jit(solution)/shard_map/ppermute | solution.py:617
  17.8 0.0 collective-permute-start.2
  17.8 7.9 %inside_part.1 = (f32[64,128,128]{2,1,0:T(8,128)S(1)}, f32[64,128,128]{2,1,0:T(8,128)S(1)}, f32[64,128]{1,0:T(8,128)S(1)}) custom-call(bf16[64,128,128]{2,1,0:T(8,128)(2,1)S(1)} %get-tuple-element.33.z_whole, bf16[64,128,128]{2,1,0:T(8,128)(2,1)S(1)} %get-tuple-element.34.eh_whole, bf16[64,128,128]{2,1,0:T(8,128)(2,1)S(1)} %get-tuple-element.35.el_whole, ...), custom_call_target="tpu_custom_call" | custom-call | flops 1879048192 | bytes 14680064 | tf_op jit(solution)/shard_map/inside_part/pallas_call | solution.py:690
  25.7 0.0 collective-permute-done
  25.7 0.0 collective-permute-done.1
  25.8 0.0 collective-permute-done.2
  25.8 0.0 copy-done
  25.8 0.0 copy-done.1
  25.8 0.7 %join_part.1 = (f32[64,1024]{1,0:T(8,128)S(1)}, f32[32,64]{1,0:T(8,128)S(1)}) custom-call(s32[1]{0:T(128)} %bitcast.2.me_ref, f32[64,1024]{1,0:T(8,128)S(1)} %get-tuple-element.40.state_ref, f32[40,1024]{1,0:T(8,128)S(1)} %get-tuple-element.41.own_ref, f32[64,128]{1,0:T(8,128)S(1)} %get-tuple-element.42.diag_ref, f32[64,128]{1,0:T(8,128)S(1)} %get-tuple-element.43.cross_ref, ...), custom_call_target="tpu_custom_call" | custom-call | tf_op jit(solution)/shard_map/join_part/pallas_call | solution.py:709
  26.5 1.0 %collective-permute-start.3 = (f32[32,64]{1,0:T(8,128)S(1)}, f32[32,64]{1,0:T(8,128)S(1)}, u32[]{:S(2)}, u32[]{:S(2)}) collective-permute-start(f32[32,64]{1,0:T(8,128)S(1)} %get-tuple-element.49.refs_0_), channel_id=1, source_target_pairs={{0,1},{1,0},{2,3},{3,2},{4,5},{5,4},{6,7},{7,6},{8,9},{9,8},{10,11... | collective-permute-start | bytes 24584 | tf_op jit(solution)/shard_map/ppermute | solution.py:617
  27.5 3.5 %collective-permute-start.4 = (f32[32,64]{1,0:T(8,128)S(1)}, f32[32,64]{1,0:T(8,128)S(1)}, u32[]{:S(2)}, u32[]{:S(2)}) collective-permute-start(f32[32,64]{1,0:T(8,128)S(1)} %get-tuple-element.49.refs_0_), channel_id=1, source_target_pairs={{0,2},{1,3},{2,0},{3,1},{4,6},{5,7},{6,4},{7,5},{8,10},{9,11},{10,... | collective-permute-start | bytes 24584 | tf_op jit(solution)/shard_map/ppermute | solution.py:617
  31.0 0.0 collective-permute-start.5
  31.0 6.1 %output_part.2 = (bf16[1024,1024]{1,0:T(8,128)(2,1)}, bf16[3,1024,1024]{2,1,0:T(8,128)(2,1)}) custom-call(bf16[3,1024,1024]{2,1,0:T(8,128)(2,1)} %edge_ref.3, bf16[3,1024,1024]{2,1,0:T(8,128)(2,1)} %edge_ref.3, f32[3,3,1024]{2,1,0:T(4,128)} %taps_ref.7, bf16[1024,1024]{1,0:T(8,128)(2,1)} %cot_ref.5, f32[16,64]{1,0:T(8,128)} %bitcast.11, f32[16,64]{1,0:T(8,128)} %bitcast.16, ...), custom_call_target="tpu_custom_call" | custom-call | flops 1073741824 | bytes 16777216 | tf_op jit(solution)/shard_map/output_part/pallas_call | solution.py:728
  37.1 0.0 collective-permute-done.3.refs_1_
  37.1 0.0 collective-permute-done.4.refs_2_
  37.1 0.0 collective-permute-done.5.refs_3_
  37.1 0.1 sum_part.1
  37.2 0.0 collective-permute-start.6
  37.2 1.1 %collective-permute-done.6 = f32[1,64]{1,0:T(1,128)S(1)} collective-permute-done((f32[1,64]{1,0:T(1,128)S(1)}, f32[1,64]{1,0:T(1,128)S(1)}, u32[]{:S(2)}, u32[]{:S(2)}) %collective-permute-start.6) | collective-permute-done | bytes 288 | tf_op jit(solution)/shard_map/ppermute | solution.py:617
  38.3 1.7 %collective-permute-start.7 = (f32[1,64]{1,0:T(1,128)S(1)}, f32[1,64]{1,0:T(1,128)S(1)}, u32[]{:S(2)}, u32[]{:S(2)}) collective-permute-start(f32[1,64]{1,0:T(1,128)S(1)} %add.18), channel_id=1, source_target_pairs={{0,8},{4,12},{8,0},{12,4},{16,24},{20,28},{24,16},{28,20},{1,9},{5... | collective-permute-start | bytes 776 | tf_op jit(solution)/shard_map/ppermute | solution.py:617
  40.0 1.5 %collective-permute-start.8 = (f32[1,64]{1,0:T(1,128)S(1)}, f32[1,64]{1,0:T(1,128)S(1)}, u32[]{:S(2)}, u32[]{:S(2)}) collective-permute-start(f32[1,64]{1,0:T(1,128)S(1)} %add.18), channel_id=1, source_target_pairs={{0,16},{4,20},{8,24},{12,28},{16,0},{20,4},{24,8},{28,12},{1,17},{... | collective-permute-start | bytes 776 | tf_op jit(solution)/shard_map/ppermute | solution.py:617
  41.6 0.3 collective-permute-start.9
  41.8 6.1 %output_part.3 = (bf16[1024,1024]{1,0:T(8,128)(2,1)}, bf16[3,1024,1024]{2,1,0:T(8,128)(2,1)}) custom-call(bf16[3,1024,1024]{2,1,0:T(8,128)(2,1)} %edge_ref.3, bf16[3,1024,1024]{2,1,0:T(8,128)(2,1)} %edge_ref.3, f32[3,3,1024]{2,1,0:T(4,128)} %taps_ref.7, bf16[1024,1024]{1,0:T(8,128)(2,1)} %cot_ref.5, ...), custom_call_target="tpu_custom_call", output_to_operand_aliasing={{0}: (11, {}), {1}: (12, {})} | custom-call | flops 1073741824 | bytes 16777216 | tf_op jit(solution)/shard_map/output_part/pallas_call | solution.py:728
  47.9 0.0 collective-permute-done.7
  47.9 0.0 collective-permute-done.8
  47.9 0.0 collective-permute-done.9
  48.0 0.6 %slice_bitcast_fusion = (f32[64,16]{0,1:T(8,128)}, f32[64,16]{0,1:T(8,128)}) fusion(f32[32,64]{1,0:T(8,128)S(1)} %broadcast_multiply_fusion), kind=kLoop, calls=%fused_computation.3 | loop fusion | bytes 16384 | tf_op jit(solution)/shard_map/transpose | solution.py:800
  (8 shorter events, 0.1 us)
Async XLA Ops:
  12.1 13.7 %copy-start = (f32[3,3,1024]{2,1,0:T(4,128)S(1)}, f32[3,3,1024]{2,1,0:T(4,128)}, u32[]{:S(2)}) copy-start(f32[3,3,1024]{2,1,0:T(4,128)} %taps_ref.7) | copy-start | bytes 110596
  12.1 13.7 %copy-start.1 = (f32[64,16]{0,1:T(8,128)S(1)}, f32[64,16]{0,1:T(8,128)}, u32[]{:S(2)}) copy-start(f32[64,16]{0,1:T(8,128)} %param.7) | copy-start | bytes 12292
  12.1 13.7 %copy-start.2 = (f32[64,16]{0,1:T(8,128)S(1)}, f32[64,16]{0,1:T(8,128)}, u32[]{:S(2)}) copy-start(f32[64,16]{0,1:T(8,128)} %param.8) | copy-start | bytes 12292
  12.1 13.6 %collective-permute-start = (bf16[40,1024]{1,0:T(8,128)(2,1)S(1)}, bf16[40,1024]{1,0:T(8,128)(2,1)S(1)}, u32[]{:S(2)}, u32[]{:S(2)}) collective-permute-start(bf16[40,1024]{1,0:T(8,128)(2,1)S(1)} %get-tuple-element.64), channel_id=1, source_target_pairs={{0,1},{1,0},{2,3},{3,2},{4,5},{5,4},{6,7},{7,6},{8,9},{9,8},{10,11... | collective-permute-start | bytes 245768 | tf_op jit(solution)/shard_map/ppermute | solution.py:617
  15.2 10.5 %collective-permute-start.1 = (bf16[40,1024]{1,0:T(8,128)(2,1)S(1)}, bf16[40,1024]{1,0:T(8,128)(2,1)S(1)}, u32[]{:S(2)}, u32[]{:S(2)}) collective-permute-start(bf16[40,1024]{1,0:T(8,128)(2,1)S(1)} %get-tuple-element.63), channel_id=1, source_target_pairs={{0,2},{1,3},{2,0},{3,1},{4,6},{5,7},{6,4},{7,5},{8,10},{9,11},{10,... | collective-permute-start | bytes 245768 | tf_op jit(solution)/shard_map/ppermute | solution.py:617
  17.8 7.9 %collective-permute-start.2 = (bf16[40,1024]{1,0:T(8,128)(2,1)S(1)}, bf16[40,1024]{1,0:T(8,128)(2,1)S(1)}, u32[]{:S(2)}, u32[]{:S(2)}) collective-permute-start(bf16[40,1024]{1,0:T(8,128)(2,1)S(1)} %get-tuple-element.62), channel_id=1, source_target_pairs={{0,3},{1,2},{2,1},{3,0},{4,7},{5,6},{6,5},{7,4},{8,11},{9,10},{10,... | collective-permute-start | bytes 245768 | tf_op jit(solution)/shard_map/ppermute | solution.py:617
  26.5 10.6 %collective-permute-start.3 = (f32[32,64]{1,0:T(8,128)S(1)}, f32[32,64]{1,0:T(8,128)S(1)}, u32[]{:S(2)}, u32[]{:S(2)}) collective-permute-start(f32[32,64]{1,0:T(8,128)S(1)} %get-tuple-element.49.refs_0_), channel_id=1, source_target_pairs={{0,1},{1,0},{2,3},{3,2},{4,5},{5,4},{6,7},{7,6},{8,9},{9,8},{10,11... | collective-permute-start | bytes 24584 | tf_op jit(solution)/shard_map/ppermute | solution.py:617
  27.5 9.6 %collective-permute-start.4 = (f32[32,64]{1,0:T(8,128)S(1)}, f32[32,64]{1,0:T(8,128)S(1)}, u32[]{:S(2)}, u32[]{:S(2)}) collective-permute-start(f32[32,64]{1,0:T(8,128)S(1)} %get-tuple-element.49.refs_0_), channel_id=1, source_target_pairs={{0,2},{1,3},{2,0},{3,1},{4,6},{5,7},{6,4},{7,5},{8,10},{9,11},{10,... | collective-permute-start | bytes 24584 | tf_op jit(solution)/shard_map/ppermute | solution.py:617
  31.0 6.1 %collective-permute-start.5 = (f32[32,64]{1,0:T(8,128)S(1)}, f32[32,64]{1,0:T(8,128)S(1)}, u32[]{:S(2)}, u32[]{:S(2)}) collective-permute-start(f32[32,64]{1,0:T(8,128)S(1)} %get-tuple-element.49.refs_0_), channel_id=1, source_target_pairs={{0,3},{1,2},{2,1},{3,0},{4,7},{5,6},{6,5},{7,4},{8,11},{9,10},{10,... | collective-permute-start | bytes 24584 | tf_op jit(solution)/shard_map/ppermute | solution.py:617
  37.2 1.1 %collective-permute-start.6 = (f32[1,64]{1,0:T(1,128)S(1)}, f32[1,64]{1,0:T(1,128)S(1)}, u32[]{:S(2)}, u32[]{:S(2)}) collective-permute-start(f32[1,64]{1,0:T(1,128)S(1)} %get-tuple-element.53), channel_id=1, source_target_pairs={{0,4},{4,0},{8,12},{12,8},{16,20},{20,16},{24,28},{28,24},{1,5},{5... | collective-permute-start | bytes 776 | tf_op jit(solution)/shard_map/ppermute | solution.py:617
  38.3 9.6 %collective-permute-start.7 = (f32[1,64]{1,0:T(1,128)S(1)}, f32[1,64]{1,0:T(1,128)S(1)}, u32[]{:S(2)}, u32[]{:S(2)}) collective-permute-start(f32[1,64]{1,0:T(1,128)S(1)} %add.18), channel_id=1, source_target_pairs={{0,8},{4,12},{8,0},{12,4},{16,24},{20,28},{24,16},{28,20},{1,9},{5... | collective-permute-start | bytes 776 | tf_op jit(solution)/shard_map/ppermute | solution.py:617
  40.0 7.9 %collective-permute-start.8 = (f32[1,64]{1,0:T(1,128)S(1)}, f32[1,64]{1,0:T(1,128)S(1)}, u32[]{:S(2)}, u32[]{:S(2)}) collective-permute-start(f32[1,64]{1,0:T(1,128)S(1)} %add.18), channel_id=1, source_target_pairs={{0,16},{4,20},{8,24},{12,28},{16,0},{20,4},{24,8},{28,12},{1,17},{... | collective-permute-start | bytes 776 | tf_op jit(solution)/shard_map/ppermute | solution.py:617
  41.6 6.4 %collective-permute-start.9 = (f32[1,64]{1,0:T(1,128)S(1)}, f32[1,64]{1,0:T(1,128)S(1)}, u32[]{:S(2)}, u32[]{:S(2)}) collective-permute-start(f32[1,64]{1,0:T(1,128)S(1)} %add.18), channel_id=1, source_target_pairs={{0,24},{4,28},{8,16},{12,20},{16,8},{20,12},{24,0},{28,4},{1,25},{... | collective-permute-start | bytes 776 | tf_op jit(solution)/shard_map/ppermute | solution.py:617

commit v9 on v8

--- a/solution.py
+++ b/solution.py
@@ -16,6 +16,7 @@
 bf16 = jnp.bfloat16
 STATE_PER = 2
 OUTPUT_PER = 2
+INSIDE_PER = 2
 STATE_ROOM = 18
 OUTPUT_ROOM = 18
 
@@ -272,10 +273,26 @@
     inner_whole, grad_whole, diag_ref,
     toep_all, power_all, fold_all, rate_rows, gain_rows,
 ):
-    tile = pl.program_id(0)
-    z_ref, eh_ref, el_ref = [of_tile(ref, tile) for ref in (z_whole, eh_whole, el_whole)]
-    inner_ref, grad_ref = of_tile(inner_whole, tile), of_tile(grad_whole, tile)
     fill_tables(rate_ref, gain_ref, rate_rows, gain_rows)
+    count = diag_ref.shape[0] // TILE_GROUPS
+    parts = []
+    for u in range(count):
+        tile = pl.program_id(0) * count + u
+        parts.append(
+            inside_tile(
+                tile, of_tile(z_whole, tile), of_tile(eh_whole, tile), of_tile(el_whole, tile),
+                of_tile(inner_whole, tile), of_tile(grad_whole, tile),
+                diag_ref.at[u * TILE_GROUPS : (u + 1) * TILE_GROUPS],
+                toep_all.at[u], power_all.at[u], fold_all.at[u], rate_rows, gain_rows,
+            )
+        )
+    staggered(parts)
+
+
+def inside_tile(
+    tile, z_ref, eh_ref, el_ref, inner_ref, grad_ref, diag_ref,
+    toep_all, power_all, fold_all, rate_rows, gain_rows,
+):
     rate_tile, coef_tile = parameters(tile, rate_rows, gain_rows)
     rates, coefs = per_mode(rate_tile), per_mode(coef_tile)
     lag = iota(1, (LANES, LANES)).astype(f32)
@@ -297,10 +314,12 @@
         while len(folded) > 1:
             folded = [folded[i] + folded[i + 1] for i in range(0, len(folded), 2)]
         fold_all[8 * g : 8 * g + 8, :] = folded[0]
+        yield 1
     for g in range(TILE_GROUPS):
         high, low = split(jnp.where(lane_at >= row_at, circulant(taps[g : g + 1]), 0.0))
         toep_all[g, 0:LANES, :] = high
         toep_all[g, LANES:, :] = low
+        yield 2
     for g in range(TILE_GROUPS):
         z, eh, el = z_ref[g], eh_ref[g], el_ref[g]
         high = toep_all[g, 0:LANES, :]
@@ -309,6 +328,7 @@
             jnp.concatenate([eh, el, eh], axis=1),
             jnp.concatenate([high, high, toep_all[g, LANES:, :]], axis=1),
         )
+        yield 3
     corr = jnp.sum(sheared(fold_all[...], 8).reshape(TILE_GROUPS, 8, LANES), axis=1)
     weighted = power_all[...] * per_member(corr)
     first_col = jnp.sum(weighted, axis=1, keepdims=True)
@@ -635,7 +655,6 @@
     taps_spec = pl.BlockSpec((3, 3, per * LANES), lambda j: (0, 0, j))
     cot_spec = pl.BlockSpec((tokens, per * LANES), lambda j: (0, j))
     table_spec = pl.BlockSpec((MODES, groups), lambda j: (0, 0))
-    slot_spec = pl.BlockSpec((TILE_GROUPS, LANES), lambda j: (j, 0))
     me_spec = pl.BlockSpec(memory_space=pltpu.SMEM)
     rows = blocks * MEMBERS
     turned = resident((groups, rows, LANES), bf16)
@@ -687,16 +706,21 @@
         sent = jnp.where((ctx_index ^ key) < ctx_index, early, later)
         gots.append(swapped(sent.astype(bf16), "ctx", key).astype(f32))
 
+    inside_per = INSIDE_PER if tiles % INSIDE_PER == 0 else 1
     inner, grad, diag = pl.pallas_call(
         inside_kernel,
-        grid=(tiles,),
+        grid=(tiles // inside_per,),
         in_specs=[whole, whole, whole, table_spec, table_spec],
-        out_specs=[whole, whole, slot_spec],
+        out_specs=[
+            whole,
+            whole,
+            pl.BlockSpec((inside_per * TILE_GROUPS, LANES), lambda j: (j, 0)),
+        ],
         out_shape=[wide_turned, wide_turned, slots],
         scratch_shapes=[
-            pltpu.VMEM((TILE_GROUPS, 2 * LANES, LANES), bf16),
-            pltpu.VMEM((LANES, LANES), f32),
-            pltpu.VMEM((8 * TILE_GROUPS, LANES), f32),
+            pltpu.VMEM((inside_per, TILE_GROUPS, 2 * LANES, LANES), bf16),
+            pltpu.VMEM((inside_per, LANES, LANES), f32),
+            pltpu.VMEM((inside_per, 8 * TILE_GROUPS, LANES), f32),
         ]
         + table_scratch,
         compiler_params=room(14),

time: 48.8 us -> 47.8 us (0.980)
  Pallas kernels: 32.3 us -> 31.3 us
    pallas_call x1, Pallas kernels: 7.87 us -> 6.88 us  [per_device(): pl.pallas_call(inside_kernel, grid=(tiles // inside_per,), in_specs=[whol...]
  transfers between devices with their start and end apart: 10 -> 10, of which waited for: 1 -> 1; matrix products, arithmetic and copies ran while one was open for 0% -> 0% of each run, Pallas kernels for 41% -> 40%
where the time goes in v9:
time: 47.8 us; the launch traced here: 47.6 us
  Pallas kernels  31.3 us (65%)
  starting transfers between devices  13.6 us (28%)
  waiting for transfers between devices  1.14 us (2%)
  between operations  0.83 us (2%)
  local copies, waits for them, and re-layouts  0.62 us (1%)
    ppermute x10, starting transfers between devices, swapped(): return lax.ppermute(value, axis, [(i, i ^ key) for i in range(count)])  13.6 us
    pallas_call x2, Pallas kernels, outputs(): pl.pallas_call(functools.partial(output_kernel, first), grid=(count // pe...  12.2 us
    pallas_call x1, Pallas kernels, per_device(): pl.pallas_call(state_kernel, grid=(tiles // per,), in_specs=[feat_spec, t...  11.4 us
    pallas_call x1, Pallas kernels, per_device(): pl.pallas_call(inside_kernel, grid=(tiles // inside_per,), in_specs=[whol...  6.88 us
    ppermute x10, waiting for transfers between devices, swapped(): return lax.ppermute(value, axis, [(i, i ^ key) for i in range(count)])  1.14 us
  transfers between devices with their start and end apart: 10, of which 1 were waited for; matrix products, arithmetic and copies ran while one was open for 0% of the time, Pallas kernels for 40%

profile of v9, /device:TPU:0, one launch (start us, length us, event | category | flops | bytes accessed | tf_op | source)
XLA Modules:
  0.0 47.6 jit_solution(6734541214095629187)
XLA Ops:
  0.6 11.4 %state_part.1 = (bf16[64,128,128]{2,1,0:T(8,128)(2,1)S(1)}, bf16[64,128,128]{2,1,0:T(8,128)(2,1)S(1)}, bf16[64,128,128]{2,1,0:T(8,128)(2,1)S(1)}, f32[8,8,128,12...) custom-call(bf16[3,1024,1024]{2,1,0:T(8,128)(2,1)} %edge_ref.3, ...), custom_call_target="tpu_custom_call" | custom-call | tf_op jit(solution)/shard_map/state_part/pallas_call | solution.py:668
  12.1 0.0 copy-start
  12.1 0.0 copy-start.1
  12.1 0.0 copy-start.2
  12.1 3.1 %collective-permute-start = (bf16[40,1024]{1,0:T(8,128)(2,1)S(1)}, bf16[40,1024]{1,0:T(8,128)(2,1)S(1)}, u32[]{:S(2)}, u32[]{:S(2)}) collective-permute-start(bf16[40,1024]{1,0:T(8,128)(2,1)S(1)} %get-tuple-element.64), channel_id=1, source_target_pairs={{0,1},{1,0},{2,3},{3,2},{4,5},{5,4},{6,7},{7,6},{8,9},{9,8},{10,11... | collective-permute-start | bytes 245768 | tf_op jit(solution)/shard_map/ppermute | solution.py:637
  15.2 2.6 %collective-permute-start.1 = (bf16[40,1024]{1,0:T(8,128)(2,1)S(1)}, bf16[40,1024]{1,0:T(8,128)(2,1)S(1)}, u32[]{:S(2)}, u32[]{:S(2)}) collective-permute-start(bf16[40,1024]{1,0:T(8,128)(2,1)S(1)} %get-tuple-element.63), channel_id=1, source_target_pairs={{0,2},{1,3},{2,0},{3,1},{4,6},{5,7},{6,4},{7,5},{8,10},{9,11},{10,... | collective-permute-start | bytes 245768 | tf_op jit(solution)/shard_map/ppermute | solution.py:637
  17.8 0.0 collective-permute-start.2
  17.8 6.9 %inside_part.1 = (f32[64,128,128]{2,1,0:T(8,128)S(1)}, f32[64,128,128]{2,1,0:T(8,128)S(1)}, f32[64,128]{1,0:T(8,128)S(1)}) custom-call(bf16[64,128,128]{2,1,0:T(8,128)(2,1)S(1)} %get-tuple-element.33.z_whole, bf16[64,128,128]{2,1,0:T(8,128)(2,1)S(1)} %get-tuple-element.34.eh_whole, bf16[64,128,128]{2,1,0:T(8,128)(2,1)S(1)} %get-tuple-element.35.el_whole, ...), custom_call_target="tpu_custom_call" | custom-call | flops 1879048192 | bytes 14680064 | tf_op jit(solution)/shard_map/inside_part/pallas_call | solution.py:710
  24.7 0.0 collective-permute-done
  24.7 0.0 collective-permute-done.1
  24.8 0.0 collective-permute-done.2
  24.8 0.0 copy-done
  24.8 0.0 copy-done.1
  24.8 0.7 %join_part.1 = (f32[64,1024]{1,0:T(8,128)S(1)}, f32[32,64]{1,0:T(8,128)S(1)}) custom-call(s32[1]{0:T(128)} %bitcast.2.me_ref, f32[64,1024]{1,0:T(8,128)S(1)} %get-tuple-element.40.state_ref, f32[40,1024]{1,0:T(8,128)S(1)} %get-tuple-element.41.own_ref, f32[64,128]{1,0:T(8,128)S(1)} %get-tuple-element.42.diag_ref, f32[64,128]{1,0:T(8,128)S(1)} %get-tuple-element.43.cross_ref, ...), custom_call_target="tpu_custom_call" | custom-call | tf_op jit(solution)/shard_map/join_part/pallas_call | solution.py:733
  25.5 1.1 %collective-permute-start.3 = (f32[32,64]{1,0:T(8,128)S(1)}, f32[32,64]{1,0:T(8,128)S(1)}, u32[]{:S(2)}, u32[]{:S(2)}) collective-permute-start(f32[32,64]{1,0:T(8,128)S(1)} %get-tuple-element.49.refs_0_), channel_id=1, source_target_pairs={{0,1},{1,0},{2,3},{3,2},{4,5},{5,4},{6,7},{7,6},{8,9},{9,8},{10,11... | collective-permute-start | bytes 24584 | tf_op jit(solution)/shard_map/ppermute | solution.py:637
  26.7 3.3 %collective-permute-start.4 = (f32[32,64]{1,0:T(8,128)S(1)}, f32[32,64]{1,0:T(8,128)S(1)}, u32[]{:S(2)}, u32[]{:S(2)}) collective-permute-start(f32[32,64]{1,0:T(8,128)S(1)} %get-tuple-element.49.refs_0_), channel_id=1, source_target_pairs={{0,2},{1,3},{2,0},{3,1},{4,6},{5,7},{6,4},{7,5},{8,10},{9,11},{10,... | collective-permute-start | bytes 24584 | tf_op jit(solution)/shard_map/ppermute | solution.py:637
  30.0 0.0 collective-permute-start.5
  30.0 6.1 %output_part.2 = (bf16[1024,1024]{1,0:T(8,128)(2,1)}, bf16[3,1024,1024]{2,1,0:T(8,128)(2,1)}) custom-call(bf16[3,1024,1024]{2,1,0:T(8,128)(2,1)} %edge_ref.3, bf16[3,1024,1024]{2,1,0:T(8,128)(2,1)} %edge_ref.3, f32[3,3,1024]{2,1,0:T(4,128)} %taps_ref.7, bf16[1024,1024]{1,0:T(8,128)(2,1)} %cot_ref.5, f32[16,64]{1,0:T(8,128)} %bitcast.11, f32[16,64]{1,0:T(8,128)} %bitcast.16, ...), custom_call_target="tpu_custom_call" | custom-call | flops 1073741824 | bytes 16777216 | tf_op jit(solution)/shard_map/output_part/pallas_call | solution.py:752
  36.1 0.0 collective-permute-done.3.refs_1_
  36.1 0.0 collective-permute-done.4.refs_2_
  36.1 0.0 collective-permute-done.5.refs_3_
  36.1 0.1 sum_part.1
  36.2 0.0 collective-permute-start.6
  36.2 1.1 %collective-permute-done.6 = f32[1,64]{1,0:T(1,128)S(1)} collective-permute-done((f32[1,64]{1,0:T(1,128)S(1)}, f32[1,64]{1,0:T(1,128)S(1)}, u32[]{:S(2)}, u32[]{:S(2)}) %collective-permute-start.6) | collective-permute-done | bytes 288 | tf_op jit(solution)/shard_map/ppermute | solution.py:637
  37.4 1.7 %collective-permute-start.7 = (f32[1,64]{1,0:T(1,128)S(1)}, f32[1,64]{1,0:T(1,128)S(1)}, u32[]{:S(2)}, u32[]{:S(2)}) collective-permute-start(f32[1,64]{1,0:T(1,128)S(1)} %add.18), channel_id=1, source_target_pairs={{0,8},{4,12},{8,0},{12,4},{16,24},{20,28},{24,16},{28,20},{1,9},{5... | collective-permute-start | bytes 776 | tf_op jit(solution)/shard_map/ppermute | solution.py:637
  39.0 1.5 %collective-permute-start.8 = (f32[1,64]{1,0:T(1,128)S(1)}, f32[1,64]{1,0:T(1,128)S(1)}, u32[]{:S(2)}, u32[]{:S(2)}) collective-permute-start(f32[1,64]{1,0:T(1,128)S(1)} %add.18), channel_id=1, source_target_pairs={{0,16},{4,20},{8,24},{12,28},{16,0},{20,4},{24,8},{28,12},{1,17},{... | collective-permute-start | bytes 776 | tf_op jit(solution)/shard_map/ppermute | solution.py:637
  40.6 0.3 collective-permute-start.9
  40.8 6.1 %output_part.3 = (bf16[1024,1024]{1,0:T(8,128)(2,1)}, bf16[3,1024,1024]{2,1,0:T(8,128)(2,1)}) custom-call(bf16[3,1024,1024]{2,1,0:T(8,128)(2,1)} %edge_ref.3, bf16[3,1024,1024]{2,1,0:T(8,128)(2,1)} %edge_ref.3, f32[3,3,1024]{2,1,0:T(4,128)} %taps_ref.7, bf16[1024,1024]{1,0:T(8,128)(2,1)} %cot_ref.5, ...), custom_call_target="tpu_custom_call", output_to_operand_aliasing={{0}: (11, {}), {1}: (12, {})} | custom-call | flops 1073741824 | bytes 16777216 | tf_op jit(solution)/shard_map/output_part/pallas_call | solution.py:752
  46.9 0.0 collective-permute-done.7
  46.9 0.0 collective-permute-done.8
  46.9 0.0 collective-permute-done.9
  47.0 0.6 %slice_bitcast_fusion = (f32[64,16]{0,1:T(8,128)}, f32[64,16]{0,1:T(8,128)}) fusion(f32[32,64]{1,0:T(8,128)S(1)} %broadcast_multiply_fusion), kind=kLoop, calls=%fused_computation.3 | loop fusion | bytes 16384 | tf_op jit(solution)/shard_map/transpose | solution.py:824
  (8 shorter events, 0.1 us)
Async XLA Ops:
  12.1 12.8 %copy-start = (f32[3,3,1024]{2,1,0:T(4,128)S(1)}, f32[3,3,1024]{2,1,0:T(4,128)}, u32[]{:S(2)}) copy-start(f32[3,3,1024]{2,1,0:T(4,128)} %taps_ref.7) | copy-start | bytes 110596
  12.1 12.8 %copy-start.1 = (f32[64,16]{0,1:T(8,128)S(1)}, f32[64,16]{0,1:T(8,128)}, u32[]{:S(2)}) copy-start(f32[64,16]{0,1:T(8,128)} %param.7) | copy-start | bytes 12292
  12.1 12.8 %copy-start.2 = (f32[64,16]{0,1:T(8,128)S(1)}, f32[64,16]{0,1:T(8,128)}, u32[]{:S(2)}) copy-start(f32[64,16]{0,1:T(8,128)} %param.8) | copy-start | bytes 12292
  12.1 12.6 %collective-permute-start = (bf16[40,1024]{1,0:T(8,128)(2,1)S(1)}, bf16[40,1024]{1,0:T(8,128)(2,1)S(1)}, u32[]{:S(2)}, u32[]{:S(2)}) collective-permute-start(bf16[40,1024]{1,0:T(8,128)(2,1)S(1)} %get-tuple-element.64), channel_id=1, source_target_pairs={{0,1},{1,0},{2,3},{3,2},{4,5},{5,4},{6,7},{7,6},{8,9},{9,8},{10,11... | collective-permute-start | bytes 245768 | tf_op jit(solution)/shard_map/ppermute | solution.py:637
  15.2 9.5 %collective-permute-start.1 = (bf16[40,1024]{1,0:T(8,128)(2,1)S(1)}, bf16[40,1024]{1,0:T(8,128)(2,1)S(1)}, u32[]{:S(2)}, u32[]{:S(2)}) collective-permute-start(bf16[40,1024]{1,0:T(8,128)(2,1)S(1)} %get-tuple-element.63), channel_id=1, source_target_pairs={{0,2},{1,3},{2,0},{3,1},{4,6},{5,7},{6,4},{7,5},{8,10},{9,11},{10,... | collective-permute-start | bytes 245768 | tf_op jit(solution)/shard_map/ppermute | solution.py:637
  17.8 7.0 %collective-permute-start.2 = (bf16[40,1024]{1,0:T(8,128)(2,1)S(1)}, bf16[40,1024]{1,0:T(8,128)(2,1)S(1)}, u32[]{:S(2)}, u32[]{:S(2)}) collective-permute-start(bf16[40,1024]{1,0:T(8,128)(2,1)S(1)} %get-tuple-element.62), channel_id=1, source_target_pairs={{0,3},{1,2},{2,1},{3,0},{4,7},{5,6},{6,5},{7,4},{8,11},{9,10},{10,... | collective-permute-start | bytes 245768 | tf_op jit(solution)/shard_map/ppermute | solution.py:637
  25.5 10.6 %collective-permute-start.3 = (f32[32,64]{1,0:T(8,128)S(1)}, f32[32,64]{1,0:T(8,128)S(1)}, u32[]{:S(2)}, u32[]{:S(2)}) collective-permute-start(f32[32,64]{1,0:T(8,128)S(1)} %get-tuple-element.49.refs_0_), channel_id=1, source_target_pairs={{0,1},{1,0},{2,3},{3,2},{4,5},{5,4},{6,7},{7,6},{8,9},{9,8},{10,11... | collective-permute-start | bytes 24584 | tf_op jit(solution)/shard_map/ppermute | solution.py:637
  26.7 9.4 %collective-permute-start.4 = (f32[32,64]{1,0:T(8,128)S(1)}, f32[32,64]{1,0:T(8,128)S(1)}, u32[]{:S(2)}, u32[]{:S(2)}) collective-permute-start(f32[32,64]{1,0:T(8,128)S(1)} %get-tuple-element.49.refs_0_), channel_id=1, source_target_pairs={{0,2},{1,3},{2,0},{3,1},{4,6},{5,7},{6,4},{7,5},{8,10},{9,11},{10,... | collective-permute-start | bytes 24584 | tf_op jit(solution)/shard_map/ppermute | solution.py:637
  30.0 6.1 %collective-permute-start.5 = (f32[32,64]{1,0:T(8,128)S(1)}, f32[32,64]{1,0:T(8,128)S(1)}, u32[]{:S(2)}, u32[]{:S(2)}) collective-permute-start(f32[32,64]{1,0:T(8,128)S(1)} %get-tuple-element.49.refs_0_), channel_id=1, source_target_pairs={{0,3},{1,2},{2,1},{3,0},{4,7},{5,6},{6,5},{7,4},{8,11},{9,10},{10,... | collective-permute-start | bytes 24584 | tf_op jit(solution)/shard_map/ppermute | solution.py:637
  36.2 1.1 %collective-permute-start.6 = (f32[1,64]{1,0:T(1,128)S(1)}, f32[1,64]{1,0:T(1,128)S(1)}, u32[]{:S(2)}, u32[]{:S(2)}) collective-permute-start(f32[1,64]{1,0:T(1,128)S(1)} %get-tuple-element.53), channel_id=1, source_target_pairs={{0,4},{4,0},{8,12},{12,8},{16,20},{20,16},{24,28},{28,24},{1,5},{5... | collective-permute-start | bytes 776 | tf_op jit(solution)/shard_map/ppermute | solution.py:637
  37.4 9.6 %collective-permute-start.7 = (f32[1,64]{1,0:T(1,128)S(1)}, f32[1,64]{1,0:T(1,128)S(1)}, u32[]{:S(2)}, u32[]{:S(2)}) collective-permute-start(f32[1,64]{1,0:T(1,128)S(1)} %add.18), channel_id=1, source_target_pairs={{0,8},{4,12},{8,0},{12,4},{16,24},{20,28},{24,16},{28,20},{1,9},{5... | collective-permute-start | bytes 776 | tf_op jit(solution)/shard_map/ppermute | solution.py:637
  39.0 7.9 %collective-permute-start.8 = (f32[1,64]{1,0:T(1,128)S(1)}, f32[1,64]{1,0:T(1,128)S(1)}, u32[]{:S(2)}, u32[]{:S(2)}) collective-permute-start(f32[1,64]{1,0:T(1,128)S(1)} %add.18), channel_id=1, source_target_pairs={{0,16},{4,20},{8,24},{12,28},{16,0},{20,4},{24,8},{28,12},{1,17},{... | collective-permute-start | bytes 776 | tf_op jit(solution)/shard_map/ppermute | solution.py:637
  40.6 6.4 %collective-permute-start.9 = (f32[1,64]{1,0:T(1,128)S(1)}, f32[1,64]{1,0:T(1,128)S(1)}, u32[]{:S(2)}, u32[]{:S(2)}) collective-permute-start(f32[1,64]{1,0:T(1,128)S(1)} %add.18), channel_id=1, source_target_pairs={{0,24},{4,28},{8,16},{12,20},{16,8},{20,12},{24,0},{28,4},{1,25},{... | collective-permute-start | bytes 776 | tf_op jit(solution)/shard_map/ppermute | solution.py:637

commit v10 on v9

--- a/solution.py
+++ b/solution.py
@@ -460,9 +460,25 @@
     inner_whole, grad_whole, carry_whole, short_whole, bound_ref,
     *refs,
 ):
-    mixer_ref, fgrad_ref, wide, adj, inner_t, grad_t, left_all, rate_rows, gain_rows = refs[-9:]
+    (
+        mixer_hbm, fgrad_hbm, mixer_all, fgrad_all, sems,
+        wide, adj, inner_t, grad_t, left_all, rate_rows, gain_rows,
+    ) = refs[-12:]
     fill_tables(rate_ref, gain_ref, rate_rows, gain_rows)
     count = cot_ref.shape[1] // LANES
+    total = mixer_all.shape[0]
+
+    def copies(local):
+        lanes = pl.ds(pl.multiple_of((local + first) * LANES, LANES), LANES)
+        return [
+            pltpu.make_async_copy(mixer_all.at[local], mixer_hbm.at[:, lanes], sems.at[local, 3])
+        ] + [
+            pltpu.make_async_copy(
+                fgrad_all.at[local, i], fgrad_hbm.at[i, :, lanes], sems.at[local, i]
+            )
+            for i in range(3)
+        ]
+
     parts = []
     for u in range(count):
         tile = pl.program_id(0) * count + u + first
@@ -473,18 +489,24 @@
                 taps_ref.at[:, :, lanes], cot_ref.at[:, lanes],
                 of_tile(inner_whole, tile), of_tile(grad_whole, tile),
                 carry_whole.at[tile], short_whole.at[tile], bound_ref.at[:, lanes],
-                mixer_ref.at[:, lanes], fgrad_ref.at[:, :, lanes],
+                mixer_all.at[tile - first], fgrad_all.at[tile - first], copies(tile - first),
                 wide.at[u], adj.at[u], inner_t.at[u], grad_t.at[u], left_all.at[u],
                 rate_rows, gain_rows,
             )
         )
     staggered(parts)
 
+    @pl.when(pl.program_id(0) == pl.num_programs(0) - 1)
+    def _():
+        for local in range(total):
+            for copy in copies(local):
+                copy.wait()
+
 
 def output_tile(
     tile, start_ref, edge_ref, taps_ref, cot_ref,
     inner_ref, grad_ref, carry_ref, short_ref, bound_ref,
-    mixer_ref, fgrad_ref,
+    mixer_ref, fgrad_ref, copies,
     wide, adj, inner_t, grad_t, left_all, rate_rows, gain_rows,
 ):
     tokens = cot_ref.shape[0]
@@ -513,6 +535,7 @@
             left_all[g, b * MEMBERS : (b + 1) * MEMBERS, :] = mixed[
                 g * MEMBERS : (g + 1) * MEMBERS
             ]
+        yield 0.5
     cz_parts = split(coefs * jnp.exp(-rates * (lag + 1.0)))
     ce_parts = split(coefs * jnp.exp(-rates * (LANES - 1.0 - lag)))
     for g in range(TILE_GROUPS):
@@ -565,6 +588,7 @@
         mixer_ref[at, :] = (query * inner).astype(bf16)
         adj[0, at, :] = cot_ref[at, :].astype(f32) * inner
         yield 2
+    copies[0].start()
     for b in range(blocks):
         at = slice(b * LANES, (b + 1) * LANES)
         grad = jnp.transpose(grad_t[b])
@@ -606,6 +630,7 @@
                 + taps_ref[i, 2:3, :] * adj[i, start + 2 : start + 2 + LANES, :]
             ).astype(bf16)
             yield 3
+        copies[1 + i].start()
 
 
 def resident(shape, dtype):
@@ -748,7 +773,6 @@
         wide_lanes = per * LANES
         columns = lambda j: (0, j + first // per)
         layers = lambda j: (0, 0, j + first // per)
-        mine = [pl.BlockSpec((tokens, wide_lanes), columns), pl.BlockSpec((3, tokens, wide_lanes), layers)]
         return pl.pallas_call(
             functools.partial(output_kernel, first),
             grid=(count // per,),
@@ -766,12 +790,15 @@
                 pl.BlockSpec((64, wide_lanes), columns),
             ]
             + [pl.BlockSpec(memory_space=pl.ANY)] * len(written),
-            out_specs=mine,
+            out_specs=[pl.BlockSpec(memory_space=pl.ANY)] * 2,
             out_shape=[
                 jax.ShapeDtypeStruct((tokens, channels), bf16),
                 jax.ShapeDtypeStruct((3, tokens, channels), bf16),
             ],
             scratch_shapes=[
+                pltpu.VMEM((count, tokens, LANES), bf16),
+                pltpu.VMEM((count, 3, tokens, LANES), bf16),
+                pltpu.SemaphoreType.DMA((count, 4)),
                 pltpu.VMEM((per, 3, 16, LANES), f32),
                 pltpu.VMEM((per, 3, tokens + 8, LANES), f32),
                 pltpu.VMEM((per, blocks, LANES, LANES), f32),

time: 47.8 us -> 46.9 us (0.981)
  Pallas kernels: 31.3 us -> 30.4 us
    pallas_call x2, Pallas kernels: 12.2 us -> 11.3 us  [outputs(): pl.pallas_call(functools.partial(output_kernel, first), grid=(count // pe...]
  transfers between devices with their start and end apart: 10 -> 10, of which waited for: 1 -> 1; matrix products, arithmetic and copies ran while one was open for 0% -> 0% of each run, Pallas kernels for 40% -> 39%
where the time goes in v10:
time: 46.9 us; the launch traced here: 46.7 us
  Pallas kernels  30.4 us (65%)
  starting transfers between devices  13.6 us (29%)
  waiting for transfers between devices  1.14 us (2%)
  between operations  0.85 us (2%)
  local copies, waits for them, and re-layouts  0.62 us (1%)
    ppermute x10, starting transfers between devices, swapped(): return lax.ppermute(value, axis, [(i, i ^ key) for i in range(count)])  13.6 us
    pallas_call x1, Pallas kernels, per_device(): pl.pallas_call(state_kernel, grid=(tiles // per,), in_specs=[feat_spec, t...  11.4 us
    pallas_call x2, Pallas kernels, outputs(): pl.pallas_call(functools.partial(output_kernel, first), grid=(count // pe...  11.3 us
    pallas_call x1, Pallas kernels, per_device(): pl.pallas_call(inside_kernel, grid=(tiles // inside_per,), in_specs=[whol...  6.88 us
    ppermute x10, waiting for transfers between devices, swapped(): return lax.ppermute(value, axis, [(i, i ^ key) for i in range(count)])  1.14 us
  transfers between devices with their start and end apart: 10, of which 1 were waited for; matrix products, arithmetic and copies ran while one was open for 0% of the time, Pallas kernels for 39%

profile of v10, /device:TPU:0, one launch (start us, length us, event | category | flops | bytes accessed | tf_op | source)
XLA Modules:
  0.0 46.7 jit_solution(2280692115292821671)
XLA Ops:
  0.6 11.4 %state_part.1 = (bf16[64,128,128]{2,1,0:T(8,128)(2,1)S(1)}, bf16[64,128,128]{2,1,0:T(8,128)(2,1)S(1)}, bf16[64,128,128]{2,1,0:T(8,128)(2,1)S(1)}, f32[8,8,128,12...) custom-call(bf16[3,1024,1024]{2,1,0:T(8,128)(2,1)} %edge_ref.3, ...), custom_call_target="tpu_custom_call" | custom-call | tf_op jit(solution)/shard_map/state_part/pallas_call | solution.py:693
  12.1 0.0 copy-start
  12.1 0.0 copy-start.1
  12.1 0.0 copy-start.2
  12.1 3.1 %collective-permute-start = (bf16[40,1024]{1,0:T(8,128)(2,1)S(1)}, bf16[40,1024]{1,0:T(8,128)(2,1)S(1)}, u32[]{:S(2)}, u32[]{:S(2)}) collective-permute-start(bf16[40,1024]{1,0:T(8,128)(2,1)S(1)} %get-tuple-element.64), channel_id=1, source_target_pairs={{0,1},{1,0},{2,3},{3,2},{4,5},{5,4},{6,7},{7,6},{8,9},{9,8},{10,11... | collective-permute-start | bytes 245768 | tf_op jit(solution)/shard_map/ppermute | solution.py:662
  15.2 2.6 %collective-permute-start.1 = (bf16[40,1024]{1,0:T(8,128)(2,1)S(1)}, bf16[40,1024]{1,0:T(8,128)(2,1)S(1)}, u32[]{:S(2)}, u32[]{:S(2)}) collective-permute-start(bf16[40,1024]{1,0:T(8,128)(2,1)S(1)} %get-tuple-element.63), channel_id=1, source_target_pairs={{0,2},{1,3},{2,0},{3,1},{4,6},{5,7},{6,4},{7,5},{8,10},{9,11},{10,... | collective-permute-start | bytes 245768 | tf_op jit(solution)/shard_map/ppermute | solution.py:662
  17.8 0.0 collective-permute-start.2
  17.8 6.9 %inside_part.1 = (f32[64,128,128]{2,1,0:T(8,128)S(1)}, f32[64,128,128]{2,1,0:T(8,128)S(1)}, f32[64,128]{1,0:T(8,128)S(1)}) custom-call(bf16[64,128,128]{2,1,0:T(8,128)(2,1)S(1)} %get-tuple-element.33.z_whole, bf16[64,128,128]{2,1,0:T(8,128)(2,1)S(1)} %get-tuple-element.34.eh_whole, bf16[64,128,128]{2,1,0:T(8,128)(2,1)S(1)} %get-tuple-element.35.el_whole, ...), custom_call_target="tpu_custom_call" | custom-call | flops 1879048192 | bytes 14680064 | tf_op jit(solution)/shard_map/inside_part/pallas_call | solution.py:735
  24.7 0.0 collective-permute-done
  24.7 0.0 collective-permute-done.1
  24.8 0.0 collective-permute-done.2
  24.8 0.0 copy-done
  24.8 0.0 copy-done.1
  24.8 0.7 %join_part.1 = (f32[64,1024]{1,0:T(8,128)S(1)}, f32[32,64]{1,0:T(8,128)S(1)}) custom-call(s32[1]{0:T(128)} %bitcast.2.me_ref, f32[64,1024]{1,0:T(8,128)S(1)} %get-tuple-element.40.state_ref, f32[40,1024]{1,0:T(8,128)S(1)} %get-tuple-element.41.own_ref, f32[64,128]{1,0:T(8,128)S(1)} %get-tuple-element.42.diag_ref, f32[64,128]{1,0:T(8,128)S(1)} %get-tuple-element.43.cross_ref, ...), custom_call_target="tpu_custom_call" | custom-call | tf_op jit(solution)/shard_map/join_part/pallas_call | solution.py:758
  25.5 1.1 %collective-permute-start.3 = (f32[32,64]{1,0:T(8,128)S(1)}, f32[32,64]{1,0:T(8,128)S(1)}, u32[]{:S(2)}, u32[]{:S(2)}) collective-permute-start(f32[32,64]{1,0:T(8,128)S(1)} %get-tuple-element.49.refs_0_), channel_id=1, source_target_pairs={{0,1},{1,0},{2,3},{3,2},{4,5},{5,4},{6,7},{7,6},{8,9},{9,8},{10,11... | collective-permute-start | bytes 24584 | tf_op jit(solution)/shard_map/ppermute | solution.py:662
  26.7 3.3 %collective-permute-start.4 = (f32[32,64]{1,0:T(8,128)S(1)}, f32[32,64]{1,0:T(8,128)S(1)}, u32[]{:S(2)}, u32[]{:S(2)}) collective-permute-start(f32[32,64]{1,0:T(8,128)S(1)} %get-tuple-element.49.refs_0_), channel_id=1, source_target_pairs={{0,2},{1,3},{2,0},{3,1},{4,6},{5,7},{6,4},{7,5},{8,10},{9,11},{10,... | collective-permute-start | bytes 24584 | tf_op jit(solution)/shard_map/ppermute | solution.py:662
  30.0 0.0 collective-permute-start.5
  30.0 5.6 %output_part.2 = (bf16[1024,1024]{1,0:T(8,128)(2,1)}, bf16[3,1024,1024]{2,1,0:T(8,128)(2,1)}) custom-call(bf16[3,1024,1024]{2,1,0:T(8,128)(2,1)} %edge_ref.3, bf16[3,1024,1024]{2,1,0:T(8,128)(2,1)} %edge_ref.3, f32[3,3,1024]{2,1,0:T(4,128)} %taps_ref.7, bf16[1024,1024]{1,0:T(8,128)(2,1)} %cot_ref.5, f32[16,64]{1,0:T(8,128)} %bitcast.11, f32[16,64]{1,0:T(8,128)} %bitcast.16, ...), custom_call_target="tpu_custom_call" | custom-call | flops 1073741824 | bytes 16777216 | tf_op jit(solution)/shard_map/output_part/pallas_call | solution.py:776
  35.6 0.0 collective-permute-done.3.refs_1_
  35.7 0.0 collective-permute-done.4.refs_2_
  35.7 0.0 collective-permute-done.5.refs_3_
  35.7 0.1 sum_part.1
  35.8 0.0 collective-permute-start.6
  35.8 1.1 %collective-permute-done.6 = f32[1,64]{1,0:T(1,128)S(1)} collective-permute-done((f32[1,64]{1,0:T(1,128)S(1)}, f32[1,64]{1,0:T(1,128)S(1)}, u32[]{:S(2)}, u32[]{:S(2)}) %collective-permute-start.6) | collective-permute-done | bytes 288 | tf_op jit(solution)/shard_map/ppermute | solution.py:662
  36.9 1.7 %collective-permute-start.7 = (f32[1,64]{1,0:T(1,128)S(1)}, f32[1,64]{1,0:T(1,128)S(1)}, u32[]{:S(2)}, u32[]{:S(2)}) collective-permute-start(f32[1,64]{1,0:T(1,128)S(1)} %add.18), channel_id=1, source_target_pairs={{0,8},{4,12},{8,0},{12,4},{16,24},{20,28},{24,16},{28,20},{1,9},{5... | collective-permute-start | bytes 776 | tf_op jit(solution)/shard_map/ppermute | solution.py:662
  38.6 1.5 %collective-permute-start.8 = (f32[1,64]{1,0:T(1,128)S(1)}, f32[1,64]{1,0:T(1,128)S(1)}, u32[]{:S(2)}, u32[]{:S(2)}) collective-permute-start(f32[1,64]{1,0:T(1,128)S(1)} %add.18), channel_id=1, source_target_pairs={{0,16},{4,20},{8,24},{12,28},{16,0},{20,4},{24,8},{28,12},{1,17},{... | collective-permute-start | bytes 776 | tf_op jit(solution)/shard_map/ppermute | solution.py:662
  40.1 0.2 collective-permute-start.9
  40.4 5.6 %output_part.3 = (bf16[1024,1024]{1,0:T(8,128)(2,1)}, bf16[3,1024,1024]{2,1,0:T(8,128)(2,1)}) custom-call(bf16[3,1024,1024]{2,1,0:T(8,128)(2,1)} %edge_ref.3, bf16[3,1024,1024]{2,1,0:T(8,128)(2,1)} %edge_ref.3, f32[3,3,1024]{2,1,0:T(4,128)} %taps_ref.7, bf16[1024,1024]{1,0:T(8,128)(2,1)} %cot_ref.5, ...), custom_call_target="tpu_custom_call", output_to_operand_aliasing={{0}: (11, {}), {1}: (12, {})} | custom-call | flops 1073741824 | bytes 16777216 | tf_op jit(solution)/shard_map/output_part/pallas_call | solution.py:776
  46.0 0.0 collective-permute-done.7
  46.1 0.0 collective-permute-done.8
  46.1 0.0 collective-permute-done.9
  46.1 0.6 %slice_bitcast_fusion = (f32[64,16]{0,1:T(8,128)}, f32[64,16]{0,1:T(8,128)}) fusion(f32[32,64]{1,0:T(8,128)S(1)} %broadcast_multiply_fusion), kind=kLoop, calls=%fused_computation.3 | loop fusion | bytes 16384 | tf_op jit(solution)/shard_map/transpose | solution.py:851
  (8 shorter events, 0.1 us)
Async XLA Ops:
  12.1 12.8 %copy-start = (f32[3,3,1024]{2,1,0:T(4,128)S(1)}, f32[3,3,1024]{2,1,0:T(4,128)}, u32[]{:S(2)}) copy-start(f32[3,3,1024]{2,1,0:T(4,128)} %taps_ref.7) | copy-start | bytes 110596
  12.1 12.8 %copy-start.1 = (f32[64,16]{0,1:T(8,128)S(1)}, f32[64,16]{0,1:T(8,128)}, u32[]{:S(2)}) copy-start(f32[64,16]{0,1:T(8,128)} %param.7) | copy-start | bytes 12292
  12.1 12.8 %copy-start.2 = (f32[64,16]{0,1:T(8,128)S(1)}, f32[64,16]{0,1:T(8,128)}, u32[]{:S(2)}) copy-start(f32[64,16]{0,1:T(8,128)} %param.8) | copy-start | bytes 12292
  12.1 12.6 %collective-permute-start = (bf16[40,1024]{1,0:T(8,128)(2,1)S(1)}, bf16[40,1024]{1,0:T(8,128)(2,1)S(1)}, u32[]{:S(2)}, u32[]{:S(2)}) collective-permute-start(bf16[40,1024]{1,0:T(8,128)(2,1)S(1)} %get-tuple-element.64), channel_id=1, source_target_pairs={{0,1},{1,0},{2,3},{3,2},{4,5},{5,4},{6,7},{7,6},{8,9},{9,8},{10,11... | collective-permute-start | bytes 245768 | tf_op jit(solution)/shard_map/ppermute | solution.py:662
  15.2 9.5 %collective-permute-start.1 = (bf16[40,1024]{1,0:T(8,128)(2,1)S(1)}, bf16[40,1024]{1,0:T(8,128)(2,1)S(1)}, u32[]{:S(2)}, u32[]{:S(2)}) collective-permute-start(bf16[40,1024]{1,0:T(8,128)(2,1)S(1)} %get-tuple-element.63), channel_id=1, source_target_pairs={{0,2},{1,3},{2,0},{3,1},{4,6},{5,7},{6,4},{7,5},{8,10},{9,11},{10,... | collective-permute-start | bytes 245768 | tf_op jit(solution)/shard_map/ppermute | solution.py:662
  17.8 7.0 %collective-permute-start.2 = (bf16[40,1024]{1,0:T(8,128)(2,1)S(1)}, bf16[40,1024]{1,0:T(8,128)(2,1)S(1)}, u32[]{:S(2)}, u32[]{:S(2)}) collective-permute-start(bf16[40,1024]{1,0:T(8,128)(2,1)S(1)} %get-tuple-element.62), channel_id=1, source_target_pairs={{0,3},{1,2},{2,1},{3,0},{4,7},{5,6},{6,5},{7,4},{8,11},{9,10},{10,... | collective-permute-start | bytes 245768 | tf_op jit(solution)/shard_map/ppermute | solution.py:662
  25.5 10.1 %collective-permute-start.3 = (f32[32,64]{1,0:T(8,128)S(1)}, f32[32,64]{1,0:T(8,128)S(1)}, u32[]{:S(2)}, u32[]{:S(2)}) collective-permute-start(f32[32,64]{1,0:T(8,128)S(1)} %get-tuple-element.49.refs_0_), channel_id=1, source_target_pairs={{0,1},{1,0},{2,3},{3,2},{4,5},{5,4},{6,7},{7,6},{8,9},{9,8},{10,11... | collective-permute-start | bytes 24584 | tf_op jit(solution)/shard_map/ppermute | solution.py:662
  26.7 9.0 %collective-permute-start.4 = (f32[32,64]{1,0:T(8,128)S(1)}, f32[32,64]{1,0:T(8,128)S(1)}, u32[]{:S(2)}, u32[]{:S(2)}) collective-permute-start(f32[32,64]{1,0:T(8,128)S(1)} %get-tuple-element.49.refs_0_), channel_id=1, source_target_pairs={{0,2},{1,3},{2,0},{3,1},{4,6},{5,7},{6,4},{7,5},{8,10},{9,11},{10,... | collective-permute-start | bytes 24584 | tf_op jit(solution)/shard_map/ppermute | solution.py:662
  30.0 5.7 %collective-permute-start.5 = (f32[32,64]{1,0:T(8,128)S(1)}, f32[32,64]{1,0:T(8,128)S(1)}, u32[]{:S(2)}, u32[]{:S(2)}) collective-permute-start(f32[32,64]{1,0:T(8,128)S(1)} %get-tuple-element.49.refs_0_), channel_id=1, source_target_pairs={{0,3},{1,2},{2,1},{3,0},{4,7},{5,6},{6,5},{7,4},{8,11},{9,10},{10,... | collective-permute-start | bytes 24584 | tf_op jit(solution)/shard_map/ppermute | solution.py:662
  35.8 1.1 %collective-permute-start.6 = (f32[1,64]{1,0:T(1,128)S(1)}, f32[1,64]{1,0:T(1,128)S(1)}, u32[]{:S(2)}, u32[]{:S(2)}) collective-permute-start(f32[1,64]{1,0:T(1,128)S(1)} %get-tuple-element.53), channel_id=1, source_target_pairs={{0,4},{4,0},{8,12},{12,8},{16,20},{20,16},{24,28},{28,24},{1,5},{5... | collective-permute-start | bytes 776 | tf_op jit(solution)/shard_map/ppermute | solution.py:662
  36.9 9.1 %collective-permute-start.7 = (f32[1,64]{1,0:T(1,128)S(1)}, f32[1,64]{1,0:T(1,128)S(1)}, u32[]{:S(2)}, u32[]{:S(2)}) collective-permute-start(f32[1,64]{1,0:T(1,128)S(1)} %add.18), channel_id=1, source_target_pairs={{0,8},{4,12},{8,0},{12,4},{16,24},{20,28},{24,16},{28,20},{1,9},{5... | collective-permute-start | bytes 776 | tf_op jit(solution)/shard_map/ppermute | solution.py:662
  38.6 7.4 %collective-permute-start.8 = (f32[1,64]{1,0:T(1,128)S(1)}, f32[1,64]{1,0:T(1,128)S(1)}, u32[]{:S(2)}, u32[]{:S(2)}) collective-permute-start(f32[1,64]{1,0:T(1,128)S(1)} %add.18), channel_id=1, source_target_pairs={{0,16},{4,20},{8,24},{12,28},{16,0},{20,4},{24,8},{28,12},{1,17},{... | collective-permute-start | bytes 776 | tf_op jit(solution)/shard_map/ppermute | solution.py:662
  40.1 5.9 %collective-permute-start.9 = (f32[1,64]{1,0:T(1,128)S(1)}, f32[1,64]{1,0:T(1,128)S(1)}, u32[]{:S(2)}, u32[]{:S(2)}) collective-permute-start(f32[1,64]{1,0:T(1,128)S(1)} %add.18), channel_id=1, source_target_pairs={{0,24},{4,28},{8,16},{12,20},{16,8},{20,12},{24,0},{28,4},{1,25},{... | collective-permute-start | bytes 776 | tf_op jit(solution)/shard_map/ppermute | solution.py:662

commit v11 on v10

--- a/solution.py
+++ b/solution.py
@@ -169,6 +169,7 @@
             table_all[g, :, part * LANES : (part + 1) * LANES] = jnp.concatenate(
                 [s_of, s_of, s_of, l_of, m_of, m_of, n_of, m_of], axis=0
             )
+        yield 0.5
 
     widen(feat_ref, wide, tokens)
     for b in range(blocks):

time: 46.9 us -> 46.9 us (level)
  no operation moved by 1% of the time
where the time goes in v11:
time: 46.9 us; the launch traced here: 46.7 us
  Pallas kernels  30.4 us (65%)
  starting transfers between devices  13.6 us (29%)
  waiting for transfers between devices  1.14 us (2%)
  between operations  0.85 us (2%)
  local copies, waits for them, and re-layouts  0.62 us (1%)
    ppermute x10, starting transfers between devices, swapped(): return lax.ppermute(value, axis, [(i, i ^ key) for i in range(count)])  13.6 us
    pallas_call x1, Pallas kernels, per_device(): pl.pallas_call(state_kernel, grid=(tiles // per,), in_specs=[feat_spec, t...  11.4 us
    pallas_call x2, Pallas kernels, outputs(): pl.pallas_call(functools.partial(output_kernel, first), grid=(count // pe...  11.3 us
    pallas_call x1, Pallas kernels, per_device(): pl.pallas_call(inside_kernel, grid=(tiles // inside_per,), in_specs=[whol...  6.88 us
    ppermute x10, waiting for transfers between devices, swapped(): return lax.ppermute(value, axis, [(i, i ^ key) for i in range(count)])  1.14 us
  transfers between devices with their start and end apart: 10, of which 1 were waited for; matrix products, arithmetic and copies ran while one was open for 0% of the time, Pallas kernels for 39%

profile of v11, /device:TPU:0, one launch (start us, length us, event | category | flops | bytes accessed | tf_op | source)
XLA Modules:
  0.0 46.7 jit_solution(2280692115292821671)
XLA Ops:
  0.6 11.4 %state_part.1 = (bf16[64,128,128]{2,1,0:T(8,128)(2,1)S(1)}, bf16[64,128,128]{2,1,0:T(8,128)(2,1)S(1)}, bf16[64,128,128]{2,1,0:T(8,128)(2,1)S(1)}, f32[8,8,128,12...) custom-call(bf16[3,1024,1024]{2,1,0:T(8,128)(2,1)} %edge_ref.3, ...), custom_call_target="tpu_custom_call" | custom-call | tf_op jit(solution)/shard_map/state_part/pallas_call | solution.py:694
  12.1 0.0 copy-start
  12.1 0.0 copy-start.1
  12.1 0.0 copy-start.2
  12.1 3.1 %collective-permute-start = (bf16[40,1024]{1,0:T(8,128)(2,1)S(1)}, bf16[40,1024]{1,0:T(8,128)(2,1)S(1)}, u32[]{:S(2)}, u32[]{:S(2)}) collective-permute-start(bf16[40,1024]{1,0:T(8,128)(2,1)S(1)} %get-tuple-element.64), channel_id=1, source_target_pairs={{0,1},{1,0},{2,3},{3,2},{4,5},{5,4},{6,7},{7,6},{8,9},{9,8},{10,11... | collective-permute-start | bytes 245768 | tf_op jit(solution)/shard_map/ppermute | solution.py:663
  15.2 2.6 %collective-permute-start.1 = (bf16[40,1024]{1,0:T(8,128)(2,1)S(1)}, bf16[40,1024]{1,0:T(8,128)(2,1)S(1)}, u32[]{:S(2)}, u32[]{:S(2)}) collective-permute-start(bf16[40,1024]{1,0:T(8,128)(2,1)S(1)} %get-tuple-element.63), channel_id=1, source_target_pairs={{0,2},{1,3},{2,0},{3,1},{4,6},{5,7},{6,4},{7,5},{8,10},{9,11},{10,... | collective-permute-start | bytes 245768 | tf_op jit(solution)/shard_map/ppermute | solution.py:663
  17.8 0.0 collective-permute-start.2
  17.8 6.9 %inside_part.1 = (f32[64,128,128]{2,1,0:T(8,128)S(1)}, f32[64,128,128]{2,1,0:T(8,128)S(1)}, f32[64,128]{1,0:T(8,128)S(1)}) custom-call(bf16[64,128,128]{2,1,0:T(8,128)(2,1)S(1)} %get-tuple-element.33.z_whole, bf16[64,128,128]{2,1,0:T(8,128)(2,1)S(1)} %get-tuple-element.34.eh_whole, bf16[64,128,128]{2,1,0:T(8,128)(2,1)S(1)} %get-tuple-element.35.el_whole, ...), custom_call_target="tpu_custom_call" | custom-call | flops 1879048192 | bytes 14680064 | tf_op jit(solution)/shard_map/inside_part/pallas_call | solution.py:736
  24.7 0.0 collective-permute-done
  24.7 0.0 collective-permute-done.1
  24.8 0.0 collective-permute-done.2
  24.8 0.0 copy-done
  24.8 0.0 copy-done.1
  24.8 0.7 %join_part.1 = (f32[64,1024]{1,0:T(8,128)S(1)}, f32[32,64]{1,0:T(8,128)S(1)}) custom-call(s32[1]{0:T(128)} %bitcast.2.me_ref, f32[64,1024]{1,0:T(8,128)S(1)} %get-tuple-element.40.state_ref, f32[40,1024]{1,0:T(8,128)S(1)} %get-tuple-element.41.own_ref, f32[64,128]{1,0:T(8,128)S(1)} %get-tuple-element.42.diag_ref, f32[64,128]{1,0:T(8,128)S(1)} %get-tuple-element.43.cross_ref, ...), custom_call_target="tpu_custom_call" | custom-call | tf_op jit(solution)/shard_map/join_part/pallas_call | solution.py:759
  25.5 1.1 %collective-permute-start.3 = (f32[32,64]{1,0:T(8,128)S(1)}, f32[32,64]{1,0:T(8,128)S(1)}, u32[]{:S(2)}, u32[]{:S(2)}) collective-permute-start(f32[32,64]{1,0:T(8,128)S(1)} %get-tuple-element.49.refs_0_), channel_id=1, source_target_pairs={{0,1},{1,0},{2,3},{3,2},{4,5},{5,4},{6,7},{7,6},{8,9},{9,8},{10,11... | collective-permute-start | bytes 24584 | tf_op jit(solution)/shard_map/ppermute | solution.py:663
  26.7 3.3 %collective-permute-start.4 = (f32[32,64]{1,0:T(8,128)S(1)}, f32[32,64]{1,0:T(8,128)S(1)}, u32[]{:S(2)}, u32[]{:S(2)}) collective-permute-start(f32[32,64]{1,0:T(8,128)S(1)} %get-tuple-element.49.refs_0_), channel_id=1, source_target_pairs={{0,2},{1,3},{2,0},{3,1},{4,6},{5,7},{6,4},{7,5},{8,10},{9,11},{10,... | collective-permute-start | bytes 24584 | tf_op jit(solution)/shard_map/ppermute | solution.py:663
  30.0 0.0 collective-permute-start.5
  30.0 5.6 %output_part.2 = (bf16[1024,1024]{1,0:T(8,128)(2,1)}, bf16[3,1024,1024]{2,1,0:T(8,128)(2,1)}) custom-call(bf16[3,1024,1024]{2,1,0:T(8,128)(2,1)} %edge_ref.3, bf16[3,1024,1024]{2,1,0:T(8,128)(2,1)} %edge_ref.3, f32[3,3,1024]{2,1,0:T(4,128)} %taps_ref.7, bf16[1024,1024]{1,0:T(8,128)(2,1)} %cot_ref.5, f32[16,64]{1,0:T(8,128)} %bitcast.11, f32[16,64]{1,0:T(8,128)} %bitcast.16, ...), custom_call_target="tpu_custom_call" | custom-call | flops 1073741824 | bytes 16777216 | tf_op jit(solution)/shard_map/output_part/pallas_call | solution.py:777
  35.6 0.0 collective-permute-done.3.refs_1_
  35.7 0.0 collective-permute-done.4.refs_2_
  35.7 0.0 collective-permute-done.5.refs_3_
  35.7 0.1 sum_part.1
  35.8 0.0 collective-permute-start.6
  35.8 1.1 %collective-permute-done.6 = f32[1,64]{1,0:T(1,128)S(1)} collective-permute-done((f32[1,64]{1,0:T(1,128)S(1)}, f32[1,64]{1,0:T(1,128)S(1)}, u32[]{:S(2)}, u32[]{:S(2)}) %collective-permute-start.6) | collective-permute-done | bytes 288 | tf_op jit(solution)/shard_map/ppermute | solution.py:663
  36.9 1.7 %collective-permute-start.7 = (f32[1,64]{1,0:T(1,128)S(1)}, f32[1,64]{1,0:T(1,128)S(1)}, u32[]{:S(2)}, u32[]{:S(2)}) collective-permute-start(f32[1,64]{1,0:T(1,128)S(1)} %add.18), channel_id=1, source_target_pairs={{0,8},{4,12},{8,0},{12,4},{16,24},{20,28},{24,16},{28,20},{1,9},{5... | collective-permute-start | bytes 776 | tf_op jit(solution)/shard_map/ppermute | solution.py:663
  38.6 1.5 %collective-permute-start.8 = (f32[1,64]{1,0:T(1,128)S(1)}, f32[1,64]{1,0:T(1,128)S(1)}, u32[]{:S(2)}, u32[]{:S(2)}) collective-permute-start(f32[1,64]{1,0:T(1,128)S(1)} %add.18), channel_id=1, source_target_pairs={{0,16},{4,20},{8,24},{12,28},{16,0},{20,4},{24,8},{28,12},{1,17},{... | collective-permute-start | bytes 776 | tf_op jit(solution)/shard_map/ppermute | solution.py:663
  40.1 0.2 collective-permute-start.9
  40.4 5.6 %output_part.3 = (bf16[1024,1024]{1,0:T(8,128)(2,1)}, bf16[3,1024,1024]{2,1,0:T(8,128)(2,1)}) custom-call(bf16[3,1024,1024]{2,1,0:T(8,128)(2,1)} %edge_ref.3, bf16[3,1024,1024]{2,1,0:T(8,128)(2,1)} %edge_ref.3, f32[3,3,1024]{2,1,0:T(4,128)} %taps_ref.7, bf16[1024,1024]{1,0:T(8,128)(2,1)} %cot_ref.5, ...), custom_call_target="tpu_custom_call", output_to_operand_aliasing={{0}: (11, {}), {1}: (12, {})} | custom-call | flops 1073741824 | bytes 16777216 | tf_op jit(solution)/shard_map/output_part/pallas_call | solution.py:777
  46.0 0.0 collective-permute-done.7
  46.1 0.0 collective-permute-done.8
  46.1 0.0 collective-permute-done.9
  46.1 0.6 %slice_bitcast_fusion = (f32[64,16]{0,1:T(8,128)}, f32[64,16]{0,1:T(8,128)}) fusion(f32[32,64]{1,0:T(8,128)S(1)} %broadcast_multiply_fusion), kind=kLoop, calls=%fused_computation.3 | loop fusion | bytes 16384 | tf_op jit(solution)/shard_map/transpose | solution.py:852
  (8 shorter events, 0.1 us)
Async XLA Ops:
  12.1 12.8 %copy-start = (f32[3,3,1024]{2,1,0:T(4,128)S(1)}, f32[3,3,1024]{2,1,0:T(4,128)}, u32[]{:S(2)}) copy-start(f32[3,3,1024]{2,1,0:T(4,128)} %taps_ref.7) | copy-start | bytes 110596
  12.1 12.8 %copy-start.1 = (f32[64,16]{0,1:T(8,128)S(1)}, f32[64,16]{0,1:T(8,128)}, u32[]{:S(2)}) copy-start(f32[64,16]{0,1:T(8,128)} %param.7) | copy-start | bytes 12292
  12.1 12.8 %copy-start.2 = (f32[64,16]{0,1:T(8,128)S(1)}, f32[64,16]{0,1:T(8,128)}, u32[]{:S(2)}) copy-start(f32[64,16]{0,1:T(8,128)} %param.8) | copy-start | bytes 12292
  12.1 12.6 %collective-permute-start = (bf16[40,1024]{1,0:T(8,128)(2,1)S(1)}, bf16[40,1024]{1,0:T(8,128)(2,1)S(1)}, u32[]{:S(2)}, u32[]{:S(2)}) collective-permute-start(bf16[40,1024]{1,0:T(8,128)(2,1)S(1)} %get-tuple-element.64), channel_id=1, source_target_pairs={{0,1},{1,0},{2,3},{3,2},{4,5},{5,4},{6,7},{7,6},{8,9},{9,8},{10,11... | collective-permute-start | bytes 245768 | tf_op jit(solution)/shard_map/ppermute | solution.py:663
  15.2 9.5 %collective-permute-start.1 = (bf16[40,1024]{1,0:T(8,128)(2,1)S(1)}, bf16[40,1024]{1,0:T(8,128)(2,1)S(1)}, u32[]{:S(2)}, u32[]{:S(2)}) collective-permute-start(bf16[40,1024]{1,0:T(8,128)(2,1)S(1)} %get-tuple-element.63), channel_id=1, source_target_pairs={{0,2},{1,3},{2,0},{3,1},{4,6},{5,7},{6,4},{7,5},{8,10},{9,11},{10,... | collective-permute-start | bytes 245768 | tf_op jit(solution)/shard_map/ppermute | solution.py:663
  17.8 7.0 %collective-permute-start.2 = (bf16[40,1024]{1,0:T(8,128)(2,1)S(1)}, bf16[40,1024]{1,0:T(8,128)(2,1)S(1)}, u32[]{:S(2)}, u32[]{:S(2)}) collective-permute-start(bf16[40,1024]{1,0:T(8,128)(2,1)S(1)} %get-tuple-element.62), channel_id=1, source_target_pairs={{0,3},{1,2},{2,1},{3,0},{4,7},{5,6},{6,5},{7,4},{8,11},{9,10},{10,... | collective-permute-start | bytes 245768 | tf_op jit(solution)/shard_map/ppermute | solution.py:663
  25.5 10.1 %collective-permute-start.3 = (f32[32,64]{1,0:T(8,128)S(1)}, f32[32,64]{1,0:T(8,128)S(1)}, u32[]{:S(2)}, u32[]{:S(2)}) collective-permute-start(f32[32,64]{1,0:T(8,128)S(1)} %get-tuple-element.49.refs_0_), channel_id=1, source_target_pairs={{0,1},{1,0},{2,3},{3,2},{4,5},{5,4},{6,7},{7,6},{8,9},{9,8},{10,11... | collective-permute-start | bytes 24584 | tf_op jit(solution)/shard_map/ppermute | solution.py:663
  26.7 9.0 %collective-permute-start.4 = (f32[32,64]{1,0:T(8,128)S(1)}, f32[32,64]{1,0:T(8,128)S(1)}, u32[]{:S(2)}, u32[]{:S(2)}) collective-permute-start(f32[32,64]{1,0:T(8,128)S(1)} %get-tuple-element.49.refs_0_), channel_id=1, source_target_pairs={{0,2},{1,3},{2,0},{3,1},{4,6},{5,7},{6,4},{7,5},{8,10},{9,11},{10,... | collective-permute-start | bytes 24584 | tf_op jit(solution)/shard_map/ppermute | solution.py:663
  30.0 5.7 %collective-permute-start.5 = (f32[32,64]{1,0:T(8,128)S(1)}, f32[32,64]{1,0:T(8,128)S(1)}, u32[]{:S(2)}, u32[]{:S(2)}) collective-permute-start(f32[32,64]{1,0:T(8,128)S(1)} %get-tuple-element.49.refs_0_), channel_id=1, source_target_pairs={{0,3},{1,2},{2,1},{3,0},{4,7},{5,6},{6,5},{7,4},{8,11},{9,10},{10,... | collective-permute-start | bytes 24584 | tf_op jit(solution)/shard_map/ppermute | solution.py:663
  35.8 1.1 %collective-permute-start.6 = (f32[1,64]{1,0:T(1,128)S(1)}, f32[1,64]{1,0:T(1,128)S(1)}, u32[]{:S(2)}, u32[]{:S(2)}) collective-permute-start(f32[1,64]{1,0:T(1,128)S(1)} %get-tuple-element.53), channel_id=1, source_target_pairs={{0,4},{4,0},{8,12},{12,8},{16,20},{20,16},{24,28},{28,24},{1,5},{5... | collective-permute-start | bytes 776 | tf_op jit(solution)/shard_map/ppermute | solution.py:663
  36.9 9.1 %collective-permute-start.7 = (f32[1,64]{1,0:T(1,128)S(1)}, f32[1,64]{1,0:T(1,128)S(1)}, u32[]{:S(2)}, u32[]{:S(2)}) collective-permute-start(f32[1,64]{1,0:T(1,128)S(1)} %add.18), channel_id=1, source_target_pairs={{0,8},{4,12},{8,0},{12,4},{16,24},{20,28},{24,16},{28,20},{1,9},{5... | collective-permute-start | bytes 776 | tf_op jit(solution)/shard_map/ppermute | solution.py:663
  38.6 7.4 %collective-permute-start.8 = (f32[1,64]{1,0:T(1,128)S(1)}, f32[1,64]{1,0:T(1,128)S(1)}, u32[]{:S(2)}, u32[]{:S(2)}) collective-permute-start(f32[1,64]{1,0:T(1,128)S(1)} %add.18), channel_id=1, source_target_pairs={{0,16},{4,20},{8,24},{12,28},{16,0},{20,4},{24,8},{28,12},{1,17},{... | collective-permute-start | bytes 776 | tf_op jit(solution)/shard_map/ppermute | solution.py:663
  40.1 5.9 %collective-permute-start.9 = (f32[1,64]{1,0:T(1,128)S(1)}, f32[1,64]{1,0:T(1,128)S(1)}, u32[]{:S(2)}, u32[]{:S(2)}) collective-permute-start(f32[1,64]{1,0:T(1,128)S(1)} %add.18), channel_id=1, source_target_pairs={{0,24},{4,28},{8,16},{12,20},{16,8},{20,12},{24,0},{28,4},{1,25},{... | collective-permute-start | bytes 776 | tf_op jit(solution)/shard_map/ppermute | solution.py:663
